TPU v7x, 128 devices: a whole 4x4x4 slice. The times are simulated.
128 devices in a mesh: row: 4 (over x), col: 2 (over core), depth: 16 (over z, y).
Axes of the slice: x: 4, y: 4, z: 4, core: 2. Of those that a mesh axis runs over, the one named last changes fastest.
Arguments:
- tokens: bfloat16 [4096, 3072], P(('col', 'depth'), 'row'), may hold values from -6 to 6
- up_weight: bfloat16 [3072, 12288], P('row', ('col', 'depth')), may hold values from -0.109375 to 0.109375
- down_weight: bfloat16 [12288, 3072], P(('col', 'depth'), 'row'), may hold values from -0.0546875 to 0.0546875
- out_grad: bfloat16 [4096, 3072], P(('col', 'depth'), 'row'), may hold values from -6 to 6
Outputs:
- mixed: bfloat16 [4096, 3072], P(('col', 'depth'), 'row')
- input_grad: bfloat16 [4096, 3072], P(('col', 'depth'), 'row')
- up_grad: float32 [3072, 12288], P('row', ('col', 'depth'))
- down_grad: float32 [12288, 3072], P(('col', 'depth'), 'row')
All inputs are finite; a program needn't handle non-finite values.
Results may differ from a plain program's by a relative error of at most 0.029.
Values may be sent and summed in bfloat16 or wider, within the bound.
No kernel may reach another device: no remote copies, remote signals or barrier semaphores. Data moves between devices by JAX's collectives and lax.ppermute only.
A program may use at most 128 MiB of HBM per device.

v0:
```python
import jax
import jax.numpy as jnp
from jax import lax
from jax.experimental import pallas as pl
from jax.experimental.pallas import tpu as pltpu
from jax.sharding import PartitionSpec as P

BF = jnp.bfloat16
F32 = jnp.float32


def gelu_value(value):
    return value * 0.5 * (1.0 + lax.erf(value * 0.7071067811865476))


def gelu_slope(value):
    return (
        0.5 * (1.0 + lax.erf(value * 0.7071067811865476))
        + value * jnp.exp(-0.5 * value * value) * 0.3989422804014327
    )


def product(left, right, left_dim, right_dim):
    return lax.dot_general(
        left, right, (((left_dim,), (right_dim,)), ((), ())), preferred_element_type=F32
    )


def local_kernel(body, grid, in_specs, out_specs, out_shape, *arrays):
    return pl.pallas_call(
        body,
        grid=grid,
        in_specs=in_specs,
        out_specs=out_specs,
        out_shape=out_shape,
        compiler_params=pltpu.CompilerParams(vmem_limit_bytes=40 * 2**20),
        cost_estimate=pl.CostEstimate(flops=1, bytes_accessed=1, transcendentals=0),
    )(*arrays)


def forward(pair, up, down):
    _, rows, features = pair.shape
    units = up.shape[1]
    tile = units // 3

    def body(pair_ref, up_ref, down_ref, act_ref, grad_ref):
        hidden = product(pair_ref[0], up_ref[...], 1, 0)
        act_grad = product(pair_ref[1], down_ref[...], 1, 1)
        act_ref[...] = gelu_value(hidden).astype(BF)
        grad_ref[...] = (act_grad * gelu_slope(hidden)).astype(BF)

    out = pl.BlockSpec((rows, tile), lambda i: (0, i))
    shape = jax.ShapeDtypeStruct((rows, units), BF)
    return local_kernel(
        body,
        (3,),
        [
            pl.BlockSpec((2, rows, features), lambda i: (0, 0, 0)),
            pl.BlockSpec((features, tile), lambda i: (0, i)),
            pl.BlockSpec((tile, features), lambda i: (i, 0)),
        ],
        [out, out],
        [shape, shape],
        pair,
        up,
        down,
    )


def backward(acts, grads, up, down):
    rows, units = acts.shape
    features = up.shape[0]
    tile = features // 4

    def body(act_ref, grad_ref, up_ref, down_ref, out_ref):
        out_ref[0] = product(act_ref[...], down_ref[...], 1, 0).astype(BF)
        out_ref[1] = product(grad_ref[...], up_ref[...], 1, 1).astype(BF)

    whole = pl.BlockSpec((rows, units), lambda i: (0, 0))
    return local_kernel(
        body,
        (4,),
        [
            whole,
            whole,
            pl.BlockSpec((tile, units), lambda i: (i, 0)),
            pl.BlockSpec((units, tile), lambda i: (0, i)),
        ],
        pl.BlockSpec((2, rows, tile), lambda i: (0, 0, i)),
        jax.ShapeDtypeStruct((2, rows, features), BF),
        acts,
        grads,
        up,
        down,
    )


def weight_sums(sets, acts, grads, core):
    units = acts[0].shape[1] // 2
    features = sets[0].shape[2]
    tile = features // 4
    count = len(sets)

    def body(*refs):
        down_ref, up_ref = refs[-2:]
        down_sum = up_sum = None
        for i in range(count):
            down_part = product(refs[count + i][...], refs[i][1], 0, 0)
            up_part = product(refs[i][0], refs[2 * count + i][...], 0, 0)
            down_sum = down_part if i == 0 else down_sum + down_part
            up_sum = up_part if i == 0 else up_sum + up_part
        down_ref[...] = down_sum.astype(BF)
        up_ref[...] = up_sum.astype(BF)

    halves = [pl.BlockSpec((a.shape[0], units), lambda i: (0, core)) for a in acts]
    return local_kernel(
        body,
        (4,),
        [pl.BlockSpec((2, s.shape[1], tile), lambda i: (0, 0, i)) for s in sets] + halves + halves,
        [
            pl.BlockSpec((units, tile), lambda i: (0, i)),
            pl.BlockSpec((tile, units), lambda i: (i, 0)),
        ],
        [
            jax.ShapeDtypeStruct((units, features), BF),
            jax.ShapeDtypeStruct((features, units), BF),
        ],
        *sets,
        *acts,
        *grads,
    )


def along_x(value, hop):
    pairs = []
    for row in range(4):
        for core in range(2):
            to = (row + (hop if core == 0 else -hop)) % 4
            pairs.append((row * 2 + core, to * 2 + core))
    return lax.ppermute(value, ("row", "col"), pairs)


def across(value):
    return lax.ppermute(value, "col", [(0, 1), (1, 0)])


def plane(value, phase, hop):
    pairs = []
    for core in range(2):
        for z in range(4):
            for y in range(4):
                if core == phase:
                    to = ((z + hop) % 4) * 4 + y
                else:
                    to = z * 4 + (y + hop) % 4
                pairs.append((core * 16 + z * 4 + y, core * 16 + to))
    return lax.ppermute(value, ("col", "depth"), pairs)


def held(*values):
    return lax.optimization_barrier(values)


def on_device(tokens, up_weight, down_weight, out_grad):
    x = lax.axis_index("row")
    sign = 1 - 2 * lax.axis_index("col")
    rows, width = tokens.shape
    sub, half = rows // 4, rows // 2
    hid = up_weight.shape[1]

    turned = (0, 3, 2, 1)

    both = jnp.stack([tokens, out_grad]).reshape(2, 4, sub, width)

    def piece(k):
        return lax.dynamic_index_in_dim(both, (x + sign * k + 4) % 4, 1, keepdims=False)

    got = [piece(0)] + [along_x(piece(k), k) for k in (1, 2, 3)]
    own = jnp.stack(
        [
            jnp.concatenate([got[k][0] for k in range(4)], axis=1),
            jnp.concatenate([got[k][1] for k in turned], axis=1),
        ]
    )

    ups, downs = [up_weight], [down_weight]
    ups.append(along_x(ups[-1], 1))
    own, ups[1] = held(own, ups[1])

    ups.append(along_x(ups[1], 1))
    downs.append(along_x(downs[0], -1))
    first = jnp.concatenate([own] + [plane(own, 0, hop) for hop in (1, 2, 3)], axis=1)
    first, ups[2], downs[1] = held(first, ups[2], downs[1])

    def join(parts, axis):
        return parts[0] if len(parts) == 1 else jnp.concatenate(parts, axis=axis)

    ups.append(along_x(ups[2], 1))
    downs.append(along_x(downs[1], -1))
    downs.append(along_x(downs[2], -1))
    up_early, down_early = across(join(ups[:3], 0)), across(join(downs[:2], 1))
    left, right = plane(first, 1, 1), plane(first, 1, -1)
    left, right, ups[3], downs[2], downs[3], up_early, down_early = held(
        left, right, ups[3], downs[2], downs[3], up_early, down_early
    )

    far = [plane(left[:, :half], 1, 1), plane(right[:, half:], 1, -1)]
    up_late, down_late = across(ups[3]), across(join(downs[2:], 1))

    def rows_of(value, k):
        return lax.slice_in_dim(value, k * width, (k + 1) * width, axis=0)

    def columns(value, k):
        return lax.slice_in_dim(value, k * width, (k + 1) * width, axis=1)

    up = held(
        join(ups, 0), join([rows_of(up_early, 0), up_late, up_early[2 * width :], rows_of(up_early, 1)], 0)
    )
    down = held(
        join(downs, 1),
        join([columns(down_early, 0), columns(down_late, 1), columns(down_late, 0), columns(down_early, 1)], 1),
    )
    up, down = held(join(up, 1), join(down, 0))

    near = join([first, left, right], 1)
    near_acts, near_grads = forward(near, up, down)
    *far, near_acts, near_grads = held(*far, near_acts, near_grads)
    far = join(far, 1)
    far_acts, far_grads = forward(far, up, down)

    far_sums = backward(far_acts, far_grads, up, down)
    far_sums, near_acts, near_grads, far_acts, far_grads = held(
        far_sums, near_acts, near_grads, far_acts, far_grads
    )
    far_back = [plane(far_sums[:, :half], 1, -1), plane(far_sums[:, half:], 1, 1)]
    sets, acts, grads = (near, far), (near_acts, far_acts), (near_grads, far_grads)
    down_theirs, up_theirs = (across(value) for value in weight_sums(sets, acts, grads, 1))
    near_sums = backward(near_acts, near_grads, up, down)
    down_mine, up_mine = weight_sums(sets, acts, grads, 0)
    *far_back, near_sums, down_theirs, up_theirs, down_mine, up_mine = held(
        *far_back, near_sums, down_theirs, up_theirs, down_mine, up_mine
    )

    def total(*parts):
        value = parts[0].astype(F32)
        for part in parts[1:]:
            value = value + part.astype(F32)
        return value

    here, left, right = (near_sums[:, i * rows : (i + 1) * rows] for i in range(3))
    left = join([total(left[:, :half], far_back[0]).astype(BF), left[:, half:]], 1)
    right = join([right[:, :half], total(right[:, half:], far_back[1]).astype(BF)], 1)
    left, right = plane(left, 1, -1), plane(right, 1, 1)

    def down_part(k, *more):
        return total(columns(down_mine, k), columns(down_theirs, turned[k]), *more)

    def up_part(k, *more):
        return total(rows_of(up_mine, k), rows_of(up_theirs, turned[k]), *more)

    down_grad = along_x(down_part(1).astype(BF), -1)
    up_grad = along_x(up_part(1).astype(BF), 1)
    down_grad = along_x(down_part(2, down_grad).astype(BF), -1)
    up_grad = along_x(up_part(2, up_grad).astype(BF), 1)
    left, right, down_grad, up_grad = held(left, right, down_grad, up_grad)

    sums = total(here, left, right).astype(BF).reshape(2, 4, sub, 4 * width)
    down_grad = along_x(down_part(3, down_grad).astype(BF), -1)
    up_grad = along_x(up_part(3, up_grad).astype(BF), 1)
    end = total(sums[:, 0], *(plane(sums[:, hop], 0, -hop) for hop in (1, 2, 3)))
    end, down_grad, up_grad = held(end.astype(BF), down_grad, up_grad)
    down_grad, up_grad = down_part(0, down_grad), up_part(0, up_grad)

    out = jnp.zeros((2, rows, width), BF)
    for k in range(4):
        sent = jnp.stack([columns(end[0], turned[k]), columns(end[1], k)])
        got = along_x(sent, -k) if k else sent
        at = (x + sign * k + 4) % 4 * sub
        out = lax.dynamic_update_slice_in_dim(out, got, at, axis=1)
    return out[0], out[1], up_grad, down_grad


def solution(mesh):
    spec = P(("col", "depth"), "row")
    wide = P("row", ("col", "depth"))
    return jax.shard_map(
        on_device,
        mesh=mesh,
        in_specs=(spec, wide, spec, spec),
        out_specs=(spec, spec, wide, spec),
        check_vma=False,
    )
```

profile of v0, /device:TPU:0, one launch (start us, length us, event | category | flops | bytes accessed | tf_op | source)
XLA Modules:
  0.0 188.5 jit_solution(10301229196121523646)
XLA Ops:
  1.8 2.9 %collective-permute-start.2 = (bf16[2,32,768]{2,1,0:T(8,128)(2,1)S(1)}, bf16[2,32,768]{2,1,0:T(8,128)(2,1)S(1)}, u32[]{:S(2)}, u32[]{:S(2)}) collective-permute-start(bf16[2,32,768]{2,1,0:T(8,128)(2,1)S(1)} %get-tuple-element.125), channel_id=1, source_target_pairs={{0,96},{16,48},{32,0},{48,80},{64,32},{80,112},{96,64},{112,16},{1... | collective-permute-start | bytes 294920 | tf_op jit(solution)/shard_map/ppermute | solution.py:140
  6.4 1.8 collective-permute-start.3
  8.8 2.1 %collective-permute-done.1 = bf16[2,32,768]{2,1,0:T(8,128)(2,1)S(1)} collective-permute-done((bf16[2,32,768]{2,1,0:T(8,128)(2,1)S(1)}, bf16[2,32,768]{2,1,0:T(8,128)(2,1)S(1)}, u32[]{:S(2)}, u32[]{:S(2)}) %collective-permute-start.1) | collective-permute-done | bytes 98336 | tf_op jit(solution)/shard_map/ppermute | solution.py:140
  12.0 6.2 %collective-permute-done.3 = bf16[768,384]{1,0:T(8,128)(2,1)S(1)} collective-permute-done((bf16[768,384]{1,0:T(8,128)(2,1)}, bf16[768,384]{1,0:T(8,128)(2,1)S(1)}, u32[]{:S(2)}, u32[]{:S(2)}) %collective-permute-start.3) | collective-permute-done | bytes 589856 | tf_op jit(solution)/shard_map/ppermute | solution.py:140
  18.2 4.0 %collective-permute-start.6 = (bf16[2,32,3072]{2,1,0:T(8,128)(2,1)S(1)}, bf16[2,32,3072]{2,1,0:T(8,128)(2,1)S(1)}, u32[]{:S(2)}, u32[]{:S(2)}) collective-permute-start(bf16[2,32,3072]{2,1,0:T(8,128)(2,1)S(1)} %pad_maximum_fusion.12), channel_id=1, source_target_pairs={{0,12},{1,13},{2,14},{3,15},{4,0},{5,1},{6,2},{7,3},{8,4},{9,5},{1... | collective-permute-start | bytes 1179656 | tf_op jit(solution)/shard_map/ppermute | solution.py:157
  22.2 1.3 collective-permute-start.4
  24.1 1.4 collective-permute-start.7
  25.5 6.2 %collective-permute-done.6 = bf16[2,32,3072]{2,1,0:T(8,128)(2,1)S(1)} collective-permute-done((bf16[2,32,3072]{2,1,0:T(8,128)(2,1)S(1)}, bf16[2,32,3072]{2,1,0:T(8,128)(2,1)S(1)}, u32[]{:S(2)}, u32[]{:S(2)}) %collective-permute-start.6) | collective-permute-done | bytes 393248 | tf_op jit(solution)/shard_map/ppermute | solution.py:157
  31.7 3.7 %collective-permute-done.4 = bf16[2,32,3072]{2,1,0:T(8,128)(2,1)S(1)} collective-permute-done((bf16[2,32,3072]{2,1,0:T(8,128)(2,1)S(1)}, bf16[2,32,3072]{2,1,0:T(8,128)(2,1)S(1)}, u32[]{:S(2)}, u32[]{:S(2)}) %collective-permute-start.4) | collective-permute-done | bytes 393248 | tf_op jit(solution)/shard_map/ppermute | solution.py:157
  38.1 2.0 %collective-permute-start.9 = (bf16[2,128,3072]{2,1,0:T(8,128)(2,1)S(1)}, bf16[2,128,3072]{2,1,0:T(8,128)(2,1)S(1)}, u32[]{:S(2)}, u32[]{:S(2)}) collective-permute-start(bf16[2,128,3072]{2,1,0:T(8,128)(2,1)S(1)} %pad_maximum_fusion.7), channel_id=1, source_target_pairs={{0,1},{1,2},{2,3},{3,0},{4,5},{5,6},{6,7},{7,4},{8,9},{9,10},{10,1... | collective-permute-start | bytes 4718600 | tf_op jit(solution)/shard_map/ppermute | solution.py:157
  40.1 1.3 collective-permute-start.10
  41.5 2.1 %collective-permute-start.12 = (bf16[384,768]{1,0:T(8,128)(2,1)S(1)}, bf16[384,768]{1,0:T(8,128)(2,1)S(1)}, u32[]{:S(2)}, u32[]{:S(2)}) collective-permute-start(bf16[384,768]{1,0:T(8,128)(2,1)S(1)} %collective-permute-done.8), channel_id=1, source_target_pairs={{0,96},{16,48},{32,0},{48,80},{64,32},{80,112},{96,64},{112,16},{1... | collective-permute-start | bytes 1769480 | tf_op jit(solution)/shard_map/ppermute | solution.py:140
  43.6 4.9 %collective-permute-done.11 = bf16[768,384]{1,0:T(8,128)(2,1)S(1)} collective-permute-done((bf16[768,384]{1,0:T(8,128)(2,1)S(1)}, bf16[768,384]{1,0:T(8,128)(2,1)S(1)}, u32[]{:S(2)}, u32[]{:S(2)}) %collective-permute-start.11) | collective-permute-done | bytes 589856 | tf_op jit(solution)/shard_map/ppermute | solution.py:140
  48.5 2.8 %collective-permute-done.12 = bf16[384,768]{1,0:T(8,128)(2,1)S(1)} collective-permute-done((bf16[384,768]{1,0:T(8,128)(2,1)S(1)}, bf16[384,768]{1,0:T(8,128)(2,1)S(1)}, u32[]{:S(2)}, u32[]{:S(2)}) %collective-permute-start.12) | collective-permute-done | bytes 589856 | tf_op jit(solution)/shard_map/ppermute | solution.py:140
  51.3 3.3 %collective-permute-start.13 = (bf16[384,768]{1,0:T(8,128)(2,1)S(1)}, bf16[384,768]{1,0:T(8,128)(2,1)S(1)}, u32[]{:S(2)}, u32[]{:S(2)}) collective-permute-start(bf16[384,768]{1,0:T(8,128)(2,1)S(1)} %collective-permute-done.12), channel_id=1, source_target_pairs={{0,96},{16,48},{32,0},{48,80},{64,32},{80,112},{96,64},{112,16},{1... | collective-permute-start | bytes 1769480 | tf_op jit(solution)/shard_map/ppermute | solution.py:140
  54.7 7.3 %collective-permute-done.13 = bf16[384,768]{1,0:T(8,128)(2,1)S(1)} collective-permute-done((bf16[384,768]{1,0:T(8,128)(2,1)S(1)}, bf16[384,768]{1,0:T(8,128)(2,1)S(1)}, u32[]{:S(2)}, u32[]{:S(2)}) %collective-permute-start.13) | collective-permute-done | bytes 589856 | tf_op jit(solution)/shard_map/ppermute | solution.py:140
  62.3 2.2 %collective-permute-start.18 = (bf16[768,384]{1,0:T(8,128)(2,1)S(1)}, bf16[768,384]{1,0:T(8,128)(2,1)S(1)}, u32[]{:S(2)}, u32[]{:S(2)}) collective-permute-start(bf16[768,384]{1,0:T(8,128)(2,1)S(1)} %collective-permute-done.11), channel_id=1, source_target_pairs={{0,16},{16,0},{1,17},{17,1},{2,18},{18,2},{3,19},{19,3},{4,20},{20... | collective-permute-start | bytes 1769480 | tf_op jit(solution)/shard_map/ppermute | solution.py:144
  64.6 1.7 collective-permute-start.16
  66.3 1.7 collective-permute-start.17
  68.6 1.9 %copy-done.1 = bf16[2,384,3072]{2,1,0:T(8,128)(2,1)} copy-done((bf16[2,384,3072]{2,1,0:T(8,128)(2,1)}, bf16[2,384,3072]{2,1,0:T(8,128)(2,1)S(1)}, u32[]{:S(2)}) %copy-start.1) | copy-done | bytes 4718616
  72.3 1.6 collective-permute-done.19
  74.2 2.7 %pad_maximum_fusion.1.down_ref = bf16[768,3072]{1,0:T(8,128)(2,1)} fusion(bf16[384,3072]{1,0:T(8,128)(2,1)S(1)} %pad_maximum_fusion.5, bf16[384,3072]{1,0:T(8,128)(2,1)S(1)} %pad_maximum_fusion.4), kind=kLoop, calls=%fused_computation.1 | loop fusion | flops 9437184 | bytes 9437184 | tf_op jit(solution)/shard_map/concatenate | solution.py:196
  78.0 6.4 %shard_map.75 = (bf16[384,768]{1,0:T(8,128)(2,1)S(1)}, bf16[384,768]{1,0:T(8,128)(2,1)S(1)}) custom-call(bf16[2,384,3072]{2,1,0:T(8,128)(2,1)S(1)} %bitcast.73, bf16[3072,768]{1,0:T(8,128)(2,1)S(1)} %pad_maximum_fusion.up_ref, bf16[768,3072]{1,0:T(8,128)(2,1)} %pad_maximum_fusion.1.down_ref), custom_call_target="tpu_custom_call" | custom-call | flops 1 | bytes 1 | tf_op jit(solution)/shard_map/pallas_call | solution.py:30
  84.5 3.0 %shard_map.76 = (bf16[128,768]{1,0:T(8,128)(2,1)S(1)}, bf16[128,768]{1,0:T(8,128)(2,1)S(1)}) custom-call(bf16[2,128,3072]{2,1,0:T(8,128)(2,1)S(1)} %constant_dynamic-update-slice_fusion.3.pair_ref.refs_1_, bf16[3072,768]{1,0:T(8,128)(2,1)S(1)} %pad_maximum_fusion.up_ref, bf16[768,3072]{1,0:T(8,128)(2,1)S(1)} %copy-done), custom_call_target="tpu_custom_call" | custom-call | flops 1 | bytes 1 | tf_op jit(solution)/shard_map/pallas_call | solution.py:30
  87.5 3.1 %shard_map.77 = bf16[2,128,3072]{2,1,0:T(8,128)(2,1)S(1)} custom-call(bf16[128,768]{1,0:T(8,128)(2,1)S(1)} %get-tuple-element.82.act_ref.refs_3_, bf16[128,768]{1,0:T(8,128)(2,1)S(1)} %get-tuple-element.83.grad_ref.refs_5_, bf16[3072,768]{1,0:T(8,128)(2,1)S(1)} %pad_maximum_fusion.up_ref, bf16[768,3072]{1,0:T(8,128)(2,1)S(1)} %copy-done), custom_call_target="tpu_custom_call" | custom-call | flops 1 | bytes 1 | tf_op jit(solution)/shard_map/pallas_call | solution.py:30
  90.6 6.1 %shard_map.79 = (bf16[384,3072]{1,0:T(8,128)(2,1)}, bf16[3072,384]{1,0:T(8,128)(2,1)}) custom-call(bf16[2,384,3072]{2,1,0:T(8,128)(2,1)S(1)} %bitcast.75, bf16[2,128,3072]{2,1,0:T(8,128)(2,1)S(1)} %constant_dynamic-update-slice_fusion.3.pair_ref.refs_1_, bf16[384,768]{1,0:T(8,128)(2,1)S(1)} %get-tuple-element.80.act_ref.refs_2_, ...), custom_call_target="tpu_custom_call" | custom-call | flops 1 | bytes 1 | tf_op jit(solution)/shard_map/pallas_call | solution.py:30
  97.3 1.2 fusion.12
  98.5 2.3 %collective-permute-start.20 = (bf16[2,64,3072]{2,1,0:T(8,128)(2,1)}, bf16[2,64,3072]{2,1,0:T(8,128)(2,1)S(1)}, u32[]{:S(2)}, u32[]{:S(2)}) collective-permute-start(bf16[2,64,3072]{2,1,0:T(8,128)(2,1)} %get-tuple-element.113), channel_id=1, source_target_pairs={{0,3},{1,0},{2,1},{3,2},{4,7},{5,4},{6,5},{7,6},{8,11},{9,8},{10,9... | collective-permute-start | bytes 2359304 | tf_op jit(solution)/shard_map/ppermute | solution.py:157
  100.8 6.1 %shard_map.78 = bf16[2,384,3072]{2,1,0:T(8,128)(2,1)S(1)} custom-call(bf16[384,768]{1,0:T(8,128)(2,1)S(1)} %get-tuple-element.80.act_ref.refs_2_, bf16[384,768]{1,0:T(8,128)(2,1)S(1)} %get-tuple-element.81.grad_ref.refs_4_, bf16[3072,768]{1,0:T(8,128)(2,1)S(1)} %pad_maximum_fusion.up_ref, bf16[768,3072]{1,0:T(8,128)(2,1)} %pad_maximum_fusion.1.down_ref), custom_call_target="tpu_custom_call" | custom-call | flops 1 | bytes 1 | tf_op jit(solution)/shard_map/pallas_call | solution.py:30
  107.0 5.4 %shard_map.80 = (bf16[384,3072]{1,0:T(8,128)(2,1)S(1)}, bf16[3072,384]{1,0:T(8,128)(2,1)S(1)}) custom-call(bf16[2,384,3072]{2,1,0:T(8,128)(2,1)S(1)} %bitcast.77, bf16[2,128,3072]{2,1,0:T(8,128)(2,1)S(1)} %constant_dynamic-update-slice_fusion.3.pair_ref.refs_1_, bf16[384,768]{1,0:T(8,128)(2,1)S(1)} %get-tuple-element.80.act_ref.refs_2_, ...), custom_call_target="tpu_custom_call" | custom-call | flops 1 | bytes 1 | tf_op jit(solution)/shard_map/pallas_call | solution.py:30
  112.4 1.8 collective-permute-done.21
  115.1 1.5 collective-permute-start.24
  116.7 3.2 %collective-permute-start.26 = (bf16[384,768]{1,0:T(8,128)(2,1)S(1)}, bf16[384,768]{1,0:T(8,128)(2,1)S(1)}, u32[]{:S(2)}, u32[]{:S(2)}) collective-permute-start(bf16[384,768]{1,0:T(8,128)(2,1)S(1)} %add_convert_fusion.8), channel_id=1, source_target_pairs={{0,96},{16,48},{32,0},{48,80},{64,32},{80,112},{96,64},{112,16},{1... | collective-permute-start | bytes 1769480 | tf_op jit(solution)/shard_map/ppermute | solution.py:140
  121.2 12.2 %collective-permute-done.26 = bf16[384,768]{1,0:T(8,128)(2,1)S(1)} collective-permute-done((bf16[384,768]{1,0:T(8,128)(2,1)S(1)}, bf16[384,768]{1,0:T(8,128)(2,1)S(1)}, u32[]{:S(2)}, u32[]{:S(2)}) %collective-permute-start.26) | collective-permute-done | bytes 589856 | tf_op jit(solution)/shard_map/ppermute | solution.py:140
  134.5 3.7 %collective-permute-start.27 = (bf16[384,768]{1,0:T(8,128)(2,1)}, bf16[384,768]{1,0:T(8,128)(2,1)}, u32[]{:S(2)}, u32[]{:S(2)}) collective-permute-start(bf16[384,768]{1,0:T(8,128)(2,1)} %add_convert_fusion.7), channel_id=1, source_target_pairs={{0,96},{16,48},{32,0},{48,80},{64,32},{80,112},{96,64},{112,16},{1... | collective-permute-start | bytes 1769480 | tf_op jit(solution)/shard_map/ppermute | solution.py:140
  139.2 12.5 %collective-permute-done.27 = bf16[384,768]{1,0:T(8,128)(2,1)} collective-permute-done((bf16[384,768]{1,0:T(8,128)(2,1)}, bf16[384,768]{1,0:T(8,128)(2,1)}, u32[]{:S(2)}, u32[]{:S(2)}) %collective-permute-start.27) | collective-permute-done | bytes 589856 | tf_op jit(solution)/shard_map/ppermute | solution.py:140
  151.7 3.3 %add_convert_fusion = bf16[2,128,3072]{2,1,0:T(8,128)(2,1)S(1)} fusion(bf16[2,128,3072]{2,1,0:T(8,128)(2,1)} %collective-permute-done.25, bf16[2,128,3072]{2,1,0:T(8,128)(2,1)} %collective-permute-done.24, bf16[2,384,3072]{2,1,0:T(8,128)(2,1)} %copy-done.2), kind=kLoop, calls=%fused_computation.2 | loop fusion | flops 4718592 | bytes 6291456 | tf_op jit(solution)/shard_map/convert_element_type | solution.py:267
  155.2 3.0 %collective-permute-start.31 = (bf16[2,32,3072]{2,1,0:T(8,128)(2,1)S(1)}, bf16[2,32,3072]{2,1,0:T(8,128)(2,1)S(1)}, u32[]{:S(2)}, u32[]{:S(2)}) collective-permute-start(bf16[2,32,3072]{2,1,0:T(8,128)(2,1)S(1)} %get-tuple-element.110), channel_id=1, source_target_pairs={{0,8},{1,9},{2,10},{3,11},{4,12},{5,13},{6,14},{7,15},{8,0},{9,1},... | collective-permute-start | bytes 1179656 | tf_op jit(solution)/shard_map/ppermute | solution.py:157
  158.2 1.2 collective-permute-start.30
  159.3 1.3 add_convert_fusion.4
  160.6 3.8 %collective-permute-start.33 = (bf16[384,768]{1,0:T(8,128)(2,1)S(1)}, bf16[384,768]{1,0:T(8,128)(2,1)S(1)}, u32[]{:S(2)}, u32[]{:S(2)}) collective-permute-start(bf16[384,768]{1,0:T(8,128)(2,1)S(1)} %add_convert_fusion.4), channel_id=1, source_target_pairs={{0,96},{16,48},{32,0},{48,80},{64,32},{80,112},{96,64},{112,16},{1... | collective-permute-start | bytes 1769480 | tf_op jit(solution)/shard_map/ppermute | solution.py:140
  164.4 1.3 add_convert_fusion.3
  165.8 2.6 %collective-permute-done.32 = bf16[2,32,3072]{2,1,0:T(8,128)(2,1)S(1)} collective-permute-done((bf16[2,32,3072]{2,1,0:T(8,128)(2,1)S(1)}, bf16[2,32,3072]{2,1,0:T(8,128)(2,1)S(1)}, u32[]{:S(2)}, u32[]{:S(2)}) %collective-permute-start.32) | collective-permute-done | bytes 393248 | tf_op jit(solution)/shard_map/ppermute | solution.py:157
  169.5 7.3 %collective-permute-done.33 = bf16[384,768]{1,0:T(8,128)(2,1)S(1)} collective-permute-done((bf16[384,768]{1,0:T(8,128)(2,1)S(1)}, bf16[384,768]{1,0:T(8,128)(2,1)S(1)}, u32[]{:S(2)}, u32[]{:S(2)}) %collective-permute-start.33) | collective-permute-done | bytes 589856 | tf_op jit(solution)/shard_map/ppermute | solution.py:140
  176.9 3.7 %collective-permute-start.35 = (bf16[2,32,768]{2,1,0:T(8,128)(2,1)S(1)}, bf16[2,32,768]{2,1,0:T(8,128)(2,1)S(1)}, u32[]{:S(2)}, u32[]{:S(2)}) collective-permute-start(bf16[2,32,768]{2,1,0:T(8,128)(2,1)S(1)} %pad_maximum_fusion.13), channel_id=1, source_target_pairs={{0,96},{16,48},{32,0},{48,80},{64,32},{80,112},{96,64},{112,16},{1... | collective-permute-start | bytes 294920 | tf_op jit(solution)/shard_map/ppermute | solution.py:140
  181.7 1.2 convert_add_fusion.1
  182.9 1.2 convert_add_fusion
  184.2 2.7 %collective-permute-done.36 = bf16[2,32,768]{2,1,0:T(8,128)(2,1)S(1)} collective-permute-done((bf16[2,32,768]{2,1,0:T(8,128)(2,1)S(1)}, bf16[2,32,768]{2,1,0:T(8,128)(2,1)S(1)}, u32[]{:S(2)}, u32[]{:S(2)}) %collective-permute-start.36) | collective-permute-done | bytes 98336 | tf_op jit(solution)/shard_map/ppermute | solution.py:140
  (130 shorter events, 21.2 us)
Async XLA Ops:
  0.6 22.8 %copy-start.8 = (bf16[384,768]{1,0:T(8,128)(2,1)S(1)}, bf16[384,768]{1,0:T(8,128)(2,1)}, u32[]{:S(2)}) copy-start(bf16[384,768]{1,0:T(8,128)(2,1)} %param.6) | copy-start | bytes 1769476
  1.8 7.0 %collective-permute-start.2 = (bf16[2,32,768]{2,1,0:T(8,128)(2,1)S(1)}, bf16[2,32,768]{2,1,0:T(8,128)(2,1)S(1)}, u32[]{:S(2)}, u32[]{:S(2)}) collective-permute-start(bf16[2,32,768]{2,1,0:T(8,128)(2,1)S(1)} %get-tuple-element.125), channel_id=1, source_target_pairs={{0,96},{16,48},{32,0},{48,80},{64,32},{80,112},{96,64},{112,16},{1... | collective-permute-start | bytes 294920 | tf_op jit(solution)/shard_map/ppermute | solution.py:140
  4.7 6.2 %collective-permute-start.1 = (bf16[2,32,768]{2,1,0:T(8,128)(2,1)S(1)}, bf16[2,32,768]{2,1,0:T(8,128)(2,1)S(1)}, u32[]{:S(2)}, u32[]{:S(2)}) collective-permute-start(bf16[2,32,768]{2,1,0:T(8,128)(2,1)S(1)} %get-tuple-element.124), channel_id=1, source_target_pairs={{0,64},{16,80},{32,96},{48,112},{64,0},{80,16},{96,32},{112,48},{1... | collective-permute-start | bytes 294920 | tf_op jit(solution)/shard_map/ppermute | solution.py:140
  5.5 6.4 %collective-permute-start = (bf16[2,32,768]{2,1,0:T(8,128)(2,1)S(1)}, bf16[2,32,768]{2,1,0:T(8,128)(2,1)S(1)}, u32[]{:S(2)}, u32[]{:S(2)}) collective-permute-start(bf16[2,32,768]{2,1,0:T(8,128)(2,1)S(1)} %get-tuple-element.123), channel_id=1, source_target_pairs={{0,32},{16,112},{32,64},{48,16},{64,96},{80,48},{96,0},{112,80},{1... | collective-permute-start | bytes 294920 | tf_op jit(solution)/shard_map/ppermute | solution.py:140
  6.4 11.8 %collective-permute-start.3 = (bf16[768,384]{1,0:T(8,128)(2,1)}, bf16[768,384]{1,0:T(8,128)(2,1)S(1)}, u32[]{:S(2)}, u32[]{:S(2)}) collective-permute-start(bf16[768,384]{1,0:T(8,128)(2,1)} %param.5), channel_id=1, source_target_pairs={{0,32},{16,112},{32,64},{48,16},{64,96},{80,48},{96,0},{112,80},{1... | collective-permute-start | bytes 1769480 | tf_op jit(solution)/shard_map/ppermute | solution.py:140
  11.9 26.0 %copy-start.7 = (bf16[768,384]{1,0:T(8,128)(2,1)S(1)}, bf16[768,384]{1,0:T(8,128)(2,1)}, u32[]{:S(2)}) copy-start(bf16[768,384]{1,0:T(8,128)(2,1)} %param.5) | copy-start | bytes 1769476
  18.2 13.5 %collective-permute-start.6 = (bf16[2,32,3072]{2,1,0:T(8,128)(2,1)S(1)}, bf16[2,32,3072]{2,1,0:T(8,128)(2,1)S(1)}, u32[]{:S(2)}, u32[]{:S(2)}) collective-permute-start(bf16[2,32,3072]{2,1,0:T(8,128)(2,1)S(1)} %pad_maximum_fusion.12), channel_id=1, source_target_pairs={{0,12},{1,13},{2,14},{3,15},{4,0},{5,1},{6,2},{7,3},{8,4},{9,5},{1... | collective-permute-start | bytes 1179656 | tf_op jit(solution)/shard_map/ppermute | solution.py:157
  22.2 9.5 %collective-permute-start.5 = (bf16[2,32,3072]{2,1,0:T(8,128)(2,1)S(1)}, bf16[2,32,3072]{2,1,0:T(8,128)(2,1)S(1)}, u32[]{:S(2)}, u32[]{:S(2)}) collective-permute-start(bf16[2,32,3072]{2,1,0:T(8,128)(2,1)S(1)} %pad_maximum_fusion.12), channel_id=1, source_target_pairs={{0,8},{1,9},{2,10},{3,11},{4,12},{5,13},{6,14},{7,15},{8,0},{9,1},... | collective-permute-start | bytes 1179656 | tf_op jit(solution)/shard_map/ppermute | solution.py:157
  22.2 13.2 %collective-permute-start.4 = (bf16[2,32,3072]{2,1,0:T(8,128)(2,1)S(1)}, bf16[2,32,3072]{2,1,0:T(8,128)(2,1)S(1)}, u32[]{:S(2)}, u32[]{:S(2)}) collective-permute-start(bf16[2,32,3072]{2,1,0:T(8,128)(2,1)S(1)} %pad_maximum_fusion.12), channel_id=1, source_target_pairs={{0,4},{1,5},{2,6},{3,7},{4,8},{5,9},{6,10},{7,11},{8,12},{9,13},{1... | collective-permute-start | bytes 1179656 | tf_op jit(solution)/shard_map/ppermute | solution.py:157
  23.5 12.9 %collective-permute-start.8 = (bf16[384,768]{1,0:T(8,128)(2,1)S(1)}, bf16[384,768]{1,0:T(8,128)(2,1)S(1)}, u32[]{:S(2)}, u32[]{:S(2)}) collective-permute-start(bf16[384,768]{1,0:T(8,128)(2,1)S(1)} %copy-done.8), channel_id=1, source_target_pairs={{0,96},{16,48},{32,0},{48,80},{64,32},{80,112},{96,64},{112,16},{1... | collective-permute-start | bytes 1769480 | tf_op jit(solution)/shard_map/ppermute | solution.py:140
  24.1 12.6 %collective-permute-start.7 = (bf16[768,384]{1,0:T(8,128)(2,1)S(1)}, bf16[768,384]{1,0:T(8,128)(2,1)S(1)}, u32[]{:S(2)}, u32[]{:S(2)}) collective-permute-start(bf16[768,384]{1,0:T(8,128)(2,1)S(1)} %collective-permute-done.3), channel_id=1, source_target_pairs={{0,32},{16,112},{32,64},{48,16},{64,96},{80,48},{96,0},{112,80},{1... | collective-permute-start | bytes 1769480 | tf_op jit(solution)/shard_map/ppermute | solution.py:140
  36.7 11.8 %collective-permute-start.11 = (bf16[768,384]{1,0:T(8,128)(2,1)S(1)}, bf16[768,384]{1,0:T(8,128)(2,1)S(1)}, u32[]{:S(2)}, u32[]{:S(2)}) collective-permute-start(bf16[768,384]{1,0:T(8,128)(2,1)S(1)} %collective-permute-done.7), channel_id=1, source_target_pairs={{0,32},{16,112},{32,64},{48,16},{64,96},{80,48},{96,0},{112,80},{1... | collective-permute-start | bytes 1769480 | tf_op jit(solution)/shard_map/ppermute | solution.py:140
  38.1 24.0 %collective-permute-start.14 = (bf16[2304,384]{1,0:T(8,128)(2,1)S(1)}, bf16[2304,384]{1,0:T(8,128)(2,1)S(1)}, u32[]{:S(2)}, u32[]{:S(2)}) collective-permute-start(bf16[2304,384]{1,0:T(8,128)(2,1)S(1)} %pad_maximum_fusion.6), channel_id=1, source_target_pairs={{0,16},{16,0},{1,17},{17,1},{2,18},{18,2},{3,19},{19,3},{4,20},{20... | collective-permute-start | bytes 5308424 | tf_op jit(solution)/shard_map/ppermute | solution.py:144
  38.1 23.9 %collective-permute-start.9 = (bf16[2,128,3072]{2,1,0:T(8,128)(2,1)S(1)}, bf16[2,128,3072]{2,1,0:T(8,128)(2,1)S(1)}, u32[]{:S(2)}, u32[]{:S(2)}) collective-permute-start(bf16[2,128,3072]{2,1,0:T(8,128)(2,1)S(1)} %pad_maximum_fusion.7), channel_id=1, source_target_pairs={{0,1},{1,2},{2,3},{3,0},{4,5},{5,6},{6,7},{7,4},{8,9},{9,10},{10,1... | collective-permute-start | bytes 4718600 | tf_op jit(solution)/shard_map/ppermute | solution.py:157
  40.1 21.9 %collective-permute-start.10 = (bf16[2,128,3072]{2,1,0:T(8,128)(2,1)S(1)}, bf16[2,128,3072]{2,1,0:T(8,128)(2,1)S(1)}, u32[]{:S(2)}, u32[]{:S(2)}) collective-permute-start(bf16[2,128,3072]{2,1,0:T(8,128)(2,1)S(1)} %pad_maximum_fusion.7), channel_id=1, source_target_pairs={{0,3},{1,0},{2,1},{3,2},{4,7},{5,4},{6,5},{7,6},{8,11},{9,8},{10,9... | collective-permute-start | bytes 4718600 | tf_op jit(solution)/shard_map/ppermute | solution.py:157
  41.5 9.9 %collective-permute-start.12 = (bf16[384,768]{1,0:T(8,128)(2,1)S(1)}, bf16[384,768]{1,0:T(8,128)(2,1)S(1)}, u32[]{:S(2)}, u32[]{:S(2)}) collective-permute-start(bf16[384,768]{1,0:T(8,128)(2,1)S(1)} %collective-permute-done.8), channel_id=1, source_target_pairs={{0,96},{16,48},{32,0},{48,80},{64,32},{80,112},{96,64},{112,16},{1... | collective-permute-start | bytes 1769480 | tf_op jit(solution)/shard_map/ppermute | solution.py:140
  48.5 13.5 %collective-permute-start.15 = (bf16[384,1536]{1,0:T(8,128)(2,1)S(1)}, bf16[384,1536]{1,0:T(8,128)(2,1)S(1)}, u32[]{:S(2)}, u32[]{:S(2)}) collective-permute-start(bf16[384,1536]{1,0:T(8,128)(2,1)S(1)} %pad_maximum_fusion.10), channel_id=1, source_target_pairs={{0,16},{16,0},{1,17},{17,1},{2,18},{18,2},{3,19},{19,3},{4,20},{20... | collective-permute-start | bytes 3538952 | tf_op jit(solution)/shard_map/ppermute | solution.py:144
  51.3 10.7 %collective-permute-start.13 = (bf16[384,768]{1,0:T(8,128)(2,1)S(1)}, bf16[384,768]{1,0:T(8,128)(2,1)S(1)}, u32[]{:S(2)}, u32[]{:S(2)}) collective-permute-start(bf16[384,768]{1,0:T(8,128)(2,1)S(1)} %collective-permute-done.12), channel_id=1, source_target_pairs={{0,96},{16,48},{32,0},{48,80},{64,32},{80,112},{96,64},{112,16},{1... | collective-permute-start | bytes 1769480 | tf_op jit(solution)/shard_map/ppermute | solution.py:140
  62.3 9.3 %collective-permute-start.18 = (bf16[768,384]{1,0:T(8,128)(2,1)S(1)}, bf16[768,384]{1,0:T(8,128)(2,1)S(1)}, u32[]{:S(2)}, u32[]{:S(2)}) collective-permute-start(bf16[768,384]{1,0:T(8,128)(2,1)S(1)} %collective-permute-done.11), channel_id=1, source_target_pairs={{0,16},{16,0},{1,17},{17,1},{2,18},{18,2},{3,19},{19,3},{4,20},{20... | collective-permute-start | bytes 1769480 | tf_op jit(solution)/shard_map/ppermute | solution.py:144
  64.6 19.8 %collective-permute-start.16 = (bf16[2,64,3072]{2,1,0:T(8,128)(2,1)S(1)}, bf16[2,64,3072]{2,1,0:T(8,128)(2,1)S(1)}, u32[]{:S(2)}, u32[]{:S(2)}) collective-permute-start(bf16[2,64,3072]{2,1,0:T(8,128)(2,1)S(1)} %slice.190), channel_id=1, source_target_pairs={{0,1},{1,2},{2,3},{3,0},{4,5},{5,6},{6,7},{7,4},{8,9},{9,10},{10,1... | collective-permute-start | bytes 2359304 | tf_op jit(solution)/shard_map/ppermute | solution.py:157
  66.3 18.1 %collective-permute-start.17 = (bf16[2,64,3072]{2,1,0:T(8,128)(2,1)S(1)}, bf16[2,64,3072]{2,1,0:T(8,128)(2,1)S(1)}, u32[]{:S(2)}, u32[]{:S(2)}) collective-permute-start(bf16[2,64,3072]{2,1,0:T(8,128)(2,1)S(1)} %slice.191), channel_id=1, source_target_pairs={{0,3},{1,0},{2,1},{3,2},{4,7},{5,4},{6,5},{7,6},{8,11},{9,8},{10,9... | collective-permute-start | bytes 2359304 | tf_op jit(solution)/shard_map/ppermute | solution.py:157
  70.5 3.3 %collective-permute-start.19 = (bf16[384,1536]{1,0:T(8,128)(2,1)S(1)}, bf16[384,1536]{1,0:T(8,128)(2,1)S(1)}, u32[]{:S(2)}, u32[]{:S(2)}) collective-permute-start(bf16[384,1536]{1,0:T(8,128)(2,1)S(1)} %pad_maximum_fusion.11), channel_id=1, source_target_pairs={{0,16},{16,0},{1,17},{17,1},{2,18},{18,2},{3,19},{19,3},{4,20},{20... | collective-permute-start | bytes 3538952 | tf_op jit(solution)/shard_map/ppermute | solution.py:144
  96.8 17.4 %collective-permute-start.22 = (bf16[384,3072]{1,0:T(8,128)(2,1)}, bf16[384,3072]{1,0:T(8,128)(2,1)S(1)}, u32[]{:S(2)}, u32[]{:S(2)}) collective-permute-start(bf16[384,3072]{1,0:T(8,128)(2,1)} %get-tuple-element.84), channel_id=1, source_target_pairs={{0,16},{16,0},{1,17},{17,1},{2,18},{18,2},{3,19},{19,3},{4,20},{20... | collective-permute-start | bytes 7077896 | tf_op jit(solution)/shard_map/ppermute | solution.py:144
  97.2 17.1 %collective-permute-start.23 = (bf16[3072,384]{1,0:T(8,128)(2,1)}, bf16[3072,384]{1,0:T(8,128)(2,1)S(1)}, u32[]{:S(2)}, u32[]{:S(2)}) collective-permute-start(bf16[3072,384]{1,0:T(8,128)(2,1)} %get-tuple-element.85), channel_id=1, source_target_pairs={{0,16},{16,0},{1,17},{17,1},{2,18},{18,2},{3,19},{19,3},{4,20},{20... | collective-permute-start | bytes 7077896 | tf_op jit(solution)/shard_map/ppermute | solution.py:144
  97.3 9.6 %slice-start.4 = ((s8[4718592]{0:T(1024)(128)(4,1)}), s8[4194304]{0:T(1024)(128)(4,1)S(1)}, s32[]{:S(2)}) async-start(s8[4718592]{0:T(1024)(128)(4,1)} %bitcast.76), calls=%async_computation.4 | async-start | bytes 8388608
  98.5 13.9 %collective-permute-start.20 = (bf16[2,64,3072]{2,1,0:T(8,128)(2,1)}, bf16[2,64,3072]{2,1,0:T(8,128)(2,1)S(1)}, u32[]{:S(2)}, u32[]{:S(2)}) collective-permute-start(bf16[2,64,3072]{2,1,0:T(8,128)(2,1)} %get-tuple-element.113), channel_id=1, source_target_pairs={{0,3},{1,0},{2,1},{3,2},{4,7},{5,4},{6,5},{7,6},{8,11},{9,8},{10,9... | collective-permute-start | bytes 2359304 | tf_op jit(solution)/shard_map/ppermute | solution.py:157
  100.8 13.4 %collective-permute-start.21 = (bf16[2,64,3072]{2,1,0:T(8,128)(2,1)}, bf16[2,64,3072]{2,1,0:T(8,128)(2,1)S(1)}, u32[]{:S(2)}, u32[]{:S(2)}) collective-permute-start(bf16[2,64,3072]{2,1,0:T(8,128)(2,1)} %get-tuple-element.112), channel_id=1, source_target_pairs={{0,1},{1,2},{2,3},{3,0},{4,5},{5,6},{6,7},{7,4},{8,9},{9,10},{10,1... | collective-permute-start | bytes 2359304 | tf_op jit(solution)/shard_map/ppermute | solution.py:157
  112.4 21.0 %copy-start.3 = (bf16[384,3072]{1,0:T(8,128)(2,1)}, bf16[384,3072]{1,0:T(8,128)(2,1)S(1)}, u32[]{:S(2)}) copy-start(bf16[384,3072]{1,0:T(8,128)(2,1)S(1)} %get-tuple-element.91) | copy-start | bytes 7077892
  112.4 25.8 %copy-start.5 = (bf16[3072,384]{1,0:T(8,128)(2,1)}, bf16[3072,384]{1,0:T(8,128)(2,1)S(1)}, u32[]{:S(2)}) copy-start(bf16[3072,384]{1,0:T(8,128)(2,1)S(1)} %get-tuple-element.93) | copy-start | bytes 7077892
  114.2 19.2 %copy-start.9 = (bf16[384,3072]{1,0:T(8,128)(2,1)}, bf16[384,3072]{1,0:T(8,128)(2,1)S(1)}, u32[]{:S(2)}) copy-start(bf16[384,3072]{1,0:T(8,128)(2,1)S(1)} %collective-permute-done.22) | copy-start | bytes 7077892
  114.2 23.9 %copy-start.11 = (bf16[3072,384]{1,0:T(8,128)(2,1)}, bf16[3072,384]{1,0:T(8,128)(2,1)S(1)}, u32[]{:S(2)}) copy-start(bf16[3072,384]{1,0:T(8,128)(2,1)S(1)} %collective-permute-done.23) | copy-start | bytes 7077892
  115.1 36.6 %collective-permute-start.24 = (bf16[2,128,3072]{2,1,0:T(8,128)(2,1)S(1)}, bf16[2,128,3072]{2,1,0:T(8,128)(2,1)}, u32[]{:S(2)}, u32[]{:S(2)}) collective-permute-start(bf16[2,128,3072]{2,1,0:T(8,128)(2,1)S(1)} %pad_maximum_fusion.8), channel_id=1, source_target_pairs={{0,3},{1,0},{2,1},{3,2},{4,7},{5,4},{6,5},{7,6},{8,11},{9,8},{10,9... | collective-permute-start | bytes 4718600 | tf_op jit(solution)/shard_map/ppermute | solution.py:157
  116.7 16.7 %collective-permute-start.26 = (bf16[384,768]{1,0:T(8,128)(2,1)S(1)}, bf16[384,768]{1,0:T(8,128)(2,1)S(1)}, u32[]{:S(2)}, u32[]{:S(2)}) collective-permute-start(bf16[384,768]{1,0:T(8,128)(2,1)S(1)} %add_convert_fusion.8), channel_id=1, source_target_pairs={{0,96},{16,48},{32,0},{48,80},{64,32},{80,112},{96,64},{112,16},{1... | collective-permute-start | bytes 1769480 | tf_op jit(solution)/shard_map/ppermute | solution.py:140
  120.0 31.7 %collective-permute-start.25 = (bf16[2,128,3072]{2,1,0:T(8,128)(2,1)S(1)}, bf16[2,128,3072]{2,1,0:T(8,128)(2,1)}, u32[]{:S(2)}, u32[]{:S(2)}) collective-permute-start(bf16[2,128,3072]{2,1,0:T(8,128)(2,1)S(1)} %pad_maximum_fusion.9), channel_id=1, source_target_pairs={{0,1},{1,2},{2,3},{3,0},{4,5},{5,6},{6,7},{7,4},{8,9},{9,10},{10,1... | collective-permute-start | bytes 4718600 | tf_op jit(solution)/shard_map/ppermute | solution.py:157
  120.9 17.2 %collective-permute-start.28 = (bf16[768,384]{1,0:T(8,128)(2,1)S(1)}, bf16[768,384]{1,0:T(8,128)(2,1)S(1)}, u32[]{:S(2)}, u32[]{:S(2)}) collective-permute-start(bf16[768,384]{1,0:T(8,128)(2,1)S(1)} %add_convert_fusion.6), channel_id=1, source_target_pairs={{0,32},{16,112},{32,64},{48,16},{64,96},{80,48},{96,0},{112,80},{1... | collective-permute-start | bytes 1769480 | tf_op jit(solution)/shard_map/ppermute | solution.py:140
  134.5 17.2 %collective-permute-start.27 = (bf16[384,768]{1,0:T(8,128)(2,1)}, bf16[384,768]{1,0:T(8,128)(2,1)}, u32[]{:S(2)}, u32[]{:S(2)}) collective-permute-start(bf16[384,768]{1,0:T(8,128)(2,1)} %add_convert_fusion.7), channel_id=1, source_target_pairs={{0,96},{16,48},{32,0},{48,80},{64,32},{80,112},{96,64},{112,16},{1... | collective-permute-start | bytes 1769480 | tf_op jit(solution)/shard_map/ppermute | solution.py:140
  139.2 12.5 %collective-permute-start.29 = (bf16[768,384]{1,0:T(8,128)(2,1)}, bf16[768,384]{1,0:T(8,128)(2,1)}, u32[]{:S(2)}, u32[]{:S(2)}) collective-permute-start(bf16[768,384]{1,0:T(8,128)(2,1)} %add_convert_fusion.5), channel_id=1, source_target_pairs={{0,32},{16,112},{32,64},{48,16},{64,96},{80,48},{96,0},{112,80},{1... | collective-permute-start | bytes 1769480 | tf_op jit(solution)/shard_map/ppermute | solution.py:140
  151.7 7.6 %copy-start.10 = (bf16[384,3072]{1,0:T(8,128)(2,1)S(1)}, bf16[384,3072]{1,0:T(8,128)(2,1)}, u32[]{:S(2)}) copy-start(bf16[384,3072]{1,0:T(8,128)(2,1)} %copy-done.9) | copy-start | bytes 7077892
  151.7 12.7 %copy-start.12 = (bf16[3072,384]{1,0:T(8,128)(2,1)S(1)}, bf16[3072,384]{1,0:T(8,128)(2,1)}, u32[]{:S(2)}) copy-start(bf16[3072,384]{1,0:T(8,128)(2,1)} %copy-done.11) | copy-start | bytes 7077892
  155.0 9.4 %copy-start.6 = (bf16[3072,384]{1,0:T(8,128)(2,1)S(1)}, bf16[3072,384]{1,0:T(8,128)(2,1)}, u32[]{:S(2)}) copy-start(bf16[3072,384]{1,0:T(8,128)(2,1)} %copy-done.5) | copy-start | bytes 7077892
  155.1 13.3 %collective-permute-start.32 = (bf16[2,32,3072]{2,1,0:T(8,128)(2,1)S(1)}, bf16[2,32,3072]{2,1,0:T(8,128)(2,1)S(1)}, u32[]{:S(2)}, u32[]{:S(2)}) collective-permute-start(bf16[2,32,3072]{2,1,0:T(8,128)(2,1)S(1)} %get-tuple-element.111), channel_id=1, source_target_pairs={{0,4},{1,5},{2,6},{3,7},{4,8},{5,9},{6,10},{7,11},{8,12},{9,13},{1... | collective-permute-start | bytes 1179656 | tf_op jit(solution)/shard_map/ppermute | solution.py:157
  155.2 13.2 %collective-permute-start.31 = (bf16[2,32,3072]{2,1,0:T(8,128)(2,1)S(1)}, bf16[2,32,3072]{2,1,0:T(8,128)(2,1)S(1)}, u32[]{:S(2)}, u32[]{:S(2)}) collective-permute-start(bf16[2,32,3072]{2,1,0:T(8,128)(2,1)S(1)} %get-tuple-element.110), channel_id=1, source_target_pairs={{0,8},{1,9},{2,10},{3,11},{4,12},{5,13},{6,14},{7,15},{8,0},{9,1},... | collective-permute-start | bytes 1179656 | tf_op jit(solution)/shard_map/ppermute | solution.py:157
  158.2 11.1 %collective-permute-start.30 = (bf16[2,32,3072]{2,1,0:T(8,128)(2,1)S(1)}, bf16[2,32,3072]{2,1,0:T(8,128)(2,1)S(1)}, u32[]{:S(2)}, u32[]{:S(2)}) collective-permute-start(bf16[2,32,3072]{2,1,0:T(8,128)(2,1)S(1)} %get-tuple-element.109), channel_id=1, source_target_pairs={{0,12},{1,13},{2,14},{3,15},{4,0},{5,1},{6,2},{7,3},{8,4},{9,5},{1... | collective-permute-start | bytes 1179656 | tf_op jit(solution)/shard_map/ppermute | solution.py:157
  160.6 16.1 %collective-permute-start.33 = (bf16[384,768]{1,0:T(8,128)(2,1)S(1)}, bf16[384,768]{1,0:T(8,128)(2,1)S(1)}, u32[]{:S(2)}, u32[]{:S(2)}) collective-permute-start(bf16[384,768]{1,0:T(8,128)(2,1)S(1)} %add_convert_fusion.4), channel_id=1, source_target_pairs={{0,96},{16,48},{32,0},{48,80},{64,32},{80,112},{96,64},{112,16},{1... | collective-permute-start | bytes 1769480 | tf_op jit(solution)/shard_map/ppermute | solution.py:140
  165.7 11.2 %collective-permute-start.34 = (bf16[768,384]{1,0:T(8,128)(2,1)S(1)}, bf16[768,384]{1,0:T(8,128)(2,1)S(1)}, u32[]{:S(2)}, u32[]{:S(2)}) collective-permute-start(bf16[768,384]{1,0:T(8,128)(2,1)S(1)} %add_convert_fusion.3), channel_id=1, source_target_pairs={{0,32},{16,112},{32,64},{48,16},{64,96},{80,48},{96,0},{112,80},{1... | collective-permute-start | bytes 1769480 | tf_op jit(solution)/shard_map/ppermute | solution.py:140
  176.9 7.2 %collective-permute-start.35 = (bf16[2,32,768]{2,1,0:T(8,128)(2,1)S(1)}, bf16[2,32,768]{2,1,0:T(8,128)(2,1)S(1)}, u32[]{:S(2)}, u32[]{:S(2)}) collective-permute-start(bf16[2,32,768]{2,1,0:T(8,128)(2,1)S(1)} %pad_maximum_fusion.13), channel_id=1, source_target_pairs={{0,96},{16,48},{32,0},{48,80},{64,32},{80,112},{96,64},{112,16},{1... | collective-permute-start | bytes 294920 | tf_op jit(solution)/shard_map/ppermute | solution.py:140
  180.6 6.3 %collective-permute-start.36 = (bf16[2,32,768]{2,1,0:T(8,128)(2,1)S(1)}, bf16[2,32,768]{2,1,0:T(8,128)(2,1)S(1)}, u32[]{:S(2)}, u32[]{:S(2)}) collective-permute-start(bf16[2,32,768]{2,1,0:T(8,128)(2,1)S(1)} %pad_maximum_fusion.14), channel_id=1, source_target_pairs={{0,64},{16,80},{32,96},{48,112},{64,0},{80,16},{96,32},{112,48},{1... | collective-permute-start | bytes 294920 | tf_op jit(solution)/shard_map/ppermute | solution.py:140
  180.8 6.9 %collective-permute-start.37 = (bf16[2,32,768]{2,1,0:T(8,128)(2,1)S(1)}, bf16[2,32,768]{2,1,0:T(8,128)(2,1)S(1)}, u32[]{:S(2)}, u32[]{:S(2)}) collective-permute-start(bf16[2,32,768]{2,1,0:T(8,128)(2,1)S(1)} %pad_maximum_fusion.15), channel_id=1, source_target_pairs={{0,32},{16,112},{32,64},{48,16},{64,96},{80,48},{96,0},{112,80},{1... | collective-permute-start | bytes 294920 | tf_op jit(solution)/shard_map/ppermute | solution.py:140
  (9 other events, 43.2 us)
where the time goes:
time: 189 us; the launch traced here: 188 us
  waiting for transfers between devices  78.4 us (41%)
  starting transfers between devices  54.9 us (29%)
  Pallas kernels  30.1 us (16%)
  other arithmetic  17.6 us (9%)
  local copies, waits for them, and re-layouts  6.17 us (3%)
    ppermute x18, waiting for transfers between devices, along_x(): return lax.ppermute(value, ('row', 'col'), pairs)  61.5 us
    ppermute x18, starting transfers between devices, along_x(): return lax.ppermute(value, ('row', 'col'), pairs)  30.7 us
    pallas_call x6, Pallas kernels, local_kernel(): pl.pallas_call(body, grid=grid, in_specs=in_specs, out_specs=out_specs, o...  30.1 us
    ppermute x14, starting transfers between devices, plane(): return lax.ppermute(value, ('col', 'depth'), pairs)  20.6 us
    ppermute x14, waiting for transfers between devices, plane(): return lax.ppermute(value, ('col', 'depth'), pairs)  15.3 us
    concatenate x11, other arithmetic, join(): return parts[0] if len(parts) == 1 else jnp.concatenate(parts, axis=axis)  4.71 us
  transfers between devices with their start and end apart: 38, of which 21 were waited for; matrix products, arithmetic and copies ran while one was open for 8% of the time, Pallas kernels for 9%

commit v1 on v0

--- a/solution.py
+++ b/solution.py
@@ -184,28 +184,25 @@
     )
 
     ups, downs = [up_weight], [down_weight]
-    ups.append(along_x(ups[-1], 1))
-    own, ups[1] = held(own, ups[1])
-
-    ups.append(along_x(ups[1], 1))
-    downs.append(along_x(downs[0], -1))
-    first = jnp.concatenate([own] + [plane(own, 0, hop) for hop in (1, 2, 3)], axis=1)
-    first, ups[2], downs[1] = held(first, ups[2], downs[1])
+
+    def step(*values):
+        ups.append(along_x(ups[-1], 1))
+        downs.append(along_x(downs[-1], -1))
+        *values, ups[-1], downs[-1] = held(*values, ups[-1], downs[-1])
+        return values
 
     def join(parts, axis):
-        return parts[0] if len(parts) == 1 else jnp.concatenate(parts, axis=axis)
-
-    ups.append(along_x(ups[2], 1))
-    downs.append(along_x(downs[1], -1))
-    downs.append(along_x(downs[2], -1))
-    up_early, down_early = across(join(ups[:3], 0)), across(join(downs[:2], 1))
+        return jnp.concatenate(parts, axis=axis)
+
+    (own,) = step(own)
+    (first,) = step(join([own] + [plane(own, 0, hop) for hop in (1, 2, 3)], 1))
+
+    up_early = across(join(ups[:3], 0))
     left, right = plane(first, 1, 1), plane(first, 1, -1)
-    left, right, ups[3], downs[2], downs[3], up_early, down_early = held(
-        left, right, ups[3], downs[2], downs[3], up_early, down_early
-    )
-
+    left, right, up_early = step(left, right, up_early)
+    (down_mine,) = held(join(downs, 1))
+    up_late, down_theirs = across(ups[3]), across(down_mine)
     far = [plane(left[:, :half], 1, 1), plane(right[:, half:], 1, -1)]
-    up_late, down_late = across(ups[3]), across(join(downs[2:], 1))
 
     def rows_of(value, k):
         return lax.slice_in_dim(value, k * width, (k + 1) * width, axis=0)
@@ -214,12 +211,10 @@
         return lax.slice_in_dim(value, k * width, (k + 1) * width, axis=1)
 
     up = held(
-        join(ups, 0), join([rows_of(up_early, 0), up_late, up_early[2 * width :], rows_of(up_early, 1)], 0)
-    )
-    down = held(
-        join(downs, 1),
-        join([columns(down_early, 0), columns(down_late, 1), columns(down_late, 0), columns(down_early, 1)], 1),
-    )
+        join(ups, 0),
+        join([rows_of(up_early, 0), up_late, rows_of(up_early, 2), rows_of(up_early, 1)], 0),
+    )
+    down = held(down_mine, join([columns(down_theirs, k) for k in turned], 1))
     up, down = held(join(up, 1), join(down, 0))
 
     near = join([first, left, right], 1)
@@ -237,9 +232,7 @@
     down_theirs, up_theirs = (across(value) for value in weight_sums(sets, acts, grads, 1))
     near_sums = backward(near_acts, near_grads, up, down)
     down_mine, up_mine = weight_sums(sets, acts, grads, 0)
-    *far_back, near_sums, down_theirs, up_theirs, down_mine, up_mine = held(
-        *far_back, near_sums, down_theirs, up_theirs, down_mine, up_mine
-    )
+    *far_back, near_sums, down_mine, up_mine = held(*far_back, near_sums, down_mine, up_mine)
 
     def total(*parts):
         value = parts[0].astype(F32)
@@ -260,15 +253,15 @@
 
     down_grad = along_x(down_part(1).astype(BF), -1)
     up_grad = along_x(up_part(1).astype(BF), 1)
+    left, right, down_grad, up_grad = held(left, right, down_grad, up_grad)
+
     down_grad = along_x(down_part(2, down_grad).astype(BF), -1)
     up_grad = along_x(up_part(2, up_grad).astype(BF), 1)
-    left, right, down_grad, up_grad = held(left, right, down_grad, up_grad)
-
     sums = total(here, left, right).astype(BF).reshape(2, 4, sub, 4 * width)
+    end = total(sums[:, 0], *(plane(sums[:, hop], 0, -hop) for hop in (1, 2, 3)))
+    end, down_grad, up_grad = held(end.astype(BF), down_grad, up_grad)
     down_grad = along_x(down_part(3, down_grad).astype(BF), -1)
     up_grad = along_x(up_part(3, up_grad).astype(BF), 1)
-    end = total(sums[:, 0], *(plane(sums[:, hop], 0, -hop) for hop in (1, 2, 3)))
-    end, down_grad, up_grad = held(end.astype(BF), down_grad, up_grad)
     down_grad, up_grad = down_part(0, down_grad), up_part(0, up_grad)
 
     out = jnp.zeros((2, rows, width), BF)

time: 189 us -> 190 us (level)
  starting transfers between devices: 54.9 us -> 46.1 us
  waiting for transfers between devices: 78.4 us -> 85 us
  other arithmetic: 17.6 us -> 19.9 us
    ppermute x14, waiting for transfers between devices: 15.3 us -> 35.1 us  [plane(): return lax.ppermute(value, ('col', 'depth'), pairs)]
    ppermute x18, waiting for transfers between devices: 61.5 us -> 50 us  [along_x(): return lax.ppermute(value, ('row', 'col'), pairs)]
    ppermute x18, starting transfers between devices: 30.7 us -> 25.9 us  [along_x(): return lax.ppermute(value, ('row', 'col'), pairs)]
    ppermute x14, starting transfers between devices: 20.6 us -> 18.3 us  [plane(): return lax.ppermute(value, ('col', 'depth'), pairs)]
    concatenate x12 -> x10, other arithmetic: 4.81 us -> 6.96 us  [join(): return jnp.concatenate(parts, axis=axis)]
    unnamed x41 -> x33, local copies, waits for them, and re-layouts: 3.24 us -> 4.9 us
  transfers between devices with their start and end apart: 38 -> 37, of which waited for: 21 -> 21; matrix products, arithmetic and copies ran while one was open for 8% -> 8% of each run, Pallas kernels for 9% -> 12%
where the time goes in v1:
time: 190 us; the launch traced here: 189 us
  waiting for transfers between devices  85 us (45%)
  starting transfers between devices  46.1 us (24%)
  Pallas kernels  29.2 us (15%)
  other arithmetic  19.9 us (10%)
  local copies, waits for them, and re-layouts  7.58 us (4%)
    ppermute x18, waiting for transfers between devices, along_x(): return lax.ppermute(value, ('row', 'col'), pairs)  50 us
    ppermute x14, waiting for transfers between devices, plane(): return lax.ppermute(value, ('col', 'depth'), pairs)  35.1 us
    pallas_call x6, Pallas kernels, local_kernel(): pl.pallas_call(body, grid=grid, in_specs=in_specs, out_specs=out_specs, o...  29.2 us
    ppermute x18, starting transfers between devices, along_x(): return lax.ppermute(value, ('row', 'col'), pairs)  25.9 us
    ppermute x14, starting transfers between devices, plane(): return lax.ppermute(value, ('col', 'depth'), pairs)  18.3 us
    concatenate x10, other arithmetic, join(): return jnp.concatenate(parts, axis=axis)  6.96 us
    unnamed x33, local copies, waits for them, and re-layouts  4.9 us
  transfers between devices with their start and end apart: 37, of which 21 were waited for; matrix products, arithmetic and copies ran while one was open for 8% of the time, Pallas kernels for 12%

profile of v1, /device:TPU:0, one launch (start us, length us, event | category | flops | bytes accessed | tf_op | source)
XLA Modules:
  0.0 189.1 jit_solution(12957419608864583213)
XLA Ops:
  1.7 1.6 collective-permute-start
  3.4 2.7 %collective-permute-start.1 = (bf16[2,32,768]{2,1,0:T(8,128)(2,1)S(1)}, bf16[2,32,768]{2,1,0:T(8,128)(2,1)S(1)}, u32[]{:S(2)}, u32[]{:S(2)}) collective-permute-start(bf16[2,32,768]{2,1,0:T(8,128)(2,1)S(1)} %get-tuple-element.118), channel_id=1, source_target_pairs={{0,64},{16,80},{32,96},{48,112},{64,0},{80,16},{96,32},{112,48},{1... | collective-permute-start | bytes 294920 | tf_op jit(solution)/shard_map/ppermute | solution.py:140
  6.1 1.4 collective-permute-start.2
  7.6 2.0 %collective-permute-start.3 = (bf16[768,384]{1,0:T(8,128)(2,1)}, bf16[768,384]{1,0:T(8,128)(2,1)S(1)}, u32[]{:S(2)}, u32[]{:S(2)}) collective-permute-start(bf16[768,384]{1,0:T(8,128)(2,1)} %param.5), channel_id=1, source_target_pairs={{0,32},{16,112},{32,64},{48,16},{64,96},{80,48},{96,0},{112,80},{1... | collective-permute-start | bytes 1769480 | tf_op jit(solution)/shard_map/ppermute | solution.py:140
  9.6 1.7 collective-permute-done.1
  11.9 11.5 %collective-permute-done.4 = bf16[384,768]{1,0:T(8,128)(2,1)S(1)} collective-permute-done((bf16[384,768]{1,0:T(8,128)(2,1)}, bf16[384,768]{1,0:T(8,128)(2,1)S(1)}, u32[]{:S(2)}, u32[]{:S(2)}) %collective-permute-start.4) | collective-permute-done | bytes 589856 | tf_op jit(solution)/shard_map/ppermute | solution.py:140
  24.2 4.0 %collective-permute-start.7 = (bf16[2,32,3072]{2,1,0:T(8,128)(2,1)S(1)}, bf16[2,32,3072]{2,1,0:T(8,128)(2,1)S(1)}, u32[]{:S(2)}, u32[]{:S(2)}) collective-permute-start(bf16[2,32,3072]{2,1,0:T(8,128)(2,1)S(1)} %pad_maximum_fusion.10), channel_id=1, source_target_pairs={{0,12},{1,13},{2,14},{3,15},{4,0},{5,1},{6,2},{7,3},{8,4},{9,5},{1... | collective-permute-start | bytes 1179656 | tf_op jit(solution)/shard_map/ppermute | solution.py:157
  28.2 1.3 collective-permute-start.5
  29.5 1.8 collective-permute-start.9
  31.5 6.2 %collective-permute-done.7 = bf16[2,32,3072]{2,1,0:T(8,128)(2,1)S(1)} collective-permute-done((bf16[2,32,3072]{2,1,0:T(8,128)(2,1)S(1)}, bf16[2,32,3072]{2,1,0:T(8,128)(2,1)S(1)}, u32[]{:S(2)}, u32[]{:S(2)}) %collective-permute-start.7) | collective-permute-done | bytes 393248 | tf_op jit(solution)/shard_map/ppermute | solution.py:157
  37.7 3.7 %collective-permute-done.5 = bf16[2,32,3072]{2,1,0:T(8,128)(2,1)S(1)} collective-permute-done((bf16[2,32,3072]{2,1,0:T(8,128)(2,1)S(1)}, bf16[2,32,3072]{2,1,0:T(8,128)(2,1)S(1)}, u32[]{:S(2)}, u32[]{:S(2)}) %collective-permute-start.5) | collective-permute-done | bytes 393248 | tf_op jit(solution)/shard_map/ppermute | solution.py:157
  43.7 2.3 %collective-permute-start.11 = (bf16[2,128,3072]{2,1,0:T(8,128)(2,1)S(1)}, bf16[2,128,3072]{2,1,0:T(8,128)(2,1)S(1)}, u32[]{:S(2)}, u32[]{:S(2)}) collective-permute-start(bf16[2,128,3072]{2,1,0:T(8,128)(2,1)S(1)} %pad_maximum_fusion.7), channel_id=1, source_target_pairs={{0,3},{1,0},{2,1},{3,2},{4,7},{5,4},{6,5},{7,6},{8,11},{9,8},{10,9... | collective-permute-start | bytes 4718600 | tf_op jit(solution)/shard_map/ppermute | solution.py:157
  46.0 3.0 %collective-permute-start.14 = (bf16[384,768]{1,0:T(8,128)(2,1)S(1)}, bf16[384,768]{1,0:T(8,128)(2,1)S(1)}, u32[]{:S(2)}, u32[]{:S(2)}) collective-permute-start(bf16[384,768]{1,0:T(8,128)(2,1)S(1)} %collective-permute-done.9), channel_id=1, source_target_pairs={{0,96},{16,48},{32,0},{48,80},{64,32},{80,112},{96,64},{112,16},{1... | collective-permute-start | bytes 1769480 | tf_op jit(solution)/shard_map/ppermute | solution.py:140
  49.0 12.8 %collective-permute-done.14 = bf16[384,768]{1,0:T(8,128)(2,1)S(1)} collective-permute-done((bf16[384,768]{1,0:T(8,128)(2,1)S(1)}, bf16[384,768]{1,0:T(8,128)(2,1)S(1)}, u32[]{:S(2)}, u32[]{:S(2)}) %collective-permute-start.14) | collective-permute-done | bytes 589856 | tf_op jit(solution)/shard_map/ppermute | solution.py:140
  61.8 2.6 %collective-permute-done.13 = bf16[768,384]{1,0:T(8,128)(2,1)S(1)} collective-permute-done((bf16[768,384]{1,0:T(8,128)(2,1)S(1)}, bf16[768,384]{1,0:T(8,128)(2,1)S(1)}, u32[]{:S(2)}, u32[]{:S(2)}) %collective-permute-start.13) | collective-permute-done | bytes 589856 | tf_op jit(solution)/shard_map/ppermute | solution.py:140
  64.4 3.2 %collective-permute-done.10 = bf16[2,128,3072]{2,1,0:T(8,128)(2,1)S(1)} collective-permute-done((bf16[2,128,3072]{2,1,0:T(8,128)(2,1)S(1)}, bf16[2,128,3072]{2,1,0:T(8,128)(2,1)S(1)}, u32[]{:S(2)}, u32[]{:S(2)}) %collective-permute-start.10) | collective-permute-done | bytes 1572896 | tf_op jit(solution)/shard_map/ppermute | solution.py:157
  69.1 2.3 %collective-permute-start.16 = (bf16[2,64,3072]{2,1,0:T(8,128)(2,1)S(1)}, bf16[2,64,3072]{2,1,0:T(8,128)(2,1)S(1)}, u32[]{:S(2)}, u32[]{:S(2)}) collective-permute-start(bf16[2,64,3072]{2,1,0:T(8,128)(2,1)S(1)} %slice.191), channel_id=1, source_target_pairs={{0,3},{1,0},{2,1},{3,2},{4,7},{5,4},{6,5},{7,6},{8,11},{9,8},{10,9... | collective-permute-start | bytes 2359304 | tf_op jit(solution)/shard_map/ppermute | solution.py:157
  71.7 2.2 %copy-done.1 = bf16[2,384,3072]{2,1,0:T(8,128)(2,1)} copy-done((bf16[2,384,3072]{2,1,0:T(8,128)(2,1)}, bf16[2,384,3072]{2,1,0:T(8,128)(2,1)S(1)}, u32[]{:S(2)}) %copy-start.1) | copy-done | bytes 4718616
  75.4 2.7 %pad_maximum_fusion.1.down_ref = bf16[768,3072]{1,0:T(8,128)(2,1)} fusion(bf16[384,3072]{1,0:T(8,128)(2,1)S(1)} %pad_maximum_fusion.5, bf16[384,3072]{1,0:T(8,128)(2,1)S(1)} %pad_maximum_fusion.4), kind=kLoop, calls=%fused_computation.1 | loop fusion | flops 9437184 | bytes 9437184 | tf_op jit(solution)/shard_map/concatenate | solution.py:195
  79.2 6.3 %shard_map.75 = (bf16[384,768]{1,0:T(8,128)(2,1)S(1)}, bf16[384,768]{1,0:T(8,128)(2,1)S(1)}) custom-call(bf16[2,384,3072]{2,1,0:T(8,128)(2,1)S(1)} %bitcast.73, bf16[3072,768]{1,0:T(8,128)(2,1)S(1)} %pad_maximum_fusion.up_ref, bf16[768,3072]{1,0:T(8,128)(2,1)} %pad_maximum_fusion.1.down_ref), custom_call_target="tpu_custom_call" | custom-call | flops 1 | bytes 1 | tf_op jit(solution)/shard_map/pallas_call | solution.py:30
  85.6 3.0 %shard_map.76 = (bf16[128,768]{1,0:T(8,128)(2,1)S(1)}, bf16[128,768]{1,0:T(8,128)(2,1)S(1)}) custom-call(bf16[2,128,3072]{2,1,0:T(8,128)(2,1)S(1)} %constant_dynamic-update-slice_fusion.3.pair_ref.refs_1_, bf16[3072,768]{1,0:T(8,128)(2,1)S(1)} %pad_maximum_fusion.up_ref, bf16[768,3072]{1,0:T(8,128)(2,1)S(1)} %copy-done), custom_call_target="tpu_custom_call" | custom-call | flops 1 | bytes 1 | tf_op jit(solution)/shard_map/pallas_call | solution.py:30
  88.6 3.1 %shard_map.77 = bf16[2,128,3072]{2,1,0:T(8,128)(2,1)S(1)} custom-call(bf16[128,768]{1,0:T(8,128)(2,1)S(1)} %get-tuple-element.78.act_ref.refs_3_, bf16[128,768]{1,0:T(8,128)(2,1)S(1)} %get-tuple-element.79.grad_ref.refs_5_, bf16[3072,768]{1,0:T(8,128)(2,1)S(1)} %pad_maximum_fusion.up_ref, bf16[768,3072]{1,0:T(8,128)(2,1)S(1)} %copy-done), custom_call_target="tpu_custom_call" | custom-call | flops 1 | bytes 1 | tf_op jit(solution)/shard_map/pallas_call | solution.py:30
  92.7 1.6 collective-permute-start.20
  94.4 1.6 collective-permute-start.19
  96.0 6.0 %shard_map.78 = bf16[2,384,3072]{2,1,0:T(8,128)(2,1)S(1)} custom-call(bf16[384,768]{1,0:T(8,128)(2,1)S(1)} %get-tuple-element.76.act_ref.refs_2_, bf16[384,768]{1,0:T(8,128)(2,1)S(1)} %get-tuple-element.77.grad_ref.refs_4_, bf16[3072,768]{1,0:T(8,128)(2,1)S(1)} %pad_maximum_fusion.up_ref, bf16[768,3072]{1,0:T(8,128)(2,1)} %pad_maximum_fusion.1.down_ref), custom_call_target="tpu_custom_call" | custom-call | flops 1 | bytes 1 | tf_op jit(solution)/shard_map/pallas_call | solution.py:30
  102.0 5.4 %shard_map.80 = (bf16[384,3072]{1,0:T(8,128)(2,1)S(1)}, bf16[3072,384]{1,0:T(8,128)(2,1)S(1)}) custom-call(bf16[2,384,3072]{2,1,0:T(8,128)(2,1)S(1)} %bitcast.75, bf16[2,128,3072]{2,1,0:T(8,128)(2,1)S(1)} %constant_dynamic-update-slice_fusion.3.pair_ref.refs_1_, bf16[384,768]{1,0:T(8,128)(2,1)S(1)} %get-tuple-element.76.act_ref.refs_2_, ...), custom_call_target="tpu_custom_call" | custom-call | flops 1 | bytes 1 | tf_op jit(solution)/shard_map/pallas_call | solution.py:30
  107.5 5.4 %shard_map.79 = (bf16[384,3072]{1,0:T(8,128)(2,1)S(1)}, bf16[3072,384]{1,0:T(8,128)(2,1)S(1)}) custom-call(bf16[2,384,3072]{2,1,0:T(8,128)(2,1)S(1)} %bitcast.75, bf16[2,128,3072]{2,1,0:T(8,128)(2,1)S(1)} %constant_dynamic-update-slice_fusion.3.pair_ref.refs_1_, bf16[384,768]{1,0:T(8,128)(2,1)S(1)} %get-tuple-element.76.act_ref.refs_2_, ...), custom_call_target="tpu_custom_call" | custom-call | flops 1 | bytes 1 | tf_op jit(solution)/shard_map/pallas_call | solution.py:30
  113.9 1.7 add_convert_fusion.1
  116.8 1.8 collective-permute-start.21
  118.7 1.3 pad_maximum_fusion.9
  120.3 3.2 %collective-permute-start.24 = (bf16[384,768]{1,0:T(8,128)(2,1)S(1)}, bf16[384,768]{1,0:T(8,128)(2,1)}, u32[]{:S(2)}, u32[]{:S(2)}) collective-permute-start(bf16[384,768]{1,0:T(8,128)(2,1)S(1)} %add_convert_fusion.8), channel_id=1, source_target_pairs={{0,96},{16,48},{32,0},{48,80},{64,32},{80,112},{96,64},{112,16},{1... | collective-permute-start | bytes 1769480 | tf_op jit(solution)/shard_map/ppermute | solution.py:140
  123.5 1.4 copy-done.6
  125.9 11.6 %collective-permute-done.21 = bf16[2,128,3072]{2,1,0:T(8,128)(2,1)} collective-permute-done((bf16[2,128,3072]{2,1,0:T(8,128)(2,1)}, bf16[2,128,3072]{2,1,0:T(8,128)(2,1)}, u32[]{:S(2)}, u32[]{:S(2)}) %collective-permute-start.21) | collective-permute-done | bytes 1572896 | tf_op jit(solution)/shard_map/ppermute | solution.py:157
  137.5 4.3 %collective-permute-done.22 = bf16[2,128,3072]{2,1,0:T(8,128)(2,1)} collective-permute-done((bf16[2,128,3072]{2,1,0:T(8,128)(2,1)}, bf16[2,128,3072]{2,1,0:T(8,128)(2,1)}, u32[]{:S(2)}, u32[]{:S(2)}) %collective-permute-start.22) | collective-permute-done | bytes 1572896 | tf_op jit(solution)/shard_map/ppermute | solution.py:157
  141.9 3.3 %add_convert_fusion = bf16[2,128,3072]{2,1,0:T(8,128)(2,1)S(1)} fusion(bf16[2,128,3072]{2,1,0:T(8,128)(2,1)} %collective-permute-done.22, bf16[2,128,3072]{2,1,0:T(8,128)(2,1)} %collective-permute-done.21, bf16[2,384,3072]{2,1,0:T(8,128)(2,1)} %copy-done.2), kind=kLoop, calls=%fused_computation.2 | loop fusion | flops 4718592 | bytes 6291456 | tf_op jit(solution)/shard_map/convert_element_type | solution.py:260
  145.3 1.8 collective-permute-start.27
  147.1 1.3 collective-permute-start.29
  148.4 1.3 add_convert_fusion.5
  149.8 1.3 add_convert_fusion.6
  151.2 3.2 %collective-permute-start.30 = (bf16[384,768]{1,0:T(8,128)(2,1)S(1)}, bf16[384,768]{1,0:T(8,128)(2,1)S(1)}, u32[]{:S(2)}, u32[]{:S(2)}) collective-permute-start(bf16[384,768]{1,0:T(8,128)(2,1)S(1)} %add_convert_fusion.6), channel_id=1, source_target_pairs={{0,96},{16,48},{32,0},{48,80},{64,32},{80,112},{96,64},{112,16},{1... | collective-permute-start | bytes 1769480 | tf_op jit(solution)/shard_map/ppermute | solution.py:140
  154.4 2.3 %collective-permute-done.27 = bf16[2,32,3072]{2,1,0:T(8,128)(2,1)S(1)} collective-permute-done((bf16[2,32,3072]{2,1,0:T(8,128)(2,1)S(1)}, bf16[2,32,3072]{2,1,0:T(8,128)(2,1)S(1)}, u32[]{:S(2)}, u32[]{:S(2)}) %collective-permute-start.27) | collective-permute-done | bytes 393248 | tf_op jit(solution)/shard_map/ppermute | solution.py:157
  156.7 3.7 %collective-permute-done.29 = bf16[2,32,3072]{2,1,0:T(8,128)(2,1)S(1)} collective-permute-done((bf16[2,32,3072]{2,1,0:T(8,128)(2,1)S(1)}, bf16[2,32,3072]{2,1,0:T(8,128)(2,1)S(1)}, u32[]{:S(2)}, u32[]{:S(2)}) %collective-permute-start.29) | collective-permute-done | bytes 393248 | tf_op jit(solution)/shard_map/ppermute | solution.py:157
  160.5 4.9 %collective-permute-done.31 = bf16[768,384]{1,0:T(8,128)(2,1)S(1)} collective-permute-done((bf16[768,384]{1,0:T(8,128)(2,1)S(1)}, bf16[768,384]{1,0:T(8,128)(2,1)S(1)}, u32[]{:S(2)}, u32[]{:S(2)}) %collective-permute-start.31) | collective-permute-done | bytes 589856 | tf_op jit(solution)/shard_map/ppermute | solution.py:140
  165.5 2.6 %collective-permute-start.32 = (bf16[2,32,768]{2,1,0:T(8,128)(2,1)S(1)}, bf16[2,32,768]{2,1,0:T(8,128)(2,1)S(1)}, u32[]{:S(2)}, u32[]{:S(2)}) collective-permute-start(bf16[2,32,768]{2,1,0:T(8,128)(2,1)S(1)} %pad_maximum_fusion.11), channel_id=1, source_target_pairs={{0,96},{16,48},{32,0},{48,80},{64,32},{80,112},{96,64},{112,16},{1... | collective-permute-start | bytes 294920 | tf_op jit(solution)/shard_map/ppermute | solution.py:140
  169.4 2.4 %collective-permute-start.36 = (bf16[384,768]{1,0:T(8,128)(2,1)S(1)}, bf16[384,768]{1,0:T(8,128)(2,1)S(1)}, u32[]{:S(2)}, u32[]{:S(2)}) collective-permute-start(bf16[384,768]{1,0:T(8,128)(2,1)S(1)} %add_convert_fusion.3), channel_id=1, source_target_pairs={{0,96},{16,48},{32,0},{48,80},{64,32},{80,112},{96,64},{112,16},{1... | collective-permute-start | bytes 1769480 | tf_op jit(solution)/shard_map/ppermute | solution.py:140
  172.8 2.2 %collective-permute-done.33 = bf16[2,32,768]{2,1,0:T(8,128)(2,1)S(1)} collective-permute-done((bf16[2,32,768]{2,1,0:T(8,128)(2,1)S(1)}, bf16[2,32,768]{2,1,0:T(8,128)(2,1)S(1)}, u32[]{:S(2)}, u32[]{:S(2)}) %collective-permute-start.33) | collective-permute-done | bytes 98336 | tf_op jit(solution)/shard_map/ppermute | solution.py:140
  176.7 9.7 %collective-permute-done.36 = bf16[384,768]{1,0:T(8,128)(2,1)S(1)} collective-permute-done((bf16[384,768]{1,0:T(8,128)(2,1)S(1)}, bf16[384,768]{1,0:T(8,128)(2,1)S(1)}, u32[]{:S(2)}, u32[]{:S(2)}) %collective-permute-start.36) | collective-permute-done | bytes 589856 | tf_op jit(solution)/shard_map/ppermute | solution.py:140
  186.3 1.2 convert_add_fusion
  (116 shorter events, 19.5 us)
Async XLA Ops:
  1.7 7.8 %collective-permute-start = (bf16[2,32,768]{2,1,0:T(8,128)(2,1)S(1)}, bf16[2,32,768]{2,1,0:T(8,128)(2,1)S(1)}, u32[]{:S(2)}, u32[]{:S(2)}) collective-permute-start(bf16[2,32,768]{2,1,0:T(8,128)(2,1)S(1)} %get-tuple-element.117), channel_id=1, source_target_pairs={{0,32},{16,112},{32,64},{48,16},{64,96},{80,48},{96,0},{112,80},{1... | collective-permute-start | bytes 294920 | tf_op jit(solution)/shard_map/ppermute | solution.py:140
  3.4 7.9 %collective-permute-start.1 = (bf16[2,32,768]{2,1,0:T(8,128)(2,1)S(1)}, bf16[2,32,768]{2,1,0:T(8,128)(2,1)S(1)}, u32[]{:S(2)}, u32[]{:S(2)}) collective-permute-start(bf16[2,32,768]{2,1,0:T(8,128)(2,1)S(1)} %get-tuple-element.118), channel_id=1, source_target_pairs={{0,64},{16,80},{32,96},{48,112},{64,0},{80,16},{96,32},{112,48},{1... | collective-permute-start | bytes 294920 | tf_op jit(solution)/shard_map/ppermute | solution.py:140
  6.1 5.7 %collective-permute-start.2 = (bf16[2,32,768]{2,1,0:T(8,128)(2,1)S(1)}, bf16[2,32,768]{2,1,0:T(8,128)(2,1)S(1)}, u32[]{:S(2)}, u32[]{:S(2)}) collective-permute-start(bf16[2,32,768]{2,1,0:T(8,128)(2,1)S(1)} %get-tuple-element.119), channel_id=1, source_target_pairs={{0,96},{16,48},{32,0},{48,80},{64,32},{80,112},{96,64},{112,16},{1... | collective-permute-start | bytes 294920 | tf_op jit(solution)/shard_map/ppermute | solution.py:140
  7.5 15.8 %collective-permute-start.4 = (bf16[384,768]{1,0:T(8,128)(2,1)}, bf16[384,768]{1,0:T(8,128)(2,1)S(1)}, u32[]{:S(2)}, u32[]{:S(2)}) collective-permute-start(bf16[384,768]{1,0:T(8,128)(2,1)} %param.6), channel_id=1, source_target_pairs={{0,96},{16,48},{32,0},{48,80},{64,32},{80,112},{96,64},{112,16},{1... | collective-permute-start | bytes 1769480 | tf_op jit(solution)/shard_map/ppermute | solution.py:140
  7.6 16.6 %collective-permute-start.3 = (bf16[768,384]{1,0:T(8,128)(2,1)}, bf16[768,384]{1,0:T(8,128)(2,1)S(1)}, u32[]{:S(2)}, u32[]{:S(2)}) collective-permute-start(bf16[768,384]{1,0:T(8,128)(2,1)} %param.5), channel_id=1, source_target_pairs={{0,32},{16,112},{32,64},{48,16},{64,96},{80,48},{96,0},{112,80},{1... | collective-permute-start | bytes 1769480 | tf_op jit(solution)/shard_map/ppermute | solution.py:140
  11.8 31.7 %copy-start.5 = (bf16[768,384]{1,0:T(8,128)(2,1)S(1)}, bf16[768,384]{1,0:T(8,128)(2,1)}, u32[]{:S(2)}) copy-start(bf16[768,384]{1,0:T(8,128)(2,1)} %param.5) | copy-start | bytes 1769476
  24.2 13.5 %collective-permute-start.7 = (bf16[2,32,3072]{2,1,0:T(8,128)(2,1)S(1)}, bf16[2,32,3072]{2,1,0:T(8,128)(2,1)S(1)}, u32[]{:S(2)}, u32[]{:S(2)}) collective-permute-start(bf16[2,32,3072]{2,1,0:T(8,128)(2,1)S(1)} %pad_maximum_fusion.10), channel_id=1, source_target_pairs={{0,12},{1,13},{2,14},{3,15},{4,0},{5,1},{6,2},{7,3},{8,4},{9,5},{1... | collective-permute-start | bytes 1179656 | tf_op jit(solution)/shard_map/ppermute | solution.py:157
  28.2 9.5 %collective-permute-start.6 = (bf16[2,32,3072]{2,1,0:T(8,128)(2,1)S(1)}, bf16[2,32,3072]{2,1,0:T(8,128)(2,1)S(1)}, u32[]{:S(2)}, u32[]{:S(2)}) collective-permute-start(bf16[2,32,3072]{2,1,0:T(8,128)(2,1)S(1)} %pad_maximum_fusion.10), channel_id=1, source_target_pairs={{0,8},{1,9},{2,10},{3,11},{4,12},{5,13},{6,14},{7,15},{8,0},{9,1},... | collective-permute-start | bytes 1179656 | tf_op jit(solution)/shard_map/ppermute | solution.py:157
  28.2 13.2 %collective-permute-start.5 = (bf16[2,32,3072]{2,1,0:T(8,128)(2,1)S(1)}, bf16[2,32,3072]{2,1,0:T(8,128)(2,1)S(1)}, u32[]{:S(2)}, u32[]{:S(2)}) collective-permute-start(bf16[2,32,3072]{2,1,0:T(8,128)(2,1)S(1)} %pad_maximum_fusion.10), channel_id=1, source_target_pairs={{0,4},{1,5},{2,6},{3,7},{4,8},{5,9},{6,10},{7,11},{8,12},{9,13},{1... | collective-permute-start | bytes 1179656 | tf_op jit(solution)/shard_map/ppermute | solution.py:157
  29.5 13.2 %collective-permute-start.9 = (bf16[384,768]{1,0:T(8,128)(2,1)S(1)}, bf16[384,768]{1,0:T(8,128)(2,1)S(1)}, u32[]{:S(2)}, u32[]{:S(2)}) collective-permute-start(bf16[384,768]{1,0:T(8,128)(2,1)S(1)} %collective-permute-done.4), channel_id=1, source_target_pairs={{0,96},{16,48},{32,0},{48,80},{64,32},{80,112},{96,64},{112,16},{1... | collective-permute-start | bytes 1769480 | tf_op jit(solution)/shard_map/ppermute | solution.py:140
  31.3 12.1 %collective-permute-start.8 = (bf16[768,384]{1,0:T(8,128)(2,1)S(1)}, bf16[768,384]{1,0:T(8,128)(2,1)S(1)}, u32[]{:S(2)}, u32[]{:S(2)}) collective-permute-start(bf16[768,384]{1,0:T(8,128)(2,1)S(1)} %collective-permute-done.3), channel_id=1, source_target_pairs={{0,32},{16,112},{32,64},{48,16},{64,96},{80,48},{96,0},{112,80},{1... | collective-permute-start | bytes 1769480 | tf_op jit(solution)/shard_map/ppermute | solution.py:140
  41.5 26.2 %copy-start.10 = (bf16[384,768]{1,0:T(8,128)(2,1)S(1)}, bf16[384,768]{1,0:T(8,128)(2,1)}, u32[]{:S(2)}) copy-start(bf16[384,768]{1,0:T(8,128)(2,1)} %param.6) | copy-start | bytes 1769476
  43.6 24.1 %collective-permute-start.12 = (bf16[2304,384]{1,0:T(8,128)(2,1)S(1)}, bf16[2304,384]{1,0:T(8,128)(2,1)S(1)}, u32[]{:S(2)}, u32[]{:S(2)}) collective-permute-start(bf16[2304,384]{1,0:T(8,128)(2,1)S(1)} %pad_maximum_fusion.6), channel_id=1, source_target_pairs={{0,16},{16,0},{1,17},{17,1},{2,18},{18,2},{3,19},{19,3},{4,20},{20... | collective-permute-start | bytes 5308424 | tf_op jit(solution)/shard_map/ppermute | solution.py:144
  43.7 20.7 %collective-permute-start.11 = (bf16[2,128,3072]{2,1,0:T(8,128)(2,1)S(1)}, bf16[2,128,3072]{2,1,0:T(8,128)(2,1)S(1)}, u32[]{:S(2)}, u32[]{:S(2)}) collective-permute-start(bf16[2,128,3072]{2,1,0:T(8,128)(2,1)S(1)} %pad_maximum_fusion.7), channel_id=1, source_target_pairs={{0,3},{1,0},{2,1},{3,2},{4,7},{5,4},{6,5},{7,6},{8,11},{9,8},{10,9... | collective-permute-start | bytes 4718600 | tf_op jit(solution)/shard_map/ppermute | solution.py:157
  46.0 21.6 %collective-permute-start.10 = (bf16[2,128,3072]{2,1,0:T(8,128)(2,1)S(1)}, bf16[2,128,3072]{2,1,0:T(8,128)(2,1)S(1)}, u32[]{:S(2)}, u32[]{:S(2)}) collective-permute-start(bf16[2,128,3072]{2,1,0:T(8,128)(2,1)S(1)} %pad_maximum_fusion.7), channel_id=1, source_target_pairs={{0,1},{1,2},{2,3},{3,0},{4,5},{5,6},{6,7},{7,4},{8,9},{9,10},{10,1... | collective-permute-start | bytes 4718600 | tf_op jit(solution)/shard_map/ppermute | solution.py:157
  46.0 15.7 %collective-permute-start.14 = (bf16[384,768]{1,0:T(8,128)(2,1)S(1)}, bf16[384,768]{1,0:T(8,128)(2,1)S(1)}, u32[]{:S(2)}, u32[]{:S(2)}) collective-permute-start(bf16[384,768]{1,0:T(8,128)(2,1)S(1)} %collective-permute-done.9), channel_id=1, source_target_pairs={{0,96},{16,48},{32,0},{48,80},{64,32},{80,112},{96,64},{112,16},{1... | collective-permute-start | bytes 1769480 | tf_op jit(solution)/shard_map/ppermute | solution.py:140
  49.0 15.4 %collective-permute-start.13 = (bf16[768,384]{1,0:T(8,128)(2,1)S(1)}, bf16[768,384]{1,0:T(8,128)(2,1)S(1)}, u32[]{:S(2)}, u32[]{:S(2)}) collective-permute-start(bf16[768,384]{1,0:T(8,128)(2,1)S(1)} %collective-permute-done.8), channel_id=1, source_target_pairs={{0,32},{16,112},{32,64},{48,16},{64,96},{80,48},{96,0},{112,80},{1... | collective-permute-start | bytes 1769480 | tf_op jit(solution)/shard_map/ppermute | solution.py:140
  68.0 7.0 %collective-permute-start.18 = (bf16[384,3072]{1,0:T(8,128)(2,1)S(1)}, bf16[384,3072]{1,0:T(8,128)(2,1)S(1)}, u32[]{:S(2)}, u32[]{:S(2)}) collective-permute-start(bf16[384,3072]{1,0:T(8,128)(2,1)S(1)} %pad_maximum_fusion.4), channel_id=1, source_target_pairs={{0,16},{16,0},{1,17},{17,1},{2,18},{18,2},{3,19},{19,3},{4,20},{20... | collective-permute-start | bytes 7077896 | tf_op jit(solution)/shard_map/ppermute | solution.py:144
  68.9 5.4 %collective-permute-start.17 = (bf16[768,384]{1,0:T(8,128)(2,1)S(1)}, bf16[768,384]{1,0:T(8,128)(2,1)S(1)}, u32[]{:S(2)}, u32[]{:S(2)}) collective-permute-start(bf16[768,384]{1,0:T(8,128)(2,1)S(1)} %collective-permute-done.13), channel_id=1, source_target_pairs={{0,16},{16,0},{1,17},{17,1},{2,18},{18,2},{3,19},{19,3},{4,20},{20... | collective-permute-start | bytes 1769480 | tf_op jit(solution)/shard_map/ppermute | solution.py:144
  69.1 16.4 %collective-permute-start.16 = (bf16[2,64,3072]{2,1,0:T(8,128)(2,1)S(1)}, bf16[2,64,3072]{2,1,0:T(8,128)(2,1)S(1)}, u32[]{:S(2)}, u32[]{:S(2)}) collective-permute-start(bf16[2,64,3072]{2,1,0:T(8,128)(2,1)S(1)} %slice.191), channel_id=1, source_target_pairs={{0,3},{1,0},{2,1},{3,2},{4,7},{5,4},{6,5},{7,6},{8,11},{9,8},{10,9... | collective-permute-start | bytes 2359304 | tf_op jit(solution)/shard_map/ppermute | solution.py:157
  71.5 14.0 %collective-permute-start.15 = (bf16[2,64,3072]{2,1,0:T(8,128)(2,1)S(1)}, bf16[2,64,3072]{2,1,0:T(8,128)(2,1)S(1)}, u32[]{:S(2)}, u32[]{:S(2)}) collective-permute-start(bf16[2,64,3072]{2,1,0:T(8,128)(2,1)S(1)} %slice.190), channel_id=1, source_target_pairs={{0,1},{1,2},{2,3},{3,0},{4,5},{5,6},{6,7},{7,4},{8,9},{9,10},{10,1... | collective-permute-start | bytes 2359304 | tf_op jit(solution)/shard_map/ppermute | solution.py:157
  75.4 3.8 %slice-start.1 = ((s8[4718592]{0:T(1024)(128)(4,1)}), s8[524288]{0:T(1024)(128)(4,1)S(1)}, s32[]{:S(2)}) async-start(s8[4718592]{0:T(1024)(128)(4,1)} %bitcast.72), calls=%async_computation.1 | async-start | bytes 1048576
  79.2 6.5 %copy-start = (bf16[768,3072]{1,0:T(8,128)(2,1)S(1)}, bf16[768,3072]{1,0:T(8,128)(2,1)}, u32[]{:S(2)}) copy-start(bf16[768,3072]{1,0:T(8,128)(2,1)} %pad_maximum_fusion.1.down_ref) | copy-start | bytes 14155780
  91.7 10.3 %slice-start.2 = ((s8[4718592]{0:T(1024)(128)(4,1)}), s8[4194304]{0:T(1024)(128)(4,1)S(1)}, s32[]{:S(2)}) async-start(s8[4718592]{0:T(1024)(128)(4,1)} %bitcast.74), calls=%async_computation.2 | async-start | bytes 8388608
  92.7 21.0 %collective-permute-start.20 = (bf16[2,64,3072]{2,1,0:T(8,128)(2,1)}, bf16[2,64,3072]{2,1,0:T(8,128)(2,1)S(1)}, u32[]{:S(2)}, u32[]{:S(2)}) collective-permute-start(bf16[2,64,3072]{2,1,0:T(8,128)(2,1)} %get-tuple-element.110), channel_id=1, source_target_pairs={{0,1},{1,2},{2,3},{3,0},{4,5},{5,6},{6,7},{7,4},{8,9},{9,10},{10,1... | collective-permute-start | bytes 2359304 | tf_op jit(solution)/shard_map/ppermute | solution.py:157
  94.4 7.7 %slice-start.3 = ((s8[4718592]{0:T(1024)(128)(4,1)}), s8[524288]{0:T(1024)(128)(4,1)S(1)}, s32[]{:S(2)}) async-start(s8[4718592]{0:T(1024)(128)(4,1)} %bitcast.74), calls=%async_computation.3 | async-start | bytes 1048576
  94.4 19.4 %collective-permute-start.19 = (bf16[2,64,3072]{2,1,0:T(8,128)(2,1)S(1)}, bf16[2,64,3072]{2,1,0:T(8,128)(2,1)}, u32[]{:S(2)}, u32[]{:S(2)}) collective-permute-start(bf16[2,64,3072]{2,1,0:T(8,128)(2,1)S(1)} %get-tuple-element.111), channel_id=1, source_target_pairs={{0,3},{1,0},{2,1},{3,2},{4,7},{5,4},{6,5},{7,6},{8,11},{9,8},{10,9... | collective-permute-start | bytes 2359304 | tf_op jit(solution)/shard_map/ppermute | solution.py:157
  102.0 11.8 %copy-start.2 = (bf16[2,384,3072]{2,1,0:T(8,128)(2,1)}, bf16[2,384,3072]{2,1,0:T(8,128)(2,1)S(1)}, u32[]{:S(2)}) copy-start(bf16[2,384,3072]{2,1,0:T(8,128)(2,1)S(1)} %shard_map.78) | copy-start | bytes 14155780
  112.9 7.2 %copy-start.3 = (bf16[384,3072]{1,0:T(8,128)(2,1)}, bf16[384,3072]{1,0:T(8,128)(2,1)S(1)}, u32[]{:S(2)}) copy-start(bf16[384,3072]{1,0:T(8,128)(2,1)S(1)} %get-tuple-element.85) | copy-start | bytes 7077892
  112.9 7.2 %collective-permute-start.23 = (bf16[384,3072]{1,0:T(8,128)(2,1)S(1)}, bf16[384,3072]{1,0:T(8,128)(2,1)S(1)}, u32[]{:S(2)}, u32[]{:S(2)}) collective-permute-start(bf16[384,3072]{1,0:T(8,128)(2,1)S(1)} %get-tuple-element.86), channel_id=1, source_target_pairs={{0,16},{16,0},{1,17},{17,1},{2,18},{18,2},{3,19},{19,3},{4,20},{20... | collective-permute-start | bytes 7077896 | tf_op jit(solution)/shard_map/ppermute | solution.py:144
  113.6 9.9 %collective-permute-start.25 = (bf16[3072,384]{1,0:T(8,128)(2,1)S(1)}, bf16[3072,384]{1,0:T(8,128)(2,1)S(1)}, u32[]{:S(2)}, u32[]{:S(2)}) collective-permute-start(bf16[3072,384]{1,0:T(8,128)(2,1)S(1)} %get-tuple-element.88), channel_id=1, source_target_pairs={{0,16},{16,0},{1,17},{17,1},{2,18},{18,2},{3,19},{19,3},{4,20},{20... | collective-permute-start | bytes 7077896 | tf_op jit(solution)/shard_map/ppermute | solution.py:144
  116.8 20.7 %collective-permute-start.21 = (bf16[2,128,3072]{2,1,0:T(8,128)(2,1)}, bf16[2,128,3072]{2,1,0:T(8,128)(2,1)}, u32[]{:S(2)}, u32[]{:S(2)}) collective-permute-start(bf16[2,128,3072]{2,1,0:T(8,128)(2,1)} %pad_maximum_fusion.8), channel_id=1, source_target_pairs={{0,3},{1,0},{2,1},{3,2},{4,7},{5,4},{6,5},{7,6},{8,11},{9,8},{10,9... | collective-permute-start | bytes 4718600 | tf_op jit(solution)/shard_map/ppermute | solution.py:157
  119.9 21.9 %collective-permute-start.22 = (bf16[2,128,3072]{2,1,0:T(8,128)(2,1)}, bf16[2,128,3072]{2,1,0:T(8,128)(2,1)}, u32[]{:S(2)}, u32[]{:S(2)}) collective-permute-start(bf16[2,128,3072]{2,1,0:T(8,128)(2,1)} %pad_maximum_fusion.9), channel_id=1, source_target_pairs={{0,1},{1,2},{2,3},{3,0},{4,5},{5,6},{6,7},{7,4},{8,9},{9,10},{10,1... | collective-permute-start | bytes 4718600 | tf_op jit(solution)/shard_map/ppermute | solution.py:157
  120.1 5.8 %copy-start.8 = (bf16[384,3072]{1,0:T(8,128)(2,1)}, bf16[384,3072]{1,0:T(8,128)(2,1)S(1)}, u32[]{:S(2)}) copy-start(bf16[384,3072]{1,0:T(8,128)(2,1)S(1)} %collective-permute-done.23) | copy-start | bytes 7077892
  120.3 21.6 %collective-permute-start.24 = (bf16[384,768]{1,0:T(8,128)(2,1)S(1)}, bf16[384,768]{1,0:T(8,128)(2,1)}, u32[]{:S(2)}, u32[]{:S(2)}) collective-permute-start(bf16[384,768]{1,0:T(8,128)(2,1)S(1)} %add_convert_fusion.8), channel_id=1, source_target_pairs={{0,96},{16,48},{32,0},{48,80},{64,32},{80,112},{96,64},{112,16},{1... | collective-permute-start | bytes 1769480 | tf_op jit(solution)/shard_map/ppermute | solution.py:140
  125.9 16.0 %collective-permute-start.26 = (bf16[768,384]{1,0:T(8,128)(2,1)}, bf16[768,384]{1,0:T(8,128)(2,1)}, u32[]{:S(2)}, u32[]{:S(2)}) collective-permute-start(bf16[768,384]{1,0:T(8,128)(2,1)} %add_convert_fusion.7), channel_id=1, source_target_pairs={{0,32},{16,112},{32,64},{48,16},{64,96},{80,48},{96,0},{112,80},{1... | collective-permute-start | bytes 1769480 | tf_op jit(solution)/shard_map/ppermute | solution.py:140
  141.9 7.9 %copy-start.9 = (bf16[384,3072]{1,0:T(8,128)(2,1)S(1)}, bf16[384,3072]{1,0:T(8,128)(2,1)}, u32[]{:S(2)}) copy-start(bf16[384,3072]{1,0:T(8,128)(2,1)} %copy-done.8) | copy-start | bytes 7077892
  145.2 4.6 %copy-start.4 = (bf16[384,3072]{1,0:T(8,128)(2,1)S(1)}, bf16[384,3072]{1,0:T(8,128)(2,1)}, u32[]{:S(2)}) copy-start(bf16[384,3072]{1,0:T(8,128)(2,1)} %copy-done.3) | copy-start | bytes 7077892
  145.3 11.4 %collective-permute-start.27 = (bf16[2,32,3072]{2,1,0:T(8,128)(2,1)S(1)}, bf16[2,32,3072]{2,1,0:T(8,128)(2,1)S(1)}, u32[]{:S(2)}, u32[]{:S(2)}) collective-permute-start(bf16[2,32,3072]{2,1,0:T(8,128)(2,1)S(1)} %get-tuple-element.107), channel_id=1, source_target_pairs={{0,12},{1,13},{2,14},{3,15},{4,0},{5,1},{6,2},{7,3},{8,4},{9,5},{1... | collective-permute-start | bytes 1179656 | tf_op jit(solution)/shard_map/ppermute | solution.py:157
  147.1 9.5 %collective-permute-start.28 = (bf16[2,32,3072]{2,1,0:T(8,128)(2,1)S(1)}, bf16[2,32,3072]{2,1,0:T(8,128)(2,1)S(1)}, u32[]{:S(2)}, u32[]{:S(2)}) collective-permute-start(bf16[2,32,3072]{2,1,0:T(8,128)(2,1)S(1)} %get-tuple-element.108), channel_id=1, source_target_pairs={{0,8},{1,9},{2,10},{3,11},{4,12},{5,13},{6,14},{7,15},{8,0},{9,1},... | collective-permute-start | bytes 1179656 | tf_op jit(solution)/shard_map/ppermute | solution.py:157
  147.1 13.2 %collective-permute-start.29 = (bf16[2,32,3072]{2,1,0:T(8,128)(2,1)S(1)}, bf16[2,32,3072]{2,1,0:T(8,128)(2,1)S(1)}, u32[]{:S(2)}, u32[]{:S(2)}) collective-permute-start(bf16[2,32,3072]{2,1,0:T(8,128)(2,1)S(1)} %get-tuple-element.109), channel_id=1, source_target_pairs={{0,4},{1,5},{2,6},{3,7},{4,8},{5,9},{6,10},{7,11},{8,12},{9,13},{1... | collective-permute-start | bytes 1179656 | tf_op jit(solution)/shard_map/ppermute | solution.py:157
  149.7 15.7 %collective-permute-start.31 = (bf16[768,384]{1,0:T(8,128)(2,1)S(1)}, bf16[768,384]{1,0:T(8,128)(2,1)S(1)}, u32[]{:S(2)}, u32[]{:S(2)}) collective-permute-start(bf16[768,384]{1,0:T(8,128)(2,1)S(1)} %add_convert_fusion.5), channel_id=1, source_target_pairs={{0,32},{16,112},{32,64},{48,16},{64,96},{80,48},{96,0},{112,80},{1... | collective-permute-start | bytes 1769480 | tf_op jit(solution)/shard_map/ppermute | solution.py:140
  151.2 14.2 %collective-permute-start.30 = (bf16[384,768]{1,0:T(8,128)(2,1)S(1)}, bf16[384,768]{1,0:T(8,128)(2,1)S(1)}, u32[]{:S(2)}, u32[]{:S(2)}) collective-permute-start(bf16[384,768]{1,0:T(8,128)(2,1)S(1)} %add_convert_fusion.6), channel_id=1, source_target_pairs={{0,96},{16,48},{32,0},{48,80},{64,32},{80,112},{96,64},{112,16},{1... | collective-permute-start | bytes 1769480 | tf_op jit(solution)/shard_map/ppermute | solution.py:140
  165.5 7.3 %collective-permute-start.32 = (bf16[2,32,768]{2,1,0:T(8,128)(2,1)S(1)}, bf16[2,32,768]{2,1,0:T(8,128)(2,1)S(1)}, u32[]{:S(2)}, u32[]{:S(2)}) collective-permute-start(bf16[2,32,768]{2,1,0:T(8,128)(2,1)S(1)} %pad_maximum_fusion.11), channel_id=1, source_target_pairs={{0,96},{16,48},{32,0},{48,80},{64,32},{80,112},{96,64},{112,16},{1... | collective-permute-start | bytes 294920 | tf_op jit(solution)/shard_map/ppermute | solution.py:140
  168.1 6.8 %collective-permute-start.33 = (bf16[2,32,768]{2,1,0:T(8,128)(2,1)S(1)}, bf16[2,32,768]{2,1,0:T(8,128)(2,1)S(1)}, u32[]{:S(2)}, u32[]{:S(2)}) collective-permute-start(bf16[2,32,768]{2,1,0:T(8,128)(2,1)S(1)} %pad_maximum_fusion.12), channel_id=1, source_target_pairs={{0,64},{16,80},{32,96},{48,112},{64,0},{80,16},{96,32},{112,48},{1... | collective-permute-start | bytes 294920 | tf_op jit(solution)/shard_map/ppermute | solution.py:140
  168.3 7.6 %collective-permute-start.34 = (bf16[2,32,768]{2,1,0:T(8,128)(2,1)S(1)}, bf16[2,32,768]{2,1,0:T(8,128)(2,1)S(1)}, u32[]{:S(2)}, u32[]{:S(2)}) collective-permute-start(bf16[2,32,768]{2,1,0:T(8,128)(2,1)S(1)} %pad_maximum_fusion.13), channel_id=1, source_target_pairs={{0,32},{16,112},{32,64},{48,16},{64,96},{80,48},{96,0},{112,80},{1... | collective-permute-start | bytes 294920 | tf_op jit(solution)/shard_map/ppermute | solution.py:140
  169.4 16.9 %collective-permute-start.36 = (bf16[384,768]{1,0:T(8,128)(2,1)S(1)}, bf16[384,768]{1,0:T(8,128)(2,1)S(1)}, u32[]{:S(2)}, u32[]{:S(2)}) collective-permute-start(bf16[384,768]{1,0:T(8,128)(2,1)S(1)} %add_convert_fusion.3), channel_id=1, source_target_pairs={{0,96},{16,48},{32,0},{48,80},{64,32},{80,112},{96,64},{112,16},{1... | collective-permute-start | bytes 1769480 | tf_op jit(solution)/shard_map/ppermute | solution.py:140
  172.1 15.8 %collective-permute-start.35 = (bf16[768,384]{1,0:T(8,128)(2,1)S(1)}, bf16[768,384]{1,0:T(8,128)(2,1)S(1)}, u32[]{:S(2)}, u32[]{:S(2)}) collective-permute-start(bf16[768,384]{1,0:T(8,128)(2,1)S(1)} %add_convert_fusion.4), channel_id=1, source_target_pairs={{0,32},{16,112},{32,64},{48,16},{64,96},{80,48},{96,0},{112,80},{1... | collective-permute-start | bytes 1769480 | tf_op jit(solution)/shard_map/ppermute | solution.py:140
  (4 other events, 10.5 us)

commit v2 on v1

--- a/solution.py
+++ b/solution.py
@@ -185,21 +185,23 @@
 
     ups, downs = [up_weight], [down_weight]
 
-    def step(*values):
+    def step():
         ups.append(along_x(ups[-1], 1))
         downs.append(along_x(downs[-1], -1))
-        *values, ups[-1], downs[-1] = held(*values, ups[-1], downs[-1])
-        return values
 
     def join(parts, axis):
         return jnp.concatenate(parts, axis=axis)
 
-    (own,) = step(own)
-    (first,) = step(join([own] + [plane(own, 0, hop) for hop in (1, 2, 3)], 1))
+    step()
+    own, ups[0], downs[0] = held(own, ups[0], downs[0])
+    step()
+    first = join([own] + [plane(own, 0, hop) for hop in (1, 2, 3)], 1)
+    first, ups[1], downs[1] = held(first, ups[1], downs[1])
 
     up_early = across(join(ups[:3], 0))
     left, right = plane(first, 1, 1), plane(first, 1, -1)
-    left, right, up_early = step(left, right, up_early)
+    step()
+    left, right, up_early, ups[3], downs[3] = held(left, right, up_early, ups[3], downs[3])
     (down_mine,) = held(join(downs, 1))
     up_late, down_theirs = across(ups[3]), across(down_mine)
     far = [plane(left[:, :half], 1, 1), plane(right[:, half:], 1, -1)]
@@ -224,15 +226,21 @@
     far_acts, far_grads = forward(far, up, down)
 
     far_sums = backward(far_acts, far_grads, up, down)
-    far_sums, near_acts, near_grads, far_acts, far_grads = held(
-        far_sums, near_acts, near_grads, far_acts, far_grads
-    )
-    far_back = [plane(far_sums[:, :half], 1, -1), plane(far_sums[:, half:], 1, 1)]
+    far_back = [far_sums[:, :half], far_sums[:, half:]]
+    *far_back, near_acts, near_grads, far_acts, far_grads = held(
+        *far_back, near_acts, near_grads, far_acts, far_grads
+    )
+    far_back = [plane(far_back[0], 1, -1), plane(far_back[1], 1, 1)]
     sets, acts, grads = (near, far), (near_acts, far_acts), (near_grads, far_grads)
-    down_theirs, up_theirs = (across(value) for value in weight_sums(sets, acts, grads, 1))
+    theirs = weight_sums(sets, acts, grads, 1)
+    near_acts, near_grads, *theirs = held(near_acts, near_grads, *theirs)
+    down_theirs, up_theirs = (across(value) for value in theirs)
     near_sums = backward(near_acts, near_grads, up, down)
+    acts, grads = (near_acts, far_acts), (near_grads, far_grads)
     down_mine, up_mine = weight_sums(sets, acts, grads, 0)
-    *far_back, near_sums, down_mine, up_mine = held(*far_back, near_sums, down_mine, up_mine)
+    *far_back, near_sums, down_mine, up_mine, down_theirs, up_theirs = held(
+        *far_back, near_sums, down_mine, up_mine, down_theirs, up_theirs
+    )
 
     def total(*parts):
         value = parts[0].astype(F32)

time: 190 us -> 190 us (level)
  waiting for transfers between devices: 85 us -> 74.2 us
  starting transfers between devices: 46.1 us -> 52.1 us
  other arithmetic: 19.9 us -> 24.5 us
    ppermute x14, waiting for transfers between devices: 35.1 us -> 12.7 us  [plane(): return lax.ppermute(value, ('col', 'depth'), pairs)]
    ppermute x18, waiting for transfers between devices: 50 us -> 61.5 us  [along_x(): return lax.ppermute(value, ('row', 'col'), pairs)]
    ppermute x14, starting transfers between devices: 18.3 us -> 21.8 us  [plane(): return lax.ppermute(value, ('col', 'depth'), pairs)]
    ppermute x18, starting transfers between devices: 25.9 us -> 29.1 us  [along_x(): return lax.ppermute(value, ('row', 'col'), pairs)]
    add x2, other arithmetic: 2.45 us -> 4.54 us  [total(): value = value + part.astype(F32)]
    unnamed x33 -> x25, local copies, waits for them, and re-layouts: 4.9 us -> 4.89 us
  transfers between devices with their start and end apart: 37 -> 37, of which waited for: 21 -> 16; matrix products, arithmetic and copies ran while one was open for 8% -> 9% of each run, Pallas kernels for 12% -> 10%
where the time goes in v2:
time: 190 us; the launch traced here: 189 us
  waiting for transfers between devices  74.2 us (39%)
  starting transfers between devices  52.1 us (27%)
  Pallas kernels  30.6 us (16%)
  other arithmetic  24.5 us (13%)
  local copies, waits for them, and re-layouts  6.69 us (4%)
    ppermute x18, waiting for transfers between devices, along_x(): return lax.ppermute(value, ('row', 'col'), pairs)  61.5 us
    pallas_call x6, Pallas kernels, local_kernel(): pl.pallas_call(body, grid=grid, in_specs=in_specs, out_specs=out_specs, o...  30.6 us
    ppermute x18, starting transfers between devices, along_x(): return lax.ppermute(value, ('row', 'col'), pairs)  29.1 us
    ppermute x14, starting transfers between devices, plane(): return lax.ppermute(value, ('col', 'depth'), pairs)  21.8 us
    ppermute x14, waiting for transfers between devices, plane(): return lax.ppermute(value, ('col', 'depth'), pairs)  12.7 us
    concatenate x10, other arithmetic, join(): return jnp.concatenate(parts, axis=axis)  6.98 us
    unnamed x25, local copies, waits for them, and re-layouts  4.89 us
    add x2, other arithmetic, total(): value = value + part.astype(F32)  4.54 us
  transfers between devices with their start and end apart: 37, of which 16 were waited for; matrix products, arithmetic and copies ran while one was open for 9% of the time, Pallas kernels for 10%

profile of v2, /device:TPU:0, one launch (start us, length us, event | category | flops | bytes accessed | tf_op | source)
XLA Modules:
  0.0 189.4 jit_solution(15699184941385687572)
XLA Ops:
  1.8 1.6 collective-permute-start
  3.4 2.7 %collective-permute-start.1 = (bf16[2,32,768]{2,1,0:T(8,128)(2,1)S(1)}, bf16[2,32,768]{2,1,0:T(8,128)(2,1)S(1)}, u32[]{:S(2)}, u32[]{:S(2)}) collective-permute-start(bf16[2,32,768]{2,1,0:T(8,128)(2,1)S(1)} %get-tuple-element.132), channel_id=1, source_target_pairs={{0,64},{16,80},{32,96},{48,112},{64,0},{80,16},{96,32},{112,48},{1... | collective-permute-start | bytes 294920 | tf_op jit(solution)/shard_map/ppermute | solution.py:140
  6.1 1.4 collective-permute-start.2
  8.2 3.1 %collective-permute-done.1 = bf16[2,32,768]{2,1,0:T(8,128)(2,1)S(1)} collective-permute-done((bf16[2,32,768]{2,1,0:T(8,128)(2,1)S(1)}, bf16[2,32,768]{2,1,0:T(8,128)(2,1)S(1)}, u32[]{:S(2)}, u32[]{:S(2)}) %collective-permute-start.1) | collective-permute-done | bytes 98336 | tf_op jit(solution)/shard_map/ppermute | solution.py:140
  12.0 2.0 %collective-permute-start.3 = (bf16[2,32,3072]{2,1,0:T(8,128)(2,1)S(1)}, bf16[2,32,3072]{2,1,0:T(8,128)(2,1)S(1)}, u32[]{:S(2)}, u32[]{:S(2)}) collective-permute-start(bf16[2,32,3072]{2,1,0:T(8,128)(2,1)S(1)} %pad_maximum_fusion.10), channel_id=1, source_target_pairs={{0,4},{1,5},{2,6},{3,7},{4,8},{5,9},{6,10},{7,11},{8,12},{9,13},{1... | collective-permute-start | bytes 1179656 | tf_op jit(solution)/shard_map/ppermute | solution.py:157
  14.0 3.6 %collective-permute-start.4 = (bf16[2,32,3072]{2,1,0:T(8,128)(2,1)S(1)}, bf16[2,32,3072]{2,1,0:T(8,128)(2,1)S(1)}, u32[]{:S(2)}, u32[]{:S(2)}) collective-permute-start(bf16[2,32,3072]{2,1,0:T(8,128)(2,1)S(1)} %pad_maximum_fusion.10), channel_id=1, source_target_pairs={{0,8},{1,9},{2,10},{3,11},{4,12},{5,13},{6,14},{7,15},{8,0},{9,1},... | collective-permute-start | bytes 1179656 | tf_op jit(solution)/shard_map/ppermute | solution.py:157
  18.6 2.5 %collective-permute-start.7 = (bf16[384,768]{1,0:T(8,128)(2,1)S(1)}, bf16[384,768]{1,0:T(8,128)(2,1)S(1)}, u32[]{:S(2)}, u32[]{:S(2)}) collective-permute-start(bf16[384,768]{1,0:T(8,128)(2,1)S(1)} %copy-done.6), channel_id=1, source_target_pairs={{0,96},{16,48},{32,0},{48,80},{64,32},{80,112},{96,64},{112,16},{1... | collective-permute-start | bytes 1769480 | tf_op jit(solution)/shard_map/ppermute | solution.py:140
  21.8 5.7 %collective-permute-done.4 = bf16[2,32,3072]{2,1,0:T(8,128)(2,1)S(1)} collective-permute-done((bf16[2,32,3072]{2,1,0:T(8,128)(2,1)S(1)}, bf16[2,32,3072]{2,1,0:T(8,128)(2,1)S(1)}, u32[]{:S(2)}, u32[]{:S(2)}) %collective-permute-start.4) | collective-permute-done | bytes 393248 | tf_op jit(solution)/shard_map/ppermute | solution.py:157
  27.6 4.7 %collective-permute-done.7 = bf16[384,768]{1,0:T(8,128)(2,1)S(1)} collective-permute-done((bf16[384,768]{1,0:T(8,128)(2,1)S(1)}, bf16[384,768]{1,0:T(8,128)(2,1)S(1)}, u32[]{:S(2)}, u32[]{:S(2)}) %collective-permute-start.7) | collective-permute-done | bytes 589856 | tf_op jit(solution)/shard_map/ppermute | solution.py:140
  34.1 2.5 %collective-permute-start.9 = (bf16[2,128,3072]{2,1,0:T(8,128)(2,1)S(1)}, bf16[2,128,3072]{2,1,0:T(8,128)(2,1)S(1)}, u32[]{:S(2)}, u32[]{:S(2)}) collective-permute-start(bf16[2,128,3072]{2,1,0:T(8,128)(2,1)S(1)} %pad_maximum_fusion.7), channel_id=1, source_target_pairs={{0,3},{1,0},{2,1},{3,2},{4,7},{5,4},{6,5},{7,6},{8,11},{9,8},{10,9... | collective-permute-start | bytes 4718600 | tf_op jit(solution)/shard_map/ppermute | solution.py:157
  36.6 3.0 %collective-permute-start.13 = (bf16[384,768]{1,0:T(8,128)(2,1)S(1)}, bf16[384,768]{1,0:T(8,128)(2,1)S(1)}, u32[]{:S(2)}, u32[]{:S(2)}) collective-permute-start(bf16[384,768]{1,0:T(8,128)(2,1)S(1)} %collective-permute-done.7), channel_id=1, source_target_pairs={{0,96},{16,48},{32,0},{48,80},{64,32},{80,112},{96,64},{112,16},{1... | collective-permute-start | bytes 1769480 | tf_op jit(solution)/shard_map/ppermute | solution.py:140
  39.6 13.7 %collective-permute-done.13 = bf16[384,768]{1,0:T(8,128)(2,1)S(1)} collective-permute-done((bf16[384,768]{1,0:T(8,128)(2,1)S(1)}, bf16[384,768]{1,0:T(8,128)(2,1)S(1)}, u32[]{:S(2)}, u32[]{:S(2)}) %collective-permute-start.13) | collective-permute-done | bytes 589856 | tf_op jit(solution)/shard_map/ppermute | solution.py:140
  53.3 3.7 %collective-permute-start.14 = (bf16[384,768]{1,0:T(8,128)(2,1)S(1)}, bf16[384,768]{1,0:T(8,128)(2,1)S(1)}, u32[]{:S(2)}, u32[]{:S(2)}) collective-permute-start(bf16[384,768]{1,0:T(8,128)(2,1)S(1)} %collective-permute-done.13), channel_id=1, source_target_pairs={{0,96},{16,48},{32,0},{48,80},{64,32},{80,112},{96,64},{112,16},{1... | collective-permute-start | bytes 1769480 | tf_op jit(solution)/shard_map/ppermute | solution.py:140
  57.0 7.4 %collective-permute-done.14 = bf16[384,768]{1,0:T(8,128)(2,1)S(1)} collective-permute-done((bf16[384,768]{1,0:T(8,128)(2,1)S(1)}, bf16[384,768]{1,0:T(8,128)(2,1)S(1)}, u32[]{:S(2)}, u32[]{:S(2)}) %collective-permute-start.14) | collective-permute-done | bytes 589856 | tf_op jit(solution)/shard_map/ppermute | solution.py:140
  65.7 3.5 %collective-permute-start.16 = (bf16[2,64,3072]{2,1,0:T(8,128)(2,1)S(1)}, bf16[2,64,3072]{2,1,0:T(8,128)(2,1)S(1)}, u32[]{:S(2)}, u32[]{:S(2)}) collective-permute-start(bf16[2,64,3072]{2,1,0:T(8,128)(2,1)S(1)} %slice.191), channel_id=1, source_target_pairs={{0,3},{1,0},{2,1},{3,2},{4,7},{5,4},{6,5},{7,6},{8,11},{9,8},{10,9... | collective-permute-start | bytes 2359304 | tf_op jit(solution)/shard_map/ppermute | solution.py:157
  69.4 2.2 %copy-done.1 = bf16[2,384,3072]{2,1,0:T(8,128)(2,1)} copy-done((bf16[2,384,3072]{2,1,0:T(8,128)(2,1)}, bf16[2,384,3072]{2,1,0:T(8,128)(2,1)S(1)}, u32[]{:S(2)}) %copy-start.1) | copy-done | bytes 4718616
  73.1 2.7 %pad_maximum_fusion.1.down_ref = bf16[768,3072]{1,0:T(8,128)(2,1)} fusion(bf16[384,3072]{1,0:T(8,128)(2,1)S(1)} %pad_maximum_fusion.5, bf16[384,3072]{1,0:T(8,128)(2,1)S(1)} %pad_maximum_fusion.4), kind=kLoop, calls=%fused_computation.1 | loop fusion | flops 9437184 | bytes 9437184 | tf_op jit(solution)/shard_map/concatenate | solution.py:193
  76.9 6.3 %shard_map.75 = (bf16[384,768]{1,0:T(8,128)(2,1)S(1)}, bf16[384,768]{1,0:T(8,128)(2,1)S(1)}) custom-call(bf16[2,384,3072]{2,1,0:T(8,128)(2,1)S(1)} %bitcast.73, bf16[3072,768]{1,0:T(8,128)(2,1)S(1)} %pad_maximum_fusion.up_ref, bf16[768,3072]{1,0:T(8,128)(2,1)} %pad_maximum_fusion.1.down_ref), custom_call_target="tpu_custom_call" | custom-call | flops 1 | bytes 1 | tf_op jit(solution)/shard_map/pallas_call | solution.py:30
  83.3 3.0 %shard_map.76 = (bf16[128,768]{1,0:T(8,128)(2,1)S(1)}, bf16[128,768]{1,0:T(8,128)(2,1)S(1)}) custom-call(bf16[2,128,3072]{2,1,0:T(8,128)(2,1)S(1)} %constant_dynamic-update-slice_fusion.3.pair_ref.refs_1_, bf16[3072,768]{1,0:T(8,128)(2,1)S(1)} %pad_maximum_fusion.up_ref, bf16[768,3072]{1,0:T(8,128)(2,1)S(1)} %copy-done), custom_call_target="tpu_custom_call" | custom-call | flops 1 | bytes 1 | tf_op jit(solution)/shard_map/pallas_call | solution.py:30
  86.3 3.1 %shard_map.77 = bf16[2,128,3072]{2,1,0:T(8,128)(2,1)S(1)} custom-call(bf16[128,768]{1,0:T(8,128)(2,1)S(1)} %get-tuple-element.86.act_ref.refs_3_, bf16[128,768]{1,0:T(8,128)(2,1)S(1)} %get-tuple-element.87.grad_ref.refs_5_, bf16[3072,768]{1,0:T(8,128)(2,1)S(1)} %pad_maximum_fusion.up_ref, bf16[768,3072]{1,0:T(8,128)(2,1)S(1)} %copy-done), custom_call_target="tpu_custom_call" | custom-call | flops 1 | bytes 1 | tf_op jit(solution)/shard_map/pallas_call | solution.py:30
  89.6 5.9 %shard_map.78 = (bf16[384,3072]{1,0:T(8,128)(2,1)}, bf16[3072,384]{1,0:T(8,128)(2,1)S(1)}) custom-call(bf16[2,384,3072]{2,1,0:T(8,128)(2,1)S(1)} %bitcast.75, bf16[2,128,3072]{2,1,0:T(8,128)(2,1)S(1)} %constant_dynamic-update-slice_fusion.3.pair_ref.refs_1_, bf16[384,768]{1,0:T(8,128)(2,1)S(1)} %get-tuple-element.90.refs_2_.act_ref, ...), custom_call_target="tpu_custom_call" | custom-call | flops 1 | bytes 1 | tf_op jit(solution)/shard_map/pallas_call | solution.py:30
  96.0 2.0 %collective-permute-start.20 = (bf16[2,64,3072]{2,1,0:T(8,128)(2,1)S(1)}, bf16[2,64,3072]{2,1,0:T(8,128)(2,1)S(1)}, u32[]{:S(2)}, u32[]{:S(2)}) collective-permute-start(bf16[2,64,3072]{2,1,0:T(8,128)(2,1)S(1)} %get-tuple-element.83), channel_id=1, source_target_pairs={{0,1},{1,2},{2,3},{3,0},{4,5},{5,6},{6,7},{7,4},{8,9},{9,10},{10,1... | collective-permute-start | bytes 2359304 | tf_op jit(solution)/shard_map/ppermute | solution.py:157
  98.0 5.4 %shard_map.80 = (bf16[384,3072]{1,0:T(8,128)(2,1)S(1)}, bf16[3072,384]{1,0:T(8,128)(2,1)S(1)}) custom-call(bf16[2,384,3072]{2,1,0:T(8,128)(2,1)S(1)} %bitcast.75, bf16[2,128,3072]{2,1,0:T(8,128)(2,1)S(1)} %constant_dynamic-update-slice_fusion.3.pair_ref.refs_1_, bf16[384,768]{1,0:T(8,128)(2,1)S(1)} %get-tuple-element.90.refs_2_.act_ref, ...), custom_call_target="tpu_custom_call" | custom-call | flops 1 | bytes 1 | tf_op jit(solution)/shard_map/pallas_call | solution.py:30
  103.4 6.9 %shard_map.79 = bf16[2,384,3072]{2,1,0:T(8,128)(2,1)S(1)} custom-call(bf16[384,768]{1,0:T(8,128)(2,1)S(1)} %get-tuple-element.90.refs_2_.act_ref, bf16[384,768]{1,0:T(8,128)(2,1)S(1)} %get-tuple-element.91.refs_4_.grad_ref, bf16[3072,768]{1,0:T(8,128)(2,1)S(1)} %pad_maximum_fusion.up_ref, bf16[768,3072]{1,0:T(8,128)(2,1)} %pad_maximum_fusion.1.down_ref), custom_call_target="tpu_custom_call" | custom-call | flops 1 | bytes 1 | tf_op jit(solution)/shard_map/pallas_call | solution.py:30
  111.1 1.4 copy-done.2
  112.5 1.3 pad_maximum_fusion.9
  113.8 1.3 pad_maximum_fusion.8
  115.0 3.2 %collective-permute-start.23 = (bf16[2,128,3072]{2,1,0:T(8,128)(2,1)}, bf16[2,128,3072]{2,1,0:T(8,128)(2,1)}, u32[]{:S(2)}, u32[]{:S(2)}) collective-permute-start(bf16[2,128,3072]{2,1,0:T(8,128)(2,1)} %pad_maximum_fusion.8), channel_id=1, source_target_pairs={{0,3},{1,0},{2,1},{3,2},{4,7},{5,4},{6,5},{7,6},{8,11},{9,8},{10,9... | collective-permute-start | bytes 4718600 | tf_op jit(solution)/shard_map/ppermute | solution.py:157
  118.3 1.2 add_convert_fusion.7
  119.8 1.2 add_convert_fusion.8
  121.0 3.8 %collective-permute-start.25 = (bf16[384,768]{1,0:T(8,128)(2,1)S(1)}, bf16[384,768]{1,0:T(8,128)(2,1)}, u32[]{:S(2)}, u32[]{:S(2)}) collective-permute-start(bf16[384,768]{1,0:T(8,128)(2,1)S(1)} %add_convert_fusion.8), channel_id=1, source_target_pairs={{0,96},{16,48},{32,0},{48,80},{64,32},{80,112},{96,64},{112,16},{1... | collective-permute-start | bytes 1769480 | tf_op jit(solution)/shard_map/ppermute | solution.py:140
  124.8 10.7 %collective-permute-done.26 = bf16[768,384]{1,0:T(8,128)(2,1)} collective-permute-done((bf16[768,384]{1,0:T(8,128)(2,1)S(1)}, bf16[768,384]{1,0:T(8,128)(2,1)}, u32[]{:S(2)}, u32[]{:S(2)}) %collective-permute-start.26) | collective-permute-done | bytes 589856 | tf_op jit(solution)/shard_map/ppermute | solution.py:140
  136.5 3.1 %add_convert_fusion = bf16[2,128,3072]{2,1,0:T(8,128)(2,1)S(1)} fusion(bf16[2,128,3072]{2,1,0:T(8,128)(2,1)} %collective-permute-done.24, bf16[2,128,3072]{2,1,0:T(8,128)(2,1)} %collective-permute-done.23, bf16[2,384,3072]{2,1,0:T(8,128)(2,1)} %copy-done.2), kind=kLoop, calls=%fused_computation.2 | loop fusion | flops 4718592 | bytes 6291456 | tf_op jit(solution)/shard_map/convert_element_type | solution.py:268
  139.8 1.8 collective-permute-start.27
  141.7 1.1 collective-permute-start.29
  142.9 1.5 add_convert_fusion.5
  144.4 1.5 add_convert_fusion.6
  145.9 3.8 %collective-permute-start.30 = (bf16[384,768]{1,0:T(8,128)(2,1)S(1)}, bf16[384,768]{1,0:T(8,128)(2,1)S(1)}, u32[]{:S(2)}, u32[]{:S(2)}) collective-permute-start(bf16[384,768]{1,0:T(8,128)(2,1)S(1)} %add_convert_fusion.6), channel_id=1, source_target_pairs={{0,96},{16,48},{32,0},{48,80},{64,32},{80,112},{96,64},{112,16},{1... | collective-permute-start | bytes 1769480 | tf_op jit(solution)/shard_map/ppermute | solution.py:140
  149.6 1.5 collective-permute-done.27
  151.1 3.8 %collective-permute-done.29 = bf16[2,32,3072]{2,1,0:T(8,128)(2,1)S(1)} collective-permute-done((bf16[2,32,3072]{2,1,0:T(8,128)(2,1)S(1)}, bf16[2,32,3072]{2,1,0:T(8,128)(2,1)S(1)}, u32[]{:S(2)}, u32[]{:S(2)}) %collective-permute-start.29) | collective-permute-done | bytes 393248 | tf_op jit(solution)/shard_map/ppermute | solution.py:157
  155.1 6.8 %collective-permute-done.31 = bf16[768,384]{1,0:T(8,128)(2,1)S(1)} collective-permute-done((bf16[768,384]{1,0:T(8,128)(2,1)S(1)}, bf16[768,384]{1,0:T(8,128)(2,1)S(1)}, u32[]{:S(2)}, u32[]{:S(2)}) %collective-permute-start.31) | collective-permute-done | bytes 589856 | tf_op jit(solution)/shard_map/ppermute | solution.py:140
  161.9 1.3 add_convert_fusion.3
  163.3 1.3 add_convert_fusion.4
  164.6 2.1 %collective-permute-start.35 = (bf16[768,384]{1,0:T(8,128)(2,1)S(1)}, bf16[768,384]{1,0:T(8,128)(2,1)S(1)}, u32[]{:S(2)}, u32[]{:S(2)}) collective-permute-start(bf16[768,384]{1,0:T(8,128)(2,1)S(1)} %add_convert_fusion.4), channel_id=1, source_target_pairs={{0,32},{16,112},{32,64},{48,16},{64,96},{80,48},{96,0},{112,80},{1... | collective-permute-start | bytes 1769480 | tf_op jit(solution)/shard_map/ppermute | solution.py:140
  166.9 2.7 %collective-permute-start.33 = (bf16[2,32,768]{2,1,0:T(8,128)(2,1)S(1)}, bf16[2,32,768]{2,1,0:T(8,128)(2,1)S(1)}, u32[]{:S(2)}, u32[]{:S(2)}) collective-permute-start(bf16[2,32,768]{2,1,0:T(8,128)(2,1)S(1)} %pad_maximum_fusion.12), channel_id=1, source_target_pairs={{0,64},{16,80},{32,96},{48,112},{64,0},{80,16},{96,32},{112,48},{1... | collective-permute-start | bytes 294920 | tf_op jit(solution)/shard_map/ppermute | solution.py:140
  170.3 12.9 %collective-permute-done.32 = bf16[2,32,768]{2,1,0:T(8,128)(2,1)S(1)} collective-permute-done((bf16[2,32,768]{2,1,0:T(8,128)(2,1)S(1)}, bf16[2,32,768]{2,1,0:T(8,128)(2,1)S(1)}, u32[]{:S(2)}, u32[]{:S(2)}) %collective-permute-start.32) | collective-permute-done | bytes 98336 | tf_op jit(solution)/shard_map/ppermute | solution.py:140
  184.9 2.3 %convert_add_fusion = f32[384,768]{1,0:T(8,128)} fusion(bf16[384,768]{1,0:T(8,128)(2,1)S(1)} %collective-permute-done.36, bf16[384,3072]{1,0:T(8,128)(2,1)} %collective-permute-done.21, bf16[384,3072]{1,0:T(8,128)(2,1)S(1)} %copy-done.4), kind=kLoop, calls=%fused_computation.13 | loop fusion | flops 1474560 | bytes 2949120 | tf_op jit(solution)/shard_map/add | solution.py:248
  187.2 2.3 %convert_add_fusion.1 = f32[768,384]{1,0:T(8,128)} fusion(bf16[768,384]{1,0:T(8,128)(2,1)S(1)} %collective-permute-done.35, bf16[3072,384]{1,0:T(8,128)(2,1)} %collective-permute-done.22, bf16[3072,384]{1,0:T(8,128)(2,1)S(1)} %get-tuple-element.101), kind=kLoop, calls=%fused_computation.15 | loop fusion | flops 1474560 | bytes 2949120 | tf_op jit(solution)/shard_map/add | solution.py:248
  (108 shorter events, 15.7 us)
Async XLA Ops:
  0.6 17.9 %copy-start.6 = (bf16[384,768]{1,0:T(8,128)(2,1)S(1)}, bf16[384,768]{1,0:T(8,128)(2,1)}, u32[]{:S(2)}) copy-start(bf16[384,768]{1,0:T(8,128)(2,1)} %param.6) | copy-start | bytes 1769476
  1.8 6.4 %collective-permute-start = (bf16[2,32,768]{2,1,0:T(8,128)(2,1)S(1)}, bf16[2,32,768]{2,1,0:T(8,128)(2,1)S(1)}, u32[]{:S(2)}, u32[]{:S(2)}) collective-permute-start(bf16[2,32,768]{2,1,0:T(8,128)(2,1)S(1)} %get-tuple-element.131), channel_id=1, source_target_pairs={{0,32},{16,112},{32,64},{48,16},{64,96},{80,48},{96,0},{112,80},{1... | collective-permute-start | bytes 294920 | tf_op jit(solution)/shard_map/ppermute | solution.py:140
  3.4 7.9 %collective-permute-start.1 = (bf16[2,32,768]{2,1,0:T(8,128)(2,1)S(1)}, bf16[2,32,768]{2,1,0:T(8,128)(2,1)S(1)}, u32[]{:S(2)}, u32[]{:S(2)}) collective-permute-start(bf16[2,32,768]{2,1,0:T(8,128)(2,1)S(1)} %get-tuple-element.132), channel_id=1, source_target_pairs={{0,64},{16,80},{32,96},{48,112},{64,0},{80,16},{96,32},{112,48},{1... | collective-permute-start | bytes 294920 | tf_op jit(solution)/shard_map/ppermute | solution.py:140
  6.1 5.7 %collective-permute-start.2 = (bf16[2,32,768]{2,1,0:T(8,128)(2,1)S(1)}, bf16[2,32,768]{2,1,0:T(8,128)(2,1)S(1)}, u32[]{:S(2)}, u32[]{:S(2)}) collective-permute-start(bf16[2,32,768]{2,1,0:T(8,128)(2,1)S(1)} %get-tuple-element.133), channel_id=1, source_target_pairs={{0,96},{16,48},{32,0},{48,80},{64,32},{80,112},{96,64},{112,16},{1... | collective-permute-start | bytes 294920 | tf_op jit(solution)/shard_map/ppermute | solution.py:140
  7.6 13.5 %collective-permute-start.6 = (bf16[768,384]{1,0:T(8,128)(2,1)}, bf16[768,384]{1,0:T(8,128)(2,1)S(1)}, u32[]{:S(2)}, u32[]{:S(2)}) collective-permute-start(bf16[768,384]{1,0:T(8,128)(2,1)} %param.5), channel_id=1, source_target_pairs={{0,32},{16,112},{32,64},{48,16},{64,96},{80,48},{96,0},{112,80},{1... | collective-permute-start | bytes 1769480 | tf_op jit(solution)/shard_map/ppermute | solution.py:140
  11.9 21.2 %copy-start.5 = (bf16[768,384]{1,0:T(8,128)(2,1)S(1)}, bf16[768,384]{1,0:T(8,128)(2,1)}, u32[]{:S(2)}) copy-start(bf16[768,384]{1,0:T(8,128)(2,1)} %param.5) | copy-start | bytes 1769476
  12.0 9.9 %collective-permute-start.3 = (bf16[2,32,3072]{2,1,0:T(8,128)(2,1)S(1)}, bf16[2,32,3072]{2,1,0:T(8,128)(2,1)S(1)}, u32[]{:S(2)}, u32[]{:S(2)}) collective-permute-start(bf16[2,32,3072]{2,1,0:T(8,128)(2,1)S(1)} %pad_maximum_fusion.10), channel_id=1, source_target_pairs={{0,4},{1,5},{2,6},{3,7},{4,8},{5,9},{6,10},{7,11},{8,12},{9,13},{1... | collective-permute-start | bytes 1179656 | tf_op jit(solution)/shard_map/ppermute | solution.py:157
  14.0 13.5 %collective-permute-start.4 = (bf16[2,32,3072]{2,1,0:T(8,128)(2,1)S(1)}, bf16[2,32,3072]{2,1,0:T(8,128)(2,1)S(1)}, u32[]{:S(2)}, u32[]{:S(2)}) collective-permute-start(bf16[2,32,3072]{2,1,0:T(8,128)(2,1)S(1)} %pad_maximum_fusion.10), channel_id=1, source_target_pairs={{0,8},{1,9},{2,10},{3,11},{4,12},{5,13},{6,14},{7,15},{8,0},{9,1},... | collective-permute-start | bytes 1179656 | tf_op jit(solution)/shard_map/ppermute | solution.py:157
  17.5 10.0 %collective-permute-start.5 = (bf16[2,32,3072]{2,1,0:T(8,128)(2,1)S(1)}, bf16[2,32,3072]{2,1,0:T(8,128)(2,1)S(1)}, u32[]{:S(2)}, u32[]{:S(2)}) collective-permute-start(bf16[2,32,3072]{2,1,0:T(8,128)(2,1)S(1)} %pad_maximum_fusion.10), channel_id=1, source_target_pairs={{0,12},{1,13},{2,14},{3,15},{4,0},{5,1},{6,2},{7,3},{8,4},{9,5},{1... | collective-permute-start | bytes 1179656 | tf_op jit(solution)/shard_map/ppermute | solution.py:157
  18.6 13.8 %collective-permute-start.7 = (bf16[384,768]{1,0:T(8,128)(2,1)S(1)}, bf16[384,768]{1,0:T(8,128)(2,1)S(1)}, u32[]{:S(2)}, u32[]{:S(2)}) collective-permute-start(bf16[384,768]{1,0:T(8,128)(2,1)S(1)} %copy-done.6), channel_id=1, source_target_pairs={{0,96},{16,48},{32,0},{48,80},{64,32},{80,112},{96,64},{112,16},{1... | collective-permute-start | bytes 1769480 | tf_op jit(solution)/shard_map/ppermute | solution.py:140
  21.1 12.0 %collective-permute-start.10 = (bf16[768,384]{1,0:T(8,128)(2,1)S(1)}, bf16[768,384]{1,0:T(8,128)(2,1)S(1)}, u32[]{:S(2)}, u32[]{:S(2)}) collective-permute-start(bf16[768,384]{1,0:T(8,128)(2,1)S(1)} %collective-permute-done.6), channel_id=1, source_target_pairs={{0,32},{16,112},{32,64},{48,16},{64,96},{80,48},{96,0},{112,80},{1... | collective-permute-start | bytes 1769480 | tf_op jit(solution)/shard_map/ppermute | solution.py:140
  33.2 31.2 %collective-permute-start.11 = (bf16[2304,384]{1,0:T(8,128)(2,1)S(1)}, bf16[2304,384]{1,0:T(8,128)(2,1)S(1)}, u32[]{:S(2)}, u32[]{:S(2)}) collective-permute-start(bf16[2304,384]{1,0:T(8,128)(2,1)S(1)} %pad_maximum_fusion.6), channel_id=1, source_target_pairs={{0,16},{16,0},{1,17},{17,1},{2,18},{18,2},{3,19},{19,3},{4,20},{20... | collective-permute-start | bytes 5308424 | tf_op jit(solution)/shard_map/ppermute | solution.py:144
  33.3 31.1 %collective-permute-start.8 = (bf16[2,128,3072]{2,1,0:T(8,128)(2,1)S(1)}, bf16[2,128,3072]{2,1,0:T(8,128)(2,1)S(1)}, u32[]{:S(2)}, u32[]{:S(2)}) collective-permute-start(bf16[2,128,3072]{2,1,0:T(8,128)(2,1)S(1)} %pad_maximum_fusion.7), channel_id=1, source_target_pairs={{0,1},{1,2},{2,3},{3,0},{4,5},{5,6},{6,7},{7,4},{8,9},{9,10},{10,1... | collective-permute-start | bytes 4718600 | tf_op jit(solution)/shard_map/ppermute | solution.py:157
  34.1 30.3 %collective-permute-start.9 = (bf16[2,128,3072]{2,1,0:T(8,128)(2,1)S(1)}, bf16[2,128,3072]{2,1,0:T(8,128)(2,1)S(1)}, u32[]{:S(2)}, u32[]{:S(2)}) collective-permute-start(bf16[2,128,3072]{2,1,0:T(8,128)(2,1)S(1)} %pad_maximum_fusion.7), channel_id=1, source_target_pairs={{0,3},{1,0},{2,1},{3,2},{4,7},{5,4},{6,5},{7,6},{8,11},{9,8},{10,9... | collective-permute-start | bytes 4718600 | tf_op jit(solution)/shard_map/ppermute | solution.py:157
  36.6 16.7 %collective-permute-start.13 = (bf16[384,768]{1,0:T(8,128)(2,1)S(1)}, bf16[384,768]{1,0:T(8,128)(2,1)S(1)}, u32[]{:S(2)}, u32[]{:S(2)}) collective-permute-start(bf16[384,768]{1,0:T(8,128)(2,1)S(1)} %collective-permute-done.7), channel_id=1, source_target_pairs={{0,96},{16,48},{32,0},{48,80},{64,32},{80,112},{96,64},{112,16},{1... | collective-permute-start | bytes 1769480 | tf_op jit(solution)/shard_map/ppermute | solution.py:140
  39.6 17.4 %collective-permute-start.12 = (bf16[768,384]{1,0:T(8,128)(2,1)S(1)}, bf16[768,384]{1,0:T(8,128)(2,1)S(1)}, u32[]{:S(2)}, u32[]{:S(2)}) collective-permute-start(bf16[768,384]{1,0:T(8,128)(2,1)S(1)} %collective-permute-done.10), channel_id=1, source_target_pairs={{0,32},{16,112},{32,64},{48,16},{64,96},{80,48},{96,0},{112,80},{1... | collective-permute-start | bytes 1769480 | tf_op jit(solution)/shard_map/ppermute | solution.py:140
  53.3 11.1 %collective-permute-start.14 = (bf16[384,768]{1,0:T(8,128)(2,1)S(1)}, bf16[384,768]{1,0:T(8,128)(2,1)S(1)}, u32[]{:S(2)}, u32[]{:S(2)}) collective-permute-start(bf16[384,768]{1,0:T(8,128)(2,1)S(1)} %collective-permute-done.13), channel_id=1, source_target_pairs={{0,96},{16,48},{32,0},{48,80},{64,32},{80,112},{96,64},{112,16},{1... | collective-permute-start | bytes 1769480 | tf_op jit(solution)/shard_map/ppermute | solution.py:140
  64.7 7.9 %collective-permute-start.18 = (bf16[384,3072]{1,0:T(8,128)(2,1)S(1)}, bf16[384,3072]{1,0:T(8,128)(2,1)S(1)}, u32[]{:S(2)}, u32[]{:S(2)}) collective-permute-start(bf16[384,3072]{1,0:T(8,128)(2,1)S(1)} %pad_maximum_fusion.4), channel_id=1, source_target_pairs={{0,16},{16,0},{1,17},{17,1},{2,18},{18,2},{3,19},{19,3},{4,20},{20... | collective-permute-start | bytes 7077896 | tf_op jit(solution)/shard_map/ppermute | solution.py:144
  64.9 7.1 %collective-permute-start.17 = (bf16[768,384]{1,0:T(8,128)(2,1)S(1)}, bf16[768,384]{1,0:T(8,128)(2,1)S(1)}, u32[]{:S(2)}, u32[]{:S(2)}) collective-permute-start(bf16[768,384]{1,0:T(8,128)(2,1)S(1)} %collective-permute-done.12), channel_id=1, source_target_pairs={{0,16},{16,0},{1,17},{17,1},{2,18},{18,2},{3,19},{19,3},{4,20},{20... | collective-permute-start | bytes 1769480 | tf_op jit(solution)/shard_map/ppermute | solution.py:144
  65.5 17.7 %collective-permute-start.15 = (bf16[2,64,3072]{2,1,0:T(8,128)(2,1)S(1)}, bf16[2,64,3072]{2,1,0:T(8,128)(2,1)S(1)}, u32[]{:S(2)}, u32[]{:S(2)}) collective-permute-start(bf16[2,64,3072]{2,1,0:T(8,128)(2,1)S(1)} %slice.190), channel_id=1, source_target_pairs={{0,1},{1,2},{2,3},{3,0},{4,5},{5,6},{6,7},{7,4},{8,9},{9,10},{10,1... | collective-permute-start | bytes 2359304 | tf_op jit(solution)/shard_map/ppermute | solution.py:157
  65.7 17.5 %collective-permute-start.16 = (bf16[2,64,3072]{2,1,0:T(8,128)(2,1)S(1)}, bf16[2,64,3072]{2,1,0:T(8,128)(2,1)S(1)}, u32[]{:S(2)}, u32[]{:S(2)}) collective-permute-start(bf16[2,64,3072]{2,1,0:T(8,128)(2,1)S(1)} %slice.191), channel_id=1, source_target_pairs={{0,3},{1,0},{2,1},{3,2},{4,7},{5,4},{6,5},{7,6},{8,11},{9,8},{10,9... | collective-permute-start | bytes 2359304 | tf_op jit(solution)/shard_map/ppermute | solution.py:157
  69.4 2.2 %copy-start.1 = (bf16[2,384,3072]{2,1,0:T(8,128)(2,1)}, bf16[2,384,3072]{2,1,0:T(8,128)(2,1)S(1)}, u32[]{:S(2)}) copy-start(bf16[2,384,3072]{2,1,0:T(8,128)(2,1)S(1)} %constant_dynamic-update-slice_fusion.pair_ref.refs_0_) | copy-start | bytes 14155780
  72.8 3.7 %slice-start = ((s8[4718592]{0:T(1024)(128)(4,1)}), s8[4194304]{0:T(1024)(128)(4,1)S(1)}, s32[]{:S(2)}) async-start(s8[4718592]{0:T(1024)(128)(4,1)} %bitcast.72), calls=%async_computation | async-start | bytes 8388608
  73.1 3.8 %slice-start.1 = ((s8[4718592]{0:T(1024)(128)(4,1)}), s8[524288]{0:T(1024)(128)(4,1)S(1)}, s32[]{:S(2)}) async-start(s8[4718592]{0:T(1024)(128)(4,1)} %bitcast.72), calls=%async_computation.1 | async-start | bytes 1048576
  76.9 6.5 %copy-start = (bf16[768,3072]{1,0:T(8,128)(2,1)S(1)}, bf16[768,3072]{1,0:T(8,128)(2,1)}, u32[]{:S(2)}) copy-start(bf16[768,3072]{1,0:T(8,128)(2,1)} %pad_maximum_fusion.1.down_ref) | copy-start | bytes 14155780
  86.3 3.2 %slice-start.2 = ((s8[4718592]{0:T(1024)(128)(4,1)}), s8[4194304]{0:T(1024)(128)(4,1)S(1)}, s32[]{:S(2)}) async-start(s8[4718592]{0:T(1024)(128)(4,1)} %bitcast.74), calls=%async_computation.2 | async-start | bytes 8388608
  86.3 3.2 %slice-start.3 = ((s8[4718592]{0:T(1024)(128)(4,1)}), s8[524288]{0:T(1024)(128)(4,1)S(1)}, s32[]{:S(2)}) async-start(s8[4718592]{0:T(1024)(128)(4,1)} %bitcast.74), calls=%async_computation.3 | async-start | bytes 1048576
  95.5 14.9 %collective-permute-start.21 = (bf16[384,3072]{1,0:T(8,128)(2,1)}, bf16[384,3072]{1,0:T(8,128)(2,1)}, u32[]{:S(2)}, u32[]{:S(2)}) collective-permute-start(bf16[384,3072]{1,0:T(8,128)(2,1)} %get-tuple-element.94), channel_id=1, source_target_pairs={{0,16},{16,0},{1,17},{17,1},{2,18},{18,2},{3,19},{19,3},{4,20},{20... | collective-permute-start | bytes 7077896 | tf_op jit(solution)/shard_map/ppermute | solution.py:144
  95.5 14.9 %collective-permute-start.22 = (bf16[3072,384]{1,0:T(8,128)(2,1)S(1)}, bf16[3072,384]{1,0:T(8,128)(2,1)}, u32[]{:S(2)}, u32[]{:S(2)}) collective-permute-start(bf16[3072,384]{1,0:T(8,128)(2,1)S(1)} %get-tuple-element.95), channel_id=1, source_target_pairs={{0,16},{16,0},{1,17},{17,1},{2,18},{18,2},{3,19},{19,3},{4,20},{20... | collective-permute-start | bytes 7077896 | tf_op jit(solution)/shard_map/ppermute | solution.py:144
  96.0 14.4 %collective-permute-start.19 = (bf16[2,64,3072]{2,1,0:T(8,128)(2,1)S(1)}, bf16[2,64,3072]{2,1,0:T(8,128)(2,1)S(1)}, u32[]{:S(2)}, u32[]{:S(2)}) collective-permute-start(bf16[2,64,3072]{2,1,0:T(8,128)(2,1)S(1)} %get-tuple-element.82), channel_id=1, source_target_pairs={{0,3},{1,0},{2,1},{3,2},{4,7},{5,4},{6,5},{7,6},{8,11},{9,8},{10,9... | collective-permute-start | bytes 2359304 | tf_op jit(solution)/shard_map/ppermute | solution.py:157
  96.0 14.3 %collective-permute-start.20 = (bf16[2,64,3072]{2,1,0:T(8,128)(2,1)S(1)}, bf16[2,64,3072]{2,1,0:T(8,128)(2,1)S(1)}, u32[]{:S(2)}, u32[]{:S(2)}) collective-permute-start(bf16[2,64,3072]{2,1,0:T(8,128)(2,1)S(1)} %get-tuple-element.83), channel_id=1, source_target_pairs={{0,1},{1,2},{2,3},{3,0},{4,5},{5,6},{6,7},{7,4},{8,9},{9,10},{10,1... | collective-permute-start | bytes 2359304 | tf_op jit(solution)/shard_map/ppermute | solution.py:157
  103.4 16.4 %copy-start.3 = (bf16[384,3072]{1,0:T(8,128)(2,1)}, bf16[384,3072]{1,0:T(8,128)(2,1)S(1)}, u32[]{:S(2)}) copy-start(bf16[384,3072]{1,0:T(8,128)(2,1)S(1)} %get-tuple-element.99) | copy-start | bytes 7077892
  110.4 2.2 %copy-start.2 = (bf16[2,384,3072]{2,1,0:T(8,128)(2,1)}, bf16[2,384,3072]{2,1,0:T(8,128)(2,1)S(1)}, u32[]{:S(2)}) copy-start(bf16[2,384,3072]{2,1,0:T(8,128)(2,1)S(1)} %shard_map.79) | copy-start | bytes 14155780
  113.8 21.9 %collective-permute-start.24 = (bf16[2,128,3072]{2,1,0:T(8,128)(2,1)}, bf16[2,128,3072]{2,1,0:T(8,128)(2,1)}, u32[]{:S(2)}, u32[]{:S(2)}) collective-permute-start(bf16[2,128,3072]{2,1,0:T(8,128)(2,1)} %pad_maximum_fusion.9), channel_id=1, source_target_pairs={{0,1},{1,2},{2,3},{3,0},{4,5},{5,6},{6,7},{7,4},{8,9},{9,10},{10,1... | collective-permute-start | bytes 4718600 | tf_op jit(solution)/shard_map/ppermute | solution.py:157
  115.0 21.5 %collective-permute-start.23 = (bf16[2,128,3072]{2,1,0:T(8,128)(2,1)}, bf16[2,128,3072]{2,1,0:T(8,128)(2,1)}, u32[]{:S(2)}, u32[]{:S(2)}) collective-permute-start(bf16[2,128,3072]{2,1,0:T(8,128)(2,1)} %pad_maximum_fusion.8), channel_id=1, source_target_pairs={{0,3},{1,0},{2,1},{3,2},{4,7},{5,4},{6,5},{7,6},{8,11},{9,8},{10,9... | collective-permute-start | bytes 4718600 | tf_op jit(solution)/shard_map/ppermute | solution.py:157
  119.5 16.0 %collective-permute-start.26 = (bf16[768,384]{1,0:T(8,128)(2,1)S(1)}, bf16[768,384]{1,0:T(8,128)(2,1)}, u32[]{:S(2)}, u32[]{:S(2)}) collective-permute-start(bf16[768,384]{1,0:T(8,128)(2,1)S(1)} %add_convert_fusion.7), channel_id=1, source_target_pairs={{0,32},{16,112},{32,64},{48,16},{64,96},{80,48},{96,0},{112,80},{1... | collective-permute-start | bytes 1769480 | tf_op jit(solution)/shard_map/ppermute | solution.py:140
  121.0 14.5 %collective-permute-start.25 = (bf16[384,768]{1,0:T(8,128)(2,1)S(1)}, bf16[384,768]{1,0:T(8,128)(2,1)}, u32[]{:S(2)}, u32[]{:S(2)}) collective-permute-start(bf16[384,768]{1,0:T(8,128)(2,1)S(1)} %add_convert_fusion.8), channel_id=1, source_target_pairs={{0,96},{16,48},{32,0},{48,80},{64,32},{80,112},{96,64},{112,16},{1... | collective-permute-start | bytes 1769480 | tf_op jit(solution)/shard_map/ppermute | solution.py:140
  139.7 4.7 %copy-start.4 = (bf16[384,3072]{1,0:T(8,128)(2,1)S(1)}, bf16[384,3072]{1,0:T(8,128)(2,1)}, u32[]{:S(2)}) copy-start(bf16[384,3072]{1,0:T(8,128)(2,1)} %copy-done.3) | copy-start | bytes 7077892
  139.8 11.3 %collective-permute-start.27 = (bf16[2,32,3072]{2,1,0:T(8,128)(2,1)S(1)}, bf16[2,32,3072]{2,1,0:T(8,128)(2,1)S(1)}, u32[]{:S(2)}, u32[]{:S(2)}) collective-permute-start(bf16[2,32,3072]{2,1,0:T(8,128)(2,1)S(1)} %get-tuple-element.121), channel_id=1, source_target_pairs={{0,12},{1,13},{2,14},{3,15},{4,0},{5,1},{6,2},{7,3},{8,4},{9,5},{1... | collective-permute-start | bytes 1179656 | tf_op jit(solution)/shard_map/ppermute | solution.py:157
  141.6 9.5 %collective-permute-start.28 = (bf16[2,32,3072]{2,1,0:T(8,128)(2,1)S(1)}, bf16[2,32,3072]{2,1,0:T(8,128)(2,1)S(1)}, u32[]{:S(2)}, u32[]{:S(2)}) collective-permute-start(bf16[2,32,3072]{2,1,0:T(8,128)(2,1)S(1)} %get-tuple-element.122), channel_id=1, source_target_pairs={{0,8},{1,9},{2,10},{3,11},{4,12},{5,13},{6,14},{7,15},{8,0},{9,1},... | collective-permute-start | bytes 1179656 | tf_op jit(solution)/shard_map/ppermute | solution.py:157
  141.7 13.2 %collective-permute-start.29 = (bf16[2,32,3072]{2,1,0:T(8,128)(2,1)S(1)}, bf16[2,32,3072]{2,1,0:T(8,128)(2,1)S(1)}, u32[]{:S(2)}, u32[]{:S(2)}) collective-permute-start(bf16[2,32,3072]{2,1,0:T(8,128)(2,1)S(1)} %get-tuple-element.123), channel_id=1, source_target_pairs={{0,4},{1,5},{2,6},{3,7},{4,8},{5,9},{6,10},{7,11},{8,12},{9,13},{1... | collective-permute-start | bytes 1179656 | tf_op jit(solution)/shard_map/ppermute | solution.py:157
  144.3 17.6 %collective-permute-start.31 = (bf16[768,384]{1,0:T(8,128)(2,1)S(1)}, bf16[768,384]{1,0:T(8,128)(2,1)S(1)}, u32[]{:S(2)}, u32[]{:S(2)}) collective-permute-start(bf16[768,384]{1,0:T(8,128)(2,1)S(1)} %add_convert_fusion.5), channel_id=1, source_target_pairs={{0,32},{16,112},{32,64},{48,16},{64,96},{80,48},{96,0},{112,80},{1... | collective-permute-start | bytes 1769480 | tf_op jit(solution)/shard_map/ppermute | solution.py:140
  145.9 16.1 %collective-permute-start.30 = (bf16[384,768]{1,0:T(8,128)(2,1)S(1)}, bf16[384,768]{1,0:T(8,128)(2,1)S(1)}, u32[]{:S(2)}, u32[]{:S(2)}) collective-permute-start(bf16[384,768]{1,0:T(8,128)(2,1)S(1)} %add_convert_fusion.6), channel_id=1, source_target_pairs={{0,96},{16,48},{32,0},{48,80},{64,32},{80,112},{96,64},{112,16},{1... | collective-permute-start | bytes 1769480 | tf_op jit(solution)/shard_map/ppermute | solution.py:140
  163.2 21.6 %collective-permute-start.36 = (bf16[384,768]{1,0:T(8,128)(2,1)S(1)}, bf16[384,768]{1,0:T(8,128)(2,1)S(1)}, u32[]{:S(2)}, u32[]{:S(2)}) collective-permute-start(bf16[384,768]{1,0:T(8,128)(2,1)S(1)} %add_convert_fusion.3), channel_id=1, source_target_pairs={{0,96},{16,48},{32,0},{48,80},{64,32},{80,112},{96,64},{112,16},{1... | collective-permute-start | bytes 1769480 | tf_op jit(solution)/shard_map/ppermute | solution.py:140
  164.6 22.5 %collective-permute-start.35 = (bf16[768,384]{1,0:T(8,128)(2,1)S(1)}, bf16[768,384]{1,0:T(8,128)(2,1)S(1)}, u32[]{:S(2)}, u32[]{:S(2)}) collective-permute-start(bf16[768,384]{1,0:T(8,128)(2,1)S(1)} %add_convert_fusion.4), channel_id=1, source_target_pairs={{0,32},{16,112},{32,64},{48,16},{64,96},{80,48},{96,0},{112,80},{1... | collective-permute-start | bytes 1769480 | tf_op jit(solution)/shard_map/ppermute | solution.py:140
  166.8 17.3 %collective-permute-start.34 = (bf16[2,32,768]{2,1,0:T(8,128)(2,1)S(1)}, bf16[2,32,768]{2,1,0:T(8,128)(2,1)S(1)}, u32[]{:S(2)}, u32[]{:S(2)}) collective-permute-start(bf16[2,32,768]{2,1,0:T(8,128)(2,1)S(1)} %pad_maximum_fusion.13), channel_id=1, source_target_pairs={{0,32},{16,112},{32,64},{48,16},{64,96},{80,48},{96,0},{112,80},{1... | collective-permute-start | bytes 294920 | tf_op jit(solution)/shard_map/ppermute | solution.py:140
  166.9 16.4 %collective-permute-start.33 = (bf16[2,32,768]{2,1,0:T(8,128)(2,1)S(1)}, bf16[2,32,768]{2,1,0:T(8,128)(2,1)S(1)}, u32[]{:S(2)}, u32[]{:S(2)}) collective-permute-start(bf16[2,32,768]{2,1,0:T(8,128)(2,1)S(1)} %pad_maximum_fusion.12), channel_id=1, source_target_pairs={{0,64},{16,80},{32,96},{48,112},{64,0},{80,16},{96,32},{112,48},{1... | collective-permute-start | bytes 294920 | tf_op jit(solution)/shard_map/ppermute | solution.py:140
  169.6 13.6 %collective-permute-start.32 = (bf16[2,32,768]{2,1,0:T(8,128)(2,1)S(1)}, bf16[2,32,768]{2,1,0:T(8,128)(2,1)S(1)}, u32[]{:S(2)}, u32[]{:S(2)}) collective-permute-start(bf16[2,32,768]{2,1,0:T(8,128)(2,1)S(1)} %pad_maximum_fusion.11), channel_id=1, source_target_pairs={{0,96},{16,48},{32,0},{48,80},{64,32},{80,112},{96,64},{112,16},{1... | collective-permute-start | bytes 294920 | tf_op jit(solution)/shard_map/ppermute | solution.py:140

commit v3 on v2

--- a/solution.py
+++ b/solution.py
@@ -33,7 +33,7 @@
         in_specs=in_specs,
         out_specs=out_specs,
         out_shape=out_shape,
-        compiler_params=pltpu.CompilerParams(vmem_limit_bytes=40 * 2**20),
+        compiler_params=pltpu.CompilerParams(vmem_limit_bytes=16 * 2**20),
         cost_estimate=pl.CostEstimate(flops=1, bytes_accessed=1, transcendentals=0),
     )(*arrays)
 
@@ -55,7 +55,7 @@
         body,
         (3,),
         [
-            pl.BlockSpec((2, rows, features), lambda i: (0, 0, 0)),
+            pl.BlockSpec((2, rows, features), lambda i: (0, 0, 0), pipeline_mode=pl.Buffered(1)),
             pl.BlockSpec((features, tile), lambda i: (0, i)),
             pl.BlockSpec((tile, features), lambda i: (i, 0)),
         ],
@@ -192,18 +192,21 @@
     def join(parts, axis):
         return jnp.concatenate(parts, axis=axis)
 
+    def after(round_value):
+        ups[-1], downs[-1], _ = held(ups[-1], downs[-1], round_value)
+
     step()
-    own, ups[0], downs[0] = held(own, ups[0], downs[0])
+    after(own)
     step()
     first = join([own] + [plane(own, 0, hop) for hop in (1, 2, 3)], 1)
-    first, ups[1], downs[1] = held(first, ups[1], downs[1])
-
-    up_early = across(join(ups[:3], 0))
+    after(first)
+
+    up_early = across(join(ups[:2], 0))
     left, right = plane(first, 1, 1), plane(first, 1, -1)
     step()
     left, right, up_early, ups[3], downs[3] = held(left, right, up_early, ups[3], downs[3])
     (down_mine,) = held(join(downs, 1))
-    up_late, down_theirs = across(ups[3]), across(down_mine)
+    up_late, down_theirs = across(join(ups[2:], 0)), across(down_mine)
     far = [plane(left[:, :half], 1, 1), plane(right[:, half:], 1, -1)]
 
     def rows_of(value, k):
@@ -214,7 +217,7 @@
 
     up = held(
         join(ups, 0),
-        join([rows_of(up_early, 0), up_late, rows_of(up_early, 2), rows_of(up_early, 1)], 0),
+        join([rows_of(up_early, 0), rows_of(up_late, 1), rows_of(up_late, 0), rows_of(up_early, 1)], 0),
     )
     down = held(down_mine, join([columns(down_theirs, k) for k in turned], 1))
     up, down = held(join(up, 1), join(down, 0))
@@ -266,8 +269,8 @@
     down_grad = along_x(down_part(2, down_grad).astype(BF), -1)
     up_grad = along_x(up_part(2, up_grad).astype(BF), 1)
     sums = total(here, left, right).astype(BF).reshape(2, 4, sub, 4 * width)
-    end = total(sums[:, 0], *(plane(sums[:, hop], 0, -hop) for hop in (1, 2, 3)))
-    end, down_grad, up_grad = held(end.astype(BF), down_grad, up_grad)
+    end = total(sums[:, 0], *(plane(sums[:, hop], 0, -hop) for hop in (1, 2, 3))).astype(BF)
+    down_grad, up_grad, _ = held(down_grad, up_grad, end)
     down_grad = along_x(down_part(3, down_grad).astype(BF), -1)
     up_grad = along_x(up_part(3, up_grad).astype(BF), 1)
     down_grad, up_grad = down_part(0, down_grad), up_part(0, up_grad)

time: 190 us -> 184 us (0.968)
  the two profiles are of different devices: /device:TPU:0 before, /device:TPU:41 now
where the time goes in v3:
time: 184 us
  waiting for transfers between devices  92.7 us (50%)
  starting transfers between devices  43.2 us (23%)
  Pallas kernels  26.7 us (15%)
  other arithmetic  16.4 us (9%)
  local copies, waits for them, and re-layouts  3.5 us (2%)
    ppermute x18, waiting for transfers between devices, along_x(): return lax.ppermute(value, ('row', 'col'), pairs)  69.5 us
    pallas_call x6, Pallas kernels, local_kernel(): pl.pallas_call(body, grid=grid, in_specs=in_specs, out_specs=out_specs, o...  26.7 us
    ppermute x14, waiting for transfers between devices, plane(): return lax.ppermute(value, ('col', 'depth'), pairs)  23.1 us
    ppermute x14, starting transfers between devices, plane(): return lax.ppermute(value, ('col', 'depth'), pairs)  17.9 us
    ppermute x18, starting transfers between devices, along_x(): return lax.ppermute(value, ('row', 'col'), pairs)  17.3 us
    ppermute x5, starting transfers between devices, across(): return lax.ppermute(value, 'col', [(0, 1), (1, 0)])  8 us
    concatenate x11, other arithmetic, join(): return jnp.concatenate(parts, axis=axis)  5.25 us
  transfers between devices with their start and end apart: 37, of which 24 were waited for; matrix products, arithmetic and copies ran while one was open for 6% of the time, Pallas kernels for 8%

profile of v3, /device:TPU:41, one launch (start us, length us, event | category | flops | bytes accessed | tf_op | source)
XLA Modules:
  0.0 183.7 jit_solution(2007718118149372383)
XLA Ops:
  1.8 2.5 %collective-permute-start = (bf16[2,32,768]{2,1,0:T(8,128)(2,1)S(1)}, bf16[2,32,768]{2,1,0:T(8,128)(2,1)S(1)}, u32[]{:S(2)}, u32[]{:S(2)}) collective-permute-start(bf16[2,32,768]{2,1,0:T(8,128)(2,1)S(1)} %get-tuple-element.128), channel_id=1, source_target_pairs={{0,32},{16,112},{32,64},{48,16},{64,96},{80,48},{96,0},{112,80},{1... | collective-permute-start | bytes 294920 | tf_op jit(solution)/shard_map/ppermute | solution.py:140
  6.0 4.7 %collective-permute-done.1 = bf16[2,32,768]{2,1,0:T(8,128)(2,1)S(1)} collective-permute-done((bf16[2,32,768]{2,1,0:T(8,128)(2,1)S(1)}, bf16[2,32,768]{2,1,0:T(8,128)(2,1)S(1)}, u32[]{:S(2)}, u32[]{:S(2)}) %collective-permute-start.1) | collective-permute-done | bytes 98336 | tf_op jit(solution)/shard_map/ppermute | solution.py:140
  11.7 1.4 collective-permute-start.3
  13.9 2.0 %collective-permute-start.5 = (bf16[2,32,3072]{2,1,0:T(8,128)(2,1)S(1)}, bf16[2,32,3072]{2,1,0:T(8,128)(2,1)S(1)}, u32[]{:S(2)}, u32[]{:S(2)}) collective-permute-start(bf16[2,32,3072]{2,1,0:T(8,128)(2,1)S(1)} %get-tuple-element.126), channel_id=1, source_target_pairs={{0,12},{1,13},{2,14},{3,15},{4,0},{5,1},{6,2},{7,3},{8,4},{9,5},{1... | collective-permute-start | bytes 1179656 | tf_op jit(solution)/shard_map/ppermute | solution.py:157
  17.3 1.4 collective-permute-done.3
  18.7 2.8 %collective-permute-done.4 = bf16[2,32,3072]{2,1,0:T(8,128)(2,1)S(1)} collective-permute-done((bf16[2,32,3072]{2,1,0:T(8,128)(2,1)S(1)}, bf16[2,32,3072]{2,1,0:T(8,128)(2,1)S(1)}, u32[]{:S(2)}, u32[]{:S(2)}) %collective-permute-start.4) | collective-permute-done | bytes 393248 | tf_op jit(solution)/shard_map/ppermute | solution.py:157
  21.5 3.5 %collective-permute-done.5 = bf16[2,32,3072]{2,1,0:T(8,128)(2,1)S(1)} collective-permute-done((bf16[2,32,3072]{2,1,0:T(8,128)(2,1)S(1)}, bf16[2,32,3072]{2,1,0:T(8,128)(2,1)S(1)}, u32[]{:S(2)}, u32[]{:S(2)}) %collective-permute-start.5) | collective-permute-done | bytes 393248 | tf_op jit(solution)/shard_map/ppermute | solution.py:157
  25.1 1.7 collective-permute-start.6
  26.8 1.6 collective-permute-done.8
  28.4 3.3 %collective-permute-done.9 = bf16[384,768]{1,0:T(8,128)(2,1)S(1)} collective-permute-done((bf16[384,768]{1,0:T(8,128)(2,1)S(1)}, bf16[384,768]{1,0:T(8,128)(2,1)S(1)}, u32[]{:S(2)}, u32[]{:S(2)}) %collective-permute-start.9) | collective-permute-done | bytes 589856 | tf_op jit(solution)/shard_map/ppermute | solution.py:140
  31.7 1.5 collective-permute-start.12
  33.3 3.8 %collective-permute-start.10 = (bf16[1536,384]{1,0:T(8,128)(2,1)S(1)}, bf16[1536,384]{1,0:T(8,128)(2,1)S(1)}, u32[]{:S(2)}, u32[]{:S(2)}) collective-permute-start(bf16[1536,384]{1,0:T(8,128)(2,1)S(1)} %pad_maximum_fusion.9), channel_id=1, source_target_pairs={{0,16},{16,0},{1,17},{17,1},{2,18},{18,2},{3,19},{19,3},{4,20},{20... | collective-permute-start | bytes 3538952 | tf_op jit(solution)/shard_map/ppermute | solution.py:144
  37.2 7.4 %collective-permute-done.11 = bf16[768,384]{1,0:T(8,128)(2,1)S(1)} collective-permute-done((bf16[768,384]{1,0:T(8,128)(2,1)S(1)}, bf16[768,384]{1,0:T(8,128)(2,1)S(1)}, u32[]{:S(2)}, u32[]{:S(2)}) %collective-permute-start.11) | collective-permute-done | bytes 589856 | tf_op jit(solution)/shard_map/ppermute | solution.py:140
  44.5 1.2 collective-permute-done.12
  45.8 2.1 %collective-permute-start.14 = (bf16[384,768]{1,0:T(8,128)(2,1)S(1)}, bf16[384,768]{1,0:T(8,128)(2,1)S(1)}, u32[]{:S(2)}, u32[]{:S(2)}) collective-permute-start(bf16[384,768]{1,0:T(8,128)(2,1)S(1)} %collective-permute-done.12), channel_id=1, source_target_pairs={{0,96},{16,48},{32,0},{48,80},{64,32},{80,112},{96,64},{112,16},{1... | collective-permute-start | bytes 1769480 | tf_op jit(solution)/shard_map/ppermute | solution.py:140
  47.9 10.5 %collective-permute-done.13 = bf16[768,384]{1,0:T(8,128)(2,1)S(1)} collective-permute-done((bf16[768,384]{1,0:T(8,128)(2,1)S(1)}, bf16[768,384]{1,0:T(8,128)(2,1)S(1)}, u32[]{:S(2)}, u32[]{:S(2)}) %collective-permute-start.13) | collective-permute-done | bytes 589856 | tf_op jit(solution)/shard_map/ppermute | solution.py:140
  58.4 1.3 collective-permute-done.14
  60.1 3.5 %collective-permute-start.18 = (bf16[384,3072]{1,0:T(8,128)(2,1)S(1)}, bf16[384,3072]{1,0:T(8,128)(2,1)S(1)}, u32[]{:S(2)}, u32[]{:S(2)}) collective-permute-start(bf16[384,3072]{1,0:T(8,128)(2,1)S(1)} %pad_maximum_fusion.4), channel_id=1, source_target_pairs={{0,16},{16,0},{1,17},{17,1},{2,18},{18,2},{3,19},{19,3},{4,20},{20... | collective-permute-start | bytes 7077896 | tf_op jit(solution)/shard_map/ppermute | solution.py:144
  64.0 3.9 %collective-permute-start.15 = (bf16[2,64,3072]{2,1,0:T(8,128)(2,1)S(1)}, bf16[2,64,3072]{2,1,0:T(8,128)(2,1)S(1)}, u32[]{:S(2)}, u32[]{:S(2)}) collective-permute-start(bf16[2,64,3072]{2,1,0:T(8,128)(2,1)S(1)} %slice.193), channel_id=1, source_target_pairs={{0,1},{1,2},{2,3},{3,0},{4,5},{5,6},{6,7},{7,4},{8,9},{9,10},{10,1... | collective-permute-start | bytes 2359304 | tf_op jit(solution)/shard_map/ppermute | solution.py:157
  71.0 4.9 %shard_map.75 = (bf16[384,768]{1,0:T(8,128)(2,1)S(1)}, bf16[384,768]{1,0:T(8,128)(2,1)S(1)}) custom-call(bf16[2,384,3072]{2,1,0:T(8,128)(2,1)S(1)} %constant_dynamic-update-slice_fusion.pair_ref.refs_0_, bf16[3072,768]{1,0:T(8,128)(2,1)S(1)} %pad_maximum_fusion.up_ref, bf16[768,3072]{1,0:T(8,128)(2,1)S(1)} %pad_maximum_fusion.1.down_ref), custom_call_target="tpu_custom_call" | custom-call | flops 1 | bytes 1 | tf_op jit(solution)/shard_map/pallas_call | solution.py:30
  76.8 3.0 %collective-permute-done.16 = bf16[2,64,3072]{2,1,0:T(8,128)(2,1)S(1)} collective-permute-done((bf16[2,64,3072]{2,1,0:T(8,128)(2,1)}, bf16[2,64,3072]{2,1,0:T(8,128)(2,1)S(1)}, u32[]{:S(2)}, u32[]{:S(2)}) %collective-permute-start.16) | collective-permute-done | bytes 786464 | tf_op jit(solution)/shard_map/ppermute | solution.py:157
  80.0 3.0 %shard_map.76 = (bf16[128,768]{1,0:T(8,128)(2,1)S(1)}, bf16[128,768]{1,0:T(8,128)(2,1)S(1)}) custom-call(bf16[2,128,3072]{2,1,0:T(8,128)(2,1)S(1)} %constant_dynamic-update-slice_fusion.6.pair_ref.refs_1_, bf16[3072,768]{1,0:T(8,128)(2,1)S(1)} %pad_maximum_fusion.up_ref, bf16[768,3072]{1,0:T(8,128)(2,1)S(1)} %pad_maximum_fusion.1.down_ref), custom_call_target="tpu_custom_call" | custom-call | flops 1 | bytes 1 | tf_op jit(solution)/shard_map/pallas_call | solution.py:30
  83.0 3.1 %shard_map.77 = bf16[2,128,3072]{2,1,0:T(8,128)(2,1)S(1)} custom-call(bf16[128,768]{1,0:T(8,128)(2,1)S(1)} %get-tuple-element.81.act_ref.refs_3_, bf16[128,768]{1,0:T(8,128)(2,1)S(1)} %get-tuple-element.82.grad_ref.refs_5_, bf16[3072,768]{1,0:T(8,128)(2,1)S(1)} %pad_maximum_fusion.up_ref, bf16[768,3072]{1,0:T(8,128)(2,1)S(1)} %pad_maximum_fusion.1.down_ref), custom_call_target="tpu_custom_call" | custom-call | flops 1 | bytes 1 | tf_op jit(solution)/shard_map/pallas_call | solution.py:30
  86.2 5.4 %shard_map.78 = (bf16[384,3072]{1,0:T(8,128)(2,1)S(1)}, bf16[3072,384]{1,0:T(8,128)(2,1)S(1)}) custom-call(bf16[2,384,3072]{2,1,0:T(8,128)(2,1)S(1)} %constant_dynamic-update-slice_fusion.pair_ref.refs_0_, bf16[2,128,3072]{2,1,0:T(8,128)(2,1)S(1)} %constant_dynamic-update-slice_fusion.6.pair_ref.refs_1_, ...), custom_call_target="tpu_custom_call" | custom-call | flops 1 | bytes 1 | tf_op jit(solution)/shard_map/pallas_call | solution.py:30
  92.2 1.5 collective-permute-start.20
  93.6 5.4 %shard_map.80 = (bf16[384,3072]{1,0:T(8,128)(2,1)S(1)}, bf16[3072,384]{1,0:T(8,128)(2,1)S(1)}) custom-call(bf16[2,384,3072]{2,1,0:T(8,128)(2,1)S(1)} %constant_dynamic-update-slice_fusion.pair_ref.refs_0_, bf16[2,128,3072]{2,1,0:T(8,128)(2,1)S(1)} %constant_dynamic-update-slice_fusion.6.pair_ref.refs_1_, ...), custom_call_target="tpu_custom_call" | custom-call | flops 1 | bytes 1 | tf_op jit(solution)/shard_map/pallas_call | solution.py:30
  99.0 5.0 %shard_map.79 = bf16[2,384,3072]{2,1,0:T(8,128)(2,1)S(1)} custom-call(bf16[384,768]{1,0:T(8,128)(2,1)S(1)} %get-tuple-element.85.refs_2_.act_ref, bf16[384,768]{1,0:T(8,128)(2,1)S(1)} %get-tuple-element.86.refs_4_.grad_ref, bf16[3072,768]{1,0:T(8,128)(2,1)S(1)} %pad_maximum_fusion.up_ref, bf16[768,3072]{1,0:T(8,128)(2,1)S(1)} %pad_maximum_fusion.1.down_ref), custom_call_target="tpu_custom_call" | custom-call | flops 1 | bytes 1 | tf_op jit(solution)/shard_map/pallas_call | solution.py:30
  106.2 1.9 %pad_maximum_fusion.8 = bf16[2,128,3072]{2,1,0:T(8,128)(2,1)} fusion(bf16[2,64,3072]{2,1,0:T(8,128)(2,1)S(1)} %get-tuple-element.106, bf16[2,64,3072]{2,1,0:T(8,128)(2,1)S(1)} %get-tuple-element.104), kind=kLoop, calls=%fused_computation.9 | loop fusion | flops 3145728 | bytes 3145728 | tf_op jit(solution)/shard_map/concatenate | solution.py:193
  108.1 1.2 collective-permute-start.24
  109.3 1.3 pad_maximum_fusion.7
  111.6 1.7 collective-permute-start.25
  113.3 8.8 %collective-permute-done.26 = bf16[768,384]{1,0:T(8,128)(2,1)} collective-permute-done((bf16[768,384]{1,0:T(8,128)(2,1)S(1)}, bf16[768,384]{1,0:T(8,128)(2,1)}, u32[]{:S(2)}, u32[]{:S(2)}) %collective-permute-start.26) | collective-permute-done | bytes 589856 | tf_op jit(solution)/shard_map/ppermute | solution.py:140
  122.1 3.2 %collective-permute-done.25 = bf16[384,768]{1,0:T(8,128)(2,1)} collective-permute-done((bf16[384,768]{1,0:T(8,128)(2,1)S(1)}, bf16[384,768]{1,0:T(8,128)(2,1)}, u32[]{:S(2)}, u32[]{:S(2)}) %collective-permute-start.25) | collective-permute-done | bytes 589856 | tf_op jit(solution)/shard_map/ppermute | solution.py:140
  125.3 3.0 %collective-permute-done.24 = bf16[2,128,3072]{2,1,0:T(8,128)(2,1)} collective-permute-done((bf16[2,128,3072]{2,1,0:T(8,128)(2,1)}, bf16[2,128,3072]{2,1,0:T(8,128)(2,1)}, u32[]{:S(2)}, u32[]{:S(2)}) %collective-permute-start.24) | collective-permute-done | bytes 1572896 | tf_op jit(solution)/shard_map/ppermute | solution.py:157
  128.3 3.2 %collective-permute-done.23 = bf16[2,128,3072]{2,1,0:T(8,128)(2,1)} collective-permute-done((bf16[2,128,3072]{2,1,0:T(8,128)(2,1)}, bf16[2,128,3072]{2,1,0:T(8,128)(2,1)}, u32[]{:S(2)}, u32[]{:S(2)}) %collective-permute-start.23) | collective-permute-done | bytes 1572896 | tf_op jit(solution)/shard_map/ppermute | solution.py:157
  131.5 3.3 %add_convert_fusion = bf16[2,128,3072]{2,1,0:T(8,128)(2,1)S(1)} fusion(bf16[2,128,3072]{2,1,0:T(8,128)(2,1)} %collective-permute-done.24, bf16[2,128,3072]{2,1,0:T(8,128)(2,1)} %collective-permute-done.23, bf16[2,384,3072]{2,1,0:T(8,128)(2,1)} %copy-done), kind=kLoop, calls=%fused_computation.2 | loop fusion | flops 4718592 | bytes 6291456 | tf_op jit(solution)/shard_map/convert_element_type | solution.py:271
  136.0 1.8 collective-permute-start.28
  137.8 2.0 %collective-permute-start.29 = (bf16[2,32,3072]{2,1,0:T(8,128)(2,1)S(1)}, bf16[2,32,3072]{2,1,0:T(8,128)(2,1)S(1)}, u32[]{:S(2)}, u32[]{:S(2)}) collective-permute-start(bf16[2,32,3072]{2,1,0:T(8,128)(2,1)S(1)} %get-tuple-element.114), channel_id=1, source_target_pairs={{0,4},{1,5},{2,6},{3,7},{4,8},{5,9},{6,10},{7,11},{8,12},{9,13},{1... | collective-permute-start | bytes 1179656 | tf_op jit(solution)/shard_map/ppermute | solution.py:157
  139.7 1.3 add_convert_fusion.5
  141.0 1.6 collective-permute-start.34
  142.6 1.3 add_convert_fusion.6
  144.1 3.3 %collective-permute-done.28 = bf16[2,32,3072]{2,1,0:T(8,128)(2,1)S(1)} collective-permute-done((bf16[2,32,3072]{2,1,0:T(8,128)(2,1)S(1)}, bf16[2,32,3072]{2,1,0:T(8,128)(2,1)S(1)}, u32[]{:S(2)}, u32[]{:S(2)}) %collective-permute-start.28) | collective-permute-done | bytes 393248 | tf_op jit(solution)/shard_map/ppermute | solution.py:157
  148.6 1.6 collective-permute-start.32
  151.0 13.6 %collective-permute-done.30 = bf16[2,32,768]{2,1,0:T(8,128)(2,1)S(1)} collective-permute-done((bf16[2,32,768]{2,1,0:T(8,128)(2,1)S(1)}, bf16[2,32,768]{2,1,0:T(8,128)(2,1)S(1)}, u32[]{:S(2)}, u32[]{:S(2)}) %collective-permute-start.30) | collective-permute-done | bytes 98336 | tf_op jit(solution)/shard_map/ppermute | solution.py:140
  165.2 2.7 %collective-permute-start.35 = (bf16[768,384]{1,0:T(8,128)(2,1)S(1)}, bf16[768,384]{1,0:T(8,128)(2,1)S(1)}, u32[]{:S(2)}, u32[]{:S(2)}) collective-permute-start(bf16[768,384]{1,0:T(8,128)(2,1)S(1)} %add_convert_fusion.4), channel_id=1, source_target_pairs={{0,32},{16,112},{32,64},{48,16},{64,96},{80,48},{96,0},{112,80},{1... | collective-permute-start | bytes 1769480 | tf_op jit(solution)/shard_map/ppermute | solution.py:140
  168.7 12.6 %collective-permute-done.36 = bf16[384,768]{1,0:T(8,128)(2,1)S(1)} collective-permute-done((bf16[384,768]{1,0:T(8,128)(2,1)S(1)}, bf16[384,768]{1,0:T(8,128)(2,1)S(1)}, u32[]{:S(2)}, u32[]{:S(2)}) %collective-permute-start.36) | collective-permute-done | bytes 589856 | tf_op jit(solution)/shard_map/ppermute | solution.py:140
  181.3 1.2 convert_add_fusion
  182.5 1.2 convert_add_fusion.1
  (106 shorter events, 19.4 us)
Async XLA Ops:
  0.6 15.2 %copy-start.3 = (bf16[768,384]{1,0:T(8,128)(2,1)S(1)}, bf16[768,384]{1,0:T(8,128)(2,1)}, u32[]{:S(2)}) copy-start(bf16[768,384]{1,0:T(8,128)(2,1)} %param.5) | copy-start | bytes 1769476
  0.6 16.1 %copy-start.8 = (bf16[384,768]{1,0:T(8,128)(2,1)S(1)}, bf16[384,768]{1,0:T(8,128)(2,1)}, u32[]{:S(2)}) copy-start(bf16[384,768]{1,0:T(8,128)(2,1)} %param.6) | copy-start | bytes 1769476
  1.8 4.2 %collective-permute-start = (bf16[2,32,768]{2,1,0:T(8,128)(2,1)S(1)}, bf16[2,32,768]{2,1,0:T(8,128)(2,1)S(1)}, u32[]{:S(2)}, u32[]{:S(2)}) collective-permute-start(bf16[2,32,768]{2,1,0:T(8,128)(2,1)S(1)} %get-tuple-element.128), channel_id=1, source_target_pairs={{0,32},{16,112},{32,64},{48,16},{64,96},{80,48},{96,0},{112,80},{1... | collective-permute-start | bytes 294920 | tf_op jit(solution)/shard_map/ppermute | solution.py:140
  4.4 6.3 %collective-permute-start.1 = (bf16[2,32,768]{2,1,0:T(8,128)(2,1)S(1)}, bf16[2,32,768]{2,1,0:T(8,128)(2,1)S(1)}, u32[]{:S(2)}, u32[]{:S(2)}) collective-permute-start(bf16[2,32,768]{2,1,0:T(8,128)(2,1)S(1)} %get-tuple-element.129), channel_id=1, source_target_pairs={{0,64},{16,80},{32,96},{48,112},{64,0},{80,16},{96,32},{112,48},{1... | collective-permute-start | bytes 294920 | tf_op jit(solution)/shard_map/ppermute | solution.py:140
  4.9 6.7 %collective-permute-start.2 = (bf16[2,32,768]{2,1,0:T(8,128)(2,1)S(1)}, bf16[2,32,768]{2,1,0:T(8,128)(2,1)S(1)}, u32[]{:S(2)}, u32[]{:S(2)}) collective-permute-start(bf16[2,32,768]{2,1,0:T(8,128)(2,1)S(1)} %get-tuple-element.130), channel_id=1, source_target_pairs={{0,96},{16,48},{32,0},{48,80},{64,32},{80,112},{96,64},{112,16},{1... | collective-permute-start | bytes 294920 | tf_op jit(solution)/shard_map/ppermute | solution.py:140
  11.7 7.0 %collective-permute-start.3 = (bf16[2,32,3072]{2,1,0:T(8,128)(2,1)S(1)}, bf16[2,32,3072]{2,1,0:T(8,128)(2,1)S(1)}, u32[]{:S(2)}, u32[]{:S(2)}) collective-permute-start(bf16[2,32,3072]{2,1,0:T(8,128)(2,1)S(1)} %get-tuple-element.126), channel_id=1, source_target_pairs={{0,4},{1,5},{2,6},{3,7},{4,8},{5,9},{6,10},{7,11},{8,12},{9,13},{1... | collective-permute-start | bytes 1179656 | tf_op jit(solution)/shard_map/ppermute | solution.py:157
  13.1 8.5 %collective-permute-start.4 = (bf16[2,32,3072]{2,1,0:T(8,128)(2,1)S(1)}, bf16[2,32,3072]{2,1,0:T(8,128)(2,1)S(1)}, u32[]{:S(2)}, u32[]{:S(2)}) collective-permute-start(bf16[2,32,3072]{2,1,0:T(8,128)(2,1)S(1)} %get-tuple-element.126), channel_id=1, source_target_pairs={{0,8},{1,9},{2,10},{3,11},{4,12},{5,13},{6,14},{7,15},{8,0},{9,1},... | collective-permute-start | bytes 1179656 | tf_op jit(solution)/shard_map/ppermute | solution.py:157
  13.9 11.1 %collective-permute-start.5 = (bf16[2,32,3072]{2,1,0:T(8,128)(2,1)S(1)}, bf16[2,32,3072]{2,1,0:T(8,128)(2,1)S(1)}, u32[]{:S(2)}, u32[]{:S(2)}) collective-permute-start(bf16[2,32,3072]{2,1,0:T(8,128)(2,1)S(1)} %get-tuple-element.126), channel_id=1, source_target_pairs={{0,12},{1,13},{2,14},{3,15},{4,0},{5,1},{6,2},{7,3},{8,4},{9,5},{1... | collective-permute-start | bytes 1179656 | tf_op jit(solution)/shard_map/ppermute | solution.py:157
  15.9 12.5 %collective-permute-start.8 = (bf16[768,384]{1,0:T(8,128)(2,1)S(1)}, bf16[768,384]{1,0:T(8,128)(2,1)S(1)}, u32[]{:S(2)}, u32[]{:S(2)}) collective-permute-start(bf16[768,384]{1,0:T(8,128)(2,1)S(1)} %copy-done.3), channel_id=1, source_target_pairs={{0,32},{16,112},{32,64},{48,16},{64,96},{80,48},{96,0},{112,80},{1... | collective-permute-start | bytes 1769480 | tf_op jit(solution)/shard_map/ppermute | solution.py:140
  16.7 15.0 %collective-permute-start.9 = (bf16[384,768]{1,0:T(8,128)(2,1)S(1)}, bf16[384,768]{1,0:T(8,128)(2,1)S(1)}, u32[]{:S(2)}, u32[]{:S(2)}) collective-permute-start(bf16[384,768]{1,0:T(8,128)(2,1)S(1)} %copy-done.8), channel_id=1, source_target_pairs={{0,96},{16,48},{32,0},{48,80},{64,32},{80,112},{96,64},{112,16},{1... | collective-permute-start | bytes 1769480 | tf_op jit(solution)/shard_map/ppermute | solution.py:140
  25.1 34.7 %collective-permute-start.6 = (bf16[2,128,3072]{2,1,0:T(8,128)(2,1)S(1)}, bf16[2,128,3072]{2,1,0:T(8,128)(2,1)S(1)}, u32[]{:S(2)}, u32[]{:S(2)}) collective-permute-start(bf16[2,128,3072]{2,1,0:T(8,128)(2,1)S(1)} %pad_maximum_fusion.6), channel_id=1, source_target_pairs={{0,1},{1,2},{2,3},{3,0},{4,5},{5,6},{6,7},{7,4},{8,9},{9,10},{10,1... | collective-permute-start | bytes 4718600 | tf_op jit(solution)/shard_map/ppermute | solution.py:157
  26.8 33.0 %collective-permute-start.7 = (bf16[2,128,3072]{2,1,0:T(8,128)(2,1)S(1)}, bf16[2,128,3072]{2,1,0:T(8,128)(2,1)S(1)}, u32[]{:S(2)}, u32[]{:S(2)}) collective-permute-start(bf16[2,128,3072]{2,1,0:T(8,128)(2,1)S(1)} %pad_maximum_fusion.6), channel_id=1, source_target_pairs={{0,3},{1,0},{2,1},{3,2},{4,7},{5,4},{6,5},{7,6},{8,11},{9,8},{10,9... | collective-permute-start | bytes 4718600 | tf_op jit(solution)/shard_map/ppermute | solution.py:157
  31.7 12.8 %collective-permute-start.11 = (bf16[768,384]{1,0:T(8,128)(2,1)S(1)}, bf16[768,384]{1,0:T(8,128)(2,1)S(1)}, u32[]{:S(2)}, u32[]{:S(2)}) collective-permute-start(bf16[768,384]{1,0:T(8,128)(2,1)S(1)} %collective-permute-done.8), channel_id=1, source_target_pairs={{0,32},{16,112},{32,64},{48,16},{64,96},{80,48},{96,0},{112,80},{1... | collective-permute-start | bytes 1769480 | tf_op jit(solution)/shard_map/ppermute | solution.py:140
  31.7 14.1 %collective-permute-start.12 = (bf16[384,768]{1,0:T(8,128)(2,1)S(1)}, bf16[384,768]{1,0:T(8,128)(2,1)S(1)}, u32[]{:S(2)}, u32[]{:S(2)}) collective-permute-start(bf16[384,768]{1,0:T(8,128)(2,1)S(1)} %collective-permute-done.9), channel_id=1, source_target_pairs={{0,96},{16,48},{32,0},{48,80},{64,32},{80,112},{96,64},{112,16},{1... | collective-permute-start | bytes 1769480 | tf_op jit(solution)/shard_map/ppermute | solution.py:140
  33.3 26.5 %collective-permute-start.10 = (bf16[1536,384]{1,0:T(8,128)(2,1)S(1)}, bf16[1536,384]{1,0:T(8,128)(2,1)S(1)}, u32[]{:S(2)}, u32[]{:S(2)}) collective-permute-start(bf16[1536,384]{1,0:T(8,128)(2,1)S(1)} %pad_maximum_fusion.9), channel_id=1, source_target_pairs={{0,16},{16,0},{1,17},{17,1},{2,18},{18,2},{3,19},{19,3},{4,20},{20... | collective-permute-start | bytes 3538952 | tf_op jit(solution)/shard_map/ppermute | solution.py:144
  45.8 12.7 %collective-permute-start.13 = (bf16[768,384]{1,0:T(8,128)(2,1)S(1)}, bf16[768,384]{1,0:T(8,128)(2,1)S(1)}, u32[]{:S(2)}, u32[]{:S(2)}) collective-permute-start(bf16[768,384]{1,0:T(8,128)(2,1)S(1)} %collective-permute-done.11), channel_id=1, source_target_pairs={{0,32},{16,112},{32,64},{48,16},{64,96},{80,48},{96,0},{112,80},{1... | collective-permute-start | bytes 1769480 | tf_op jit(solution)/shard_map/ppermute | solution.py:140
  45.8 14.0 %collective-permute-start.14 = (bf16[384,768]{1,0:T(8,128)(2,1)S(1)}, bf16[384,768]{1,0:T(8,128)(2,1)S(1)}, u32[]{:S(2)}, u32[]{:S(2)}) collective-permute-start(bf16[384,768]{1,0:T(8,128)(2,1)S(1)} %collective-permute-done.12), channel_id=1, source_target_pairs={{0,96},{16,48},{32,0},{48,80},{64,32},{80,112},{96,64},{112,16},{1... | collective-permute-start | bytes 1769480 | tf_op jit(solution)/shard_map/ppermute | solution.py:140
  60.1 10.1 %collective-permute-start.18 = (bf16[384,3072]{1,0:T(8,128)(2,1)S(1)}, bf16[384,3072]{1,0:T(8,128)(2,1)S(1)}, u32[]{:S(2)}, u32[]{:S(2)}) collective-permute-start(bf16[384,3072]{1,0:T(8,128)(2,1)S(1)} %pad_maximum_fusion.4), channel_id=1, source_target_pairs={{0,16},{16,0},{1,17},{17,1},{2,18},{18,2},{3,19},{19,3},{4,20},{20... | collective-permute-start | bytes 7077896 | tf_op jit(solution)/shard_map/ppermute | solution.py:144
  63.7 5.7 %collective-permute-start.17 = (bf16[1536,384]{1,0:T(8,128)(2,1)S(1)}, bf16[1536,384]{1,0:T(8,128)(2,1)S(1)}, u32[]{:S(2)}, u32[]{:S(2)}) collective-permute-start(bf16[1536,384]{1,0:T(8,128)(2,1)S(1)} %pad_maximum_fusion.10), channel_id=1, source_target_pairs={{0,16},{16,0},{1,17},{17,1},{2,18},{18,2},{3,19},{19,3},{4,20},{20... | collective-permute-start | bytes 3538952 | tf_op jit(solution)/shard_map/ppermute | solution.py:144
  64.0 12.8 %collective-permute-start.15 = (bf16[2,64,3072]{2,1,0:T(8,128)(2,1)S(1)}, bf16[2,64,3072]{2,1,0:T(8,128)(2,1)S(1)}, u32[]{:S(2)}, u32[]{:S(2)}) collective-permute-start(bf16[2,64,3072]{2,1,0:T(8,128)(2,1)S(1)} %slice.193), channel_id=1, source_target_pairs={{0,1},{1,2},{2,3},{3,0},{4,5},{5,6},{6,7},{7,4},{8,9},{9,10},{10,1... | collective-permute-start | bytes 2359304 | tf_op jit(solution)/shard_map/ppermute | solution.py:157
  68.8 11.1 %collective-permute-start.16 = (bf16[2,64,3072]{2,1,0:T(8,128)(2,1)}, bf16[2,64,3072]{2,1,0:T(8,128)(2,1)S(1)}, u32[]{:S(2)}, u32[]{:S(2)}) collective-permute-start(bf16[2,64,3072]{2,1,0:T(8,128)(2,1)} %slice.194), channel_id=1, source_target_pairs={{0,3},{1,0},{2,1},{3,2},{4,7},{5,4},{6,5},{7,6},{8,11},{9,8},{10,9... | collective-permute-start | bytes 2359304 | tf_op jit(solution)/shard_map/ppermute | solution.py:157
  91.6 13.4 %collective-permute-start.21 = (bf16[384,3072]{1,0:T(8,128)(2,1)S(1)}, bf16[384,3072]{1,0:T(8,128)(2,1)S(1)}, u32[]{:S(2)}, u32[]{:S(2)}) collective-permute-start(bf16[384,3072]{1,0:T(8,128)(2,1)S(1)} %get-tuple-element.89), channel_id=1, source_target_pairs={{0,16},{16,0},{1,17},{17,1},{2,18},{18,2},{3,19},{19,3},{4,20},{20... | collective-permute-start | bytes 7077896 | tf_op jit(solution)/shard_map/ppermute | solution.py:144
  91.7 13.3 %collective-permute-start.22 = (bf16[3072,384]{1,0:T(8,128)(2,1)S(1)}, bf16[3072,384]{1,0:T(8,128)(2,1)S(1)}, u32[]{:S(2)}, u32[]{:S(2)}) collective-permute-start(bf16[3072,384]{1,0:T(8,128)(2,1)S(1)} %get-tuple-element.90), channel_id=1, source_target_pairs={{0,16},{16,0},{1,17},{17,1},{2,18},{18,2},{3,19},{19,3},{4,20},{20... | collective-permute-start | bytes 7077896 | tf_op jit(solution)/shard_map/ppermute | solution.py:144
  92.2 11.9 %collective-permute-start.19 = (bf16[2,64,3072]{2,1,0:T(8,128)(2,1)S(1)}, bf16[2,64,3072]{2,1,0:T(8,128)(2,1)S(1)}, u32[]{:S(2)}, u32[]{:S(2)}) collective-permute-start(bf16[2,64,3072]{2,1,0:T(8,128)(2,1)S(1)} %get-tuple-element.77), channel_id=1, source_target_pairs={{0,3},{1,0},{2,1},{3,2},{4,7},{5,4},{6,5},{7,6},{8,11},{9,8},{10,9... | collective-permute-start | bytes 2359304 | tf_op jit(solution)/shard_map/ppermute | solution.py:157
  92.2 12.8 %collective-permute-start.20 = (bf16[2,64,3072]{2,1,0:T(8,128)(2,1)S(1)}, bf16[2,64,3072]{2,1,0:T(8,128)(2,1)S(1)}, u32[]{:S(2)}, u32[]{:S(2)}) collective-permute-start(bf16[2,64,3072]{2,1,0:T(8,128)(2,1)S(1)} %get-tuple-element.78), channel_id=1, source_target_pairs={{0,1},{1,2},{2,3},{3,0},{4,5},{5,6},{6,7},{7,4},{8,9},{9,10},{10,1... | collective-permute-start | bytes 2359304 | tf_op jit(solution)/shard_map/ppermute | solution.py:157
  99.0 12.4 %copy-start.1 = (bf16[384,3072]{1,0:T(8,128)(2,1)}, bf16[384,3072]{1,0:T(8,128)(2,1)S(1)}, u32[]{:S(2)}) copy-start(bf16[384,3072]{1,0:T(8,128)(2,1)S(1)} %get-tuple-element.94) | copy-start | bytes 7077892
  104.0 2.2 %copy-start = (bf16[2,384,3072]{2,1,0:T(8,128)(2,1)}, bf16[2,384,3072]{2,1,0:T(8,128)(2,1)S(1)}, u32[]{:S(2)}) copy-start(bf16[2,384,3072]{2,1,0:T(8,128)(2,1)S(1)} %shard_map.79) | copy-start | bytes 14155780
  105.0 6.4 %copy-start.6 = (bf16[384,3072]{1,0:T(8,128)(2,1)}, bf16[384,3072]{1,0:T(8,128)(2,1)S(1)}, u32[]{:S(2)}) copy-start(bf16[384,3072]{1,0:T(8,128)(2,1)S(1)} %collective-permute-done.21) | copy-start | bytes 7077892
  105.0 6.2 %copy-start.4 = (bf16[3072,384]{1,0:T(8,128)(2,1)}, bf16[3072,384]{1,0:T(8,128)(2,1)S(1)}, u32[]{:S(2)}) copy-start(bf16[3072,384]{1,0:T(8,128)(2,1)S(1)} %collective-permute-done.22) | copy-start | bytes 7077892
  108.1 20.2 %collective-permute-start.24 = (bf16[2,128,3072]{2,1,0:T(8,128)(2,1)}, bf16[2,128,3072]{2,1,0:T(8,128)(2,1)}, u32[]{:S(2)}, u32[]{:S(2)}) collective-permute-start(bf16[2,128,3072]{2,1,0:T(8,128)(2,1)} %pad_maximum_fusion.8), channel_id=1, source_target_pairs={{0,1},{1,2},{2,3},{3,0},{4,5},{5,6},{6,7},{7,4},{8,9},{9,10},{10,1... | collective-permute-start | bytes 4718600 | tf_op jit(solution)/shard_map/ppermute | solution.py:157
  110.6 20.9 %collective-permute-start.23 = (bf16[2,128,3072]{2,1,0:T(8,128)(2,1)}, bf16[2,128,3072]{2,1,0:T(8,128)(2,1)}, u32[]{:S(2)}, u32[]{:S(2)}) collective-permute-start(bf16[2,128,3072]{2,1,0:T(8,128)(2,1)} %pad_maximum_fusion.7), channel_id=1, source_target_pairs={{0,3},{1,0},{2,1},{3,2},{4,7},{5,4},{6,5},{7,6},{8,11},{9,8},{10,9... | collective-permute-start | bytes 4718600 | tf_op jit(solution)/shard_map/ppermute | solution.py:157
  111.3 10.8 %collective-permute-start.26 = (bf16[768,384]{1,0:T(8,128)(2,1)S(1)}, bf16[768,384]{1,0:T(8,128)(2,1)}, u32[]{:S(2)}, u32[]{:S(2)}) collective-permute-start(bf16[768,384]{1,0:T(8,128)(2,1)S(1)} %add_convert_fusion.7), channel_id=1, source_target_pairs={{0,32},{16,112},{32,64},{48,16},{64,96},{80,48},{96,0},{112,80},{1... | collective-permute-start | bytes 1769480 | tf_op jit(solution)/shard_map/ppermute | solution.py:140
  111.6 13.7 %collective-permute-start.25 = (bf16[384,768]{1,0:T(8,128)(2,1)S(1)}, bf16[384,768]{1,0:T(8,128)(2,1)}, u32[]{:S(2)}, u32[]{:S(2)}) collective-permute-start(bf16[384,768]{1,0:T(8,128)(2,1)S(1)} %add_convert_fusion.8), channel_id=1, source_target_pairs={{0,96},{16,48},{32,0},{48,80},{64,32},{80,112},{96,64},{112,16},{1... | collective-permute-start | bytes 1769480 | tf_op jit(solution)/shard_map/ppermute | solution.py:140
  131.5 11.1 %copy-start.7 = (bf16[384,3072]{1,0:T(8,128)(2,1)S(1)}, bf16[384,3072]{1,0:T(8,128)(2,1)}, u32[]{:S(2)}) copy-start(bf16[384,3072]{1,0:T(8,128)(2,1)} %copy-done.6) | copy-start | bytes 7077892
  134.8 4.9 %copy-start.5 = (bf16[3072,384]{1,0:T(8,128)(2,1)S(1)}, bf16[3072,384]{1,0:T(8,128)(2,1)}, u32[]{:S(2)}) copy-start(bf16[3072,384]{1,0:T(8,128)(2,1)} %copy-done.4) | copy-start | bytes 7077892
  134.8 7.8 %copy-start.2 = (bf16[384,3072]{1,0:T(8,128)(2,1)S(1)}, bf16[384,3072]{1,0:T(8,128)(2,1)}, u32[]{:S(2)}) copy-start(bf16[384,3072]{1,0:T(8,128)(2,1)} %copy-done.1) | copy-start | bytes 7077892
  134.9 9.1 %collective-permute-start.27 = (bf16[2,32,3072]{2,1,0:T(8,128)(2,1)S(1)}, bf16[2,32,3072]{2,1,0:T(8,128)(2,1)S(1)}, u32[]{:S(2)}, u32[]{:S(2)}) collective-permute-start(bf16[2,32,3072]{2,1,0:T(8,128)(2,1)S(1)} %get-tuple-element.112), channel_id=1, source_target_pairs={{0,12},{1,13},{2,14},{3,15},{4,0},{5,1},{6,2},{7,3},{8,4},{9,5},{1... | collective-permute-start | bytes 1179656 | tf_op jit(solution)/shard_map/ppermute | solution.py:157
  136.0 11.4 %collective-permute-start.28 = (bf16[2,32,3072]{2,1,0:T(8,128)(2,1)S(1)}, bf16[2,32,3072]{2,1,0:T(8,128)(2,1)S(1)}, u32[]{:S(2)}, u32[]{:S(2)}) collective-permute-start(bf16[2,32,3072]{2,1,0:T(8,128)(2,1)S(1)} %get-tuple-element.113), channel_id=1, source_target_pairs={{0,8},{1,9},{2,10},{3,11},{4,12},{5,13},{6,14},{7,15},{8,0},{9,1},... | collective-permute-start | bytes 1179656 | tf_op jit(solution)/shard_map/ppermute | solution.py:157
  137.8 10.5 %collective-permute-start.29 = (bf16[2,32,3072]{2,1,0:T(8,128)(2,1)S(1)}, bf16[2,32,3072]{2,1,0:T(8,128)(2,1)S(1)}, u32[]{:S(2)}, u32[]{:S(2)}) collective-permute-start(bf16[2,32,3072]{2,1,0:T(8,128)(2,1)S(1)} %get-tuple-element.114), channel_id=1, source_target_pairs={{0,4},{1,5},{2,6},{3,7},{4,8},{5,9},{6,10},{7,11},{8,12},{9,13},{1... | collective-permute-start | bytes 1179656 | tf_op jit(solution)/shard_map/ppermute | solution.py:157
  141.0 23.6 %collective-permute-start.34 = (bf16[768,384]{1,0:T(8,128)(2,1)S(1)}, bf16[768,384]{1,0:T(8,128)(2,1)S(1)}, u32[]{:S(2)}, u32[]{:S(2)}) collective-permute-start(bf16[768,384]{1,0:T(8,128)(2,1)S(1)} %add_convert_fusion.5), channel_id=1, source_target_pairs={{0,32},{16,112},{32,64},{48,16},{64,96},{80,48},{96,0},{112,80},{1... | collective-permute-start | bytes 1769480 | tf_op jit(solution)/shard_map/ppermute | solution.py:140
  144.0 20.7 %collective-permute-start.33 = (bf16[384,768]{1,0:T(8,128)(2,1)S(1)}, bf16[384,768]{1,0:T(8,128)(2,1)S(1)}, u32[]{:S(2)}, u32[]{:S(2)}) collective-permute-start(bf16[384,768]{1,0:T(8,128)(2,1)S(1)} %add_convert_fusion.6), channel_id=1, source_target_pairs={{0,96},{16,48},{32,0},{48,80},{64,32},{80,112},{96,64},{112,16},{1... | collective-permute-start | bytes 1769480 | tf_op jit(solution)/shard_map/ppermute | solution.py:140
  148.6 19.3 %collective-permute-start.32 = (bf16[2,32,768]{2,1,0:T(8,128)(2,1)S(1)}, bf16[2,32,768]{2,1,0:T(8,128)(2,1)S(1)}, u32[]{:S(2)}, u32[]{:S(2)}) collective-permute-start(bf16[2,32,768]{2,1,0:T(8,128)(2,1)S(1)} %pad_maximum_fusion.14), channel_id=1, source_target_pairs={{0,32},{16,112},{32,64},{48,16},{64,96},{80,48},{96,0},{112,80},{1... | collective-permute-start | bytes 294920 | tf_op jit(solution)/shard_map/ppermute | solution.py:140
  150.2 14.4 %collective-permute-start.31 = (bf16[2,32,768]{2,1,0:T(8,128)(2,1)S(1)}, bf16[2,32,768]{2,1,0:T(8,128)(2,1)S(1)}, u32[]{:S(2)}, u32[]{:S(2)}) collective-permute-start(bf16[2,32,768]{2,1,0:T(8,128)(2,1)S(1)} %pad_maximum_fusion.13), channel_id=1, source_target_pairs={{0,64},{16,80},{32,96},{48,112},{64,0},{80,16},{96,32},{112,48},{1... | collective-permute-start | bytes 294920 | tf_op jit(solution)/shard_map/ppermute | solution.py:140
  150.5 14.1 %collective-permute-start.30 = (bf16[2,32,768]{2,1,0:T(8,128)(2,1)S(1)}, bf16[2,32,768]{2,1,0:T(8,128)(2,1)S(1)}, u32[]{:S(2)}, u32[]{:S(2)}) collective-permute-start(bf16[2,32,768]{2,1,0:T(8,128)(2,1)S(1)} %pad_maximum_fusion.12), channel_id=1, source_target_pairs={{0,96},{16,48},{32,0},{48,80},{64,32},{80,112},{96,64},{112,16},{1... | collective-permute-start | bytes 294920 | tf_op jit(solution)/shard_map/ppermute | solution.py:140
  164.9 16.4 %collective-permute-start.36 = (bf16[384,768]{1,0:T(8,128)(2,1)S(1)}, bf16[384,768]{1,0:T(8,128)(2,1)S(1)}, u32[]{:S(2)}, u32[]{:S(2)}) collective-permute-start(bf16[384,768]{1,0:T(8,128)(2,1)S(1)} %add_convert_fusion.3), channel_id=1, source_target_pairs={{0,96},{16,48},{32,0},{48,80},{64,32},{80,112},{96,64},{112,16},{1... | collective-permute-start | bytes 1769480 | tf_op jit(solution)/shard_map/ppermute | solution.py:140
  165.2 17.3 %collective-permute-start.35 = (bf16[768,384]{1,0:T(8,128)(2,1)S(1)}, bf16[768,384]{1,0:T(8,128)(2,1)S(1)}, u32[]{:S(2)}, u32[]{:S(2)}) collective-permute-start(bf16[768,384]{1,0:T(8,128)(2,1)S(1)} %add_convert_fusion.4), channel_id=1, source_target_pairs={{0,32},{16,112},{32,64},{48,16},{64,96},{80,48},{96,0},{112,80},{1... | collective-permute-start | bytes 1769480 | tf_op jit(solution)/shard_map/ppermute | solution.py:140

commit v4 on v3

--- a/solution.py
+++ b/solution.py
@@ -109,8 +109,8 @@
             up_part = product(refs[i][0], refs[2 * count + i][...], 0, 0)
             down_sum = down_part if i == 0 else down_sum + down_part
             up_sum = up_part if i == 0 else up_sum + up_part
-        down_ref[...] = down_sum.astype(BF)
-        up_ref[...] = up_sum.astype(BF)
+        down_ref[0] = down_sum.astype(BF)
+        up_ref[0] = up_sum.astype(BF)
 
     halves = [pl.BlockSpec((a.shape[0], units), lambda i: (0, core)) for a in acts]
     return local_kernel(
@@ -118,12 +118,12 @@
         (4,),
         [pl.BlockSpec((2, s.shape[1], tile), lambda i: (0, 0, i)) for s in sets] + halves + halves,
         [
-            pl.BlockSpec((units, tile), lambda i: (0, i)),
-            pl.BlockSpec((tile, units), lambda i: (i, 0)),
+            pl.BlockSpec((1, units, tile), lambda i: (i, 0, 0)),
+            pl.BlockSpec((1, tile, units), lambda i: (i, 0, 0)),
         ],
         [
-            jax.ShapeDtypeStruct((units, features), BF),
-            jax.ShapeDtypeStruct((features, units), BF),
+            jax.ShapeDtypeStruct((4, units, tile), BF),
+            jax.ShapeDtypeStruct((4, tile, units), BF),
         ],
         *sets,
         *acts,
@@ -204,10 +204,12 @@
     up_early = across(join(ups[:2], 0))
     left, right = plane(first, 1, 1), plane(first, 1, -1)
     step()
-    left, right, up_early, ups[3], downs[3] = held(left, right, up_early, ups[3], downs[3])
-    (down_mine,) = held(join(downs, 1))
-    up_late, down_theirs = across(join(ups[2:], 0)), across(down_mine)
+    up_last, down_last = across(ups[3]), across(downs[3])
+    left, right, up_early, up_last, down_last, ups[3], downs[3] = held(
+        left, right, up_early, up_last, down_last, ups[3], downs[3]
+    )
     far = [plane(left[:, :half], 1, 1), plane(right[:, half:], 1, -1)]
+    up_other, down_early = across(ups[2]), across(join(downs[:3], 1))
 
     def rows_of(value, k):
         return lax.slice_in_dim(value, k * width, (k + 1) * width, axis=0)
@@ -215,11 +217,11 @@
     def columns(value, k):
         return lax.slice_in_dim(value, k * width, (k + 1) * width, axis=1)
 
-    up = held(
-        join(ups, 0),
-        join([rows_of(up_early, 0), rows_of(up_late, 1), rows_of(up_late, 0), rows_of(up_early, 1)], 0),
-    )
-    down = held(down_mine, join([columns(down_theirs, k) for k in turned], 1))
+    up = held(join(ups, 0), join([rows_of(up_early, 0), up_last, up_other, rows_of(up_early, 1)], 0))
+    down = held(
+        join(downs, 1),
+        join([columns(down_early, 0), down_last, columns(down_early, 2), columns(down_early, 1)], 1),
+    )
     up, down = held(join(up, 1), join(down, 0))
 
     near = join([first, left, right], 1)
@@ -234,16 +236,12 @@
         *far_back, near_acts, near_grads, far_acts, far_grads
     )
     far_back = [plane(far_back[0], 1, -1), plane(far_back[1], 1, 1)]
+    near_sums = backward(near_acts, near_grads, up, down)
+    near_acts, near_grads, near_sums = held(near_acts, near_grads, near_sums)
     sets, acts, grads = (near, far), (near_acts, far_acts), (near_grads, far_grads)
     theirs = weight_sums(sets, acts, grads, 1)
-    near_acts, near_grads, *theirs = held(near_acts, near_grads, *theirs)
-    down_theirs, up_theirs = (across(value) for value in theirs)
-    near_sums = backward(near_acts, near_grads, up, down)
-    acts, grads = (near_acts, far_acts), (near_grads, far_grads)
-    down_mine, up_mine = weight_sums(sets, acts, grads, 0)
-    *far_back, near_sums, down_mine, up_mine, down_theirs, up_theirs = held(
-        *far_back, near_sums, down_mine, up_mine, down_theirs, up_theirs
-    )
+    *far_back, near_sums, down_other, up_other = held(*far_back, near_sums, *theirs)
+    mine = weight_sums(sets, acts, grads, 0)
 
     def total(*parts):
         value = parts[0].astype(F32)
@@ -256,24 +254,30 @@
     right = join([right[:, :half], total(right[:, half:], far_back[1]).astype(BF)], 1)
     left, right = plane(left, 1, -1), plane(right, 1, 1)
 
-    def down_part(k, *more):
-        return total(columns(down_mine, k), columns(down_theirs, turned[k]), *more)
-
-    def up_part(k, *more):
-        return total(rows_of(up_mine, k), rows_of(up_theirs, turned[k]), *more)
-
-    down_grad = along_x(down_part(1).astype(BF), -1)
-    up_grad = along_x(up_part(1).astype(BF), 1)
+    def swap(k, round_value):
+        down_sum, up_sum, _ = held(down_other[turned[k]], up_other[turned[k]], round_value)
+        return across(down_sum), across(up_sum)
+
+    down_theirs, up_theirs = swap(1, near_sums)
+    down_grad = along_x(total(mine[0][1], down_theirs).astype(BF), -1)
+    up_grad = along_x(total(mine[1][1], up_theirs).astype(BF), 1)
+
     left, right, down_grad, up_grad = held(left, right, down_grad, up_grad)
 
-    down_grad = along_x(down_part(2, down_grad).astype(BF), -1)
-    up_grad = along_x(up_part(2, up_grad).astype(BF), 1)
+    down_theirs, up_theirs = swap(2, left)
+    down_grad = along_x(total(mine[0][2], down_theirs, down_grad).astype(BF), -1)
+    up_grad = along_x(total(mine[1][2], up_theirs, up_grad).astype(BF), 1)
     sums = total(here, left, right).astype(BF).reshape(2, 4, sub, 4 * width)
     end = total(sums[:, 0], *(plane(sums[:, hop], 0, -hop) for hop in (1, 2, 3))).astype(BF)
-    down_grad, up_grad, _ = held(down_grad, up_grad, end)
-    down_grad = along_x(down_part(3, down_grad).astype(BF), -1)
-    up_grad = along_x(up_part(3, up_grad).astype(BF), 1)
-    down_grad, up_grad = down_part(0, down_grad), up_part(0, up_grad)
+
+    end, down_grad, up_grad = held(end, down_grad, up_grad)
+
+    down_theirs, up_theirs = swap(3, end)
+    down_grad = along_x(total(mine[0][3], down_theirs, down_grad).astype(BF), -1)
+    up_grad = along_x(total(mine[1][3], up_theirs, up_grad).astype(BF), 1)
+    down_theirs, up_theirs = swap(0, end)
+    down_grad = total(mine[0][0], down_theirs, down_grad)
+    up_grad = total(mine[1][0], up_theirs, up_grad)
 
     out = jnp.zeros((2, rows, width), BF)
     for k in range(4):

time: 184 us -> 188 us (1.022)
  the two profiles are of different devices: /device:TPU:41 before, /device:TPU:0 now
where the time goes in v4:
time: 188 us
  waiting for transfers between devices  85.3 us (45%)
  starting transfers between devices  52.9 us (28%)
  Pallas kernels  26.6 us (14%)
  other arithmetic  17.4 us (9%)
  local copies, waits for them, and re-layouts  4.79 us (3%)
    ppermute x18, waiting for transfers between devices, along_x(): return lax.ppermute(value, ('row', 'col'), pairs)  70.5 us
    pallas_call x6, Pallas kernels, local_kernel(): pl.pallas_call(body, grid=grid, in_specs=in_specs, out_specs=out_specs, o...  26.6 us
    ppermute x18, starting transfers between devices, along_x(): return lax.ppermute(value, ('row', 'col'), pairs)  25.3 us
    ppermute x14, starting transfers between devices, plane(): return lax.ppermute(value, ('col', 'depth'), pairs)  23.6 us
    ppermute x14, waiting for transfers between devices, plane(): return lax.ppermute(value, ('col', 'depth'), pairs)  12.7 us
    concatenate x11, other arithmetic, join(): return jnp.concatenate(parts, axis=axis)  4.66 us
    ppermute x13, starting transfers between devices, across(): return lax.ppermute(value, 'col', [(0, 1), (1, 0)])  3.95 us
  transfers between devices with their start and end apart: 45, of which 20 were waited for; matrix products, arithmetic and copies ran while one was open for 9% of the time, Pallas kernels for 11%

profile of v4, /device:TPU:0, one launch (start us, length us, event | category | flops | bytes accessed | tf_op | source)
XLA Modules:
  0.0 188.1 jit_solution(9524309035280249658)
XLA Ops:
  1.7 1.6 collective-permute-start
  3.4 2.7 %collective-permute-start.1 = (bf16[2,32,768]{2,1,0:T(8,128)(2,1)S(1)}, bf16[2,32,768]{2,1,0:T(8,128)(2,1)S(1)}, u32[]{:S(2)}, u32[]{:S(2)}) collective-permute-start(bf16[2,32,768]{2,1,0:T(8,128)(2,1)S(1)} %get-tuple-element.150), channel_id=1, source_target_pairs={{0,64},{16,80},{32,96},{48,112},{64,0},{80,16},{96,32},{112,48},{1... | collective-permute-start | bytes 294920 | tf_op jit(solution)/shard_map/ppermute | solution.py:140
  6.1 1.4 collective-permute-start.2
  8.1 2.6 %collective-permute-start.9 = (bf16[384,768]{1,0:T(8,128)(2,1)}, bf16[384,768]{1,0:T(8,128)(2,1)S(1)}, u32[]{:S(2)}, u32[]{:S(2)}) collective-permute-start(bf16[384,768]{1,0:T(8,128)(2,1)} %param.6), channel_id=1, source_target_pairs={{0,96},{16,48},{32,0},{48,80},{64,32},{80,112},{96,64},{112,16},{1... | collective-permute-start | bytes 1769480 | tf_op jit(solution)/shard_map/ppermute | solution.py:140
  12.0 2.0 %collective-permute-start.3 = (bf16[2,32,3072]{2,1,0:T(8,128)(2,1)S(1)}, bf16[2,32,3072]{2,1,0:T(8,128)(2,1)S(1)}, u32[]{:S(2)}, u32[]{:S(2)}) collective-permute-start(bf16[2,32,3072]{2,1,0:T(8,128)(2,1)S(1)} %get-tuple-element.147), channel_id=1, source_target_pairs={{0,4},{1,5},{2,6},{3,7},{4,8},{5,9},{6,10},{7,11},{8,12},{9,13},{1... | collective-permute-start | bytes 1179656 | tf_op jit(solution)/shard_map/ppermute | solution.py:157
  13.9 3.6 %collective-permute-start.4 = (bf16[2,32,3072]{2,1,0:T(8,128)(2,1)S(1)}, bf16[2,32,3072]{2,1,0:T(8,128)(2,1)S(1)}, u32[]{:S(2)}, u32[]{:S(2)}) collective-permute-start(bf16[2,32,3072]{2,1,0:T(8,128)(2,1)S(1)} %get-tuple-element.147), channel_id=1, source_target_pairs={{0,8},{1,9},{2,10},{3,11},{4,12},{5,13},{6,14},{7,15},{8,0},{9,1},... | collective-permute-start | bytes 1179656 | tf_op jit(solution)/shard_map/ppermute | solution.py:157
  18.5 5.6 %collective-permute-done.8 = bf16[768,384]{1,0:T(8,128)(2,1)S(1)} collective-permute-done((bf16[768,384]{1,0:T(8,128)(2,1)}, bf16[768,384]{1,0:T(8,128)(2,1)S(1)}, u32[]{:S(2)}, u32[]{:S(2)}) %collective-permute-start.8) | collective-permute-done | bytes 589856 | tf_op jit(solution)/shard_map/ppermute | solution.py:140
  24.2 3.2 %collective-permute-start.12 = (bf16[384,768]{1,0:T(8,128)(2,1)S(1)}, bf16[384,768]{1,0:T(8,128)(2,1)S(1)}, u32[]{:S(2)}, u32[]{:S(2)}) collective-permute-start(bf16[384,768]{1,0:T(8,128)(2,1)S(1)} %collective-permute-done.9), channel_id=1, source_target_pairs={{0,96},{16,48},{32,0},{48,80},{64,32},{80,112},{96,64},{112,16},{1... | collective-permute-start | bytes 1769480 | tf_op jit(solution)/shard_map/ppermute | solution.py:140
  27.6 1.6 collective-permute-start.6
  29.3 1.7 collective-permute-start.7
  31.1 10.2 %collective-permute-done.11 = bf16[768,384]{1,0:T(8,128)(2,1)S(1)} collective-permute-done((bf16[768,384]{1,0:T(8,128)(2,1)S(1)}, bf16[768,384]{1,0:T(8,128)(2,1)S(1)}, u32[]{:S(2)}, u32[]{:S(2)}) %collective-permute-start.11) | collective-permute-done | bytes 589856 | tf_op jit(solution)/shard_map/ppermute | solution.py:140
  41.4 3.2 %collective-permute-start.15 = (bf16[384,768]{1,0:T(8,128)(2,1)S(1)}, bf16[384,768]{1,0:T(8,128)(2,1)S(1)}, u32[]{:S(2)}, u32[]{:S(2)}) collective-permute-start(bf16[384,768]{1,0:T(8,128)(2,1)S(1)} %collective-permute-done.12), channel_id=1, source_target_pairs={{0,96},{16,48},{32,0},{48,80},{64,32},{80,112},{96,64},{112,16},{1... | collective-permute-start | bytes 1769480 | tf_op jit(solution)/shard_map/ppermute | solution.py:140
  44.7 13.0 %collective-permute-done.13 = bf16[768,384]{1,0:T(8,128)(2,1)S(1)} collective-permute-done((bf16[768,384]{1,0:T(8,128)(2,1)S(1)}, bf16[768,384]{1,0:T(8,128)(2,1)S(1)}, u32[]{:S(2)}, u32[]{:S(2)}) %collective-permute-start.13) | collective-permute-done | bytes 589856 | tf_op jit(solution)/shard_map/ppermute | solution.py:140
  61.7 1.6 collective-permute-start.17
  63.4 1.9 %collective-permute-start.18 = (bf16[2,64,3072]{2,1,0:T(8,128)(2,1)S(1)}, bf16[2,64,3072]{2,1,0:T(8,128)(2,1)S(1)}, u32[]{:S(2)}, u32[]{:S(2)}) collective-permute-start(bf16[2,64,3072]{2,1,0:T(8,128)(2,1)S(1)} %slice.185), channel_id=1, source_target_pairs={{0,3},{1,0},{2,1},{3,2},{4,7},{5,4},{6,5},{7,6},{8,11},{9,8},{10,9... | collective-permute-start | bytes 2359304 | tf_op jit(solution)/shard_map/ppermute | solution.py:157
  67.0 4.9 %shard_map.75 = (bf16[384,768]{1,0:T(8,128)(2,1)S(1)}, bf16[384,768]{1,0:T(8,128)(2,1)S(1)}) custom-call(bf16[2,384,3072]{2,1,0:T(8,128)(2,1)S(1)} %constant_dynamic-update-slice_fusion.pair_ref.refs_0_, bf16[3072,768]{1,0:T(8,128)(2,1)S(1)} %pad_maximum_fusion.up_ref, bf16[768,3072]{1,0:T(8,128)(2,1)S(1)} %pad_maximum_fusion.1.down_ref), custom_call_target="tpu_custom_call" | custom-call | flops 1 | bytes 1 | tf_op jit(solution)/shard_map/pallas_call | solution.py:30
  71.9 3.1 %collective-permute-done.17 = bf16[2,64,3072]{2,1,0:T(8,128)(2,1)S(1)} collective-permute-done((bf16[2,64,3072]{2,1,0:T(8,128)(2,1)S(1)}, bf16[2,64,3072]{2,1,0:T(8,128)(2,1)S(1)}, u32[]{:S(2)}, u32[]{:S(2)}) %collective-permute-start.17) | collective-permute-done | bytes 786464 | tf_op jit(solution)/shard_map/ppermute | solution.py:157
  75.8 3.0 %shard_map.76 = (bf16[128,768]{1,0:T(8,128)(2,1)S(1)}, bf16[128,768]{1,0:T(8,128)(2,1)S(1)}) custom-call(bf16[2,128,3072]{2,1,0:T(8,128)(2,1)S(1)} %constant_dynamic-update-slice_fusion.6.pair_ref.refs_1_, bf16[3072,768]{1,0:T(8,128)(2,1)S(1)} %pad_maximum_fusion.up_ref, bf16[768,3072]{1,0:T(8,128)(2,1)S(1)} %pad_maximum_fusion.1.down_ref), custom_call_target="tpu_custom_call" | custom-call | flops 1 | bytes 1 | tf_op jit(solution)/shard_map/pallas_call | solution.py:30
  78.8 3.1 %shard_map.77 = bf16[2,128,3072]{2,1,0:T(8,128)(2,1)S(1)} custom-call(bf16[128,768]{1,0:T(8,128)(2,1)S(1)} %get-tuple-element.93.act_ref.refs_3_, bf16[128,768]{1,0:T(8,128)(2,1)S(1)} %get-tuple-element.95.grad_ref.refs_5_, bf16[3072,768]{1,0:T(8,128)(2,1)S(1)} %pad_maximum_fusion.up_ref, bf16[768,3072]{1,0:T(8,128)(2,1)S(1)} %pad_maximum_fusion.1.down_ref), custom_call_target="tpu_custom_call" | custom-call | flops 1 | bytes 1 | tf_op jit(solution)/shard_map/pallas_call | solution.py:30
  82.0 2.9 %collective-permute-start.21 = (bf16[2,64,3072]{2,1,0:T(8,128)(2,1)S(1)}, bf16[2,64,3072]{2,1,0:T(8,128)(2,1)S(1)}, u32[]{:S(2)}, u32[]{:S(2)}) collective-permute-start(bf16[2,64,3072]{2,1,0:T(8,128)(2,1)S(1)} %get-tuple-element.87), channel_id=1, source_target_pairs={{0,3},{1,0},{2,1},{3,2},{4,7},{5,4},{6,5},{7,6},{8,11},{9,8},{10,9... | collective-permute-start | bytes 2359304 | tf_op jit(solution)/shard_map/ppermute | solution.py:157
  84.9 5.0 %shard_map.78 = bf16[2,384,3072]{2,1,0:T(8,128)(2,1)S(1)} custom-call(bf16[384,768]{1,0:T(8,128)(2,1)S(1)} %get-tuple-element.92.act_ref.refs_2_, bf16[384,768]{1,0:T(8,128)(2,1)S(1)} %get-tuple-element.94.grad_ref.refs_4_, bf16[3072,768]{1,0:T(8,128)(2,1)S(1)} %pad_maximum_fusion.up_ref, bf16[768,3072]{1,0:T(8,128)(2,1)S(1)} %pad_maximum_fusion.1.down_ref), custom_call_target="tpu_custom_call" | custom-call | flops 1 | bytes 1 | tf_op jit(solution)/shard_map/pallas_call | solution.py:30
  89.9 5.3 %shard_map.79 = (bf16[4,384,768]{2,1,0:T(8,128)(2,1)S(1)}, bf16[4,768,384]{2,1,0:T(8,128)(2,1)S(1)}) custom-call(bf16[2,384,3072]{2,1,0:T(8,128)(2,1)S(1)} %constant_dynamic-update-slice_fusion.pair_ref.refs_0_, bf16[2,128,3072]{2,1,0:T(8,128)(2,1)S(1)} %constant_dynamic-update-slice_fusion.6.pair_ref.refs_1_, ...), custom_call_target="tpu_custom_call" | custom-call | flops 1 | bytes 1 | tf_op jit(solution)/shard_map/pallas_call | solution.py:30
  95.2 2.9 %collective-permute-done.22 = bf16[2,64,3072]{2,1,0:T(8,128)(2,1)S(1)} collective-permute-done((bf16[2,64,3072]{2,1,0:T(8,128)(2,1)S(1)}, bf16[2,64,3072]{2,1,0:T(8,128)(2,1)S(1)}, u32[]{:S(2)}, u32[]{:S(2)}) %collective-permute-start.22) | collective-permute-done | bytes 786464 | tf_op jit(solution)/shard_map/ppermute | solution.py:157
  98.1 1.2 slice_bitcast_fusion.2
  99.4 1.2 slice_bitcast_fusion.3
  101.4 1.3 pad_maximum_fusion.9
  102.7 1.3 pad_maximum_fusion.8
  103.9 3.2 %collective-permute-start.23 = (bf16[2,128,3072]{2,1,0:T(8,128)(2,1)}, bf16[2,128,3072]{2,1,0:T(8,128)(2,1)}, u32[]{:S(2)}, u32[]{:S(2)}) collective-permute-start(bf16[2,128,3072]{2,1,0:T(8,128)(2,1)} %pad_maximum_fusion.8), channel_id=1, source_target_pairs={{0,3},{1,0},{2,1},{3,2},{4,7},{5,4},{6,5},{7,6},{8,11},{9,8},{10,9... | collective-permute-start | bytes 4718600 | tf_op jit(solution)/shard_map/ppermute | solution.py:157
  108.2 5.3 %shard_map.80 = (bf16[4,384,768]{2,1,0:T(8,128)(2,1)S(1)}, bf16[4,768,384]{2,1,0:T(8,128)(2,1)S(1)}) custom-call(bf16[2,384,3072]{2,1,0:T(8,128)(2,1)S(1)} %constant_dynamic-update-slice_fusion.pair_ref.refs_0_, bf16[2,128,3072]{2,1,0:T(8,128)(2,1)S(1)} %constant_dynamic-update-slice_fusion.6.pair_ref.refs_1_, ...), custom_call_target="tpu_custom_call" | custom-call | flops 1 | bytes 1 | tf_op jit(solution)/shard_map/pallas_call | solution.py:30
  113.5 1.2 fusion.10
  116.0 2.9 %collective-permute-start.26 = (bf16[384,768]{1,0:T(8,128)(2,1)}, bf16[384,768]{1,0:T(8,128)(2,1)}, u32[]{:S(2)}, u32[]{:S(2)}) collective-permute-start(bf16[384,768]{1,0:T(8,128)(2,1)} %fusion.11), channel_id=1, source_target_pairs={{0,96},{16,48},{32,0},{48,80},{64,32},{80,112},{96,64},{112,16},{1... | collective-permute-start | bytes 1769480 | tf_op jit(solution)/shard_map/ppermute | solution.py:140
  118.9 13.2 %collective-permute-done.28 = bf16[768,384]{1,0:T(8,128)(2,1)} collective-permute-done((bf16[768,384]{1,0:T(8,128)(2,1)}, bf16[768,384]{1,0:T(8,128)(2,1)}, u32[]{:S(2)}, u32[]{:S(2)}) %collective-permute-start.28) | collective-permute-done | bytes 589856 | tf_op jit(solution)/shard_map/ppermute | solution.py:140
  132.6 3.1 %add_convert_fusion = bf16[2,128,3072]{2,1,0:T(8,128)(2,1)S(1)} fusion(bf16[2,128,3072]{2,1,0:T(8,128)(2,1)} %collective-permute-done.24, bf16[2,128,3072]{2,1,0:T(8,128)(2,1)} %collective-permute-done.23, bf16[2,384,3072]{2,1,0:T(8,128)(2,1)} %copy-done), kind=kLoop, calls=%fused_computation.2 | loop fusion | flops 4718592 | bytes 6291456 | tf_op jit(solution)/shard_map/convert_element_type | solution.py:270
  135.9 2.7 %collective-permute-start.29 = (bf16[2,32,3072]{2,1,0:T(8,128)(2,1)S(1)}, bf16[2,32,3072]{2,1,0:T(8,128)(2,1)S(1)}, u32[]{:S(2)}, u32[]{:S(2)}) collective-permute-start(bf16[2,32,3072]{2,1,0:T(8,128)(2,1)S(1)} %get-tuple-element.135), channel_id=1, source_target_pairs={{0,12},{1,13},{2,14},{3,15},{4,0},{5,1},{6,2},{7,3},{8,4},{9,5},{1... | collective-permute-start | bytes 1179656 | tf_op jit(solution)/shard_map/ppermute | solution.py:157
  138.6 1.3 collective-permute-start.31
  139.9 1.3 fusion.7
  141.3 1.4 fusion.9
  142.7 3.2 %collective-permute-start.33 = (bf16[384,768]{1,0:T(8,128)(2,1)S(1)}, bf16[384,768]{1,0:T(8,128)(2,1)S(1)}, u32[]{:S(2)}, u32[]{:S(2)}) collective-permute-start(bf16[384,768]{1,0:T(8,128)(2,1)S(1)} %fusion.9), channel_id=1, source_target_pairs={{0,96},{16,48},{32,0},{48,80},{64,32},{80,112},{96,64},{112,16},{1... | collective-permute-start | bytes 1769480 | tf_op jit(solution)/shard_map/ppermute | solution.py:140
  145.9 2.3 %collective-permute-done.29 = bf16[2,32,3072]{2,1,0:T(8,128)(2,1)S(1)} collective-permute-done((bf16[2,32,3072]{2,1,0:T(8,128)(2,1)S(1)}, bf16[2,32,3072]{2,1,0:T(8,128)(2,1)S(1)}, u32[]{:S(2)}, u32[]{:S(2)}) %collective-permute-start.29) | collective-permute-done | bytes 393248 | tf_op jit(solution)/shard_map/ppermute | solution.py:157
  148.2 3.7 %collective-permute-done.31 = bf16[2,32,3072]{2,1,0:T(8,128)(2,1)S(1)} collective-permute-done((bf16[2,32,3072]{2,1,0:T(8,128)(2,1)S(1)}, bf16[2,32,3072]{2,1,0:T(8,128)(2,1)S(1)}, u32[]{:S(2)}, u32[]{:S(2)}) %collective-permute-start.31) | collective-permute-done | bytes 393248 | tf_op jit(solution)/shard_map/ppermute | solution.py:157
  152.0 4.8 %collective-permute-done.35 = bf16[768,384]{1,0:T(8,128)(2,1)S(1)} collective-permute-done((bf16[768,384]{1,0:T(8,128)(2,1)S(1)}, bf16[768,384]{1,0:T(8,128)(2,1)S(1)}, u32[]{:S(2)}, u32[]{:S(2)}) %collective-permute-start.35) | collective-permute-done | bytes 589856 | tf_op jit(solution)/shard_map/ppermute | solution.py:140
  158.3 4.4 %collective-permute-done.36 = bf16[2,32,768]{2,1,0:T(8,128)(2,1)S(1)} collective-permute-done((bf16[2,32,768]{2,1,0:T(8,128)(2,1)S(1)}, bf16[2,32,768]{2,1,0:T(8,128)(2,1)S(1)}, u32[]{:S(2)}, u32[]{:S(2)}) %collective-permute-start.36) | collective-permute-done | bytes 98336 | tf_op jit(solution)/shard_map/ppermute | solution.py:140
  162.8 6.2 %collective-permute-done.37 = bf16[2,32,768]{2,1,0:T(8,128)(2,1)S(1)} collective-permute-done((bf16[2,32,768]{2,1,0:T(8,128)(2,1)S(1)}, bf16[2,32,768]{2,1,0:T(8,128)(2,1)S(1)}, u32[]{:S(2)}, u32[]{:S(2)}) %collective-permute-start.37) | collective-permute-done | bytes 98336 | tf_op jit(solution)/shard_map/ppermute | solution.py:140
  169.5 3.1 %collective-permute-start.44 = (bf16[384,768]{1,0:T(8,128)(2,1)S(1)}, bf16[384,768]{1,0:T(8,128)(2,1)S(1)}, u32[]{:S(2)}, u32[]{:S(2)}) collective-permute-start(bf16[384,768]{1,0:T(8,128)(2,1)S(1)} %fusion.1), channel_id=1, source_target_pairs={{0,96},{16,48},{32,0},{48,80},{64,32},{80,112},{96,64},{112,16},{1... | collective-permute-start | bytes 1769480 | tf_op jit(solution)/shard_map/ppermute | solution.py:140
  172.9 3.1 %collective-permute-done.38 = bf16[2,32,768]{2,1,0:T(8,128)(2,1)S(1)} collective-permute-done((bf16[2,32,768]{2,1,0:T(8,128)(2,1)S(1)}, bf16[2,32,768]{2,1,0:T(8,128)(2,1)S(1)}, u32[]{:S(2)}, u32[]{:S(2)}) %collective-permute-start.38) | collective-permute-done | bytes 98336 | tf_op jit(solution)/shard_map/ppermute | solution.py:140
  176.8 8.9 %collective-permute-done.44 = bf16[384,768]{1,0:T(8,128)(2,1)S(1)} collective-permute-done((bf16[384,768]{1,0:T(8,128)(2,1)S(1)}, bf16[384,768]{1,0:T(8,128)(2,1)S(1)}, u32[]{:S(2)}, u32[]{:S(2)}) %collective-permute-start.44) | collective-permute-done | bytes 589856 | tf_op jit(solution)/shard_map/ppermute | solution.py:140
  185.7 1.2 fusion.2
  186.9 1.2 fusion.5
  (119 shorter events, 17.9 us)
Async XLA Ops:
  1.7 9.1 %collective-permute-start = (bf16[2,32,768]{2,1,0:T(8,128)(2,1)S(1)}, bf16[2,32,768]{2,1,0:T(8,128)(2,1)S(1)}, u32[]{:S(2)}, u32[]{:S(2)}) collective-permute-start(bf16[2,32,768]{2,1,0:T(8,128)(2,1)S(1)} %get-tuple-element.149), channel_id=1, source_target_pairs={{0,32},{16,112},{32,64},{48,16},{64,96},{80,48},{96,0},{112,80},{1... | collective-permute-start | bytes 294920 | tf_op jit(solution)/shard_map/ppermute | solution.py:140
  3.4 7.9 %collective-permute-start.1 = (bf16[2,32,768]{2,1,0:T(8,128)(2,1)S(1)}, bf16[2,32,768]{2,1,0:T(8,128)(2,1)S(1)}, u32[]{:S(2)}, u32[]{:S(2)}) collective-permute-start(bf16[2,32,768]{2,1,0:T(8,128)(2,1)S(1)} %get-tuple-element.150), channel_id=1, source_target_pairs={{0,64},{16,80},{32,96},{48,112},{64,0},{80,16},{96,32},{112,48},{1... | collective-permute-start | bytes 294920 | tf_op jit(solution)/shard_map/ppermute | solution.py:140
  6.1 5.7 %collective-permute-start.2 = (bf16[2,32,768]{2,1,0:T(8,128)(2,1)S(1)}, bf16[2,32,768]{2,1,0:T(8,128)(2,1)S(1)}, u32[]{:S(2)}, u32[]{:S(2)}) collective-permute-start(bf16[2,32,768]{2,1,0:T(8,128)(2,1)S(1)} %get-tuple-element.151), channel_id=1, source_target_pairs={{0,96},{16,48},{32,0},{48,80},{64,32},{80,112},{96,64},{112,16},{1... | collective-permute-start | bytes 294920 | tf_op jit(solution)/shard_map/ppermute | solution.py:140
  7.5 16.6 %collective-permute-start.8 = (bf16[768,384]{1,0:T(8,128)(2,1)}, bf16[768,384]{1,0:T(8,128)(2,1)S(1)}, u32[]{:S(2)}, u32[]{:S(2)}) collective-permute-start(bf16[768,384]{1,0:T(8,128)(2,1)} %param.5), channel_id=1, source_target_pairs={{0,32},{16,112},{32,64},{48,16},{64,96},{80,48},{96,0},{112,80},{1... | collective-permute-start | bytes 1769480 | tf_op jit(solution)/shard_map/ppermute | solution.py:140
  8.1 16.1 %collective-permute-start.9 = (bf16[384,768]{1,0:T(8,128)(2,1)}, bf16[384,768]{1,0:T(8,128)(2,1)S(1)}, u32[]{:S(2)}, u32[]{:S(2)}) collective-permute-start(bf16[384,768]{1,0:T(8,128)(2,1)} %param.6), channel_id=1, source_target_pairs={{0,96},{16,48},{32,0},{48,80},{64,32},{80,112},{96,64},{112,16},{1... | collective-permute-start | bytes 1769480 | tf_op jit(solution)/shard_map/ppermute | solution.py:140
  11.9 19.1 %copy-start.4 = (bf16[768,384]{1,0:T(8,128)(2,1)S(1)}, bf16[768,384]{1,0:T(8,128)(2,1)}, u32[]{:S(2)}) copy-start(bf16[768,384]{1,0:T(8,128)(2,1)} %param.5) | copy-start | bytes 1769476
  12.0 15.4 %collective-permute-start.3 = (bf16[2,32,3072]{2,1,0:T(8,128)(2,1)S(1)}, bf16[2,32,3072]{2,1,0:T(8,128)(2,1)S(1)}, u32[]{:S(2)}, u32[]{:S(2)}) collective-permute-start(bf16[2,32,3072]{2,1,0:T(8,128)(2,1)S(1)} %get-tuple-element.147), channel_id=1, source_target_pairs={{0,4},{1,5},{2,6},{3,7},{4,8},{5,9},{6,10},{7,11},{8,12},{9,13},{1... | collective-permute-start | bytes 1179656 | tf_op jit(solution)/shard_map/ppermute | solution.py:157
  13.9 13.5 %collective-permute-start.4 = (bf16[2,32,3072]{2,1,0:T(8,128)(2,1)S(1)}, bf16[2,32,3072]{2,1,0:T(8,128)(2,1)S(1)}, u32[]{:S(2)}, u32[]{:S(2)}) collective-permute-start(bf16[2,32,3072]{2,1,0:T(8,128)(2,1)S(1)} %get-tuple-element.147), channel_id=1, source_target_pairs={{0,8},{1,9},{2,10},{3,11},{4,12},{5,13},{6,14},{7,15},{8,0},{9,1},... | collective-permute-start | bytes 1179656 | tf_op jit(solution)/shard_map/ppermute | solution.py:157
  17.5 10.0 %collective-permute-start.5 = (bf16[2,32,3072]{2,1,0:T(8,128)(2,1)S(1)}, bf16[2,32,3072]{2,1,0:T(8,128)(2,1)S(1)}, u32[]{:S(2)}, u32[]{:S(2)}) collective-permute-start(bf16[2,32,3072]{2,1,0:T(8,128)(2,1)S(1)} %get-tuple-element.147), channel_id=1, source_target_pairs={{0,12},{1,13},{2,14},{3,15},{4,0},{5,1},{6,2},{7,3},{8,4},{9,5},{1... | collective-permute-start | bytes 1179656 | tf_op jit(solution)/shard_map/ppermute | solution.py:157
  24.2 17.2 %collective-permute-start.11 = (bf16[768,384]{1,0:T(8,128)(2,1)S(1)}, bf16[768,384]{1,0:T(8,128)(2,1)S(1)}, u32[]{:S(2)}, u32[]{:S(2)}) collective-permute-start(bf16[768,384]{1,0:T(8,128)(2,1)S(1)} %collective-permute-done.8), channel_id=1, source_target_pairs={{0,32},{16,112},{32,64},{48,16},{64,96},{80,48},{96,0},{112,80},{1... | collective-permute-start | bytes 1769480 | tf_op jit(solution)/shard_map/ppermute | solution.py:140
  24.2 17.2 %collective-permute-start.12 = (bf16[384,768]{1,0:T(8,128)(2,1)S(1)}, bf16[384,768]{1,0:T(8,128)(2,1)S(1)}, u32[]{:S(2)}, u32[]{:S(2)}) collective-permute-start(bf16[384,768]{1,0:T(8,128)(2,1)S(1)} %collective-permute-done.9), channel_id=1, source_target_pairs={{0,96},{16,48},{32,0},{48,80},{64,32},{80,112},{96,64},{112,16},{1... | collective-permute-start | bytes 1769480 | tf_op jit(solution)/shard_map/ppermute | solution.py:140
  27.6 30.6 %copy-start.3 = (bf16[384,768]{1,0:T(8,128)(2,1)S(1)}, bf16[384,768]{1,0:T(8,128)(2,1)}, u32[]{:S(2)}) copy-start(bf16[384,768]{1,0:T(8,128)(2,1)} %param.6) | copy-start | bytes 1769476
  27.6 30.9 %collective-permute-start.6 = (bf16[2,128,3072]{2,1,0:T(8,128)(2,1)S(1)}, bf16[2,128,3072]{2,1,0:T(8,128)(2,1)S(1)}, u32[]{:S(2)}, u32[]{:S(2)}) collective-permute-start(bf16[2,128,3072]{2,1,0:T(8,128)(2,1)S(1)} %pad_maximum_fusion.7), channel_id=1, source_target_pairs={{0,1},{1,2},{2,3},{3,0},{4,5},{5,6},{6,7},{7,4},{8,9},{9,10},{10,1... | collective-permute-start | bytes 4718600 | tf_op jit(solution)/shard_map/ppermute | solution.py:157
  29.3 29.7 %collective-permute-start.7 = (bf16[2,128,3072]{2,1,0:T(8,128)(2,1)S(1)}, bf16[2,128,3072]{2,1,0:T(8,128)(2,1)S(1)}, u32[]{:S(2)}, u32[]{:S(2)}) collective-permute-start(bf16[2,128,3072]{2,1,0:T(8,128)(2,1)S(1)} %pad_maximum_fusion.7), channel_id=1, source_target_pairs={{0,3},{1,0},{2,1},{3,2},{4,7},{5,4},{6,5},{7,6},{8,11},{9,8},{10,9... | collective-permute-start | bytes 4718600 | tf_op jit(solution)/shard_map/ppermute | solution.py:157
  31.0 27.3 %collective-permute-start.10 = (bf16[1536,384]{1,0:T(8,128)(2,1)S(1)}, bf16[1536,384]{1,0:T(8,128)(2,1)S(1)}, u32[]{:S(2)}, u32[]{:S(2)}) collective-permute-start(bf16[1536,384]{1,0:T(8,128)(2,1)S(1)} %pad_maximum_fusion.10), channel_id=1, source_target_pairs={{0,16},{16,0},{1,17},{17,1},{2,18},{18,2},{3,19},{19,3},{4,20},{20... | collective-permute-start | bytes 3538952 | tf_op jit(solution)/shard_map/ppermute | solution.py:144
  41.4 16.3 %collective-permute-start.13 = (bf16[768,384]{1,0:T(8,128)(2,1)S(1)}, bf16[768,384]{1,0:T(8,128)(2,1)S(1)}, u32[]{:S(2)}, u32[]{:S(2)}) collective-permute-start(bf16[768,384]{1,0:T(8,128)(2,1)S(1)} %collective-permute-done.11), channel_id=1, source_target_pairs={{0,32},{16,112},{32,64},{48,16},{64,96},{80,48},{96,0},{112,80},{1... | collective-permute-start | bytes 1769480 | tf_op jit(solution)/shard_map/ppermute | solution.py:140
  41.4 16.3 %collective-permute-start.15 = (bf16[384,768]{1,0:T(8,128)(2,1)S(1)}, bf16[384,768]{1,0:T(8,128)(2,1)S(1)}, u32[]{:S(2)}, u32[]{:S(2)}) collective-permute-start(bf16[384,768]{1,0:T(8,128)(2,1)S(1)} %collective-permute-done.12), channel_id=1, source_target_pairs={{0,96},{16,48},{32,0},{48,80},{64,32},{80,112},{96,64},{112,16},{1... | collective-permute-start | bytes 1769480 | tf_op jit(solution)/shard_map/ppermute | solution.py:140
  57.7 2.0 %collective-permute-start.14 = (bf16[768,384]{1,0:T(8,128)(2,1)S(1)}, bf16[768,384]{1,0:T(8,128)(2,1)S(1)}, u32[]{:S(2)}, u32[]{:S(2)}) collective-permute-start(bf16[768,384]{1,0:T(8,128)(2,1)S(1)} %collective-permute-done.13), channel_id=1, source_target_pairs={{0,16},{16,0},{1,17},{17,1},{2,18},{18,2},{3,19},{19,3},{4,20},{20... | collective-permute-start | bytes 1769480 | tf_op jit(solution)/shard_map/ppermute | solution.py:144
  57.7 2.8 %collective-permute-start.16 = (bf16[384,768]{1,0:T(8,128)(2,1)S(1)}, bf16[384,768]{1,0:T(8,128)(2,1)S(1)}, u32[]{:S(2)}, u32[]{:S(2)}) collective-permute-start(bf16[384,768]{1,0:T(8,128)(2,1)S(1)} %collective-permute-done.15), channel_id=1, source_target_pairs={{0,16},{16,0},{1,17},{17,1},{2,18},{18,2},{3,19},{19,3},{4,20},{20... | collective-permute-start | bytes 1769480 | tf_op jit(solution)/shard_map/ppermute | solution.py:144
  58.4 3.0 %collective-permute-start.19 = (bf16[768,384]{1,0:T(8,128)(2,1)S(1)}, bf16[768,384]{1,0:T(8,128)(2,1)S(1)}, u32[]{:S(2)}, u32[]{:S(2)}) collective-permute-start(bf16[768,384]{1,0:T(8,128)(2,1)S(1)} %collective-permute-done.11), channel_id=1, source_target_pairs={{0,16},{16,0},{1,17},{17,1},{2,18},{18,2},{3,19},{19,3},{4,20},{20... | collective-permute-start | bytes 1769480 | tf_op jit(solution)/shard_map/ppermute | solution.py:144
  58.5 7.7 %collective-permute-start.20 = (bf16[384,2304]{1,0:T(8,128)(2,1)S(1)}, bf16[384,2304]{1,0:T(8,128)(2,1)S(1)}, u32[]{:S(2)}, u32[]{:S(2)}) collective-permute-start(bf16[384,2304]{1,0:T(8,128)(2,1)S(1)} %pad_maximum_fusion.6), channel_id=1, source_target_pairs={{0,16},{16,0},{1,17},{17,1},{2,18},{18,2},{3,19},{19,3},{4,20},{20... | collective-permute-start | bytes 5308424 | tf_op jit(solution)/shard_map/ppermute | solution.py:144
  61.7 13.3 %collective-permute-start.17 = (bf16[2,64,3072]{2,1,0:T(8,128)(2,1)S(1)}, bf16[2,64,3072]{2,1,0:T(8,128)(2,1)S(1)}, u32[]{:S(2)}, u32[]{:S(2)}) collective-permute-start(bf16[2,64,3072]{2,1,0:T(8,128)(2,1)S(1)} %slice.184), channel_id=1, source_target_pairs={{0,1},{1,2},{2,3},{3,0},{4,5},{5,6},{6,7},{7,4},{8,9},{9,10},{10,1... | collective-permute-start | bytes 2359304 | tf_op jit(solution)/shard_map/ppermute | solution.py:157
  63.4 12.2 %collective-permute-start.18 = (bf16[2,64,3072]{2,1,0:T(8,128)(2,1)S(1)}, bf16[2,64,3072]{2,1,0:T(8,128)(2,1)S(1)}, u32[]{:S(2)}, u32[]{:S(2)}) collective-permute-start(bf16[2,64,3072]{2,1,0:T(8,128)(2,1)S(1)} %slice.185), channel_id=1, source_target_pairs={{0,3},{1,0},{2,1},{3,2},{4,7},{5,4},{6,5},{7,6},{8,11},{9,8},{10,9... | collective-permute-start | bytes 2359304 | tf_op jit(solution)/shard_map/ppermute | solution.py:157
  82.0 13.2 %collective-permute-start.21 = (bf16[2,64,3072]{2,1,0:T(8,128)(2,1)S(1)}, bf16[2,64,3072]{2,1,0:T(8,128)(2,1)S(1)}, u32[]{:S(2)}, u32[]{:S(2)}) collective-permute-start(bf16[2,64,3072]{2,1,0:T(8,128)(2,1)S(1)} %get-tuple-element.87), channel_id=1, source_target_pairs={{0,3},{1,0},{2,1},{3,2},{4,7},{5,4},{6,5},{7,6},{8,11},{9,8},{10,9... | collective-permute-start | bytes 2359304 | tf_op jit(solution)/shard_map/ppermute | solution.py:157
  84.9 13.2 %collective-permute-start.22 = (bf16[2,64,3072]{2,1,0:T(8,128)(2,1)S(1)}, bf16[2,64,3072]{2,1,0:T(8,128)(2,1)S(1)}, u32[]{:S(2)}, u32[]{:S(2)}) collective-permute-start(bf16[2,64,3072]{2,1,0:T(8,128)(2,1)S(1)} %get-tuple-element.88), channel_id=1, source_target_pairs={{0,1},{1,2},{2,3},{3,0},{4,5},{5,6},{6,7},{7,4},{8,9},{9,10},{10,1... | collective-permute-start | bytes 2359304 | tf_op jit(solution)/shard_map/ppermute | solution.py:157
  100.7 12.8 %collective-permute-start.27 = (bf16[768,384]{1,0:T(8,128)(2,1)S(1)}, bf16[768,384]{1,0:T(8,128)(2,1)S(1)}, u32[]{:S(2)}, u32[]{:S(2)}) collective-permute-start(bf16[768,384]{1,0:T(8,128)(2,1)S(1)} %get-tuple-element.106), channel_id=1, source_target_pairs={{0,16},{16,0},{1,17},{17,1},{2,18},{18,2},{3,19},{19,3},{4,20},{20... | collective-permute-start | bytes 1769480 | tf_op jit(solution)/shard_map/ppermute | solution.py:144
  102.6 29.4 %collective-permute-start.24 = (bf16[2,128,3072]{2,1,0:T(8,128)(2,1)}, bf16[2,128,3072]{2,1,0:T(8,128)(2,1)}, u32[]{:S(2)}, u32[]{:S(2)}) collective-permute-start(bf16[2,128,3072]{2,1,0:T(8,128)(2,1)} %pad_maximum_fusion.9), channel_id=1, source_target_pairs={{0,1},{1,2},{2,3},{3,0},{4,5},{5,6},{6,7},{7,4},{8,9},{9,10},{10,1... | collective-permute-start | bytes 4718600 | tf_op jit(solution)/shard_map/ppermute | solution.py:157
  103.9 28.1 %collective-permute-start.23 = (bf16[2,128,3072]{2,1,0:T(8,128)(2,1)}, bf16[2,128,3072]{2,1,0:T(8,128)(2,1)}, u32[]{:S(2)}, u32[]{:S(2)}) collective-permute-start(bf16[2,128,3072]{2,1,0:T(8,128)(2,1)} %pad_maximum_fusion.8), channel_id=1, source_target_pairs={{0,3},{1,0},{2,1},{3,2},{4,7},{5,4},{6,5},{7,6},{8,11},{9,8},{10,9... | collective-permute-start | bytes 4718600 | tf_op jit(solution)/shard_map/ppermute | solution.py:157
  107.2 7.5 %collective-permute-start.25 = (bf16[384,768]{1,0:T(8,128)(2,1)S(1)}, bf16[384,768]{1,0:T(8,128)(2,1)S(1)}, u32[]{:S(2)}, u32[]{:S(2)}) collective-permute-start(bf16[384,768]{1,0:T(8,128)(2,1)S(1)} %get-tuple-element.104), channel_id=1, source_target_pairs={{0,16},{16,0},{1,17},{17,1},{2,18},{18,2},{3,19},{19,3},{4,20},{20... | collective-permute-start | bytes 1769480 | tf_op jit(solution)/shard_map/ppermute | solution.py:144
  114.6 17.4 %collective-permute-start.28 = (bf16[768,384]{1,0:T(8,128)(2,1)}, bf16[768,384]{1,0:T(8,128)(2,1)}, u32[]{:S(2)}, u32[]{:S(2)}) collective-permute-start(bf16[768,384]{1,0:T(8,128)(2,1)} %fusion.10), channel_id=1, source_target_pairs={{0,32},{16,112},{32,64},{48,16},{64,96},{80,48},{96,0},{112,80},{1... | collective-permute-start | bytes 1769480 | tf_op jit(solution)/shard_map/ppermute | solution.py:140
  116.0 16.0 %collective-permute-start.26 = (bf16[384,768]{1,0:T(8,128)(2,1)}, bf16[384,768]{1,0:T(8,128)(2,1)}, u32[]{:S(2)}, u32[]{:S(2)}) collective-permute-start(bf16[384,768]{1,0:T(8,128)(2,1)} %fusion.11), channel_id=1, source_target_pairs={{0,96},{16,48},{32,0},{48,80},{64,32},{80,112},{96,64},{112,16},{1... | collective-permute-start | bytes 1769480 | tf_op jit(solution)/shard_map/ppermute | solution.py:140
  132.1 7.8 %collective-permute-start.34 = (bf16[768,384]{1,0:T(8,128)(2,1)}, bf16[768,384]{1,0:T(8,128)(2,1)S(1)}, u32[]{:S(2)}, u32[]{:S(2)}) collective-permute-start(bf16[768,384]{1,0:T(8,128)(2,1)} %get-tuple-element.111), channel_id=1, source_target_pairs={{0,16},{16,0},{1,17},{17,1},{2,18},{18,2},{3,19},{19,3},{4,20},{20... | collective-permute-start | bytes 1769480 | tf_op jit(solution)/shard_map/ppermute | solution.py:144
  132.2 9.1 %collective-permute-start.32 = (bf16[384,768]{1,0:T(8,128)(2,1)}, bf16[384,768]{1,0:T(8,128)(2,1)S(1)}, u32[]{:S(2)}, u32[]{:S(2)}) collective-permute-start(bf16[384,768]{1,0:T(8,128)(2,1)} %get-tuple-element.109), channel_id=1, source_target_pairs={{0,16},{16,0},{1,17},{17,1},{2,18},{18,2},{3,19},{19,3},{4,20},{20... | collective-permute-start | bytes 1769480 | tf_op jit(solution)/shard_map/ppermute | solution.py:144
  135.9 12.3 %collective-permute-start.29 = (bf16[2,32,3072]{2,1,0:T(8,128)(2,1)S(1)}, bf16[2,32,3072]{2,1,0:T(8,128)(2,1)S(1)}, u32[]{:S(2)}, u32[]{:S(2)}) collective-permute-start(bf16[2,32,3072]{2,1,0:T(8,128)(2,1)S(1)} %get-tuple-element.135), channel_id=1, source_target_pairs={{0,12},{1,13},{2,14},{3,15},{4,0},{5,1},{6,2},{7,3},{8,4},{9,5},{1... | collective-permute-start | bytes 1179656 | tf_op jit(solution)/shard_map/ppermute | solution.py:157
  138.6 9.5 %collective-permute-start.30 = (bf16[2,32,3072]{2,1,0:T(8,128)(2,1)S(1)}, bf16[2,32,3072]{2,1,0:T(8,128)(2,1)S(1)}, u32[]{:S(2)}, u32[]{:S(2)}) collective-permute-start(bf16[2,32,3072]{2,1,0:T(8,128)(2,1)S(1)} %get-tuple-element.136), channel_id=1, source_target_pairs={{0,8},{1,9},{2,10},{3,11},{4,12},{5,13},{6,14},{7,15},{8,0},{9,1},... | collective-permute-start | bytes 1179656 | tf_op jit(solution)/shard_map/ppermute | solution.py:157
  138.6 13.2 %collective-permute-start.31 = (bf16[2,32,3072]{2,1,0:T(8,128)(2,1)S(1)}, bf16[2,32,3072]{2,1,0:T(8,128)(2,1)S(1)}, u32[]{:S(2)}, u32[]{:S(2)}) collective-permute-start(bf16[2,32,3072]{2,1,0:T(8,128)(2,1)S(1)} %get-tuple-element.137), channel_id=1, source_target_pairs={{0,4},{1,5},{2,6},{3,7},{4,8},{5,9},{6,10},{7,11},{8,12},{9,13},{1... | collective-permute-start | bytes 1179656 | tf_op jit(solution)/shard_map/ppermute | solution.py:157
  141.2 16.4 %copy-start.5 = (bf16[768,384]{1,0:T(8,128)(2,1)S(1)}, bf16[768,384]{1,0:T(8,128)(2,1)}, u32[]{:S(2)}) copy-start(bf16[768,384]{1,0:T(8,128)(2,1)} %get-tuple-element.115) | copy-start | bytes 1769476
  141.2 15.6 %collective-permute-start.35 = (bf16[768,384]{1,0:T(8,128)(2,1)S(1)}, bf16[768,384]{1,0:T(8,128)(2,1)S(1)}, u32[]{:S(2)}, u32[]{:S(2)}) collective-permute-start(bf16[768,384]{1,0:T(8,128)(2,1)S(1)} %fusion.7), channel_id=1, source_target_pairs={{0,32},{16,112},{32,64},{48,16},{64,96},{80,48},{96,0},{112,80},{1... | collective-permute-start | bytes 1769480 | tf_op jit(solution)/shard_map/ppermute | solution.py:140
  142.7 14.2 %collective-permute-start.33 = (bf16[384,768]{1,0:T(8,128)(2,1)S(1)}, bf16[384,768]{1,0:T(8,128)(2,1)S(1)}, u32[]{:S(2)}, u32[]{:S(2)}) collective-permute-start(bf16[384,768]{1,0:T(8,128)(2,1)S(1)} %fusion.9), channel_id=1, source_target_pairs={{0,96},{16,48},{32,0},{48,80},{64,32},{80,112},{96,64},{112,16},{1... | collective-permute-start | bytes 1769480 | tf_op jit(solution)/shard_map/ppermute | solution.py:140
  156.9 12.4 %collective-permute-start.43 = (bf16[384,768]{1,0:T(8,128)(2,1)S(1)}, bf16[384,768]{1,0:T(8,128)(2,1)S(1)}, u32[]{:S(2)}, u32[]{:S(2)}) collective-permute-start(bf16[384,768]{1,0:T(8,128)(2,1)S(1)} %copy-done.6), channel_id=1, source_target_pairs={{0,16},{16,0},{1,17},{17,1},{2,18},{18,2},{3,19},{19,3},{4,20},{20... | collective-permute-start | bytes 1769480 | tf_op jit(solution)/shard_map/ppermute | solution.py:144
  157.0 19.8 %collective-permute-start.42 = (bf16[384,768]{1,0:T(8,128)(2,1)S(1)}, bf16[384,768]{1,0:T(8,128)(2,1)S(1)}, u32[]{:S(2)}, u32[]{:S(2)}) collective-permute-start(bf16[384,768]{1,0:T(8,128)(2,1)S(1)} %get-tuple-element.117), channel_id=1, source_target_pairs={{0,16},{16,0},{1,17},{17,1},{2,18},{18,2},{3,19},{19,3},{4,20},{20... | collective-permute-start | bytes 1769480 | tf_op jit(solution)/shard_map/ppermute | solution.py:144
  157.5 29.5 %collective-permute-start.39 = (bf16[768,384]{1,0:T(8,128)(2,1)S(1)}, bf16[768,384]{1,0:T(8,128)(2,1)S(1)}, u32[]{:S(2)}, u32[]{:S(2)}) collective-permute-start(bf16[768,384]{1,0:T(8,128)(2,1)S(1)} %get-tuple-element.114), channel_id=1, source_target_pairs={{0,16},{16,0},{1,17},{17,1},{2,18},{18,2},{3,19},{19,3},{4,20},{20... | collective-permute-start | bytes 1769480 | tf_op jit(solution)/shard_map/ppermute | solution.py:144
  157.6 15.1 %collective-permute-start.40 = (bf16[768,384]{1,0:T(8,128)(2,1)S(1)}, bf16[768,384]{1,0:T(8,128)(2,1)S(1)}, u32[]{:S(2)}, u32[]{:S(2)}) collective-permute-start(bf16[768,384]{1,0:T(8,128)(2,1)S(1)} %copy-done.5), channel_id=1, source_target_pairs={{0,16},{16,0},{1,17},{17,1},{2,18},{18,2},{3,19},{19,3},{4,20},{20... | collective-permute-start | bytes 1769480 | tf_op jit(solution)/shard_map/ppermute | solution.py:144
  158.0 4.7 %collective-permute-start.36 = (bf16[2,32,768]{2,1,0:T(8,128)(2,1)S(1)}, bf16[2,32,768]{2,1,0:T(8,128)(2,1)S(1)}, u32[]{:S(2)}, u32[]{:S(2)}) collective-permute-start(bf16[2,32,768]{2,1,0:T(8,128)(2,1)S(1)} %pad_maximum_fusion.12), channel_id=1, source_target_pairs={{0,96},{16,48},{32,0},{48,80},{64,32},{80,112},{96,64},{112,16},{1... | collective-permute-start | bytes 294920 | tf_op jit(solution)/shard_map/ppermute | solution.py:140
  162.7 6.4 %collective-permute-start.37 = (bf16[2,32,768]{2,1,0:T(8,128)(2,1)S(1)}, bf16[2,32,768]{2,1,0:T(8,128)(2,1)S(1)}, u32[]{:S(2)}, u32[]{:S(2)}) collective-permute-start(bf16[2,32,768]{2,1,0:T(8,128)(2,1)S(1)} %pad_maximum_fusion.13), channel_id=1, source_target_pairs={{0,64},{16,80},{32,96},{48,112},{64,0},{80,16},{96,32},{112,48},{1... | collective-permute-start | bytes 294920 | tf_op jit(solution)/shard_map/ppermute | solution.py:140
  169.1 6.9 %collective-permute-start.38 = (bf16[2,32,768]{2,1,0:T(8,128)(2,1)S(1)}, bf16[2,32,768]{2,1,0:T(8,128)(2,1)S(1)}, u32[]{:S(2)}, u32[]{:S(2)}) collective-permute-start(bf16[2,32,768]{2,1,0:T(8,128)(2,1)S(1)} %pad_maximum_fusion.14), channel_id=1, source_target_pairs={{0,32},{16,112},{32,64},{48,16},{64,96},{80,48},{96,0},{112,80},{1... | collective-permute-start | bytes 294920 | tf_op jit(solution)/shard_map/ppermute | solution.py:140
  169.5 16.2 %collective-permute-start.44 = (bf16[384,768]{1,0:T(8,128)(2,1)S(1)}, bf16[384,768]{1,0:T(8,128)(2,1)S(1)}, u32[]{:S(2)}, u32[]{:S(2)}) collective-permute-start(bf16[384,768]{1,0:T(8,128)(2,1)S(1)} %fusion.1), channel_id=1, source_target_pairs={{0,96},{16,48},{32,0},{48,80},{64,32},{80,112},{96,64},{112,16},{1... | collective-permute-start | bytes 1769480 | tf_op jit(solution)/shard_map/ppermute | solution.py:140
  172.9 14.1 %collective-permute-start.41 = (bf16[768,384]{1,0:T(8,128)(2,1)S(1)}, bf16[768,384]{1,0:T(8,128)(2,1)S(1)}, u32[]{:S(2)}, u32[]{:S(2)}) collective-permute-start(bf16[768,384]{1,0:T(8,128)(2,1)S(1)} %fusion.4), channel_id=1, source_target_pairs={{0,32},{16,112},{32,64},{48,16},{64,96},{80,48},{96,0},{112,80},{1... | collective-permute-start | bytes 1769480 | tf_op jit(solution)/shard_map/ppermute | solution.py:140
  (4 other events, 33.6 us)

commit v5 on v4

--- a/solution.py
+++ b/solution.py
@@ -252,32 +252,27 @@
     here, left, right = (near_sums[:, i * rows : (i + 1) * rows] for i in range(3))
     left = join([total(left[:, :half], far_back[0]).astype(BF), left[:, half:]], 1)
     right = join([right[:, :half], total(right[:, half:], far_back[1]).astype(BF)], 1)
+    near_sent = (left, right)
     left, right = plane(left, 1, -1), plane(right, 1, 1)
 
-    def swap(k, round_value):
-        down_sum, up_sum, _ = held(down_other[turned[k]], up_other[turned[k]], round_value)
+    def swap(blocks, round_value):
+        down_sum, up_sum, _ = held(down_other[blocks], up_other[blocks], round_value)
         return across(down_sum), across(up_sum)
 
-    down_theirs, up_theirs = swap(1, near_sums)
+    down_theirs, up_theirs = swap(3, near_sent)
     down_grad = along_x(total(mine[0][1], down_theirs).astype(BF), -1)
     up_grad = along_x(total(mine[1][1], up_theirs).astype(BF), 1)
-
     left, right, down_grad, up_grad = held(left, right, down_grad, up_grad)
 
-    down_theirs, up_theirs = swap(2, left)
-    down_grad = along_x(total(mine[0][2], down_theirs, down_grad).astype(BF), -1)
-    up_grad = along_x(total(mine[1][2], up_theirs, up_grad).astype(BF), 1)
+    down_theirs, up_theirs = swap(slice(0, 3), left)
+    down_grad = along_x(total(mine[0][2], down_theirs[2], down_grad).astype(BF), -1)
+    up_grad = along_x(total(mine[1][2], up_theirs[2], up_grad).astype(BF), 1)
     sums = total(here, left, right).astype(BF).reshape(2, 4, sub, 4 * width)
     end = total(sums[:, 0], *(plane(sums[:, hop], 0, -hop) for hop in (1, 2, 3))).astype(BF)
-
     end, down_grad, up_grad = held(end, down_grad, up_grad)
 
-    down_theirs, up_theirs = swap(3, end)
-    down_grad = along_x(total(mine[0][3], down_theirs, down_grad).astype(BF), -1)
-    up_grad = along_x(total(mine[1][3], up_theirs, up_grad).astype(BF), 1)
-    down_theirs, up_theirs = swap(0, end)
-    down_grad = total(mine[0][0], down_theirs, down_grad)
-    up_grad = total(mine[1][0], up_theirs, up_grad)
+    down_grad = along_x(total(mine[0][3], down_theirs[1], down_grad).astype(BF), -1)
+    up_grad = along_x(total(mine[1][3], up_theirs[1], up_grad).astype(BF), 1)
 
     out = jnp.zeros((2, rows, width), BF)
     for k in range(4):
@@ -285,6 +280,8 @@
         got = along_x(sent, -k) if k else sent
         at = (x + sign * k + 4) % 4 * sub
         out = lax.dynamic_update_slice_in_dim(out, got, at, axis=1)
+    down_grad = total(mine[0][0], down_theirs[0], down_grad)
+    up_grad = total(mine[1][0], up_theirs[0], up_grad)
     return out[0], out[1], up_grad, down_grad
 
 

time: 188 us -> 178 us (0.947)
  waiting for transfers between devices: 85.3 us -> 72.9 us
  local copies, waits for them, and re-layouts: 4.79 us -> 8.03 us
  other arithmetic: 17.4 us -> 14.2 us
  starting transfers between devices: 52.9 us -> 55.2 us
    ppermute x18, waiting for transfers between devices: 70.5 us -> 56.8 us  [along_x(): return lax.ppermute(value, ('row', 'col'), pairs)]
    slice x0 -> x2, local copies, waits for them, and re-layouts: none -> 2.79 us  [the longest x1 1.4 us: swap(): down_other[blocks]]
    ppermute x18, starting transfers between devices: 25.3 us -> 28.1 us  [along_x(): return lax.ppermute(value, ('row', 'col'), pairs)]
    concatenate x11, other arithmetic: 4.66 us -> 2.31 us  [join(): return jnp.concatenate(parts, axis=axis)]
    squeeze x2, local copies, waits for them, and re-layouts: 2.44 us -> 0.1 us  [the longest x1 0.06 us: swap(): up_other[blocks]]
    unnamed x19, local copies, waits for them, and re-layouts: 0.65 us -> 2.55 us
    ppermute x13 -> x9, starting transfers between devices: 3.95 us -> 2.72 us  [across(): return lax.ppermute(value, 'col', [(0, 1), (1, 0)])]
  transfers between devices with their start and end apart: 45 -> 41, of which waited for: 20 -> 17; matrix products, arithmetic and copies ran while one was open for 9% -> 9% of each run, Pallas kernels for 11% -> 11%
where the time goes in v5:
time: 178 us
  waiting for transfers between devices  72.9 us (41%)
  starting transfers between devices  55.2 us (31%)
  Pallas kernels  26.5 us (15%)
  other arithmetic  14.2 us (8%)
  local copies, waits for them, and re-layouts  8.03 us (5%)
    ppermute x18, waiting for transfers between devices, along_x(): return lax.ppermute(value, ('row', 'col'), pairs)  56.8 us
    ppermute x18, starting transfers between devices, along_x(): return lax.ppermute(value, ('row', 'col'), pairs)  28.1 us
    pallas_call x6, Pallas kernels, local_kernel(): pl.pallas_call(body, grid=grid, in_specs=in_specs, out_specs=out_specs, o...  26.5 us
    ppermute x14, starting transfers between devices, plane(): return lax.ppermute(value, ('col', 'depth'), pairs)  24.3 us
    ppermute x14, waiting for transfers between devices, plane(): return lax.ppermute(value, ('col', 'depth'), pairs)  14 us
  transfers between devices with their start and end apart: 41, of which 17 were waited for; matrix products, arithmetic and copies ran while one was open for 9% of the time, Pallas kernels for 11%

profile of v5, /device:TPU:0, one launch (start us, length us, event | category | flops | bytes accessed | tf_op | source)
XLA Modules:
  0.0 178.0 jit_solution(6694070717640383847)
XLA Ops:
  0.7 1.0 fusion.11
  1.7 1.6 collective-permute-start
  3.4 2.7 %collective-permute-start.1 = (bf16[2,32,768]{2,1,0:T(8,128)(2,1)S(1)}, bf16[2,32,768]{2,1,0:T(8,128)(2,1)S(1)}, u32[]{:S(2)}, u32[]{:S(2)}) collective-permute-start(bf16[2,32,768]{2,1,0:T(8,128)(2,1)S(1)} %get-tuple-element.134), channel_id=1, source_target_pairs={{0,64},{16,80},{32,96},{48,112},{64,0},{80,16},{96,32},{112,48},{1... | collective-permute-start | bytes 294920 | tf_op jit(solution)/shard_map/ppermute | solution.py:140
  6.1 1.4 collective-permute-start.2
  8.1 2.6 %collective-permute-start.9 = (bf16[384,768]{1,0:T(8,128)(2,1)}, bf16[384,768]{1,0:T(8,128)(2,1)S(1)}, u32[]{:S(2)}, u32[]{:S(2)}) collective-permute-start(bf16[384,768]{1,0:T(8,128)(2,1)} %param.6), channel_id=1, source_target_pairs={{0,96},{16,48},{32,0},{48,80},{64,32},{80,112},{96,64},{112,16},{1... | collective-permute-start | bytes 1769480 | tf_op jit(solution)/shard_map/ppermute | solution.py:140
  12.0 2.0 %collective-permute-start.3 = (bf16[2,32,3072]{2,1,0:T(8,128)(2,1)S(1)}, bf16[2,32,3072]{2,1,0:T(8,128)(2,1)S(1)}, u32[]{:S(2)}, u32[]{:S(2)}) collective-permute-start(bf16[2,32,3072]{2,1,0:T(8,128)(2,1)S(1)} %get-tuple-element.131), channel_id=1, source_target_pairs={{0,4},{1,5},{2,6},{3,7},{4,8},{5,9},{6,10},{7,11},{8,12},{9,13},{1... | collective-permute-start | bytes 1179656 | tf_op jit(solution)/shard_map/ppermute | solution.py:157
  13.9 3.6 %collective-permute-start.4 = (bf16[2,32,3072]{2,1,0:T(8,128)(2,1)S(1)}, bf16[2,32,3072]{2,1,0:T(8,128)(2,1)S(1)}, u32[]{:S(2)}, u32[]{:S(2)}) collective-permute-start(bf16[2,32,3072]{2,1,0:T(8,128)(2,1)S(1)} %get-tuple-element.131), channel_id=1, source_target_pairs={{0,8},{1,9},{2,10},{3,11},{4,12},{5,13},{6,14},{7,15},{8,0},{9,1},... | collective-permute-start | bytes 1179656 | tf_op jit(solution)/shard_map/ppermute | solution.py:157
  17.5 1.0 collective-permute-start.5
  18.5 5.6 %collective-permute-done.8 = bf16[768,384]{1,0:T(8,128)(2,1)S(1)} collective-permute-done((bf16[768,384]{1,0:T(8,128)(2,1)}, bf16[768,384]{1,0:T(8,128)(2,1)S(1)}, u32[]{:S(2)}, u32[]{:S(2)}) %collective-permute-start.8) | collective-permute-done | bytes 589856 | tf_op jit(solution)/shard_map/ppermute | solution.py:140
  24.2 3.2 %collective-permute-start.12 = (bf16[384,768]{1,0:T(8,128)(2,1)S(1)}, bf16[384,768]{1,0:T(8,128)(2,1)S(1)}, u32[]{:S(2)}, u32[]{:S(2)}) collective-permute-start(bf16[384,768]{1,0:T(8,128)(2,1)S(1)} %collective-permute-done.9), channel_id=1, source_target_pairs={{0,96},{16,48},{32,0},{48,80},{64,32},{80,112},{96,64},{112,16},{1... | collective-permute-start | bytes 1769480 | tf_op jit(solution)/shard_map/ppermute | solution.py:140
  27.6 1.6 collective-permute-start.6
  29.3 1.7 collective-permute-start.7
  31.1 10.2 %collective-permute-done.11 = bf16[768,384]{1,0:T(8,128)(2,1)S(1)} collective-permute-done((bf16[768,384]{1,0:T(8,128)(2,1)S(1)}, bf16[768,384]{1,0:T(8,128)(2,1)S(1)}, u32[]{:S(2)}, u32[]{:S(2)}) %collective-permute-start.11) | collective-permute-done | bytes 589856 | tf_op jit(solution)/shard_map/ppermute | solution.py:140
  41.4 3.2 %collective-permute-start.15 = (bf16[384,768]{1,0:T(8,128)(2,1)S(1)}, bf16[384,768]{1,0:T(8,128)(2,1)S(1)}, u32[]{:S(2)}, u32[]{:S(2)}) collective-permute-start(bf16[384,768]{1,0:T(8,128)(2,1)S(1)} %collective-permute-done.12), channel_id=1, source_target_pairs={{0,96},{16,48},{32,0},{48,80},{64,32},{80,112},{96,64},{112,16},{1... | collective-permute-start | bytes 1769480 | tf_op jit(solution)/shard_map/ppermute | solution.py:140
  44.7 13.0 %collective-permute-done.13 = bf16[768,384]{1,0:T(8,128)(2,1)S(1)} collective-permute-done((bf16[768,384]{1,0:T(8,128)(2,1)S(1)}, bf16[768,384]{1,0:T(8,128)(2,1)S(1)}, u32[]{:S(2)}, u32[]{:S(2)}) %collective-permute-start.13) | collective-permute-done | bytes 589856 | tf_op jit(solution)/shard_map/ppermute | solution.py:140
  61.7 1.6 collective-permute-start.17
  64.3 1.7 collective-permute-start.18
  67.6 4.9 %shard_map.75 = (bf16[384,768]{1,0:T(8,128)(2,1)S(1)}, bf16[384,768]{1,0:T(8,128)(2,1)S(1)}) custom-call(bf16[2,384,3072]{2,1,0:T(8,128)(2,1)S(1)} %constant_dynamic-update-slice_fusion.pair_ref.refs_0_, bf16[3072,768]{1,0:T(8,128)(2,1)S(1)} %pad_maximum_fusion.up_ref, bf16[768,3072]{1,0:T(8,128)(2,1)S(1)} %pad_maximum_fusion.1.down_ref), custom_call_target="tpu_custom_call" | custom-call | flops 1 | bytes 1 | tf_op jit(solution)/shard_map/pallas_call | solution.py:30
  72.5 2.4 %collective-permute-done.17 = bf16[2,64,3072]{2,1,0:T(8,128)(2,1)S(1)} collective-permute-done((bf16[2,64,3072]{2,1,0:T(8,128)(2,1)S(1)}, bf16[2,64,3072]{2,1,0:T(8,128)(2,1)S(1)}, u32[]{:S(2)}, u32[]{:S(2)}) %collective-permute-start.17) | collective-permute-done | bytes 786464 | tf_op jit(solution)/shard_map/ppermute | solution.py:157
  75.0 1.5 collective-permute-done.18
  76.6 3.0 %shard_map.76 = (bf16[128,768]{1,0:T(8,128)(2,1)S(1)}, bf16[128,768]{1,0:T(8,128)(2,1)S(1)}) custom-call(bf16[2,128,3072]{2,1,0:T(8,128)(2,1)S(1)} %constant_dynamic-update-slice_fusion.6.pair_ref.refs_1_, bf16[3072,768]{1,0:T(8,128)(2,1)S(1)} %pad_maximum_fusion.up_ref, bf16[768,3072]{1,0:T(8,128)(2,1)S(1)} %pad_maximum_fusion.1.down_ref), custom_call_target="tpu_custom_call" | custom-call | flops 1 | bytes 1 | tf_op jit(solution)/shard_map/pallas_call | solution.py:30
  79.6 3.1 %shard_map.77 = bf16[2,128,3072]{2,1,0:T(8,128)(2,1)S(1)} custom-call(bf16[128,768]{1,0:T(8,128)(2,1)S(1)} %get-tuple-element.89.act_ref.refs_3_, bf16[128,768]{1,0:T(8,128)(2,1)S(1)} %get-tuple-element.91.grad_ref.refs_5_, bf16[3072,768]{1,0:T(8,128)(2,1)S(1)} %pad_maximum_fusion.up_ref, bf16[768,3072]{1,0:T(8,128)(2,1)S(1)} %pad_maximum_fusion.1.down_ref), custom_call_target="tpu_custom_call" | custom-call | flops 1 | bytes 1 | tf_op jit(solution)/shard_map/pallas_call | solution.py:30
  82.8 2.9 %collective-permute-start.21 = (bf16[2,64,3072]{2,1,0:T(8,128)(2,1)S(1)}, bf16[2,64,3072]{2,1,0:T(8,128)(2,1)S(1)}, u32[]{:S(2)}, u32[]{:S(2)}) collective-permute-start(bf16[2,64,3072]{2,1,0:T(8,128)(2,1)S(1)} %get-tuple-element.83), channel_id=1, source_target_pairs={{0,3},{1,0},{2,1},{3,2},{4,7},{5,4},{6,5},{7,6},{8,11},{9,8},{10,9... | collective-permute-start | bytes 2359304 | tf_op jit(solution)/shard_map/ppermute | solution.py:157
  85.7 5.0 %shard_map.78 = bf16[2,384,3072]{2,1,0:T(8,128)(2,1)S(1)} custom-call(bf16[384,768]{1,0:T(8,128)(2,1)S(1)} %get-tuple-element.88.act_ref.refs_2_, bf16[384,768]{1,0:T(8,128)(2,1)S(1)} %get-tuple-element.90.grad_ref.refs_4_, bf16[3072,768]{1,0:T(8,128)(2,1)S(1)} %pad_maximum_fusion.up_ref, bf16[768,3072]{1,0:T(8,128)(2,1)S(1)} %pad_maximum_fusion.1.down_ref), custom_call_target="tpu_custom_call" | custom-call | flops 1 | bytes 1 | tf_op jit(solution)/shard_map/pallas_call | solution.py:30
  90.7 5.3 %shard_map.79 = (bf16[4,384,768]{2,1,0:T(8,128)(2,1)S(1)}, bf16[4,768,384]{2,1,0:T(8,128)(2,1)S(1)}) custom-call(bf16[2,384,3072]{2,1,0:T(8,128)(2,1)S(1)} %constant_dynamic-update-slice_fusion.pair_ref.refs_0_, bf16[2,128,3072]{2,1,0:T(8,128)(2,1)S(1)} %constant_dynamic-update-slice_fusion.6.pair_ref.refs_1_, ...), custom_call_target="tpu_custom_call" | custom-call | flops 1 | bytes 1 | tf_op jit(solution)/shard_map/pallas_call | solution.py:30
  96.0 2.9 %collective-permute-done.22 = bf16[2,64,3072]{2,1,0:T(8,128)(2,1)S(1)} collective-permute-done((bf16[2,64,3072]{2,1,0:T(8,128)(2,1)S(1)}, bf16[2,64,3072]{2,1,0:T(8,128)(2,1)S(1)}, u32[]{:S(2)}, u32[]{:S(2)}) %collective-permute-start.22) | collective-permute-done | bytes 786464 | tf_op jit(solution)/shard_map/ppermute | solution.py:157
  100.1 3.2 %collective-permute-start.23 = (bf16[2,128,3072]{2,1,0:T(8,128)(2,1)S(1)}, bf16[2,128,3072]{2,1,0:T(8,128)(2,1)S(1)}, u32[]{:S(2)}, u32[]{:S(2)}) collective-permute-start(bf16[2,128,3072]{2,1,0:T(8,128)(2,1)S(1)} %pad_maximum_fusion.8), channel_id=1, source_target_pairs={{0,3},{1,0},{2,1},{3,2},{4,7},{5,4},{6,5},{7,6},{8,11},{9,8},{10,9... | collective-permute-start | bytes 4718600 | tf_op jit(solution)/shard_map/ppermute | solution.py:157
  104.3 5.3 %shard_map.80 = (bf16[4,384,768]{2,1,0:T(8,128)(2,1)S(1)}, bf16[4,768,384]{2,1,0:T(8,128)(2,1)S(1)}) custom-call(bf16[2,384,3072]{2,1,0:T(8,128)(2,1)S(1)} %constant_dynamic-update-slice_fusion.pair_ref.refs_0_, bf16[2,128,3072]{2,1,0:T(8,128)(2,1)S(1)} %constant_dynamic-update-slice_fusion.6.pair_ref.refs_1_, ...), custom_call_target="tpu_custom_call" | custom-call | flops 1 | bytes 1 | tf_op jit(solution)/shard_map/pallas_call | solution.py:30
  110.0 3.5 %collective-permute-start.26 = (bf16[384,768]{1,0:T(8,128)(2,1)S(1)}, bf16[384,768]{1,0:T(8,128)(2,1)S(1)}, u32[]{:S(2)}, u32[]{:S(2)}) collective-permute-start(bf16[384,768]{1,0:T(8,128)(2,1)S(1)} %fusion.1), channel_id=1, source_target_pairs={{0,96},{16,48},{32,0},{48,80},{64,32},{80,112},{96,64},{112,16},{1... | collective-permute-start | bytes 1769480 | tf_op jit(solution)/shard_map/ppermute | solution.py:140
  113.5 1.4 slice.213
  114.9 1.4 slice.214
  116.3 10.4 %collective-permute-done.28 = bf16[768,384]{1,0:T(8,128)(2,1)S(1)} collective-permute-done((bf16[768,384]{1,0:T(8,128)(2,1)S(1)}, bf16[768,384]{1,0:T(8,128)(2,1)S(1)}, u32[]{:S(2)}, u32[]{:S(2)}) %collective-permute-start.28) | collective-permute-done | bytes 589856 | tf_op jit(solution)/shard_map/ppermute | solution.py:140
  126.8 1.1 copy-done.5
  127.9 1.2 copy-done.6
  129.6 3.1 %add_convert_fusion = bf16[2,128,3072]{2,1,0:T(8,128)(2,1)S(1)} fusion(bf16[2,128,3072]{2,1,0:T(8,128)(2,1)} %copy-done.5, bf16[2,128,3072]{2,1,0:T(8,128)(2,1)} %copy-done.6, bf16[2,384,3072]{2,1,0:T(8,128)(2,1)} %copy-done), kind=kLoop, calls=%fused_computation.2 | loop fusion | flops 4718592 | bytes 6291456 | tf_op jit(solution)/shard_map/convert_element_type | solution.py:270
  132.8 3.6 %collective-permute-start.29 = (bf16[2,32,3072]{2,1,0:T(8,128)(2,1)S(1)}, bf16[2,32,3072]{2,1,0:T(8,128)(2,1)S(1)}, u32[]{:S(2)}, u32[]{:S(2)}) collective-permute-start(bf16[2,32,3072]{2,1,0:T(8,128)(2,1)S(1)} %get-tuple-element.119), channel_id=1, source_target_pairs={{0,12},{1,13},{2,14},{3,15},{4,0},{5,1},{6,2},{7,3},{8,4},{9,5},{1... | collective-permute-start | bytes 1179656 | tf_op jit(solution)/shard_map/ppermute | solution.py:157
  136.5 1.3 collective-permute-start.31
  137.7 1.3 fusion.4
  139.4 3.3 %collective-permute-start.33 = (bf16[384,768]{1,0:T(8,128)(2,1)S(1)}, bf16[384,768]{1,0:T(8,128)(2,1)S(1)}, u32[]{:S(2)}, u32[]{:S(2)}) collective-permute-start(bf16[384,768]{1,0:T(8,128)(2,1)S(1)} %fusion.5), channel_id=1, source_target_pairs={{0,96},{16,48},{32,0},{48,80},{64,32},{80,112},{96,64},{112,16},{1... | collective-permute-start | bytes 1769480 | tf_op jit(solution)/shard_map/ppermute | solution.py:140
  142.6 3.3 %collective-permute-done.29 = bf16[2,32,3072]{2,1,0:T(8,128)(2,1)S(1)} collective-permute-done((bf16[2,32,3072]{2,1,0:T(8,128)(2,1)S(1)}, bf16[2,32,3072]{2,1,0:T(8,128)(2,1)S(1)}, u32[]{:S(2)}, u32[]{:S(2)}) %collective-permute-start.29) | collective-permute-done | bytes 393248 | tf_op jit(solution)/shard_map/ppermute | solution.py:157
  146.0 3.7 %collective-permute-done.31 = bf16[2,32,3072]{2,1,0:T(8,128)(2,1)S(1)} collective-permute-done((bf16[2,32,3072]{2,1,0:T(8,128)(2,1)S(1)}, bf16[2,32,3072]{2,1,0:T(8,128)(2,1)S(1)}, u32[]{:S(2)}, u32[]{:S(2)}) %collective-permute-start.31) | collective-permute-done | bytes 393248 | tf_op jit(solution)/shard_map/ppermute | solution.py:157
  149.9 3.6 %collective-permute-done.35 = bf16[768,384]{1,0:T(8,128)(2,1)S(1)} collective-permute-done((bf16[768,384]{1,0:T(8,128)(2,1)S(1)}, bf16[768,384]{1,0:T(8,128)(2,1)S(1)}, u32[]{:S(2)}, u32[]{:S(2)}) %collective-permute-start.35) | collective-permute-done | bytes 589856 | tf_op jit(solution)/shard_map/ppermute | solution.py:140
  154.0 1.3 fusion.3
  155.3 1.9 %collective-permute-start.39 = (bf16[768,384]{1,0:T(8,128)(2,1)S(1)}, bf16[768,384]{1,0:T(8,128)(2,1)S(1)}, u32[]{:S(2)}, u32[]{:S(2)}) collective-permute-start(bf16[768,384]{1,0:T(8,128)(2,1)S(1)} %fusion.3), channel_id=1, source_target_pairs={{0,32},{16,112},{32,64},{48,16},{64,96},{80,48},{96,0},{112,80},{1... | collective-permute-start | bytes 1769480 | tf_op jit(solution)/shard_map/ppermute | solution.py:140
  157.9 2.4 %collective-permute-start.37 = (bf16[2,32,768]{2,1,0:T(8,128)(2,1)S(1)}, bf16[2,32,768]{2,1,0:T(8,128)(2,1)S(1)}, u32[]{:S(2)}, u32[]{:S(2)}) collective-permute-start(bf16[2,32,768]{2,1,0:T(8,128)(2,1)S(1)} %pad_maximum_fusion.13), channel_id=1, source_target_pairs={{0,64},{16,80},{32,96},{48,112},{64,0},{80,16},{96,32},{112,48},{1... | collective-permute-start | bytes 294920 | tf_op jit(solution)/shard_map/ppermute | solution.py:140
  160.9 12.8 %collective-permute-done.36 = bf16[2,32,768]{2,1,0:T(8,128)(2,1)S(1)} collective-permute-done((bf16[2,32,768]{2,1,0:T(8,128)(2,1)S(1)}, bf16[2,32,768]{2,1,0:T(8,128)(2,1)S(1)}, u32[]{:S(2)}, u32[]{:S(2)}) %collective-permute-start.36) | collective-permute-done | bytes 98336 | tf_op jit(solution)/shard_map/ppermute | solution.py:140
  174.6 1.2 bitcast_add_fusion.1
  175.8 2.3 %bitcast_add_fusion.3 = f32[768,384]{1,0:T(8,128)} fusion(bf16[768,384]{1,0:T(8,128)(2,1)S(1)} %collective-permute-done.39, bf16[3,768,384]{2,1,0:T(8,128)(2,1)} %collective-permute-done.34, bf16[4,768,384]{2,1,0:T(8,128)(2,1)S(1)} %get-tuple-element.101), kind=kLoop, calls=%fused_computation.23 | loop fusion | flops 1474560 | bytes 2949120 | tf_op jit(solution)/shard_map/add | solution.py:249
  (113 shorter events, 15.0 us)
Async XLA Ops:
  1.7 9.1 %collective-permute-start = (bf16[2,32,768]{2,1,0:T(8,128)(2,1)S(1)}, bf16[2,32,768]{2,1,0:T(8,128)(2,1)S(1)}, u32[]{:S(2)}, u32[]{:S(2)}) collective-permute-start(bf16[2,32,768]{2,1,0:T(8,128)(2,1)S(1)} %get-tuple-element.133), channel_id=1, source_target_pairs={{0,32},{16,112},{32,64},{48,16},{64,96},{80,48},{96,0},{112,80},{1... | collective-permute-start | bytes 294920 | tf_op jit(solution)/shard_map/ppermute | solution.py:140
  3.4 7.9 %collective-permute-start.1 = (bf16[2,32,768]{2,1,0:T(8,128)(2,1)S(1)}, bf16[2,32,768]{2,1,0:T(8,128)(2,1)S(1)}, u32[]{:S(2)}, u32[]{:S(2)}) collective-permute-start(bf16[2,32,768]{2,1,0:T(8,128)(2,1)S(1)} %get-tuple-element.134), channel_id=1, source_target_pairs={{0,64},{16,80},{32,96},{48,112},{64,0},{80,16},{96,32},{112,48},{1... | collective-permute-start | bytes 294920 | tf_op jit(solution)/shard_map/ppermute | solution.py:140
  6.1 5.7 %collective-permute-start.2 = (bf16[2,32,768]{2,1,0:T(8,128)(2,1)S(1)}, bf16[2,32,768]{2,1,0:T(8,128)(2,1)S(1)}, u32[]{:S(2)}, u32[]{:S(2)}) collective-permute-start(bf16[2,32,768]{2,1,0:T(8,128)(2,1)S(1)} %get-tuple-element.135), channel_id=1, source_target_pairs={{0,96},{16,48},{32,0},{48,80},{64,32},{80,112},{96,64},{112,16},{1... | collective-permute-start | bytes 294920 | tf_op jit(solution)/shard_map/ppermute | solution.py:140
  7.5 16.6 %collective-permute-start.8 = (bf16[768,384]{1,0:T(8,128)(2,1)}, bf16[768,384]{1,0:T(8,128)(2,1)S(1)}, u32[]{:S(2)}, u32[]{:S(2)}) collective-permute-start(bf16[768,384]{1,0:T(8,128)(2,1)} %param.5), channel_id=1, source_target_pairs={{0,32},{16,112},{32,64},{48,16},{64,96},{80,48},{96,0},{112,80},{1... | collective-permute-start | bytes 1769480 | tf_op jit(solution)/shard_map/ppermute | solution.py:140
  8.1 16.1 %collective-permute-start.9 = (bf16[384,768]{1,0:T(8,128)(2,1)}, bf16[384,768]{1,0:T(8,128)(2,1)S(1)}, u32[]{:S(2)}, u32[]{:S(2)}) collective-permute-start(bf16[384,768]{1,0:T(8,128)(2,1)} %param.6), channel_id=1, source_target_pairs={{0,96},{16,48},{32,0},{48,80},{64,32},{80,112},{96,64},{112,16},{1... | collective-permute-start | bytes 1769480 | tf_op jit(solution)/shard_map/ppermute | solution.py:140
  11.9 19.1 %copy-start.4 = (bf16[768,384]{1,0:T(8,128)(2,1)S(1)}, bf16[768,384]{1,0:T(8,128)(2,1)}, u32[]{:S(2)}) copy-start(bf16[768,384]{1,0:T(8,128)(2,1)} %param.5) | copy-start | bytes 1769476
  12.0 15.4 %collective-permute-start.3 = (bf16[2,32,3072]{2,1,0:T(8,128)(2,1)S(1)}, bf16[2,32,3072]{2,1,0:T(8,128)(2,1)S(1)}, u32[]{:S(2)}, u32[]{:S(2)}) collective-permute-start(bf16[2,32,3072]{2,1,0:T(8,128)(2,1)S(1)} %get-tuple-element.131), channel_id=1, source_target_pairs={{0,4},{1,5},{2,6},{3,7},{4,8},{5,9},{6,10},{7,11},{8,12},{9,13},{1... | collective-permute-start | bytes 1179656 | tf_op jit(solution)/shard_map/ppermute | solution.py:157
  13.9 13.5 %collective-permute-start.4 = (bf16[2,32,3072]{2,1,0:T(8,128)(2,1)S(1)}, bf16[2,32,3072]{2,1,0:T(8,128)(2,1)S(1)}, u32[]{:S(2)}, u32[]{:S(2)}) collective-permute-start(bf16[2,32,3072]{2,1,0:T(8,128)(2,1)S(1)} %get-tuple-element.131), channel_id=1, source_target_pairs={{0,8},{1,9},{2,10},{3,11},{4,12},{5,13},{6,14},{7,15},{8,0},{9,1},... | collective-permute-start | bytes 1179656 | tf_op jit(solution)/shard_map/ppermute | solution.py:157
  17.5 10.0 %collective-permute-start.5 = (bf16[2,32,3072]{2,1,0:T(8,128)(2,1)S(1)}, bf16[2,32,3072]{2,1,0:T(8,128)(2,1)S(1)}, u32[]{:S(2)}, u32[]{:S(2)}) collective-permute-start(bf16[2,32,3072]{2,1,0:T(8,128)(2,1)S(1)} %get-tuple-element.131), channel_id=1, source_target_pairs={{0,12},{1,13},{2,14},{3,15},{4,0},{5,1},{6,2},{7,3},{8,4},{9,5},{1... | collective-permute-start | bytes 1179656 | tf_op jit(solution)/shard_map/ppermute | solution.py:157
  24.2 17.2 %collective-permute-start.11 = (bf16[768,384]{1,0:T(8,128)(2,1)S(1)}, bf16[768,384]{1,0:T(8,128)(2,1)S(1)}, u32[]{:S(2)}, u32[]{:S(2)}) collective-permute-start(bf16[768,384]{1,0:T(8,128)(2,1)S(1)} %collective-permute-done.8), channel_id=1, source_target_pairs={{0,32},{16,112},{32,64},{48,16},{64,96},{80,48},{96,0},{112,80},{1... | collective-permute-start | bytes 1769480 | tf_op jit(solution)/shard_map/ppermute | solution.py:140
  24.2 17.2 %collective-permute-start.12 = (bf16[384,768]{1,0:T(8,128)(2,1)S(1)}, bf16[384,768]{1,0:T(8,128)(2,1)S(1)}, u32[]{:S(2)}, u32[]{:S(2)}) collective-permute-start(bf16[384,768]{1,0:T(8,128)(2,1)S(1)} %collective-permute-done.9), channel_id=1, source_target_pairs={{0,96},{16,48},{32,0},{48,80},{64,32},{80,112},{96,64},{112,16},{1... | collective-permute-start | bytes 1769480 | tf_op jit(solution)/shard_map/ppermute | solution.py:140
  27.6 30.6 %copy-start.3 = (bf16[384,768]{1,0:T(8,128)(2,1)S(1)}, bf16[384,768]{1,0:T(8,128)(2,1)}, u32[]{:S(2)}) copy-start(bf16[384,768]{1,0:T(8,128)(2,1)} %param.6) | copy-start | bytes 1769476
  27.6 30.9 %collective-permute-start.6 = (bf16[2,128,3072]{2,1,0:T(8,128)(2,1)S(1)}, bf16[2,128,3072]{2,1,0:T(8,128)(2,1)S(1)}, u32[]{:S(2)}, u32[]{:S(2)}) collective-permute-start(bf16[2,128,3072]{2,1,0:T(8,128)(2,1)S(1)} %pad_maximum_fusion.7), channel_id=1, source_target_pairs={{0,1},{1,2},{2,3},{3,0},{4,5},{5,6},{6,7},{7,4},{8,9},{9,10},{10,1... | collective-permute-start | bytes 4718600 | tf_op jit(solution)/shard_map/ppermute | solution.py:157
  29.3 29.7 %collective-permute-start.7 = (bf16[2,128,3072]{2,1,0:T(8,128)(2,1)S(1)}, bf16[2,128,3072]{2,1,0:T(8,128)(2,1)S(1)}, u32[]{:S(2)}, u32[]{:S(2)}) collective-permute-start(bf16[2,128,3072]{2,1,0:T(8,128)(2,1)S(1)} %pad_maximum_fusion.7), channel_id=1, source_target_pairs={{0,3},{1,0},{2,1},{3,2},{4,7},{5,4},{6,5},{7,6},{8,11},{9,8},{10,9... | collective-permute-start | bytes 4718600 | tf_op jit(solution)/shard_map/ppermute | solution.py:157
  31.0 27.3 %collective-permute-start.10 = (bf16[1536,384]{1,0:T(8,128)(2,1)S(1)}, bf16[1536,384]{1,0:T(8,128)(2,1)S(1)}, u32[]{:S(2)}, u32[]{:S(2)}) collective-permute-start(bf16[1536,384]{1,0:T(8,128)(2,1)S(1)} %pad_maximum_fusion.10), channel_id=1, source_target_pairs={{0,16},{16,0},{1,17},{17,1},{2,18},{18,2},{3,19},{19,3},{4,20},{20... | collective-permute-start | bytes 3538952 | tf_op jit(solution)/shard_map/ppermute | solution.py:144
  41.4 16.3 %collective-permute-start.13 = (bf16[768,384]{1,0:T(8,128)(2,1)S(1)}, bf16[768,384]{1,0:T(8,128)(2,1)S(1)}, u32[]{:S(2)}, u32[]{:S(2)}) collective-permute-start(bf16[768,384]{1,0:T(8,128)(2,1)S(1)} %collective-permute-done.11), channel_id=1, source_target_pairs={{0,32},{16,112},{32,64},{48,16},{64,96},{80,48},{96,0},{112,80},{1... | collective-permute-start | bytes 1769480 | tf_op jit(solution)/shard_map/ppermute | solution.py:140
  41.4 16.3 %collective-permute-start.15 = (bf16[384,768]{1,0:T(8,128)(2,1)S(1)}, bf16[384,768]{1,0:T(8,128)(2,1)S(1)}, u32[]{:S(2)}, u32[]{:S(2)}) collective-permute-start(bf16[384,768]{1,0:T(8,128)(2,1)S(1)} %collective-permute-done.12), channel_id=1, source_target_pairs={{0,96},{16,48},{32,0},{48,80},{64,32},{80,112},{96,64},{112,16},{1... | collective-permute-start | bytes 1769480 | tf_op jit(solution)/shard_map/ppermute | solution.py:140
  57.7 2.0 %collective-permute-start.14 = (bf16[768,384]{1,0:T(8,128)(2,1)S(1)}, bf16[768,384]{1,0:T(8,128)(2,1)S(1)}, u32[]{:S(2)}, u32[]{:S(2)}) collective-permute-start(bf16[768,384]{1,0:T(8,128)(2,1)S(1)} %collective-permute-done.13), channel_id=1, source_target_pairs={{0,16},{16,0},{1,17},{17,1},{2,18},{18,2},{3,19},{19,3},{4,20},{20... | collective-permute-start | bytes 1769480 | tf_op jit(solution)/shard_map/ppermute | solution.py:144
  57.7 2.8 %collective-permute-start.16 = (bf16[384,768]{1,0:T(8,128)(2,1)S(1)}, bf16[384,768]{1,0:T(8,128)(2,1)S(1)}, u32[]{:S(2)}, u32[]{:S(2)}) collective-permute-start(bf16[384,768]{1,0:T(8,128)(2,1)S(1)} %collective-permute-done.15), channel_id=1, source_target_pairs={{0,16},{16,0},{1,17},{17,1},{2,18},{18,2},{3,19},{19,3},{4,20},{20... | collective-permute-start | bytes 1769480 | tf_op jit(solution)/shard_map/ppermute | solution.py:144
  58.4 3.0 %collective-permute-start.19 = (bf16[768,384]{1,0:T(8,128)(2,1)S(1)}, bf16[768,384]{1,0:T(8,128)(2,1)S(1)}, u32[]{:S(2)}, u32[]{:S(2)}) collective-permute-start(bf16[768,384]{1,0:T(8,128)(2,1)S(1)} %collective-permute-done.11), channel_id=1, source_target_pairs={{0,16},{16,0},{1,17},{17,1},{2,18},{18,2},{3,19},{19,3},{4,20},{20... | collective-permute-start | bytes 1769480 | tf_op jit(solution)/shard_map/ppermute | solution.py:144
  58.5 8.3 %collective-permute-start.20 = (bf16[384,2304]{1,0:T(8,128)(2,1)S(1)}, bf16[384,2304]{1,0:T(8,128)(2,1)S(1)}, u32[]{:S(2)}, u32[]{:S(2)}) collective-permute-start(bf16[384,2304]{1,0:T(8,128)(2,1)S(1)} %pad_maximum_fusion.6), channel_id=1, source_target_pairs={{0,16},{16,0},{1,17},{17,1},{2,18},{18,2},{3,19},{19,3},{4,20},{20... | collective-permute-start | bytes 5308424 | tf_op jit(solution)/shard_map/ppermute | solution.py:144
  61.7 13.3 %collective-permute-start.17 = (bf16[2,64,3072]{2,1,0:T(8,128)(2,1)S(1)}, bf16[2,64,3072]{2,1,0:T(8,128)(2,1)S(1)}, u32[]{:S(2)}, u32[]{:S(2)}) collective-permute-start(bf16[2,64,3072]{2,1,0:T(8,128)(2,1)S(1)} %slice.190), channel_id=1, source_target_pairs={{0,1},{1,2},{2,3},{3,0},{4,5},{5,6},{6,7},{7,4},{8,9},{9,10},{10,1... | collective-permute-start | bytes 2359304 | tf_op jit(solution)/shard_map/ppermute | solution.py:157
  64.3 12.2 %collective-permute-start.18 = (bf16[2,64,3072]{2,1,0:T(8,128)(2,1)}, bf16[2,64,3072]{2,1,0:T(8,128)(2,1)S(1)}, u32[]{:S(2)}, u32[]{:S(2)}) collective-permute-start(bf16[2,64,3072]{2,1,0:T(8,128)(2,1)} %slice.191), channel_id=1, source_target_pairs={{0,3},{1,0},{2,1},{3,2},{4,7},{5,4},{6,5},{7,6},{8,11},{9,8},{10,9... | collective-permute-start | bytes 2359304 | tf_op jit(solution)/shard_map/ppermute | solution.py:157
  82.8 13.2 %collective-permute-start.21 = (bf16[2,64,3072]{2,1,0:T(8,128)(2,1)S(1)}, bf16[2,64,3072]{2,1,0:T(8,128)(2,1)S(1)}, u32[]{:S(2)}, u32[]{:S(2)}) collective-permute-start(bf16[2,64,3072]{2,1,0:T(8,128)(2,1)S(1)} %get-tuple-element.83), channel_id=1, source_target_pairs={{0,3},{1,0},{2,1},{3,2},{4,7},{5,4},{6,5},{7,6},{8,11},{9,8},{10,9... | collective-permute-start | bytes 2359304 | tf_op jit(solution)/shard_map/ppermute | solution.py:157
  85.7 13.2 %collective-permute-start.22 = (bf16[2,64,3072]{2,1,0:T(8,128)(2,1)S(1)}, bf16[2,64,3072]{2,1,0:T(8,128)(2,1)S(1)}, u32[]{:S(2)}, u32[]{:S(2)}) collective-permute-start(bf16[2,64,3072]{2,1,0:T(8,128)(2,1)S(1)} %get-tuple-element.84), channel_id=1, source_target_pairs={{0,1},{1,2},{2,3},{3,0},{4,5},{5,6},{6,7},{7,4},{8,9},{9,10},{10,1... | collective-permute-start | bytes 2359304 | tf_op jit(solution)/shard_map/ppermute | solution.py:157
  90.7 8.4 %copy-start = (bf16[2,384,3072]{2,1,0:T(8,128)(2,1)}, bf16[2,384,3072]{2,1,0:T(8,128)(2,1)S(1)}, u32[]{:S(2)}) copy-start(bf16[2,384,3072]{2,1,0:T(8,128)(2,1)S(1)} %shard_map.78) | copy-start | bytes 14155780
  100.0 9.6 %collective-permute-start.27 = (bf16[768,384]{1,0:T(8,128)(2,1)S(1)}, bf16[768,384]{1,0:T(8,128)(2,1)S(1)}, u32[]{:S(2)}, u32[]{:S(2)}) collective-permute-start(bf16[768,384]{1,0:T(8,128)(2,1)S(1)} %slice_bitcast_fusion), channel_id=1, source_target_pairs={{0,16},{16,0},{1,17},{17,1},{2,18},{18,2},{3,19},{19,3},{4,20},{20... | collective-permute-start | bytes 1769480 | tf_op jit(solution)/shard_map/ppermute | solution.py:144
  100.1 26.7 %collective-permute-start.24 = (bf16[2,128,3072]{2,1,0:T(8,128)(2,1)S(1)}, bf16[2,128,3072]{2,1,0:T(8,128)(2,1)S(1)}, u32[]{:S(2)}, u32[]{:S(2)}) collective-permute-start(bf16[2,128,3072]{2,1,0:T(8,128)(2,1)S(1)} %pad_maximum_fusion.9), channel_id=1, source_target_pairs={{0,1},{1,2},{2,3},{3,0},{4,5},{5,6},{6,7},{7,4},{8,9},{9,10},{10,1... | collective-permute-start | bytes 4718600 | tf_op jit(solution)/shard_map/ppermute | solution.py:157
  100.1 26.6 %collective-permute-start.23 = (bf16[2,128,3072]{2,1,0:T(8,128)(2,1)S(1)}, bf16[2,128,3072]{2,1,0:T(8,128)(2,1)S(1)}, u32[]{:S(2)}, u32[]{:S(2)}) collective-permute-start(bf16[2,128,3072]{2,1,0:T(8,128)(2,1)S(1)} %pad_maximum_fusion.8), channel_id=1, source_target_pairs={{0,3},{1,0},{2,1},{3,2},{4,7},{5,4},{6,5},{7,6},{8,11},{9,8},{10,9... | collective-permute-start | bytes 4718600 | tf_op jit(solution)/shard_map/ppermute | solution.py:157
  103.4 6.5 %collective-permute-start.25 = (bf16[384,768]{1,0:T(8,128)(2,1)S(1)}, bf16[384,768]{1,0:T(8,128)(2,1)S(1)}, u32[]{:S(2)}, u32[]{:S(2)}) collective-permute-start(bf16[384,768]{1,0:T(8,128)(2,1)S(1)} %slice_bitcast_fusion.1), channel_id=1, source_target_pairs={{0,16},{16,0},{1,17},{17,1},{2,18},{18,2},{3,19},{19,3},{4,20},{20... | collective-permute-start | bytes 1769480 | tf_op jit(solution)/shard_map/ppermute | solution.py:144
  109.6 5.3 %copy-start.1 = (bf16[4,384,768]{2,1,0:T(8,128)(2,1)}, bf16[4,384,768]{2,1,0:T(8,128)(2,1)S(1)}, u32[]{:S(2)}) copy-start(bf16[4,384,768]{2,1,0:T(8,128)(2,1)S(1)} %get-tuple-element.97) | copy-start | bytes 7077892
  109.8 17.0 %collective-permute-start.28 = (bf16[768,384]{1,0:T(8,128)(2,1)S(1)}, bf16[768,384]{1,0:T(8,128)(2,1)S(1)}, u32[]{:S(2)}, u32[]{:S(2)}) collective-permute-start(bf16[768,384]{1,0:T(8,128)(2,1)S(1)} %fusion), channel_id=1, source_target_pairs={{0,32},{16,112},{32,64},{48,16},{64,96},{80,48},{96,0},{112,80},{1... | collective-permute-start | bytes 1769480 | tf_op jit(solution)/shard_map/ppermute | solution.py:140
  110.0 16.7 %collective-permute-start.26 = (bf16[384,768]{1,0:T(8,128)(2,1)S(1)}, bf16[384,768]{1,0:T(8,128)(2,1)S(1)}, u32[]{:S(2)}, u32[]{:S(2)}) collective-permute-start(bf16[384,768]{1,0:T(8,128)(2,1)S(1)} %fusion.1), channel_id=1, source_target_pairs={{0,96},{16,48},{32,0},{48,80},{64,32},{80,112},{96,64},{112,16},{1... | collective-permute-start | bytes 1769480 | tf_op jit(solution)/shard_map/ppermute | solution.py:140
  126.8 1.1 copy-start.5
  127.9 1.2 copy-start.6
  129.1 8.7 %collective-permute-start.34 = (bf16[3,768,384]{2,1,0:T(8,128)(2,1)}, bf16[3,768,384]{2,1,0:T(8,128)(2,1)}, u32[]{:S(2)}, u32[]{:S(2)}) collective-permute-start(bf16[3,768,384]{2,1,0:T(8,128)(2,1)} %slice.214), channel_id=1, source_target_pairs={{0,16},{16,0},{1,17},{17,1},{2,18},{18,2},{3,19},{19,3},{4,20},{20... | collective-permute-start | bytes 5308424 | tf_op jit(solution)/shard_map/ppermute | solution.py:144
  129.1 10.0 %collective-permute-start.32 = (bf16[3,384,768]{2,1,0:T(8,128)(2,1)}, bf16[3,384,768]{2,1,0:T(8,128)(2,1)S(1)}, u32[]{:S(2)}, u32[]{:S(2)}) collective-permute-start(bf16[3,384,768]{2,1,0:T(8,128)(2,1)} %slice.213), channel_id=1, source_target_pairs={{0,16},{16,0},{1,17},{17,1},{2,18},{18,2},{3,19},{19,3},{4,20},{20... | collective-permute-start | bytes 5308424 | tf_op jit(solution)/shard_map/ppermute | solution.py:144
  132.7 6.4 %copy-start.2 = (bf16[4,384,768]{2,1,0:T(8,128)(2,1)S(1)}, bf16[4,384,768]{2,1,0:T(8,128)(2,1)}, u32[]{:S(2)}) copy-start(bf16[4,384,768]{2,1,0:T(8,128)(2,1)} %copy-done.1) | copy-start | bytes 7077892
  132.8 13.2 %collective-permute-start.29 = (bf16[2,32,3072]{2,1,0:T(8,128)(2,1)S(1)}, bf16[2,32,3072]{2,1,0:T(8,128)(2,1)S(1)}, u32[]{:S(2)}, u32[]{:S(2)}) collective-permute-start(bf16[2,32,3072]{2,1,0:T(8,128)(2,1)S(1)} %get-tuple-element.119), channel_id=1, source_target_pairs={{0,12},{1,13},{2,14},{3,15},{4,0},{5,1},{6,2},{7,3},{8,4},{9,5},{1... | collective-permute-start | bytes 1179656 | tf_op jit(solution)/shard_map/ppermute | solution.py:157
  136.5 9.5 %collective-permute-start.30 = (bf16[2,32,3072]{2,1,0:T(8,128)(2,1)S(1)}, bf16[2,32,3072]{2,1,0:T(8,128)(2,1)S(1)}, u32[]{:S(2)}, u32[]{:S(2)}) collective-permute-start(bf16[2,32,3072]{2,1,0:T(8,128)(2,1)S(1)} %get-tuple-element.120), channel_id=1, source_target_pairs={{0,8},{1,9},{2,10},{3,11},{4,12},{5,13},{6,14},{7,15},{8,0},{9,1},... | collective-permute-start | bytes 1179656 | tf_op jit(solution)/shard_map/ppermute | solution.py:157
  136.5 13.2 %collective-permute-start.31 = (bf16[2,32,3072]{2,1,0:T(8,128)(2,1)S(1)}, bf16[2,32,3072]{2,1,0:T(8,128)(2,1)S(1)}, u32[]{:S(2)}, u32[]{:S(2)}) collective-permute-start(bf16[2,32,3072]{2,1,0:T(8,128)(2,1)S(1)} %get-tuple-element.121), channel_id=1, source_target_pairs={{0,4},{1,5},{2,6},{3,7},{4,8},{5,9},{6,10},{7,11},{8,12},{9,13},{1... | collective-permute-start | bytes 1179656 | tf_op jit(solution)/shard_map/ppermute | solution.py:157
  139.0 14.5 %collective-permute-start.35 = (bf16[768,384]{1,0:T(8,128)(2,1)S(1)}, bf16[768,384]{1,0:T(8,128)(2,1)S(1)}, u32[]{:S(2)}, u32[]{:S(2)}) collective-permute-start(bf16[768,384]{1,0:T(8,128)(2,1)S(1)} %fusion.4), channel_id=1, source_target_pairs={{0,32},{16,112},{32,64},{48,16},{64,96},{80,48},{96,0},{112,80},{1... | collective-permute-start | bytes 1769480 | tf_op jit(solution)/shard_map/ppermute | solution.py:140
  139.4 14.2 %collective-permute-start.33 = (bf16[384,768]{1,0:T(8,128)(2,1)S(1)}, bf16[384,768]{1,0:T(8,128)(2,1)S(1)}, u32[]{:S(2)}, u32[]{:S(2)}) collective-permute-start(bf16[384,768]{1,0:T(8,128)(2,1)S(1)} %fusion.5), channel_id=1, source_target_pairs={{0,96},{16,48},{32,0},{48,80},{64,32},{80,112},{96,64},{112,16},{1... | collective-permute-start | bytes 1769480 | tf_op jit(solution)/shard_map/ppermute | solution.py:140
  153.8 20.8 %collective-permute-start.40 = (bf16[384,768]{1,0:T(8,128)(2,1)S(1)}, bf16[384,768]{1,0:T(8,128)(2,1)S(1)}, u32[]{:S(2)}, u32[]{:S(2)}) collective-permute-start(bf16[384,768]{1,0:T(8,128)(2,1)S(1)} %fusion.2), channel_id=1, source_target_pairs={{0,96},{16,48},{32,0},{48,80},{64,32},{80,112},{96,64},{112,16},{1... | collective-permute-start | bytes 1769480 | tf_op jit(solution)/shard_map/ppermute | solution.py:140
  155.3 20.5 %collective-permute-start.39 = (bf16[768,384]{1,0:T(8,128)(2,1)S(1)}, bf16[768,384]{1,0:T(8,128)(2,1)S(1)}, u32[]{:S(2)}, u32[]{:S(2)}) collective-permute-start(bf16[768,384]{1,0:T(8,128)(2,1)S(1)} %fusion.3), channel_id=1, source_target_pairs={{0,32},{16,112},{32,64},{48,16},{64,96},{80,48},{96,0},{112,80},{1... | collective-permute-start | bytes 1769480 | tf_op jit(solution)/shard_map/ppermute | solution.py:140
  157.3 16.4 %collective-permute-start.38 = (bf16[2,32,768]{2,1,0:T(8,128)(2,1)S(1)}, bf16[2,32,768]{2,1,0:T(8,128)(2,1)S(1)}, u32[]{:S(2)}, u32[]{:S(2)}) collective-permute-start(bf16[2,32,768]{2,1,0:T(8,128)(2,1)S(1)} %pad_maximum_fusion.14), channel_id=1, source_target_pairs={{0,32},{16,112},{32,64},{48,16},{64,96},{80,48},{96,0},{112,80},{1... | collective-permute-start | bytes 294920 | tf_op jit(solution)/shard_map/ppermute | solution.py:140
  157.9 15.8 %collective-permute-start.37 = (bf16[2,32,768]{2,1,0:T(8,128)(2,1)S(1)}, bf16[2,32,768]{2,1,0:T(8,128)(2,1)S(1)}, u32[]{:S(2)}, u32[]{:S(2)}) collective-permute-start(bf16[2,32,768]{2,1,0:T(8,128)(2,1)S(1)} %pad_maximum_fusion.13), channel_id=1, source_target_pairs={{0,64},{16,80},{32,96},{48,112},{64,0},{80,16},{96,32},{112,48},{1... | collective-permute-start | bytes 294920 | tf_op jit(solution)/shard_map/ppermute | solution.py:140
  160.4 13.3 %collective-permute-start.36 = (bf16[2,32,768]{2,1,0:T(8,128)(2,1)S(1)}, bf16[2,32,768]{2,1,0:T(8,128)(2,1)S(1)}, u32[]{:S(2)}, u32[]{:S(2)}) collective-permute-start(bf16[2,32,768]{2,1,0:T(8,128)(2,1)S(1)} %pad_maximum_fusion.12), channel_id=1, source_target_pairs={{0,96},{16,48},{32,0},{48,80},{64,32},{80,112},{96,64},{112,16},{1... | collective-permute-start | bytes 294920 | tf_op jit(solution)/shard_map/ppermute | solution.py:140

commit v6 on v5

--- a/solution.py
+++ b/solution.py
@@ -95,36 +95,58 @@
     )
 
 
-def weight_sums(sets, acts, grads, core):
+def weight_sums(sets, acts, grads, core, apart):
     units = acts[0].shape[1] // 2
     features = sets[0].shape[2]
     tile = features // 4
     count = len(sets)
+    joint = 3 if apart else 4
 
     def body(*refs):
-        down_ref, up_ref = refs[-2:]
+        outs = refs[3 * count :]
         down_sum = up_sum = None
         for i in range(count):
             down_part = product(refs[count + i][...], refs[i][1], 0, 0)
             up_part = product(refs[i][0], refs[2 * count + i][...], 0, 0)
             down_sum = down_part if i == 0 else down_sum + down_part
             up_sum = up_part if i == 0 else up_sum + up_part
-        down_ref[0] = down_sum.astype(BF)
-        up_ref[0] = up_sum.astype(BF)
+
+        @pl.when(pl.program_id(0) < joint)
+        def _():
+            outs[0][0] = down_sum.astype(BF)
+            outs[1][0] = up_sum.astype(BF)
+
+        if apart:
+
+            @pl.when(pl.program_id(0) == joint)
+            def _():
+                outs[2][...] = down_sum.astype(BF)
+                outs[3][...] = up_sum.astype(BF)
 
     halves = [pl.BlockSpec((a.shape[0], units), lambda i: (0, core)) for a in acts]
+    out_specs = [
+        pl.BlockSpec((1, units, tile), lambda i: (jnp.minimum(i, joint - 1), 0, 0)),
+        pl.BlockSpec((1, tile, units), lambda i: (jnp.minimum(i, joint - 1), 0, 0)),
+    ]
+    out_shape = [
+        jax.ShapeDtypeStruct((joint, units, tile), BF),
+        jax.ShapeDtypeStruct((joint, tile, units), BF),
+    ]
+    if apart:
+        out_specs += [
+            pl.BlockSpec((units, tile), lambda i: (0, 0)),
+            pl.BlockSpec((tile, units), lambda i: (0, 0)),
+        ]
+        out_shape += [
+            jax.ShapeDtypeStruct((units, tile), BF),
+            jax.ShapeDtypeStruct((tile, units), BF),
+        ]
     return local_kernel(
         body,
         (4,),
         [pl.BlockSpec((2, s.shape[1], tile), lambda i: (0, 0, i)) for s in sets] + halves + halves,
-        [
-            pl.BlockSpec((1, units, tile), lambda i: (i, 0, 0)),
-            pl.BlockSpec((1, tile, units), lambda i: (i, 0, 0)),
-        ],
-        [
-            jax.ShapeDtypeStruct((4, units, tile), BF),
-            jax.ShapeDtypeStruct((4, tile, units), BF),
-        ],
+        out_specs,
+        out_shape,
         *sets,
         *acts,
         *grads,
@@ -239,9 +261,9 @@
     near_sums = backward(near_acts, near_grads, up, down)
     near_acts, near_grads, near_sums = held(near_acts, near_grads, near_sums)
     sets, acts, grads = (near, far), (near_acts, far_acts), (near_grads, far_grads)
-    theirs = weight_sums(sets, acts, grads, 1)
-    *far_back, near_sums, down_other, up_other = held(*far_back, near_sums, *theirs)
-    mine = weight_sums(sets, acts, grads, 0)
+    theirs = weight_sums(sets, acts, grads, 1, True)
+    far_back[0], far_back[1], near_sums, *theirs = held(*far_back, near_sums, *theirs)
+    mine = weight_sums(sets, acts, grads, 0, False)
 
     def total(*parts):
         value = parts[0].astype(F32)
@@ -255,16 +277,16 @@
     near_sent = (left, right)
     left, right = plane(left, 1, -1), plane(right, 1, 1)
 
-    def swap(blocks, round_value):
-        down_sum, up_sum, _ = held(down_other[blocks], up_other[blocks], round_value)
+    def swap(pair, round_value):
+        down_sum, up_sum, _ = held(*pair, round_value)
         return across(down_sum), across(up_sum)
 
-    down_theirs, up_theirs = swap(3, near_sent)
+    down_theirs, up_theirs = swap(theirs[2:], near_sent)
     down_grad = along_x(total(mine[0][1], down_theirs).astype(BF), -1)
     up_grad = along_x(total(mine[1][1], up_theirs).astype(BF), 1)
     left, right, down_grad, up_grad = held(left, right, down_grad, up_grad)
 
-    down_theirs, up_theirs = swap(slice(0, 3), left)
+    down_theirs, up_theirs = swap(theirs[:2], left)
     down_grad = along_x(total(mine[0][2], down_theirs[2], down_grad).astype(BF), -1)
     up_grad = along_x(total(mine[1][2], up_theirs[2], up_grad).astype(BF), 1)
     sums = total(here, left, right).astype(BF).reshape(2, 4, sub, 4 * width)

time: 178 us -> 184 us (1.034)
  local copies, waits for them, and re-layouts: 8.03 us -> 12 us
  starting transfers between devices: 55.2 us -> 53.3 us
    ppermute x18, waiting for transfers between devices: 56.8 us -> 61.8 us  [along_x(): return lax.ppermute(value, ('row', 'col'), pairs)]
    unnamed x19 -> x27, local copies, waits for them, and re-layouts: 2.55 us -> 7.39 us
    ppermute x14, waiting for transfers between devices: 14 us -> 10.7 us  [plane(): return lax.ppermute(value, ('col', 'depth'), pairs)]
    slice x2 -> x0, local copies, waits for them, and re-layouts: 2.79 us -> none  [the longest x1 1.4 us: swap(): down_other[blocks]]
  transfers between devices with their start and end apart: 41 -> 41, of which waited for: 17 -> 16; matrix products, arithmetic and copies ran while one was open for 9% -> 7% of each run, Pallas kernels for 11% -> 12%
where the time goes in v6:
time: 184 us; the launch traced here: 183 us
  waiting for transfers between devices  74.1 us (40%)
  starting transfers between devices  53.3 us (29%)
  Pallas kernels  28.2 us (15%)
  other arithmetic  14.2 us (8%)
  local copies, waits for them, and re-layouts  12 us (7%)
    ppermute x18, waiting for transfers between devices, along_x(): return lax.ppermute(value, ('row', 'col'), pairs)  61.8 us
    pallas_call x6, Pallas kernels, local_kernel(): pl.pallas_call(body, grid=grid, in_specs=in_specs, out_specs=out_specs, o...  28.2 us
    ppermute x18, starting transfers between devices, along_x(): return lax.ppermute(value, ('row', 'col'), pairs)  27 us
    ppermute x14, starting transfers between devices, plane(): return lax.ppermute(value, ('col', 'depth'), pairs)  23.7 us
    ppermute x14, waiting for transfers between devices, plane(): return lax.ppermute(value, ('col', 'depth'), pairs)  10.7 us
    unnamed x27, local copies, waits for them, and re-layouts  7.39 us
  transfers between devices with their start and end apart: 41, of which 16 were waited for; matrix products, arithmetic and copies ran while one was open for 7% of the time, Pallas kernels for 12%

profile of v6, /device:TPU:0, one launch (start us, length us, event | category | flops | bytes accessed | tf_op | source)
XLA Modules:
  0.0 183.1 jit_solution(12118166605759164917)
XLA Ops:
  0.7 1.0 fusion.11
  1.7 1.6 collective-permute-start
  3.4 2.7 %collective-permute-start.1 = (bf16[2,32,768]{2,1,0:T(8,128)(2,1)S(1)}, bf16[2,32,768]{2,1,0:T(8,128)(2,1)S(1)}, u32[]{:S(2)}, u32[]{:S(2)}) collective-permute-start(bf16[2,32,768]{2,1,0:T(8,128)(2,1)S(1)} %get-tuple-element.142), channel_id=1, source_target_pairs={{0,64},{16,80},{32,96},{48,112},{64,0},{80,16},{96,32},{112,48},{1... | collective-permute-start | bytes 294920 | tf_op jit(solution)/shard_map/ppermute | solution.py:162
  6.1 1.4 collective-permute-start.2
  8.1 2.6 %collective-permute-start.9 = (bf16[384,768]{1,0:T(8,128)(2,1)}, bf16[384,768]{1,0:T(8,128)(2,1)S(1)}, u32[]{:S(2)}, u32[]{:S(2)}) collective-permute-start(bf16[384,768]{1,0:T(8,128)(2,1)} %param.6), channel_id=1, source_target_pairs={{0,96},{16,48},{32,0},{48,80},{64,32},{80,112},{96,64},{112,16},{1... | collective-permute-start | bytes 1769480 | tf_op jit(solution)/shard_map/ppermute | solution.py:162
  12.0 2.0 %collective-permute-start.3 = (bf16[2,32,3072]{2,1,0:T(8,128)(2,1)S(1)}, bf16[2,32,3072]{2,1,0:T(8,128)(2,1)S(1)}, u32[]{:S(2)}, u32[]{:S(2)}) collective-permute-start(bf16[2,32,3072]{2,1,0:T(8,128)(2,1)S(1)} %get-tuple-element.139), channel_id=1, source_target_pairs={{0,4},{1,5},{2,6},{3,7},{4,8},{5,9},{6,10},{7,11},{8,12},{9,13},{1... | collective-permute-start | bytes 1179656 | tf_op jit(solution)/shard_map/ppermute | solution.py:179
  13.9 3.6 %collective-permute-start.4 = (bf16[2,32,3072]{2,1,0:T(8,128)(2,1)S(1)}, bf16[2,32,3072]{2,1,0:T(8,128)(2,1)S(1)}, u32[]{:S(2)}, u32[]{:S(2)}) collective-permute-start(bf16[2,32,3072]{2,1,0:T(8,128)(2,1)S(1)} %get-tuple-element.139), channel_id=1, source_target_pairs={{0,8},{1,9},{2,10},{3,11},{4,12},{5,13},{6,14},{7,15},{8,0},{9,1},... | collective-permute-start | bytes 1179656 | tf_op jit(solution)/shard_map/ppermute | solution.py:179
  18.5 5.6 %collective-permute-done.8 = bf16[768,384]{1,0:T(8,128)(2,1)S(1)} collective-permute-done((bf16[768,384]{1,0:T(8,128)(2,1)}, bf16[768,384]{1,0:T(8,128)(2,1)S(1)}, u32[]{:S(2)}, u32[]{:S(2)}) %collective-permute-start.8) | collective-permute-done | bytes 589856 | tf_op jit(solution)/shard_map/ppermute | solution.py:162
  24.2 3.2 %collective-permute-start.12 = (bf16[384,768]{1,0:T(8,128)(2,1)S(1)}, bf16[384,768]{1,0:T(8,128)(2,1)S(1)}, u32[]{:S(2)}, u32[]{:S(2)}) collective-permute-start(bf16[384,768]{1,0:T(8,128)(2,1)S(1)} %collective-permute-done.9), channel_id=1, source_target_pairs={{0,96},{16,48},{32,0},{48,80},{64,32},{80,112},{96,64},{112,16},{1... | collective-permute-start | bytes 1769480 | tf_op jit(solution)/shard_map/ppermute | solution.py:162
  27.6 1.6 collective-permute-start.6
  29.3 1.7 collective-permute-start.7
  31.1 10.2 %collective-permute-done.11 = bf16[768,384]{1,0:T(8,128)(2,1)S(1)} collective-permute-done((bf16[768,384]{1,0:T(8,128)(2,1)S(1)}, bf16[768,384]{1,0:T(8,128)(2,1)S(1)}, u32[]{:S(2)}, u32[]{:S(2)}) %collective-permute-start.11) | collective-permute-done | bytes 589856 | tf_op jit(solution)/shard_map/ppermute | solution.py:162
  41.4 3.2 %collective-permute-start.15 = (bf16[384,768]{1,0:T(8,128)(2,1)S(1)}, bf16[384,768]{1,0:T(8,128)(2,1)S(1)}, u32[]{:S(2)}, u32[]{:S(2)}) collective-permute-start(bf16[384,768]{1,0:T(8,128)(2,1)S(1)} %collective-permute-done.12), channel_id=1, source_target_pairs={{0,96},{16,48},{32,0},{48,80},{64,32},{80,112},{96,64},{112,16},{1... | collective-permute-start | bytes 1769480 | tf_op jit(solution)/shard_map/ppermute | solution.py:162
  44.7 13.0 %collective-permute-done.13 = bf16[768,384]{1,0:T(8,128)(2,1)S(1)} collective-permute-done((bf16[768,384]{1,0:T(8,128)(2,1)S(1)}, bf16[768,384]{1,0:T(8,128)(2,1)S(1)}, u32[]{:S(2)}, u32[]{:S(2)}) %collective-permute-start.13) | collective-permute-done | bytes 589856 | tf_op jit(solution)/shard_map/ppermute | solution.py:162
  62.6 1.6 collective-permute-start.17
  65.1 1.7 collective-permute-start.18
  69.3 4.9 %shard_map.75 = (bf16[384,768]{1,0:T(8,128)(2,1)S(1)}, bf16[384,768]{1,0:T(8,128)(2,1)S(1)}) custom-call(bf16[2,384,3072]{2,1,0:T(8,128)(2,1)S(1)} %constant_dynamic-update-slice_fusion.pair_ref.refs_0_, bf16[3072,768]{1,0:T(8,128)(2,1)S(1)} %pad_maximum_fusion.up_ref, bf16[768,3072]{1,0:T(8,128)(2,1)S(1)} %pad_maximum_fusion.1.down_ref), custom_call_target="tpu_custom_call" | custom-call | flops 1 | bytes 1 | tf_op jit(solution)/shard_map/pallas_call | solution.py:30
  74.2 1.7 collective-permute-done.17
  76.0 1.4 collective-permute-done.18
  77.4 1.2 constant_dynamic-update-slice_fusion.7
  78.6 1.2 constant_dynamic-update-slice_fusion.6.pair_ref.refs_1_
  79.8 3.0 %shard_map.76 = (bf16[128,768]{1,0:T(8,128)(2,1)S(1)}, bf16[128,768]{1,0:T(8,128)(2,1)S(1)}) custom-call(bf16[2,128,3072]{2,1,0:T(8,128)(2,1)S(1)} %constant_dynamic-update-slice_fusion.6.pair_ref.refs_1_, bf16[3072,768]{1,0:T(8,128)(2,1)S(1)} %pad_maximum_fusion.up_ref, bf16[768,3072]{1,0:T(8,128)(2,1)S(1)} %pad_maximum_fusion.1.down_ref), custom_call_target="tpu_custom_call" | custom-call | flops 1 | bytes 1 | tf_op jit(solution)/shard_map/pallas_call | solution.py:30
  82.7 3.1 %shard_map.77 = bf16[2,128,3072]{2,1,0:T(8,128)(2,1)S(1)} custom-call(bf16[128,768]{1,0:T(8,128)(2,1)S(1)} %get-tuple-element.93.act_ref.refs_3_, bf16[128,768]{1,0:T(8,128)(2,1)S(1)} %get-tuple-element.95.grad_ref.refs_5_, bf16[3072,768]{1,0:T(8,128)(2,1)S(1)} %pad_maximum_fusion.up_ref, bf16[768,3072]{1,0:T(8,128)(2,1)S(1)} %pad_maximum_fusion.1.down_ref), custom_call_target="tpu_custom_call" | custom-call | flops 1 | bytes 1 | tf_op jit(solution)/shard_map/pallas_call | solution.py:30
  85.9 2.9 %collective-permute-start.21 = (bf16[2,64,3072]{2,1,0:T(8,128)(2,1)S(1)}, bf16[2,64,3072]{2,1,0:T(8,128)(2,1)S(1)}, u32[]{:S(2)}, u32[]{:S(2)}) collective-permute-start(bf16[2,64,3072]{2,1,0:T(8,128)(2,1)S(1)} %get-tuple-element.87), channel_id=1, source_target_pairs={{0,3},{1,0},{2,1},{3,2},{4,7},{5,4},{6,5},{7,6},{8,11},{9,8},{10,9... | collective-permute-start | bytes 2359304 | tf_op jit(solution)/shard_map/ppermute | solution.py:179
  88.9 5.0 %shard_map.78 = bf16[2,384,3072]{2,1,0:T(8,128)(2,1)S(1)} custom-call(bf16[384,768]{1,0:T(8,128)(2,1)S(1)} %get-tuple-element.92.act_ref.refs_2_, bf16[384,768]{1,0:T(8,128)(2,1)S(1)} %get-tuple-element.94.grad_ref.refs_4_, bf16[3072,768]{1,0:T(8,128)(2,1)S(1)} %pad_maximum_fusion.up_ref, bf16[768,3072]{1,0:T(8,128)(2,1)S(1)} %pad_maximum_fusion.1.down_ref), custom_call_target="tpu_custom_call" | custom-call | flops 1 | bytes 1 | tf_op jit(solution)/shard_map/pallas_call | solution.py:30
  93.9 6.6 %shard_map.79 = (bf16[3,384,768]{2,1,0:T(8,128)(2,1)S(1)}, bf16[3,768,384]{2,1,0:T(8,128)(2,1)}, bf16[384,768]{1,0:T(8,128)(2,1)S(1)}, bf16[768,384]{1,0:T(8,128)(2,1)S(1)}) custom-call(bf16[2,384,3072]{2,1,0:T(8,128)(2,1)S(1)} %constant_dynamic-update-slice_fusion.pair_ref.refs_0_, ...), custom_call_target="tpu_custom_call" | custom-call | flops 1 | bytes 1 | tf_op jit(solution)/shard_map/pallas_call | solution.py:30
  100.5 1.2 copy-done.3
  103.8 2.6 %collective-permute-start.23 = (bf16[2,128,3072]{2,1,0:T(8,128)(2,1)S(1)}, bf16[2,128,3072]{2,1,0:T(8,128)(2,1)S(1)}, u32[]{:S(2)}, u32[]{:S(2)}) collective-permute-start(bf16[2,128,3072]{2,1,0:T(8,128)(2,1)S(1)} %pad_maximum_fusion.8), channel_id=1, source_target_pairs={{0,3},{1,0},{2,1},{3,2},{4,7},{5,4},{6,5},{7,6},{8,11},{9,8},{10,9... | collective-permute-start | bytes 4718600 | tf_op jit(solution)/shard_map/ppermute | solution.py:179
  107.4 5.7 %shard_map.80 = (bf16[4,384,768]{2,1,0:T(8,128)(2,1)S(1)}, bf16[4,768,384]{2,1,0:T(8,128)(2,1)S(1)}) custom-call(bf16[2,384,3072]{2,1,0:T(8,128)(2,1)S(1)} %constant_dynamic-update-slice_fusion.pair_ref.refs_0_, bf16[2,128,3072]{2,1,0:T(8,128)(2,1)S(1)} %constant_dynamic-update-slice_fusion.6.pair_ref.refs_1_, ...), custom_call_target="tpu_custom_call" | custom-call | flops 1 | bytes 1 | tf_op jit(solution)/shard_map/pallas_call | solution.py:30
  113.4 1.1 copy-done.1
  114.6 2.4 %collective-permute-start.26 = (bf16[384,768]{1,0:T(8,128)(2,1)S(1)}, bf16[384,768]{1,0:T(8,128)(2,1)S(1)}, u32[]{:S(2)}, u32[]{:S(2)}) collective-permute-start(bf16[384,768]{1,0:T(8,128)(2,1)S(1)} %fusion.1), channel_id=1, source_target_pairs={{0,96},{16,48},{32,0},{48,80},{64,32},{80,112},{96,64},{112,16},{1... | collective-permute-start | bytes 1769480 | tf_op jit(solution)/shard_map/ppermute | solution.py:162
  117.0 13.2 %collective-permute-done.28 = bf16[768,384]{1,0:T(8,128)(2,1)S(1)} collective-permute-done((bf16[768,384]{1,0:T(8,128)(2,1)S(1)}, bf16[768,384]{1,0:T(8,128)(2,1)S(1)}, u32[]{:S(2)}, u32[]{:S(2)}) %collective-permute-start.28) | collective-permute-done | bytes 589856 | tf_op jit(solution)/shard_map/ppermute | solution.py:162
  130.2 1.1 copy-done.6
  131.3 1.2 copy-done.7
  133.0 3.1 %add_convert_fusion = bf16[2,128,3072]{2,1,0:T(8,128)(2,1)S(1)} fusion(bf16[2,128,3072]{2,1,0:T(8,128)(2,1)} %copy-done.6, bf16[2,128,3072]{2,1,0:T(8,128)(2,1)} %copy-done.7, bf16[2,384,3072]{2,1,0:T(8,128)(2,1)} %copy-done), kind=kLoop, calls=%fused_computation.2 | loop fusion | flops 4718592 | bytes 6291456 | tf_op jit(solution)/shard_map/convert_element_type | solution.py:292
  136.3 3.0 %collective-permute-start.29 = (bf16[2,32,3072]{2,1,0:T(8,128)(2,1)S(1)}, bf16[2,32,3072]{2,1,0:T(8,128)(2,1)S(1)}, u32[]{:S(2)}, u32[]{:S(2)}) collective-permute-start(bf16[2,32,3072]{2,1,0:T(8,128)(2,1)S(1)} %get-tuple-element.127), channel_id=1, source_target_pairs={{0,12},{1,13},{2,14},{3,15},{4,0},{5,1},{6,2},{7,3},{8,4},{9,5},{1... | collective-permute-start | bytes 1179656 | tf_op jit(solution)/shard_map/ppermute | solution.py:179
  139.3 1.3 collective-permute-start.31
  140.6 1.3 fusion.4
  142.2 3.3 %collective-permute-start.33 = (bf16[384,768]{1,0:T(8,128)(2,1)S(1)}, bf16[384,768]{1,0:T(8,128)(2,1)S(1)}, u32[]{:S(2)}, u32[]{:S(2)}) collective-permute-start(bf16[384,768]{1,0:T(8,128)(2,1)S(1)} %fusion.5), channel_id=1, source_target_pairs={{0,96},{16,48},{32,0},{48,80},{64,32},{80,112},{96,64},{112,16},{1... | collective-permute-start | bytes 1769480 | tf_op jit(solution)/shard_map/ppermute | solution.py:162
  145.5 3.3 %collective-permute-done.29 = bf16[2,32,3072]{2,1,0:T(8,128)(2,1)S(1)} collective-permute-done((bf16[2,32,3072]{2,1,0:T(8,128)(2,1)S(1)}, bf16[2,32,3072]{2,1,0:T(8,128)(2,1)S(1)}, u32[]{:S(2)}, u32[]{:S(2)}) %collective-permute-start.29) | collective-permute-done | bytes 393248 | tf_op jit(solution)/shard_map/ppermute | solution.py:179
  148.8 3.7 %collective-permute-done.31 = bf16[2,32,3072]{2,1,0:T(8,128)(2,1)S(1)} collective-permute-done((bf16[2,32,3072]{2,1,0:T(8,128)(2,1)S(1)}, bf16[2,32,3072]{2,1,0:T(8,128)(2,1)S(1)}, u32[]{:S(2)}, u32[]{:S(2)}) %collective-permute-start.31) | collective-permute-done | bytes 393248 | tf_op jit(solution)/shard_map/ppermute | solution.py:179
  152.7 5.4 %collective-permute-done.35 = bf16[768,384]{1,0:T(8,128)(2,1)S(1)} collective-permute-done((bf16[768,384]{1,0:T(8,128)(2,1)S(1)}, bf16[768,384]{1,0:T(8,128)(2,1)S(1)}, u32[]{:S(2)}, u32[]{:S(2)}) %collective-permute-start.35) | collective-permute-done | bytes 589856 | tf_op jit(solution)/shard_map/ppermute | solution.py:162
  158.4 1.3 fusion.3
  159.7 2.1 %collective-permute-start.39 = (bf16[768,384]{1,0:T(8,128)(2,1)S(1)}, bf16[768,384]{1,0:T(8,128)(2,1)S(1)}, u32[]{:S(2)}, u32[]{:S(2)}) collective-permute-start(bf16[768,384]{1,0:T(8,128)(2,1)S(1)} %fusion.3), channel_id=1, source_target_pairs={{0,32},{16,112},{32,64},{48,16},{64,96},{80,48},{96,0},{112,80},{1... | collective-permute-start | bytes 1769480 | tf_op jit(solution)/shard_map/ppermute | solution.py:162
  162.0 2.7 %collective-permute-start.37 = (bf16[2,32,768]{2,1,0:T(8,128)(2,1)S(1)}, bf16[2,32,768]{2,1,0:T(8,128)(2,1)S(1)}, u32[]{:S(2)}, u32[]{:S(2)}) collective-permute-start(bf16[2,32,768]{2,1,0:T(8,128)(2,1)S(1)} %pad_maximum_fusion.13), channel_id=1, source_target_pairs={{0,64},{16,80},{32,96},{48,112},{64,0},{80,16},{96,32},{112,48},{1... | collective-permute-start | bytes 294920 | tf_op jit(solution)/shard_map/ppermute | solution.py:162
  165.4 13.4 %collective-permute-done.36 = bf16[2,32,768]{2,1,0:T(8,128)(2,1)S(1)} collective-permute-done((bf16[2,32,768]{2,1,0:T(8,128)(2,1)S(1)}, bf16[2,32,768]{2,1,0:T(8,128)(2,1)S(1)}, u32[]{:S(2)}, u32[]{:S(2)}) %collective-permute-start.36) | collective-permute-done | bytes 98336 | tf_op jit(solution)/shard_map/ppermute | solution.py:162
  179.6 1.2 bitcast_add_fusion.1
  180.9 2.3 %bitcast_add_fusion.3 = f32[768,384]{1,0:T(8,128)} fusion(bf16[768,384]{1,0:T(8,128)(2,1)S(1)} %collective-permute-done.39, bf16[3,768,384]{2,1,0:T(8,128)(2,1)} %collective-permute-done.34, bf16[4,768,384]{2,1,0:T(8,128)(2,1)S(1)} %get-tuple-element.107), kind=kLoop, calls=%fused_computation.23 | loop fusion | flops 1474560 | bytes 2949120 | tf_op jit(solution)/shard_map/add | solution.py:271
  (117 shorter events, 18.1 us)
Async XLA Ops:
  1.7 9.1 %collective-permute-start = (bf16[2,32,768]{2,1,0:T(8,128)(2,1)S(1)}, bf16[2,32,768]{2,1,0:T(8,128)(2,1)S(1)}, u32[]{:S(2)}, u32[]{:S(2)}) collective-permute-start(bf16[2,32,768]{2,1,0:T(8,128)(2,1)S(1)} %get-tuple-element.141), channel_id=1, source_target_pairs={{0,32},{16,112},{32,64},{48,16},{64,96},{80,48},{96,0},{112,80},{1... | collective-permute-start | bytes 294920 | tf_op jit(solution)/shard_map/ppermute | solution.py:162
  3.4 7.9 %collective-permute-start.1 = (bf16[2,32,768]{2,1,0:T(8,128)(2,1)S(1)}, bf16[2,32,768]{2,1,0:T(8,128)(2,1)S(1)}, u32[]{:S(2)}, u32[]{:S(2)}) collective-permute-start(bf16[2,32,768]{2,1,0:T(8,128)(2,1)S(1)} %get-tuple-element.142), channel_id=1, source_target_pairs={{0,64},{16,80},{32,96},{48,112},{64,0},{80,16},{96,32},{112,48},{1... | collective-permute-start | bytes 294920 | tf_op jit(solution)/shard_map/ppermute | solution.py:162
  6.1 5.7 %collective-permute-start.2 = (bf16[2,32,768]{2,1,0:T(8,128)(2,1)S(1)}, bf16[2,32,768]{2,1,0:T(8,128)(2,1)S(1)}, u32[]{:S(2)}, u32[]{:S(2)}) collective-permute-start(bf16[2,32,768]{2,1,0:T(8,128)(2,1)S(1)} %get-tuple-element.143), channel_id=1, source_target_pairs={{0,96},{16,48},{32,0},{48,80},{64,32},{80,112},{96,64},{112,16},{1... | collective-permute-start | bytes 294920 | tf_op jit(solution)/shard_map/ppermute | solution.py:162
  7.5 16.6 %collective-permute-start.8 = (bf16[768,384]{1,0:T(8,128)(2,1)}, bf16[768,384]{1,0:T(8,128)(2,1)S(1)}, u32[]{:S(2)}, u32[]{:S(2)}) collective-permute-start(bf16[768,384]{1,0:T(8,128)(2,1)} %param.5), channel_id=1, source_target_pairs={{0,32},{16,112},{32,64},{48,16},{64,96},{80,48},{96,0},{112,80},{1... | collective-permute-start | bytes 1769480 | tf_op jit(solution)/shard_map/ppermute | solution.py:162
  8.1 16.1 %collective-permute-start.9 = (bf16[384,768]{1,0:T(8,128)(2,1)}, bf16[384,768]{1,0:T(8,128)(2,1)S(1)}, u32[]{:S(2)}, u32[]{:S(2)}) collective-permute-start(bf16[384,768]{1,0:T(8,128)(2,1)} %param.6), channel_id=1, source_target_pairs={{0,96},{16,48},{32,0},{48,80},{64,32},{80,112},{96,64},{112,16},{1... | collective-permute-start | bytes 1769480 | tf_op jit(solution)/shard_map/ppermute | solution.py:162
  11.9 19.1 %copy-start.5 = (bf16[768,384]{1,0:T(8,128)(2,1)S(1)}, bf16[768,384]{1,0:T(8,128)(2,1)}, u32[]{:S(2)}) copy-start(bf16[768,384]{1,0:T(8,128)(2,1)} %param.5) | copy-start | bytes 1769476
  12.0 15.4 %collective-permute-start.3 = (bf16[2,32,3072]{2,1,0:T(8,128)(2,1)S(1)}, bf16[2,32,3072]{2,1,0:T(8,128)(2,1)S(1)}, u32[]{:S(2)}, u32[]{:S(2)}) collective-permute-start(bf16[2,32,3072]{2,1,0:T(8,128)(2,1)S(1)} %get-tuple-element.139), channel_id=1, source_target_pairs={{0,4},{1,5},{2,6},{3,7},{4,8},{5,9},{6,10},{7,11},{8,12},{9,13},{1... | collective-permute-start | bytes 1179656 | tf_op jit(solution)/shard_map/ppermute | solution.py:179
  13.9 13.5 %collective-permute-start.4 = (bf16[2,32,3072]{2,1,0:T(8,128)(2,1)S(1)}, bf16[2,32,3072]{2,1,0:T(8,128)(2,1)S(1)}, u32[]{:S(2)}, u32[]{:S(2)}) collective-permute-start(bf16[2,32,3072]{2,1,0:T(8,128)(2,1)S(1)} %get-tuple-element.139), channel_id=1, source_target_pairs={{0,8},{1,9},{2,10},{3,11},{4,12},{5,13},{6,14},{7,15},{8,0},{9,1},... | collective-permute-start | bytes 1179656 | tf_op jit(solution)/shard_map/ppermute | solution.py:179
  17.5 10.0 %collective-permute-start.5 = (bf16[2,32,3072]{2,1,0:T(8,128)(2,1)S(1)}, bf16[2,32,3072]{2,1,0:T(8,128)(2,1)S(1)}, u32[]{:S(2)}, u32[]{:S(2)}) collective-permute-start(bf16[2,32,3072]{2,1,0:T(8,128)(2,1)S(1)} %get-tuple-element.139), channel_id=1, source_target_pairs={{0,12},{1,13},{2,14},{3,15},{4,0},{5,1},{6,2},{7,3},{8,4},{9,5},{1... | collective-permute-start | bytes 1179656 | tf_op jit(solution)/shard_map/ppermute | solution.py:179
  24.2 17.2 %collective-permute-start.11 = (bf16[768,384]{1,0:T(8,128)(2,1)S(1)}, bf16[768,384]{1,0:T(8,128)(2,1)S(1)}, u32[]{:S(2)}, u32[]{:S(2)}) collective-permute-start(bf16[768,384]{1,0:T(8,128)(2,1)S(1)} %collective-permute-done.8), channel_id=1, source_target_pairs={{0,32},{16,112},{32,64},{48,16},{64,96},{80,48},{96,0},{112,80},{1... | collective-permute-start | bytes 1769480 | tf_op jit(solution)/shard_map/ppermute | solution.py:162
  24.2 17.2 %collective-permute-start.12 = (bf16[384,768]{1,0:T(8,128)(2,1)S(1)}, bf16[384,768]{1,0:T(8,128)(2,1)S(1)}, u32[]{:S(2)}, u32[]{:S(2)}) collective-permute-start(bf16[384,768]{1,0:T(8,128)(2,1)S(1)} %collective-permute-done.9), channel_id=1, source_target_pairs={{0,96},{16,48},{32,0},{48,80},{64,32},{80,112},{96,64},{112,16},{1... | collective-permute-start | bytes 1769480 | tf_op jit(solution)/shard_map/ppermute | solution.py:162
  27.6 30.6 %copy-start.4 = (bf16[384,768]{1,0:T(8,128)(2,1)S(1)}, bf16[384,768]{1,0:T(8,128)(2,1)}, u32[]{:S(2)}) copy-start(bf16[384,768]{1,0:T(8,128)(2,1)} %param.6) | copy-start | bytes 1769476
  27.6 30.9 %collective-permute-start.6 = (bf16[2,128,3072]{2,1,0:T(8,128)(2,1)S(1)}, bf16[2,128,3072]{2,1,0:T(8,128)(2,1)S(1)}, u32[]{:S(2)}, u32[]{:S(2)}) collective-permute-start(bf16[2,128,3072]{2,1,0:T(8,128)(2,1)S(1)} %pad_maximum_fusion.7), channel_id=1, source_target_pairs={{0,1},{1,2},{2,3},{3,0},{4,5},{5,6},{6,7},{7,4},{8,9},{9,10},{10,1... | collective-permute-start | bytes 4718600 | tf_op jit(solution)/shard_map/ppermute | solution.py:179
  29.3 29.7 %collective-permute-start.7 = (bf16[2,128,3072]{2,1,0:T(8,128)(2,1)S(1)}, bf16[2,128,3072]{2,1,0:T(8,128)(2,1)S(1)}, u32[]{:S(2)}, u32[]{:S(2)}) collective-permute-start(bf16[2,128,3072]{2,1,0:T(8,128)(2,1)S(1)} %pad_maximum_fusion.7), channel_id=1, source_target_pairs={{0,3},{1,0},{2,1},{3,2},{4,7},{5,4},{6,5},{7,6},{8,11},{9,8},{10,9... | collective-permute-start | bytes 4718600 | tf_op jit(solution)/shard_map/ppermute | solution.py:179
  31.0 27.3 %collective-permute-start.10 = (bf16[1536,384]{1,0:T(8,128)(2,1)S(1)}, bf16[1536,384]{1,0:T(8,128)(2,1)S(1)}, u32[]{:S(2)}, u32[]{:S(2)}) collective-permute-start(bf16[1536,384]{1,0:T(8,128)(2,1)S(1)} %pad_maximum_fusion.10), channel_id=1, source_target_pairs={{0,16},{16,0},{1,17},{17,1},{2,18},{18,2},{3,19},{19,3},{4,20},{20... | collective-permute-start | bytes 3538952 | tf_op jit(solution)/shard_map/ppermute | solution.py:166
  41.4 16.3 %collective-permute-start.13 = (bf16[768,384]{1,0:T(8,128)(2,1)S(1)}, bf16[768,384]{1,0:T(8,128)(2,1)S(1)}, u32[]{:S(2)}, u32[]{:S(2)}) collective-permute-start(bf16[768,384]{1,0:T(8,128)(2,1)S(1)} %collective-permute-done.11), channel_id=1, source_target_pairs={{0,32},{16,112},{32,64},{48,16},{64,96},{80,48},{96,0},{112,80},{1... | collective-permute-start | bytes 1769480 | tf_op jit(solution)/shard_map/ppermute | solution.py:162
  41.4 16.3 %collective-permute-start.15 = (bf16[384,768]{1,0:T(8,128)(2,1)S(1)}, bf16[384,768]{1,0:T(8,128)(2,1)S(1)}, u32[]{:S(2)}, u32[]{:S(2)}) collective-permute-start(bf16[384,768]{1,0:T(8,128)(2,1)S(1)} %collective-permute-done.12), channel_id=1, source_target_pairs={{0,96},{16,48},{32,0},{48,80},{64,32},{80,112},{96,64},{112,16},{1... | collective-permute-start | bytes 1769480 | tf_op jit(solution)/shard_map/ppermute | solution.py:162
  57.7 2.0 %collective-permute-start.14 = (bf16[768,384]{1,0:T(8,128)(2,1)S(1)}, bf16[768,384]{1,0:T(8,128)(2,1)S(1)}, u32[]{:S(2)}, u32[]{:S(2)}) collective-permute-start(bf16[768,384]{1,0:T(8,128)(2,1)S(1)} %collective-permute-done.13), channel_id=1, source_target_pairs={{0,16},{16,0},{1,17},{17,1},{2,18},{18,2},{3,19},{19,3},{4,20},{20... | collective-permute-start | bytes 1769480 | tf_op jit(solution)/shard_map/ppermute | solution.py:166
  57.7 2.8 %collective-permute-start.16 = (bf16[384,768]{1,0:T(8,128)(2,1)S(1)}, bf16[384,768]{1,0:T(8,128)(2,1)S(1)}, u32[]{:S(2)}, u32[]{:S(2)}) collective-permute-start(bf16[384,768]{1,0:T(8,128)(2,1)S(1)} %collective-permute-done.15), channel_id=1, source_target_pairs={{0,16},{16,0},{1,17},{17,1},{2,18},{18,2},{3,19},{19,3},{4,20},{20... | collective-permute-start | bytes 1769480 | tf_op jit(solution)/shard_map/ppermute | solution.py:166
  58.4 3.0 %collective-permute-start.19 = (bf16[768,384]{1,0:T(8,128)(2,1)S(1)}, bf16[768,384]{1,0:T(8,128)(2,1)S(1)}, u32[]{:S(2)}, u32[]{:S(2)}) collective-permute-start(bf16[768,384]{1,0:T(8,128)(2,1)S(1)} %collective-permute-done.11), channel_id=1, source_target_pairs={{0,16},{16,0},{1,17},{17,1},{2,18},{18,2},{3,19},{19,3},{4,20},{20... | collective-permute-start | bytes 1769480 | tf_op jit(solution)/shard_map/ppermute | solution.py:166
  58.5 9.2 %collective-permute-start.20 = (bf16[384,2304]{1,0:T(8,128)(2,1)S(1)}, bf16[384,2304]{1,0:T(8,128)(2,1)S(1)}, u32[]{:S(2)}, u32[]{:S(2)}) collective-permute-start(bf16[384,2304]{1,0:T(8,128)(2,1)S(1)} %pad_maximum_fusion.6), channel_id=1, source_target_pairs={{0,16},{16,0},{1,17},{17,1},{2,18},{18,2},{3,19},{19,3},{4,20},{20... | collective-permute-start | bytes 5308424 | tf_op jit(solution)/shard_map/ppermute | solution.py:166
  62.6 13.4 %collective-permute-start.17 = (bf16[2,64,3072]{2,1,0:T(8,128)(2,1)}, bf16[2,64,3072]{2,1,0:T(8,128)(2,1)S(1)}, u32[]{:S(2)}, u32[]{:S(2)}) collective-permute-start(bf16[2,64,3072]{2,1,0:T(8,128)(2,1)} %slice.178), channel_id=1, source_target_pairs={{0,1},{1,2},{2,3},{3,0},{4,5},{5,6},{6,7},{7,4},{8,9},{9,10},{10,1... | collective-permute-start | bytes 2359304 | tf_op jit(solution)/shard_map/ppermute | solution.py:179
  65.1 12.3 %collective-permute-start.18 = (bf16[2,64,3072]{2,1,0:T(8,128)(2,1)}, bf16[2,64,3072]{2,1,0:T(8,128)(2,1)}, u32[]{:S(2)}, u32[]{:S(2)}) collective-permute-start(bf16[2,64,3072]{2,1,0:T(8,128)(2,1)} %slice.179), channel_id=1, source_target_pairs={{0,3},{1,0},{2,1},{3,2},{4,7},{5,4},{6,5},{7,6},{8,11},{9,8},{10,9... | collective-permute-start | bytes 2359304 | tf_op jit(solution)/shard_map/ppermute | solution.py:179
  76.0 1.4 copy-start.8
  85.9 15.7 %collective-permute-start.21 = (bf16[2,64,3072]{2,1,0:T(8,128)(2,1)S(1)}, bf16[2,64,3072]{2,1,0:T(8,128)(2,1)S(1)}, u32[]{:S(2)}, u32[]{:S(2)}) collective-permute-start(bf16[2,64,3072]{2,1,0:T(8,128)(2,1)S(1)} %get-tuple-element.87), channel_id=1, source_target_pairs={{0,3},{1,0},{2,1},{3,2},{4,7},{5,4},{6,5},{7,6},{8,11},{9,8},{10,9... | collective-permute-start | bytes 2359304 | tf_op jit(solution)/shard_map/ppermute | solution.py:179
  88.9 13.2 %collective-permute-start.22 = (bf16[2,64,3072]{2,1,0:T(8,128)(2,1)S(1)}, bf16[2,64,3072]{2,1,0:T(8,128)(2,1)S(1)}, u32[]{:S(2)}, u32[]{:S(2)}) collective-permute-start(bf16[2,64,3072]{2,1,0:T(8,128)(2,1)S(1)} %get-tuple-element.88), channel_id=1, source_target_pairs={{0,1},{1,2},{2,3},{3,0},{4,5},{5,6},{6,7},{7,4},{8,9},{9,10},{10,1... | collective-permute-start | bytes 2359304 | tf_op jit(solution)/shard_map/ppermute | solution.py:179
  93.9 8.3 %copy-start = (bf16[2,384,3072]{2,1,0:T(8,128)(2,1)}, bf16[2,384,3072]{2,1,0:T(8,128)(2,1)S(1)}, u32[]{:S(2)}) copy-start(bf16[2,384,3072]{2,1,0:T(8,128)(2,1)S(1)} %shard_map.78) | copy-start | bytes 14155780
  100.5 1.2 copy-start.3
  103.0 10.1 %collective-permute-start.27 = (bf16[768,384]{1,0:T(8,128)(2,1)S(1)}, bf16[768,384]{1,0:T(8,128)(2,1)S(1)}, u32[]{:S(2)}, u32[]{:S(2)}) collective-permute-start(bf16[768,384]{1,0:T(8,128)(2,1)S(1)} %get-tuple-element.108), channel_id=1, source_target_pairs={{0,16},{16,0},{1,17},{17,1},{2,18},{18,2},{3,19},{19,3},{4,20},{20... | collective-permute-start | bytes 1769480 | tf_op jit(solution)/shard_map/ppermute | solution.py:166
  103.1 27.1 %collective-permute-start.24 = (bf16[2,128,3072]{2,1,0:T(8,128)(2,1)S(1)}, bf16[2,128,3072]{2,1,0:T(8,128)(2,1)S(1)}, u32[]{:S(2)}, u32[]{:S(2)}) collective-permute-start(bf16[2,128,3072]{2,1,0:T(8,128)(2,1)S(1)} %pad_maximum_fusion.9), channel_id=1, source_target_pairs={{0,1},{1,2},{2,3},{3,0},{4,5},{5,6},{6,7},{7,4},{8,9},{9,10},{10,1... | collective-permute-start | bytes 4718600 | tf_op jit(solution)/shard_map/ppermute | solution.py:179
  103.8 26.4 %collective-permute-start.23 = (bf16[2,128,3072]{2,1,0:T(8,128)(2,1)S(1)}, bf16[2,128,3072]{2,1,0:T(8,128)(2,1)S(1)}, u32[]{:S(2)}, u32[]{:S(2)}) collective-permute-start(bf16[2,128,3072]{2,1,0:T(8,128)(2,1)S(1)} %pad_maximum_fusion.8), channel_id=1, source_target_pairs={{0,3},{1,0},{2,1},{3,2},{4,7},{5,4},{6,5},{7,6},{8,11},{9,8},{10,9... | collective-permute-start | bytes 4718600 | tf_op jit(solution)/shard_map/ppermute | solution.py:179
  106.4 6.9 %collective-permute-start.25 = (bf16[384,768]{1,0:T(8,128)(2,1)S(1)}, bf16[384,768]{1,0:T(8,128)(2,1)S(1)}, u32[]{:S(2)}, u32[]{:S(2)}) collective-permute-start(bf16[384,768]{1,0:T(8,128)(2,1)S(1)} %get-tuple-element.106), channel_id=1, source_target_pairs={{0,16},{16,0},{1,17},{17,1},{2,18},{18,2},{3,19},{19,3},{4,20},{20... | collective-permute-start | bytes 1769480 | tf_op jit(solution)/shard_map/ppermute | solution.py:166
  113.1 1.4 copy-start.1
  113.3 16.9 %collective-permute-start.28 = (bf16[768,384]{1,0:T(8,128)(2,1)S(1)}, bf16[768,384]{1,0:T(8,128)(2,1)S(1)}, u32[]{:S(2)}, u32[]{:S(2)}) collective-permute-start(bf16[768,384]{1,0:T(8,128)(2,1)S(1)} %fusion), channel_id=1, source_target_pairs={{0,32},{16,112},{32,64},{48,16},{64,96},{80,48},{96,0},{112,80},{1... | collective-permute-start | bytes 1769480 | tf_op jit(solution)/shard_map/ppermute | solution.py:162
  114.6 15.6 %collective-permute-start.26 = (bf16[384,768]{1,0:T(8,128)(2,1)S(1)}, bf16[384,768]{1,0:T(8,128)(2,1)S(1)}, u32[]{:S(2)}, u32[]{:S(2)}) collective-permute-start(bf16[384,768]{1,0:T(8,128)(2,1)S(1)} %fusion.1), channel_id=1, source_target_pairs={{0,96},{16,48},{32,0},{48,80},{64,32},{80,112},{96,64},{112,16},{1... | collective-permute-start | bytes 1769480 | tf_op jit(solution)/shard_map/ppermute | solution.py:162
  132.5 8.1 %collective-permute-start.34 = (bf16[3,768,384]{2,1,0:T(8,128)(2,1)}, bf16[3,768,384]{2,1,0:T(8,128)(2,1)}, u32[]{:S(2)}, u32[]{:S(2)}) collective-permute-start(bf16[3,768,384]{2,1,0:T(8,128)(2,1)} %get-tuple-element.115), channel_id=1, source_target_pairs={{0,16},{16,0},{1,17},{17,1},{2,18},{18,2},{3,19},{19,3},{4,20},{20... | collective-permute-start | bytes 5308424 | tf_op jit(solution)/shard_map/ppermute | solution.py:166
  132.9 9.1 %collective-permute-start.32 = (bf16[3,384,768]{2,1,0:T(8,128)(2,1)}, bf16[3,384,768]{2,1,0:T(8,128)(2,1)S(1)}, u32[]{:S(2)}, u32[]{:S(2)}) collective-permute-start(bf16[3,384,768]{2,1,0:T(8,128)(2,1)} %copy-done.3), channel_id=1, source_target_pairs={{0,16},{16,0},{1,17},{17,1},{2,18},{18,2},{3,19},{19,3},{4,20},{20... | collective-permute-start | bytes 5308424 | tf_op jit(solution)/shard_map/ppermute | solution.py:166
  136.2 5.8 %copy-start.2 = (bf16[4,384,768]{2,1,0:T(8,128)(2,1)S(1)}, bf16[4,384,768]{2,1,0:T(8,128)(2,1)}, u32[]{:S(2)}) copy-start(bf16[4,384,768]{2,1,0:T(8,128)(2,1)} %copy-done.1) | copy-start | bytes 7077892
  136.3 12.5 %collective-permute-start.29 = (bf16[2,32,3072]{2,1,0:T(8,128)(2,1)S(1)}, bf16[2,32,3072]{2,1,0:T(8,128)(2,1)S(1)}, u32[]{:S(2)}, u32[]{:S(2)}) collective-permute-start(bf16[2,32,3072]{2,1,0:T(8,128)(2,1)S(1)} %get-tuple-element.127), channel_id=1, source_target_pairs={{0,12},{1,13},{2,14},{3,15},{4,0},{5,1},{6,2},{7,3},{8,4},{9,5},{1... | collective-permute-start | bytes 1179656 | tf_op jit(solution)/shard_map/ppermute | solution.py:179
  139.3 9.5 %collective-permute-start.30 = (bf16[2,32,3072]{2,1,0:T(8,128)(2,1)S(1)}, bf16[2,32,3072]{2,1,0:T(8,128)(2,1)S(1)}, u32[]{:S(2)}, u32[]{:S(2)}) collective-permute-start(bf16[2,32,3072]{2,1,0:T(8,128)(2,1)S(1)} %get-tuple-element.128), channel_id=1, source_target_pairs={{0,8},{1,9},{2,10},{3,11},{4,12},{5,13},{6,14},{7,15},{8,0},{9,1},... | collective-permute-start | bytes 1179656 | tf_op jit(solution)/shard_map/ppermute | solution.py:179
  139.3 13.2 %collective-permute-start.31 = (bf16[2,32,3072]{2,1,0:T(8,128)(2,1)S(1)}, bf16[2,32,3072]{2,1,0:T(8,128)(2,1)S(1)}, u32[]{:S(2)}, u32[]{:S(2)}) collective-permute-start(bf16[2,32,3072]{2,1,0:T(8,128)(2,1)S(1)} %get-tuple-element.129), channel_id=1, source_target_pairs={{0,4},{1,5},{2,6},{3,7},{4,8},{5,9},{6,10},{7,11},{8,12},{9,13},{1... | collective-permute-start | bytes 1179656 | tf_op jit(solution)/shard_map/ppermute | solution.py:179
  141.9 16.2 %collective-permute-start.35 = (bf16[768,384]{1,0:T(8,128)(2,1)S(1)}, bf16[768,384]{1,0:T(8,128)(2,1)S(1)}, u32[]{:S(2)}, u32[]{:S(2)}) collective-permute-start(bf16[768,384]{1,0:T(8,128)(2,1)S(1)} %fusion.4), channel_id=1, source_target_pairs={{0,32},{16,112},{32,64},{48,16},{64,96},{80,48},{96,0},{112,80},{1... | collective-permute-start | bytes 1769480 | tf_op jit(solution)/shard_map/ppermute | solution.py:162
  142.2 15.9 %collective-permute-start.33 = (bf16[384,768]{1,0:T(8,128)(2,1)S(1)}, bf16[384,768]{1,0:T(8,128)(2,1)S(1)}, u32[]{:S(2)}, u32[]{:S(2)}) collective-permute-start(bf16[384,768]{1,0:T(8,128)(2,1)S(1)} %fusion.5), channel_id=1, source_target_pairs={{0,96},{16,48},{32,0},{48,80},{64,32},{80,112},{96,64},{112,16},{1... | collective-permute-start | bytes 1769480 | tf_op jit(solution)/shard_map/ppermute | solution.py:162
  158.3 21.3 %collective-permute-start.40 = (bf16[384,768]{1,0:T(8,128)(2,1)S(1)}, bf16[384,768]{1,0:T(8,128)(2,1)S(1)}, u32[]{:S(2)}, u32[]{:S(2)}) collective-permute-start(bf16[384,768]{1,0:T(8,128)(2,1)S(1)} %fusion.2), channel_id=1, source_target_pairs={{0,96},{16,48},{32,0},{48,80},{64,32},{80,112},{96,64},{112,16},{1... | collective-permute-start | bytes 1769480 | tf_op jit(solution)/shard_map/ppermute | solution.py:162
  159.7 21.2 %collective-permute-start.39 = (bf16[768,384]{1,0:T(8,128)(2,1)S(1)}, bf16[768,384]{1,0:T(8,128)(2,1)S(1)}, u32[]{:S(2)}, u32[]{:S(2)}) collective-permute-start(bf16[768,384]{1,0:T(8,128)(2,1)S(1)} %fusion.3), channel_id=1, source_target_pairs={{0,32},{16,112},{32,64},{48,16},{64,96},{80,48},{96,0},{112,80},{1... | collective-permute-start | bytes 1769480 | tf_op jit(solution)/shard_map/ppermute | solution.py:162
  161.9 17.0 %collective-permute-start.38 = (bf16[2,32,768]{2,1,0:T(8,128)(2,1)S(1)}, bf16[2,32,768]{2,1,0:T(8,128)(2,1)S(1)}, u32[]{:S(2)}, u32[]{:S(2)}) collective-permute-start(bf16[2,32,768]{2,1,0:T(8,128)(2,1)S(1)} %pad_maximum_fusion.14), channel_id=1, source_target_pairs={{0,32},{16,112},{32,64},{48,16},{64,96},{80,48},{96,0},{112,80},{1... | collective-permute-start | bytes 294920 | tf_op jit(solution)/shard_map/ppermute | solution.py:162
  162.0 16.8 %collective-permute-start.37 = (bf16[2,32,768]{2,1,0:T(8,128)(2,1)S(1)}, bf16[2,32,768]{2,1,0:T(8,128)(2,1)S(1)}, u32[]{:S(2)}, u32[]{:S(2)}) collective-permute-start(bf16[2,32,768]{2,1,0:T(8,128)(2,1)S(1)} %pad_maximum_fusion.13), channel_id=1, source_target_pairs={{0,64},{16,80},{32,96},{48,112},{64,0},{80,16},{96,32},{112,48},{1... | collective-permute-start | bytes 294920 | tf_op jit(solution)/shard_map/ppermute | solution.py:162
  164.7 14.1 %collective-permute-start.36 = (bf16[2,32,768]{2,1,0:T(8,128)(2,1)S(1)}, bf16[2,32,768]{2,1,0:T(8,128)(2,1)S(1)}, u32[]{:S(2)}, u32[]{:S(2)}) collective-permute-start(bf16[2,32,768]{2,1,0:T(8,128)(2,1)S(1)} %pad_maximum_fusion.12), channel_id=1, source_target_pairs={{0,96},{16,48},{32,0},{48,80},{64,32},{80,112},{96,64},{112,16},{1... | collective-permute-start | bytes 294920 | tf_op jit(solution)/shard_map/ppermute | solution.py:162
  (4 other events, 4.2 us)

commit v7 on v5

--- a/solution.py
+++ b/solution.py
@@ -262,7 +262,7 @@
     down_theirs, up_theirs = swap(3, near_sent)
     down_grad = along_x(total(mine[0][1], down_theirs).astype(BF), -1)
     up_grad = along_x(total(mine[1][1], up_theirs).astype(BF), 1)
-    left, right, down_grad, up_grad = held(left, right, down_grad, up_grad)
+    left, right = held(left, right)
 
     down_theirs, up_theirs = swap(slice(0, 3), left)
     down_grad = along_x(total(mine[0][2], down_theirs[2], down_grad).astype(BF), -1)

time: 178 us -> 179 us (level)
  starting transfers between devices: 55.2 us -> 52.1 us
  other arithmetic: 14.2 us -> 17.2 us
  waiting for transfers between devices: 72.9 us -> 70.9 us
    ppermute x18, waiting for transfers between devices: 56.8 us -> 50.1 us  [along_x(): return lax.ppermute(value, ('row', 'col'), pairs)]
    ppermute x14, waiting for transfers between devices: 14 us -> 18.6 us  [plane(): return lax.ppermute(value, ('col', 'depth'), pairs)]
    concatenate x11, other arithmetic: 2.31 us -> 6.12 us  [join(): return jnp.concatenate(parts, axis=axis)]
    ppermute x18, starting transfers between devices: 28.1 us -> 24.7 us  [along_x(): return lax.ppermute(value, ('row', 'col'), pairs)]
    unnamed x19 -> x23, local copies, waits for them, and re-layouts: 2.55 us -> 4.14 us
  transfers between devices with their start and end apart: 41 -> 41, of which waited for: 17 -> 18; matrix products, arithmetic and copies ran while one was open for 9% -> 10% of each run, Pallas kernels for 11% -> 12%
where the time goes in v7:
time: 179 us; the launch traced here: 177 us
  waiting for transfers between devices  70.9 us (40%)
  starting transfers between devices  52.1 us (29%)
  Pallas kernels  26.5 us (15%)
  other arithmetic  17.2 us (10%)
  local copies, waits for them, and re-layouts  9.62 us (5%)
    ppermute x18, waiting for transfers between devices, along_x(): return lax.ppermute(value, ('row', 'col'), pairs)  50.1 us
    pallas_call x6, Pallas kernels, local_kernel(): pl.pallas_call(body, grid=grid, in_specs=in_specs, out_specs=out_specs, o...  26.5 us
    ppermute x14, starting transfers between devices, plane(): return lax.ppermute(value, ('col', 'depth'), pairs)  25.1 us
    ppermute x18, starting transfers between devices, along_x(): return lax.ppermute(value, ('row', 'col'), pairs)  24.7 us
    ppermute x14, waiting for transfers between devices, plane(): return lax.ppermute(value, ('col', 'depth'), pairs)  18.6 us
    concatenate x11, other arithmetic, join(): return jnp.concatenate(parts, axis=axis)  6.12 us
    unnamed x23, local copies, waits for them, and re-layouts  4.14 us
  transfers between devices with their start and end apart: 41, of which 18 were waited for; matrix products, arithmetic and copies ran while one was open for 10% of the time, Pallas kernels for 12%

profile of v7, /device:TPU:0, one launch (start us, length us, event | category | flops | bytes accessed | tf_op | source)
XLA Modules:
  0.0 177.5 jit_solution(8658503707036978056)
XLA Ops:
  0.7 1.0 fusion.11
  1.7 1.6 collective-permute-start
  3.4 2.7 %collective-permute-start.1 = (bf16[2,32,768]{2,1,0:T(8,128)(2,1)S(1)}, bf16[2,32,768]{2,1,0:T(8,128)(2,1)S(1)}, u32[]{:S(2)}, u32[]{:S(2)}) collective-permute-start(bf16[2,32,768]{2,1,0:T(8,128)(2,1)S(1)} %get-tuple-element.130), channel_id=1, source_target_pairs={{0,64},{16,80},{32,96},{48,112},{64,0},{80,16},{96,32},{112,48},{1... | collective-permute-start | bytes 294920 | tf_op jit(solution)/shard_map/ppermute | solution.py:140
  6.1 1.4 collective-permute-start.2
  8.1 2.6 %collective-permute-start.9 = (bf16[384,768]{1,0:T(8,128)(2,1)}, bf16[384,768]{1,0:T(8,128)(2,1)S(1)}, u32[]{:S(2)}, u32[]{:S(2)}) collective-permute-start(bf16[384,768]{1,0:T(8,128)(2,1)} %param.6), channel_id=1, source_target_pairs={{0,96},{16,48},{32,0},{48,80},{64,32},{80,112},{96,64},{112,16},{1... | collective-permute-start | bytes 1769480 | tf_op jit(solution)/shard_map/ppermute | solution.py:140
  12.0 2.0 %collective-permute-start.3 = (bf16[2,32,3072]{2,1,0:T(8,128)(2,1)S(1)}, bf16[2,32,3072]{2,1,0:T(8,128)(2,1)S(1)}, u32[]{:S(2)}, u32[]{:S(2)}) collective-permute-start(bf16[2,32,3072]{2,1,0:T(8,128)(2,1)S(1)} %get-tuple-element.127), channel_id=1, source_target_pairs={{0,4},{1,5},{2,6},{3,7},{4,8},{5,9},{6,10},{7,11},{8,12},{9,13},{1... | collective-permute-start | bytes 1179656 | tf_op jit(solution)/shard_map/ppermute | solution.py:157
  13.9 3.6 %collective-permute-start.4 = (bf16[2,32,3072]{2,1,0:T(8,128)(2,1)S(1)}, bf16[2,32,3072]{2,1,0:T(8,128)(2,1)S(1)}, u32[]{:S(2)}, u32[]{:S(2)}) collective-permute-start(bf16[2,32,3072]{2,1,0:T(8,128)(2,1)S(1)} %get-tuple-element.127), channel_id=1, source_target_pairs={{0,8},{1,9},{2,10},{3,11},{4,12},{5,13},{6,14},{7,15},{8,0},{9,1},... | collective-permute-start | bytes 1179656 | tf_op jit(solution)/shard_map/ppermute | solution.py:157
  18.5 5.6 %collective-permute-done.8 = bf16[768,384]{1,0:T(8,128)(2,1)S(1)} collective-permute-done((bf16[768,384]{1,0:T(8,128)(2,1)}, bf16[768,384]{1,0:T(8,128)(2,1)S(1)}, u32[]{:S(2)}, u32[]{:S(2)}) %collective-permute-start.8) | collective-permute-done | bytes 589856 | tf_op jit(solution)/shard_map/ppermute | solution.py:140
  24.2 3.2 %collective-permute-start.12 = (bf16[384,768]{1,0:T(8,128)(2,1)S(1)}, bf16[384,768]{1,0:T(8,128)(2,1)S(1)}, u32[]{:S(2)}, u32[]{:S(2)}) collective-permute-start(bf16[384,768]{1,0:T(8,128)(2,1)S(1)} %collective-permute-done.9), channel_id=1, source_target_pairs={{0,96},{16,48},{32,0},{48,80},{64,32},{80,112},{96,64},{112,16},{1... | collective-permute-start | bytes 1769480 | tf_op jit(solution)/shard_map/ppermute | solution.py:140
  27.6 1.6 collective-permute-start.6
  29.3 1.7 collective-permute-start.7
  31.1 10.2 %collective-permute-done.11 = bf16[768,384]{1,0:T(8,128)(2,1)S(1)} collective-permute-done((bf16[768,384]{1,0:T(8,128)(2,1)S(1)}, bf16[768,384]{1,0:T(8,128)(2,1)S(1)}, u32[]{:S(2)}, u32[]{:S(2)}) %collective-permute-start.11) | collective-permute-done | bytes 589856 | tf_op jit(solution)/shard_map/ppermute | solution.py:140
  41.4 3.2 %collective-permute-start.15 = (bf16[384,768]{1,0:T(8,128)(2,1)S(1)}, bf16[384,768]{1,0:T(8,128)(2,1)S(1)}, u32[]{:S(2)}, u32[]{:S(2)}) collective-permute-start(bf16[384,768]{1,0:T(8,128)(2,1)S(1)} %collective-permute-done.12), channel_id=1, source_target_pairs={{0,96},{16,48},{32,0},{48,80},{64,32},{80,112},{96,64},{112,16},{1... | collective-permute-start | bytes 1769480 | tf_op jit(solution)/shard_map/ppermute | solution.py:140
  44.7 13.0 %collective-permute-done.13 = bf16[768,384]{1,0:T(8,128)(2,1)S(1)} collective-permute-done((bf16[768,384]{1,0:T(8,128)(2,1)S(1)}, bf16[768,384]{1,0:T(8,128)(2,1)S(1)}, u32[]{:S(2)}, u32[]{:S(2)}) %collective-permute-start.13) | collective-permute-done | bytes 589856 | tf_op jit(solution)/shard_map/ppermute | solution.py:140
  59.0 1.5 collective-permute-done.14
  62.7 1.6 collective-permute-start.17
  65.2 1.7 collective-permute-start.18
  67.9 1.8 %pad_maximum_fusion.5 = bf16[384,3072]{1,0:T(8,128)(2,1)S(1)} fusion(bf16[384,768]{1,0:T(8,128)(2,1)S(1)} %get-tuple-element.113, bf16[384,768]{1,0:T(8,128)(2,1)S(1)} %get-tuple-element.114, bf16[384,768]{1,0:T(8,128)(2,1)} %collective-permute-done.16, bf16[384,768]{1,0:T(8,128)(2,1)S(1)} %get-tuple-element.112), kind=kLoop, calls=%fused_computation.6 | loop fusion | flops 9437184 | bytes 4718592 | tf_op jit(solution)/shard_map/concatenate | solution.py:193
  70.1 4.9 %shard_map.75 = (bf16[384,768]{1,0:T(8,128)(2,1)S(1)}, bf16[384,768]{1,0:T(8,128)(2,1)S(1)}) custom-call(bf16[2,384,3072]{2,1,0:T(8,128)(2,1)S(1)} %constant_dynamic-update-slice_fusion.pair_ref.refs_0_, bf16[3072,768]{1,0:T(8,128)(2,1)S(1)} %pad_maximum_fusion.up_ref, bf16[768,3072]{1,0:T(8,128)(2,1)S(1)} %pad_maximum_fusion.1.down_ref), custom_call_target="tpu_custom_call" | custom-call | flops 1 | bytes 1 | tf_op jit(solution)/shard_map/pallas_call | solution.py:30
  75.0 1.2 collective-permute-done.17
  76.1 1.3 collective-permute-done.18
  77.5 3.0 %shard_map.76 = (bf16[128,768]{1,0:T(8,128)(2,1)S(1)}, bf16[128,768]{1,0:T(8,128)(2,1)S(1)}) custom-call(bf16[2,128,3072]{2,1,0:T(8,128)(2,1)S(1)} %constant_dynamic-update-slice_fusion.6.pair_ref.refs_1_, bf16[3072,768]{1,0:T(8,128)(2,1)S(1)} %pad_maximum_fusion.up_ref, bf16[768,3072]{1,0:T(8,128)(2,1)S(1)} %pad_maximum_fusion.1.down_ref), custom_call_target="tpu_custom_call" | custom-call | flops 1 | bytes 1 | tf_op jit(solution)/shard_map/pallas_call | solution.py:30
  80.5 3.1 %shard_map.77 = bf16[2,128,3072]{2,1,0:T(8,128)(2,1)S(1)} custom-call(bf16[128,768]{1,0:T(8,128)(2,1)S(1)} %get-tuple-element.87.act_ref.refs_3_, bf16[128,768]{1,0:T(8,128)(2,1)S(1)} %get-tuple-element.89.grad_ref.refs_5_, bf16[3072,768]{1,0:T(8,128)(2,1)S(1)} %pad_maximum_fusion.up_ref, bf16[768,3072]{1,0:T(8,128)(2,1)S(1)} %pad_maximum_fusion.1.down_ref), custom_call_target="tpu_custom_call" | custom-call | flops 1 | bytes 1 | tf_op jit(solution)/shard_map/pallas_call | solution.py:30
  83.7 2.9 %collective-permute-start.21 = (bf16[2,64,3072]{2,1,0:T(8,128)(2,1)S(1)}, bf16[2,64,3072]{2,1,0:T(8,128)(2,1)S(1)}, u32[]{:S(2)}, u32[]{:S(2)}) collective-permute-start(bf16[2,64,3072]{2,1,0:T(8,128)(2,1)S(1)} %get-tuple-element.81), channel_id=1, source_target_pairs={{0,3},{1,0},{2,1},{3,2},{4,7},{5,4},{6,5},{7,6},{8,11},{9,8},{10,9... | collective-permute-start | bytes 2359304 | tf_op jit(solution)/shard_map/ppermute | solution.py:157
  86.7 5.0 %shard_map.78 = bf16[2,384,3072]{2,1,0:T(8,128)(2,1)S(1)} custom-call(bf16[384,768]{1,0:T(8,128)(2,1)S(1)} %get-tuple-element.86.act_ref.refs_2_, bf16[384,768]{1,0:T(8,128)(2,1)S(1)} %get-tuple-element.88.grad_ref.refs_4_, bf16[3072,768]{1,0:T(8,128)(2,1)S(1)} %pad_maximum_fusion.up_ref, bf16[768,3072]{1,0:T(8,128)(2,1)S(1)} %pad_maximum_fusion.1.down_ref), custom_call_target="tpu_custom_call" | custom-call | flops 1 | bytes 1 | tf_op jit(solution)/shard_map/pallas_call | solution.py:30
  91.7 5.3 %shard_map.79 = (bf16[4,384,768]{2,1,0:T(8,128)(2,1)S(1)}, bf16[4,768,384]{2,1,0:T(8,128)(2,1)S(1)}) custom-call(bf16[2,384,3072]{2,1,0:T(8,128)(2,1)S(1)} %constant_dynamic-update-slice_fusion.pair_ref.refs_0_, bf16[2,128,3072]{2,1,0:T(8,128)(2,1)S(1)} %constant_dynamic-update-slice_fusion.6.pair_ref.refs_1_, ...), custom_call_target="tpu_custom_call" | custom-call | flops 1 | bytes 1 | tf_op jit(solution)/shard_map/pallas_call | solution.py:30
  97.0 2.9 %collective-permute-done.22 = bf16[2,64,3072]{2,1,0:T(8,128)(2,1)S(1)} collective-permute-done((bf16[2,64,3072]{2,1,0:T(8,128)(2,1)S(1)}, bf16[2,64,3072]{2,1,0:T(8,128)(2,1)S(1)}, u32[]{:S(2)}, u32[]{:S(2)}) %collective-permute-start.22) | collective-permute-done | bytes 786464 | tf_op jit(solution)/shard_map/ppermute | solution.py:157
  100.6 1.3 pad_maximum_fusion.9
  101.9 1.3 pad_maximum_fusion.8
  103.1 3.2 %collective-permute-start.23 = (bf16[2,128,3072]{2,1,0:T(8,128)(2,1)}, bf16[2,128,3072]{2,1,0:T(8,128)(2,1)}, u32[]{:S(2)}, u32[]{:S(2)}) collective-permute-start(bf16[2,128,3072]{2,1,0:T(8,128)(2,1)} %pad_maximum_fusion.8), channel_id=1, source_target_pairs={{0,3},{1,0},{2,1},{3,2},{4,7},{5,4},{6,5},{7,6},{8,11},{9,8},{10,9... | collective-permute-start | bytes 4718600 | tf_op jit(solution)/shard_map/ppermute | solution.py:157
  108.6 2.3 %copy-done.1 = bf16[2,384,3072]{2,1,0:T(8,128)(2,1)S(1)} copy-done((bf16[2,384,3072]{2,1,0:T(8,128)(2,1)S(1)}, bf16[2,384,3072]{2,1,0:T(8,128)(2,1)}, u32[]{:S(2)}) %copy-start.1) | copy-done | bytes 4718616
  110.9 5.3 %shard_map.80 = (bf16[4,384,768]{2,1,0:T(8,128)(2,1)S(1)}, bf16[4,768,384]{2,1,0:T(8,128)(2,1)S(1)}) custom-call(bf16[2,384,3072]{2,1,0:T(8,128)(2,1)S(1)} %copy-done.1, bf16[2,128,3072]{2,1,0:T(8,128)(2,1)S(1)} %constant_dynamic-update-slice_fusion.6.pair_ref.refs_1_, bf16[384,768]{1,0:T(8,128)(2,1)S(1)} %get-tuple-element.86.act_ref.refs_2_, ...), custom_call_target="tpu_custom_call" | custom-call | flops 1 | bytes 1 | tf_op jit(solution)/shard_map/pallas_call | solution.py:30
  116.4 1.5 copy-done.4
  118.1 1.2 fusion
  119.4 4.4 %collective-permute-done.24 = bf16[2,128,3072]{2,1,0:T(8,128)(2,1)} collective-permute-done((bf16[2,128,3072]{2,1,0:T(8,128)(2,1)}, bf16[2,128,3072]{2,1,0:T(8,128)(2,1)}, u32[]{:S(2)}, u32[]{:S(2)}) %collective-permute-start.24) | collective-permute-done | bytes 1572896 | tf_op jit(solution)/shard_map/ppermute | solution.py:157
  124.6 1.2 fusion.1
  126.5 3.1 %add_convert_fusion = bf16[2,128,3072]{2,1,0:T(8,128)(2,1)S(1)} fusion(bf16[2,128,3072]{2,1,0:T(8,128)(2,1)} %collective-permute-done.24, bf16[2,128,3072]{2,1,0:T(8,128)(2,1)} %collective-permute-done.23, bf16[2,384,3072]{2,1,0:T(8,128)(2,1)} %copy-done.2), kind=kLoop, calls=%fused_computation.2 | loop fusion | flops 4718592 | bytes 6291456 | tf_op jit(solution)/shard_map/convert_element_type | solution.py:270
  129.8 4.1 %collective-permute-start.25 = (bf16[2,32,3072]{2,1,0:T(8,128)(2,1)S(1)}, bf16[2,32,3072]{2,1,0:T(8,128)(2,1)S(1)}, u32[]{:S(2)}, u32[]{:S(2)}) collective-permute-start(bf16[2,32,3072]{2,1,0:T(8,128)(2,1)S(1)} %get-tuple-element.115), channel_id=1, source_target_pairs={{0,12},{1,13},{2,14},{3,15},{4,0},{5,1},{6,2},{7,3},{8,4},{9,5},{1... | collective-permute-start | bytes 1179656 | tf_op jit(solution)/shard_map/ppermute | solution.py:157
  135.8 1.1 collective-permute-start.35
  137.1 2.3 %collective-permute-start.31 = (bf16[384,768]{1,0:T(8,128)(2,1)S(1)}, bf16[384,768]{1,0:T(8,128)(2,1)S(1)}, u32[]{:S(2)}, u32[]{:S(2)}) collective-permute-start(bf16[384,768]{1,0:T(8,128)(2,1)S(1)} %fusion.5), channel_id=1, source_target_pairs={{0,96},{16,48},{32,0},{48,80},{64,32},{80,112},{96,64},{112,16},{1... | collective-permute-start | bytes 1769480 | tf_op jit(solution)/shard_map/ppermute | solution.py:140
  139.4 3.9 %collective-permute-done.25 = bf16[2,32,3072]{2,1,0:T(8,128)(2,1)S(1)} collective-permute-done((bf16[2,32,3072]{2,1,0:T(8,128)(2,1)S(1)}, bf16[2,32,3072]{2,1,0:T(8,128)(2,1)S(1)}, u32[]{:S(2)}, u32[]{:S(2)}) %collective-permute-start.25) | collective-permute-done | bytes 393248 | tf_op jit(solution)/shard_map/ppermute | solution.py:157
  143.4 4.0 %collective-permute-done.27 = bf16[2,32,3072]{2,1,0:T(8,128)(2,1)S(1)} collective-permute-done((bf16[2,32,3072]{2,1,0:T(8,128)(2,1)S(1)}, bf16[2,32,3072]{2,1,0:T(8,128)(2,1)S(1)}, u32[]{:S(2)}, u32[]{:S(2)}) %collective-permute-start.27) | collective-permute-done | bytes 393248 | tf_op jit(solution)/shard_map/ppermute | solution.py:157
  147.6 5.5 %collective-permute-done.35 = bf16[768,384]{1,0:T(8,128)(2,1)S(1)} collective-permute-done((bf16[768,384]{1,0:T(8,128)(2,1)S(1)}, bf16[768,384]{1,0:T(8,128)(2,1)S(1)}, u32[]{:S(2)}, u32[]{:S(2)}) %collective-permute-start.35) | collective-permute-done | bytes 589856 | tf_op jit(solution)/shard_map/ppermute | solution.py:140
  154.1 1.6 collective-permute-start.39
  155.9 3.2 %collective-permute-start.37 = (bf16[2,32,768]{2,1,0:T(8,128)(2,1)S(1)}, bf16[2,32,768]{2,1,0:T(8,128)(2,1)S(1)}, u32[]{:S(2)}, u32[]{:S(2)}) collective-permute-start(bf16[2,32,768]{2,1,0:T(8,128)(2,1)S(1)} %pad_maximum_fusion.13), channel_id=1, source_target_pairs={{0,64},{16,80},{32,96},{48,112},{64,0},{80,16},{96,32},{112,48},{1... | collective-permute-start | bytes 294920 | tf_op jit(solution)/shard_map/ppermute | solution.py:140
  159.4 13.9 %collective-permute-done.36 = bf16[2,32,768]{2,1,0:T(8,128)(2,1)S(1)} collective-permute-done((bf16[2,32,768]{2,1,0:T(8,128)(2,1)S(1)}, bf16[2,32,768]{2,1,0:T(8,128)(2,1)S(1)}, u32[]{:S(2)}, u32[]{:S(2)}) %collective-permute-start.36) | collective-permute-done | bytes 98336 | tf_op jit(solution)/shard_map/ppermute | solution.py:140
  174.9 1.3 bitcast_add_fusion.1
  176.2 1.3 bitcast_add_fusion.3
  (117 shorter events, 19.5 us)
Async XLA Ops:
  1.7 9.1 %collective-permute-start = (bf16[2,32,768]{2,1,0:T(8,128)(2,1)S(1)}, bf16[2,32,768]{2,1,0:T(8,128)(2,1)S(1)}, u32[]{:S(2)}, u32[]{:S(2)}) collective-permute-start(bf16[2,32,768]{2,1,0:T(8,128)(2,1)S(1)} %get-tuple-element.129), channel_id=1, source_target_pairs={{0,32},{16,112},{32,64},{48,16},{64,96},{80,48},{96,0},{112,80},{1... | collective-permute-start | bytes 294920 | tf_op jit(solution)/shard_map/ppermute | solution.py:140
  3.4 7.9 %collective-permute-start.1 = (bf16[2,32,768]{2,1,0:T(8,128)(2,1)S(1)}, bf16[2,32,768]{2,1,0:T(8,128)(2,1)S(1)}, u32[]{:S(2)}, u32[]{:S(2)}) collective-permute-start(bf16[2,32,768]{2,1,0:T(8,128)(2,1)S(1)} %get-tuple-element.130), channel_id=1, source_target_pairs={{0,64},{16,80},{32,96},{48,112},{64,0},{80,16},{96,32},{112,48},{1... | collective-permute-start | bytes 294920 | tf_op jit(solution)/shard_map/ppermute | solution.py:140
  6.1 5.7 %collective-permute-start.2 = (bf16[2,32,768]{2,1,0:T(8,128)(2,1)S(1)}, bf16[2,32,768]{2,1,0:T(8,128)(2,1)S(1)}, u32[]{:S(2)}, u32[]{:S(2)}) collective-permute-start(bf16[2,32,768]{2,1,0:T(8,128)(2,1)S(1)} %get-tuple-element.131), channel_id=1, source_target_pairs={{0,96},{16,48},{32,0},{48,80},{64,32},{80,112},{96,64},{112,16},{1... | collective-permute-start | bytes 294920 | tf_op jit(solution)/shard_map/ppermute | solution.py:140
  7.5 16.6 %collective-permute-start.8 = (bf16[768,384]{1,0:T(8,128)(2,1)}, bf16[768,384]{1,0:T(8,128)(2,1)S(1)}, u32[]{:S(2)}, u32[]{:S(2)}) collective-permute-start(bf16[768,384]{1,0:T(8,128)(2,1)} %param.5), channel_id=1, source_target_pairs={{0,32},{16,112},{32,64},{48,16},{64,96},{80,48},{96,0},{112,80},{1... | collective-permute-start | bytes 1769480 | tf_op jit(solution)/shard_map/ppermute | solution.py:140
  8.1 16.1 %collective-permute-start.9 = (bf16[384,768]{1,0:T(8,128)(2,1)}, bf16[384,768]{1,0:T(8,128)(2,1)S(1)}, u32[]{:S(2)}, u32[]{:S(2)}) collective-permute-start(bf16[384,768]{1,0:T(8,128)(2,1)} %param.6), channel_id=1, source_target_pairs={{0,96},{16,48},{32,0},{48,80},{64,32},{80,112},{96,64},{112,16},{1... | collective-permute-start | bytes 1769480 | tf_op jit(solution)/shard_map/ppermute | solution.py:140
  11.9 19.1 %copy-start.8 = (bf16[768,384]{1,0:T(8,128)(2,1)S(1)}, bf16[768,384]{1,0:T(8,128)(2,1)}, u32[]{:S(2)}) copy-start(bf16[768,384]{1,0:T(8,128)(2,1)} %param.5) | copy-start | bytes 1769476
  12.0 15.4 %collective-permute-start.3 = (bf16[2,32,3072]{2,1,0:T(8,128)(2,1)S(1)}, bf16[2,32,3072]{2,1,0:T(8,128)(2,1)S(1)}, u32[]{:S(2)}, u32[]{:S(2)}) collective-permute-start(bf16[2,32,3072]{2,1,0:T(8,128)(2,1)S(1)} %get-tuple-element.127), channel_id=1, source_target_pairs={{0,4},{1,5},{2,6},{3,7},{4,8},{5,9},{6,10},{7,11},{8,12},{9,13},{1... | collective-permute-start | bytes 1179656 | tf_op jit(solution)/shard_map/ppermute | solution.py:157
  13.9 13.5 %collective-permute-start.4 = (bf16[2,32,3072]{2,1,0:T(8,128)(2,1)S(1)}, bf16[2,32,3072]{2,1,0:T(8,128)(2,1)S(1)}, u32[]{:S(2)}, u32[]{:S(2)}) collective-permute-start(bf16[2,32,3072]{2,1,0:T(8,128)(2,1)S(1)} %get-tuple-element.127), channel_id=1, source_target_pairs={{0,8},{1,9},{2,10},{3,11},{4,12},{5,13},{6,14},{7,15},{8,0},{9,1},... | collective-permute-start | bytes 1179656 | tf_op jit(solution)/shard_map/ppermute | solution.py:157
  17.5 10.0 %collective-permute-start.5 = (bf16[2,32,3072]{2,1,0:T(8,128)(2,1)S(1)}, bf16[2,32,3072]{2,1,0:T(8,128)(2,1)S(1)}, u32[]{:S(2)}, u32[]{:S(2)}) collective-permute-start(bf16[2,32,3072]{2,1,0:T(8,128)(2,1)S(1)} %get-tuple-element.127), channel_id=1, source_target_pairs={{0,12},{1,13},{2,14},{3,15},{4,0},{5,1},{6,2},{7,3},{8,4},{9,5},{1... | collective-permute-start | bytes 1179656 | tf_op jit(solution)/shard_map/ppermute | solution.py:157
  24.2 17.2 %collective-permute-start.11 = (bf16[768,384]{1,0:T(8,128)(2,1)S(1)}, bf16[768,384]{1,0:T(8,128)(2,1)S(1)}, u32[]{:S(2)}, u32[]{:S(2)}) collective-permute-start(bf16[768,384]{1,0:T(8,128)(2,1)S(1)} %collective-permute-done.8), channel_id=1, source_target_pairs={{0,32},{16,112},{32,64},{48,16},{64,96},{80,48},{96,0},{112,80},{1... | collective-permute-start | bytes 1769480 | tf_op jit(solution)/shard_map/ppermute | solution.py:140
  24.2 17.2 %collective-permute-start.12 = (bf16[384,768]{1,0:T(8,128)(2,1)S(1)}, bf16[384,768]{1,0:T(8,128)(2,1)S(1)}, u32[]{:S(2)}, u32[]{:S(2)}) collective-permute-start(bf16[384,768]{1,0:T(8,128)(2,1)S(1)} %collective-permute-done.9), channel_id=1, source_target_pairs={{0,96},{16,48},{32,0},{48,80},{64,32},{80,112},{96,64},{112,16},{1... | collective-permute-start | bytes 1769480 | tf_op jit(solution)/shard_map/ppermute | solution.py:140
  27.6 30.6 %copy-start.7 = (bf16[384,768]{1,0:T(8,128)(2,1)S(1)}, bf16[384,768]{1,0:T(8,128)(2,1)}, u32[]{:S(2)}) copy-start(bf16[384,768]{1,0:T(8,128)(2,1)} %param.6) | copy-start | bytes 1769476
  27.6 30.9 %collective-permute-start.6 = (bf16[2,128,3072]{2,1,0:T(8,128)(2,1)S(1)}, bf16[2,128,3072]{2,1,0:T(8,128)(2,1)S(1)}, u32[]{:S(2)}, u32[]{:S(2)}) collective-permute-start(bf16[2,128,3072]{2,1,0:T(8,128)(2,1)S(1)} %pad_maximum_fusion.7), channel_id=1, source_target_pairs={{0,1},{1,2},{2,3},{3,0},{4,5},{5,6},{6,7},{7,4},{8,9},{9,10},{10,1... | collective-permute-start | bytes 4718600 | tf_op jit(solution)/shard_map/ppermute | solution.py:157
  29.3 29.7 %collective-permute-start.7 = (bf16[2,128,3072]{2,1,0:T(8,128)(2,1)S(1)}, bf16[2,128,3072]{2,1,0:T(8,128)(2,1)S(1)}, u32[]{:S(2)}, u32[]{:S(2)}) collective-permute-start(bf16[2,128,3072]{2,1,0:T(8,128)(2,1)S(1)} %pad_maximum_fusion.7), channel_id=1, source_target_pairs={{0,3},{1,0},{2,1},{3,2},{4,7},{5,4},{6,5},{7,6},{8,11},{9,8},{10,9... | collective-permute-start | bytes 4718600 | tf_op jit(solution)/shard_map/ppermute | solution.py:157
  31.0 27.3 %collective-permute-start.10 = (bf16[1536,384]{1,0:T(8,128)(2,1)S(1)}, bf16[1536,384]{1,0:T(8,128)(2,1)S(1)}, u32[]{:S(2)}, u32[]{:S(2)}) collective-permute-start(bf16[1536,384]{1,0:T(8,128)(2,1)S(1)} %pad_maximum_fusion.10), channel_id=1, source_target_pairs={{0,16},{16,0},{1,17},{17,1},{2,18},{18,2},{3,19},{19,3},{4,20},{20... | collective-permute-start | bytes 3538952 | tf_op jit(solution)/shard_map/ppermute | solution.py:144
  41.4 16.3 %collective-permute-start.13 = (bf16[768,384]{1,0:T(8,128)(2,1)S(1)}, bf16[768,384]{1,0:T(8,128)(2,1)S(1)}, u32[]{:S(2)}, u32[]{:S(2)}) collective-permute-start(bf16[768,384]{1,0:T(8,128)(2,1)S(1)} %collective-permute-done.11), channel_id=1, source_target_pairs={{0,32},{16,112},{32,64},{48,16},{64,96},{80,48},{96,0},{112,80},{1... | collective-permute-start | bytes 1769480 | tf_op jit(solution)/shard_map/ppermute | solution.py:140
  41.4 16.3 %collective-permute-start.15 = (bf16[384,768]{1,0:T(8,128)(2,1)S(1)}, bf16[384,768]{1,0:T(8,128)(2,1)S(1)}, u32[]{:S(2)}, u32[]{:S(2)}) collective-permute-start(bf16[384,768]{1,0:T(8,128)(2,1)S(1)} %collective-permute-done.12), channel_id=1, source_target_pairs={{0,96},{16,48},{32,0},{48,80},{64,32},{80,112},{96,64},{112,16},{1... | collective-permute-start | bytes 1769480 | tf_op jit(solution)/shard_map/ppermute | solution.py:140
  57.7 2.8 %collective-permute-start.14 = (bf16[768,384]{1,0:T(8,128)(2,1)S(1)}, bf16[768,384]{1,0:T(8,128)(2,1)S(1)}, u32[]{:S(2)}, u32[]{:S(2)}) collective-permute-start(bf16[768,384]{1,0:T(8,128)(2,1)S(1)} %collective-permute-done.13), channel_id=1, source_target_pairs={{0,16},{16,0},{1,17},{17,1},{2,18},{18,2},{3,19},{19,3},{4,20},{20... | collective-permute-start | bytes 1769480 | tf_op jit(solution)/shard_map/ppermute | solution.py:144
  57.7 3.4 %collective-permute-start.16 = (bf16[384,768]{1,0:T(8,128)(2,1)S(1)}, bf16[384,768]{1,0:T(8,128)(2,1)}, u32[]{:S(2)}, u32[]{:S(2)}) collective-permute-start(bf16[384,768]{1,0:T(8,128)(2,1)S(1)} %collective-permute-done.15), channel_id=1, source_target_pairs={{0,16},{16,0},{1,17},{17,1},{2,18},{18,2},{3,19},{19,3},{4,20},{20... | collective-permute-start | bytes 1769480 | tf_op jit(solution)/shard_map/ppermute | solution.py:144
  58.4 3.1 %collective-permute-start.19 = (bf16[768,384]{1,0:T(8,128)(2,1)S(1)}, bf16[768,384]{1,0:T(8,128)(2,1)S(1)}, u32[]{:S(2)}, u32[]{:S(2)}) collective-permute-start(bf16[768,384]{1,0:T(8,128)(2,1)S(1)} %collective-permute-done.11), channel_id=1, source_target_pairs={{0,16},{16,0},{1,17},{17,1},{2,18},{18,2},{3,19},{19,3},{4,20},{20... | collective-permute-start | bytes 1769480 | tf_op jit(solution)/shard_map/ppermute | solution.py:144
  58.5 9.3 %collective-permute-start.20 = (bf16[384,2304]{1,0:T(8,128)(2,1)S(1)}, bf16[384,2304]{1,0:T(8,128)(2,1)S(1)}, u32[]{:S(2)}, u32[]{:S(2)}) collective-permute-start(bf16[384,2304]{1,0:T(8,128)(2,1)S(1)} %pad_maximum_fusion.6), channel_id=1, source_target_pairs={{0,16},{16,0},{1,17},{17,1},{2,18},{18,2},{3,19},{19,3},{4,20},{20... | collective-permute-start | bytes 5308424 | tf_op jit(solution)/shard_map/ppermute | solution.py:144
  62.7 13.4 %collective-permute-start.17 = (bf16[2,64,3072]{2,1,0:T(8,128)(2,1)}, bf16[2,64,3072]{2,1,0:T(8,128)(2,1)S(1)}, u32[]{:S(2)}, u32[]{:S(2)}) collective-permute-start(bf16[2,64,3072]{2,1,0:T(8,128)(2,1)} %slice.190), channel_id=1, source_target_pairs={{0,1},{1,2},{2,3},{3,0},{4,5},{5,6},{6,7},{7,4},{8,9},{9,10},{10,1... | collective-permute-start | bytes 2359304 | tf_op jit(solution)/shard_map/ppermute | solution.py:157
  65.2 12.2 %collective-permute-start.18 = (bf16[2,64,3072]{2,1,0:T(8,128)(2,1)}, bf16[2,64,3072]{2,1,0:T(8,128)(2,1)S(1)}, u32[]{:S(2)}, u32[]{:S(2)}) collective-permute-start(bf16[2,64,3072]{2,1,0:T(8,128)(2,1)} %slice.191), channel_id=1, source_target_pairs={{0,3},{1,0},{2,1},{3,2},{4,7},{5,4},{6,5},{7,6},{8,11},{9,8},{10,9... | collective-permute-start | bytes 2359304 | tf_op jit(solution)/shard_map/ppermute | solution.py:157
  67.1 24.6 %copy-start = (bf16[2,384,3072]{2,1,0:T(8,128)(2,1)}, bf16[2,384,3072]{2,1,0:T(8,128)(2,1)S(1)}, u32[]{:S(2)}) copy-start(bf16[2,384,3072]{2,1,0:T(8,128)(2,1)S(1)} %constant_dynamic-update-slice_fusion.pair_ref.refs_0_) | copy-start | bytes 14155780
  83.7 13.3 %collective-permute-start.21 = (bf16[2,64,3072]{2,1,0:T(8,128)(2,1)S(1)}, bf16[2,64,3072]{2,1,0:T(8,128)(2,1)S(1)}, u32[]{:S(2)}, u32[]{:S(2)}) collective-permute-start(bf16[2,64,3072]{2,1,0:T(8,128)(2,1)S(1)} %get-tuple-element.81), channel_id=1, source_target_pairs={{0,3},{1,0},{2,1},{3,2},{4,7},{5,4},{6,5},{7,6},{8,11},{9,8},{10,9... | collective-permute-start | bytes 2359304 | tf_op jit(solution)/shard_map/ppermute | solution.py:157
  86.7 13.2 %collective-permute-start.22 = (bf16[2,64,3072]{2,1,0:T(8,128)(2,1)S(1)}, bf16[2,64,3072]{2,1,0:T(8,128)(2,1)S(1)}, u32[]{:S(2)}, u32[]{:S(2)}) collective-permute-start(bf16[2,64,3072]{2,1,0:T(8,128)(2,1)S(1)} %get-tuple-element.82), channel_id=1, source_target_pairs={{0,1},{1,2},{2,3},{3,0},{4,5},{5,6},{6,7},{7,4},{8,9},{9,10},{10,1... | collective-permute-start | bytes 2359304 | tf_op jit(solution)/shard_map/ppermute | solution.py:157
  91.7 8.3 %copy-start.2 = (bf16[2,384,3072]{2,1,0:T(8,128)(2,1)}, bf16[2,384,3072]{2,1,0:T(8,128)(2,1)S(1)}, u32[]{:S(2)}) copy-start(bf16[2,384,3072]{2,1,0:T(8,128)(2,1)S(1)} %shard_map.78) | copy-start | bytes 14155780
  97.0 9.4 %copy-start.3 = (bf16[4,768,384]{2,1,0:T(8,128)(2,1)}, bf16[4,768,384]{2,1,0:T(8,128)(2,1)S(1)}, u32[]{:S(2)}) copy-start(bf16[4,768,384]{2,1,0:T(8,128)(2,1)S(1)} %get-tuple-element.99) | copy-start | bytes 7077892
  97.0 10.3 %copy-start.5 = (bf16[4,384,768]{2,1,0:T(8,128)(2,1)}, bf16[4,384,768]{2,1,0:T(8,128)(2,1)S(1)}, u32[]{:S(2)}) copy-start(bf16[4,384,768]{2,1,0:T(8,128)(2,1)S(1)} %get-tuple-element.98) | copy-start | bytes 7077892
  101.9 21.9 %collective-permute-start.24 = (bf16[2,128,3072]{2,1,0:T(8,128)(2,1)}, bf16[2,128,3072]{2,1,0:T(8,128)(2,1)}, u32[]{:S(2)}, u32[]{:S(2)}) collective-permute-start(bf16[2,128,3072]{2,1,0:T(8,128)(2,1)} %pad_maximum_fusion.9), channel_id=1, source_target_pairs={{0,1},{1,2},{2,3},{3,0},{4,5},{5,6},{6,7},{7,4},{8,9},{9,10},{10,1... | collective-permute-start | bytes 4718600 | tf_op jit(solution)/shard_map/ppermute | solution.py:157
  103.1 21.5 %collective-permute-start.23 = (bf16[2,128,3072]{2,1,0:T(8,128)(2,1)}, bf16[2,128,3072]{2,1,0:T(8,128)(2,1)}, u32[]{:S(2)}, u32[]{:S(2)}) collective-permute-start(bf16[2,128,3072]{2,1,0:T(8,128)(2,1)} %pad_maximum_fusion.8), channel_id=1, source_target_pairs={{0,3},{1,0},{2,1},{3,2},{4,7},{5,4},{6,5},{7,6},{8,11},{9,8},{10,9... | collective-permute-start | bytes 4718600 | tf_op jit(solution)/shard_map/ppermute | solution.py:157
  108.1 10.0 %collective-permute-start.33 = (bf16[768,384]{1,0:T(8,128)(2,1)}, bf16[768,384]{1,0:T(8,128)(2,1)}, u32[]{:S(2)}, u32[]{:S(2)}) collective-permute-start(bf16[768,384]{1,0:T(8,128)(2,1)} %slice_bitcast_fusion), channel_id=1, source_target_pairs={{0,16},{16,0},{1,17},{17,1},{2,18},{18,2},{3,19},{19,3},{4,20},{20... | collective-permute-start | bytes 1769480 | tf_op jit(solution)/shard_map/ppermute | solution.py:144
  108.1 16.5 %collective-permute-start.29 = (bf16[384,768]{1,0:T(8,128)(2,1)}, bf16[384,768]{1,0:T(8,128)(2,1)}, u32[]{:S(2)}, u32[]{:S(2)}) collective-permute-start(bf16[384,768]{1,0:T(8,128)(2,1)} %slice_bitcast_fusion.1), channel_id=1, source_target_pairs={{0,16},{16,0},{1,17},{17,1},{2,18},{18,2},{3,19},{19,3},{4,20},{20... | collective-permute-start | bytes 1769480 | tf_op jit(solution)/shard_map/ppermute | solution.py:144
  110.9 5.3 %copy-start.6 = (bf16[4,384,768]{2,1,0:T(8,128)(2,1)S(1)}, bf16[4,384,768]{2,1,0:T(8,128)(2,1)}, u32[]{:S(2)}) copy-start(bf16[4,384,768]{2,1,0:T(8,128)(2,1)} %copy-done.5) | copy-start | bytes 7077892
  119.3 14.5 %collective-permute-start.34 = (bf16[768,384]{1,0:T(8,128)(2,1)S(1)}, bf16[768,384]{1,0:T(8,128)(2,1)S(1)}, u32[]{:S(2)}, u32[]{:S(2)}) collective-permute-start(bf16[768,384]{1,0:T(8,128)(2,1)S(1)} %fusion), channel_id=1, source_target_pairs={{0,32},{16,112},{32,64},{48,16},{64,96},{80,48},{96,0},{112,80},{1... | collective-permute-start | bytes 1769480 | tf_op jit(solution)/shard_map/ppermute | solution.py:140
  124.6 10.0 %collective-permute-start.32 = (bf16[3,768,384]{2,1,0:T(8,128)(2,1)S(1)}, bf16[3,768,384]{2,1,0:T(8,128)(2,1)S(1)}, u32[]{:S(2)}, u32[]{:S(2)}) collective-permute-start(bf16[3,768,384]{2,1,0:T(8,128)(2,1)S(1)} %slice.210), channel_id=1, source_target_pairs={{0,16},{16,0},{1,17},{17,1},{2,18},{18,2},{3,19},{19,3},{4,20},{20... | collective-permute-start | bytes 5308424 | tf_op jit(solution)/shard_map/ppermute | solution.py:144
  125.8 10.0 %collective-permute-start.30 = (bf16[384,768]{1,0:T(8,128)(2,1)S(1)}, bf16[384,768]{1,0:T(8,128)(2,1)S(1)}, u32[]{:S(2)}, u32[]{:S(2)}) collective-permute-start(bf16[384,768]{1,0:T(8,128)(2,1)S(1)} %fusion.1), channel_id=1, source_target_pairs={{0,96},{16,48},{32,0},{48,80},{64,32},{80,112},{96,64},{112,16},{1... | collective-permute-start | bytes 1769480 | tf_op jit(solution)/shard_map/ppermute | solution.py:140
  125.9 11.0 %collective-permute-start.28 = (bf16[3,384,768]{2,1,0:T(8,128)(2,1)S(1)}, bf16[3,384,768]{2,1,0:T(8,128)(2,1)S(1)}, u32[]{:S(2)}, u32[]{:S(2)}) collective-permute-start(bf16[3,384,768]{2,1,0:T(8,128)(2,1)S(1)} %slice.209), channel_id=1, source_target_pairs={{0,16},{16,0},{1,17},{17,1},{2,18},{18,2},{3,19},{19,3},{4,20},{20... | collective-permute-start | bytes 5308424 | tf_op jit(solution)/shard_map/ppermute | solution.py:144
  129.8 13.6 %collective-permute-start.25 = (bf16[2,32,3072]{2,1,0:T(8,128)(2,1)S(1)}, bf16[2,32,3072]{2,1,0:T(8,128)(2,1)S(1)}, u32[]{:S(2)}, u32[]{:S(2)}) collective-permute-start(bf16[2,32,3072]{2,1,0:T(8,128)(2,1)S(1)} %get-tuple-element.115), channel_id=1, source_target_pairs={{0,12},{1,13},{2,14},{3,15},{4,0},{5,1},{6,2},{7,3},{8,4},{9,5},{1... | collective-permute-start | bytes 1179656 | tf_op jit(solution)/shard_map/ppermute | solution.py:157
  133.9 9.5 %collective-permute-start.26 = (bf16[2,32,3072]{2,1,0:T(8,128)(2,1)S(1)}, bf16[2,32,3072]{2,1,0:T(8,128)(2,1)S(1)}, u32[]{:S(2)}, u32[]{:S(2)}) collective-permute-start(bf16[2,32,3072]{2,1,0:T(8,128)(2,1)S(1)} %get-tuple-element.116), channel_id=1, source_target_pairs={{0,8},{1,9},{2,10},{3,11},{4,12},{5,13},{6,14},{7,15},{8,0},{9,1},... | collective-permute-start | bytes 1179656 | tf_op jit(solution)/shard_map/ppermute | solution.py:157
  134.6 12.8 %collective-permute-start.27 = (bf16[2,32,3072]{2,1,0:T(8,128)(2,1)S(1)}, bf16[2,32,3072]{2,1,0:T(8,128)(2,1)S(1)}, u32[]{:S(2)}, u32[]{:S(2)}) collective-permute-start(bf16[2,32,3072]{2,1,0:T(8,128)(2,1)S(1)} %get-tuple-element.117), channel_id=1, source_target_pairs={{0,4},{1,5},{2,6},{3,7},{4,8},{5,9},{6,10},{7,11},{8,12},{9,13},{1... | collective-permute-start | bytes 1179656 | tf_op jit(solution)/shard_map/ppermute | solution.py:157
  135.8 17.2 %collective-permute-start.35 = (bf16[768,384]{1,0:T(8,128)(2,1)S(1)}, bf16[768,384]{1,0:T(8,128)(2,1)S(1)}, u32[]{:S(2)}, u32[]{:S(2)}) collective-permute-start(bf16[768,384]{1,0:T(8,128)(2,1)S(1)} %fusion.4), channel_id=1, source_target_pairs={{0,32},{16,112},{32,64},{48,16},{64,96},{80,48},{96,0},{112,80},{1... | collective-permute-start | bytes 1769480 | tf_op jit(solution)/shard_map/ppermute | solution.py:140
  137.1 16.0 %collective-permute-start.31 = (bf16[384,768]{1,0:T(8,128)(2,1)S(1)}, bf16[384,768]{1,0:T(8,128)(2,1)S(1)}, u32[]{:S(2)}, u32[]{:S(2)}) collective-permute-start(bf16[384,768]{1,0:T(8,128)(2,1)S(1)} %fusion.5), channel_id=1, source_target_pairs={{0,96},{16,48},{32,0},{48,80},{64,32},{80,112},{96,64},{112,16},{1... | collective-permute-start | bytes 1769480 | tf_op jit(solution)/shard_map/ppermute | solution.py:140
  153.3 21.6 %collective-permute-start.40 = (bf16[384,768]{1,0:T(8,128)(2,1)S(1)}, bf16[384,768]{1,0:T(8,128)(2,1)S(1)}, u32[]{:S(2)}, u32[]{:S(2)}) collective-permute-start(bf16[384,768]{1,0:T(8,128)(2,1)S(1)} %fusion.2), channel_id=1, source_target_pairs={{0,96},{16,48},{32,0},{48,80},{64,32},{80,112},{96,64},{112,16},{1... | collective-permute-start | bytes 1769480 | tf_op jit(solution)/shard_map/ppermute | solution.py:140
  154.1 22.1 %collective-permute-start.39 = (bf16[768,384]{1,0:T(8,128)(2,1)S(1)}, bf16[768,384]{1,0:T(8,128)(2,1)S(1)}, u32[]{:S(2)}, u32[]{:S(2)}) collective-permute-start(bf16[768,384]{1,0:T(8,128)(2,1)S(1)} %fusion.3), channel_id=1, source_target_pairs={{0,32},{16,112},{32,64},{48,16},{64,96},{80,48},{96,0},{112,80},{1... | collective-permute-start | bytes 1769480 | tf_op jit(solution)/shard_map/ppermute | solution.py:140
  155.8 18.3 %collective-permute-start.38 = (bf16[2,32,768]{2,1,0:T(8,128)(2,1)S(1)}, bf16[2,32,768]{2,1,0:T(8,128)(2,1)S(1)}, u32[]{:S(2)}, u32[]{:S(2)}) collective-permute-start(bf16[2,32,768]{2,1,0:T(8,128)(2,1)S(1)} %pad_maximum_fusion.14), channel_id=1, source_target_pairs={{0,32},{16,112},{32,64},{48,16},{64,96},{80,48},{96,0},{112,80},{1... | collective-permute-start | bytes 294920 | tf_op jit(solution)/shard_map/ppermute | solution.py:140
  155.9 17.4 %collective-permute-start.37 = (bf16[2,32,768]{2,1,0:T(8,128)(2,1)S(1)}, bf16[2,32,768]{2,1,0:T(8,128)(2,1)S(1)}, u32[]{:S(2)}, u32[]{:S(2)}) collective-permute-start(bf16[2,32,768]{2,1,0:T(8,128)(2,1)S(1)} %pad_maximum_fusion.13), channel_id=1, source_target_pairs={{0,64},{16,80},{32,96},{48,112},{64,0},{80,16},{96,32},{112,48},{1... | collective-permute-start | bytes 294920 | tf_op jit(solution)/shard_map/ppermute | solution.py:140
  159.2 14.1 %collective-permute-start.36 = (bf16[2,32,768]{2,1,0:T(8,128)(2,1)S(1)}, bf16[2,32,768]{2,1,0:T(8,128)(2,1)S(1)}, u32[]{:S(2)}, u32[]{:S(2)}) collective-permute-start(bf16[2,32,768]{2,1,0:T(8,128)(2,1)S(1)} %pad_maximum_fusion.12), channel_id=1, source_target_pairs={{0,96},{16,48},{32,0},{48,80},{64,32},{80,112},{96,64},{112,16},{1... | collective-permute-start | bytes 294920 | tf_op jit(solution)/shard_map/ppermute | solution.py:140
  (2 other events, 4.0 us)
